TPU v7x, 128 devices: a whole 4x4x4 slice. The times are simulated.
128 devices in a mesh: gx: 8 (over y, core), gy: 8 (over x, z_hi), sa: 2 (over z_lo).
Axes of the slice: x: 4, y: 4, z: 4 (z_hi: 2, z_lo: 2; z = z_hi * 2 + z_lo), core: 2. Of those that a mesh axis runs over, the one named last changes fastest.
Arguments:
- fields: float32 [2, 7, 32, 64, 512], P('sa', None, 'gx', 'gy'), may hold values from -6 to 6
- sources: float32 [2, 7, 32, 64, 512], P('sa', None, 'gx', 'gy'), may hold values from -5 to 5
- diagonal: float32 [7, 32, 64, 512], P(None, 'gx', 'gy'), may hold values from 0.25 to 2
- block_inverse: float32 [7, 7, 32, 64, 512], P(None, None, 'gx', 'gy'), may hold values from -0.035 to 0.14
- coupling: float32 [7], replicated, may hold values from 0.25 to 0.75
- donors: int32 [64, 3], replicated, may hold values from 0 to 895, as said below
- returns: int32 [8, 896], P('gy'), may hold values from 0 to 63
Outputs:
- fields_out: float32 [2, 7, 32, 64, 512], P('sa', None, 'gx', 'gy')
Inputs may be any that keep to these rules, and one draw needn't show every extreme that they name: `donors`: column 0 is a gy position, column 1 a block index on that position's exit face, column 2 the inflow slot filled; column 2 is a permutation of 0 to 63.
All inputs are finite; a program needn't handle non-finite values.
Results may differ from a plain program's by a relative error of at most 0.00002.
Values sent between devices are 32-bit elements; how exact they have to be, the bound alone decides.
No kernel may reach another device: no remote copies, remote signals or barrier semaphores. Data moves between devices by JAX's collectives and lax.ppermute only.
A program may use at most 128 MiB of HBM per device.

v0:
```python
import jax
import jax.numpy as jnp
from jax import lax
from jax.sharding import PartitionSpec as P

SWEEPS = 4
BLK = 32


def swapped(array, axis, apart):
    return lax.ppermute(array, axis, [(i, i ^ 1 << apart) for i in range(lax.axis_size(axis))])


def padded_2(array, sides, width):
    for axis, dim in sides:
        peers, length = (lax.axis_size(axis), array.shape[dim])
        up = [(i, (i + 1) % peers) for i in range(peers - 1)]
        down = [(j, i) for i, j in up]
        last = lax.slice_in_dim(array, length - width, length, axis=dim)
        initial = lax.slice_in_dim(array, 0, width, axis=dim)
        before = lax.ppermute(last, axis, up)
        after = lax.ppermute(initial, axis, down)
        array = jnp.concatenate([before, array, after], axis=dim)
    return array


def z_terms_combustor(values):
    blank_cap = jnp.zeros_like(values[:1, :, :, :1])
    upper_cap = jnp.concatenate([values[1:, :, :, :1], blank_cap], axis=0)
    lower_cap = jnp.concatenate([blank_cap, values[:-1, :, :, -1:]], axis=0)
    upper_terms = jnp.concatenate([values[:, :, :, 1:], upper_cap], axis=3)
    lower_terms = jnp.concatenate([lower_cap, values[:, :, :, :-1]], axis=3)
    return (upper_terms, lower_terms)


def z_terms_turbine(values, inflow):
    upper_cap = jnp.zeros_like(values[:, :, :, :1])
    lower_cap = jnp.concatenate([inflow[None, :, :, None], values[1:, :, :, :1]], axis=0)
    upper_terms = jnp.concatenate([values[:, :, :, 1:], upper_cap], axis=3)
    lower_terms = jnp.concatenate([lower_cap, values[:, :, :, :-1]], axis=3)
    return (upper_terms, lower_terms)


def neighbour_sum(padded, upper_terms, lower_terms):
    summed = padded[:, 2:, 1:-1] + padded[:, :-2, 1:-1]
    summed = summed + padded[:, 1:-1, 2:] + padded[:, 1:-1, :-2]
    return summed + upper_terms + lower_terms


def apply_inverse(block_inverse, driving):
    result = block_inverse[:, 0] * driving[0]
    for column in range(1, driving.shape[0]):
        result = result + block_inverse[:, column] * driving[column]
    return result


def shards(fields, sources, diagonal, block_inverse, coupling, donors, returns):
    values = fields[0]
    source = sources[0]
    state_stack, cells_x, cells_y, cells_z = values.shape
    rows_x = lax.axis_size("gx")
    vertical_rows = lax.axis_size("gy")
    plane_cell_count = rows_x * vertical_rows
    slot_count = cells_x * cells_y // BLK
    face_count = state_stack * cells_y * cells_z // BLK
    slot_total = donors.shape[0]
    section = lax.axis_index("sa")
    place_x = lax.axis_index("gx")
    placement_vertical = lax.axis_index("gy")
    combustor = section == 0
    at_exit = place_x == rows_x - 1
    matches = donors[None, :, 2] == jnp.arange(slot_total, dtype=jnp.int32)[:, None]
    slot_source = jnp.sum(jnp.where(matches, donors[None, :, 0], 0), axis=1)
    slot_block = jnp.sum(jnp.where(matches, donors[None, :, 1], 0), axis=1)
    exit_face = values[:, cells_x - 1].reshape(face_count, BLK)
    sending = combustor & at_exit & (slot_source == placement_vertical)
    downward = jnp.where(sending[:, None], jnp.take(exit_face, slot_block, axis=0), 0.0)
    downward = downward.reshape(plane_cell_count, slot_count, BLK)
    inlet_blocks = values[0, :, :, 0].reshape(slot_count, BLK)
    exit_rows = jnp.arange(plane_cell_count, dtype=jnp.int32) // vertical_rows == rows_x - 1
    upward = jnp.where(
        (exit_rows & jnp.logical_not(combustor))[:, None, None], inlet_blocks[None], 0.0
    )
    outgoing = jnp.stack([upward, downward], axis=1)
    partner_blocks = swapped(outgoing, "sa", 0)
    arrived = lax.all_to_all(partner_blocks, ("gx", "gy"), split_axis=0, concat_axis=0, tiled=True)
    incoming_blocks = arrived[:, ::-1]
    own_index = place_x * vertical_rows + placement_vertical
    own_sources = lax.dynamic_slice_in_dim(slot_source, own_index * slot_count, slot_count)
    inflow_rows = incoming_blocks[
        (rows_x - 1) * vertical_rows + own_sources, 0, jnp.arange(slot_count)
    ]
    inflow = inflow_rows.reshape(cells_x, cells_y)
    wanted = returns[0]
    pressure_back = incoming_blocks[wanted // slot_count, 1, wanted % slot_count].reshape(
        state_stack, cells_y, cells_z
    )
    back_active = combustor & at_exit
    parity = (
        jnp.arange(cells_x)[:, None, None]
        + jnp.arange(cells_y)[None, :, None]
        + jnp.arange(cells_z)[None, None, :]
    ) % 2
    divisor = 6.0 + diagonal
    weights = coupling[:, None, None, None]
    current = values
    for sweep_index in range(SWEEPS):
        for colour in (0, 1):
            padded = padded_2(current, (("gx", 1), ("gy", 2)), 1)
            padded = padded.at[:, -1, 1:-1, :].set(
                jnp.where(back_active, pressure_back, padded[:, -1, 1:-1, :])
            )

            def combustor_step(present):
                upper_terms, lower_terms = z_terms_combustor(present)
                return (source + neighbour_sum(padded, upper_terms, lower_terms)) / divisor

            def turbine_step(present):
                upper_terms, lower_terms = z_terms_turbine(present, inflow)
                driving = source + weights * neighbour_sum(padded, upper_terms, lower_terms)
                return apply_inverse(block_inverse, driving)

            updated = lax.cond(combustor, combustor_step, turbine_step, current)
            current = jnp.where(parity == colour, updated, current)
    return current[None]


def solution(mesh):
    return jax.shard_map(
        shards,
        mesh=mesh,
        in_specs=(
            P("sa", None, "gx", "gy", None),
            P("sa", None, "gx", "gy", None),
            P(None, "gx", "gy", None),
            P(None, None, "gx", "gy", None),
            P(),
            P(),
            P("gy", None),
        ),
        out_specs=P("sa", None, "gx", "gy", None),
        check_vma=False,
    )
```

profile of v0, /device:TPU:40, one launch (start us, length us, event | category | flops | bytes accessed | tf_op | source)
XLA Modules:
  0.0 340.3 jit_solution(1177872966611160393)
XLA Ops:
  4.6 3.5 %collective-permute-start.1 = (f32[7,1,8,512]{3,2,0,1:T(8,128)S(1)}, f32[7,1,8,512]{3,2,0,1:T(8,128)S(1)}, u32[]{:S(2)}, u32[]{:S(2)}) collective-permute-start(f32[7,1,8,512]{3,2,0,1:T(8,128)S(1)} %get-tuple-element.841), channel_id=1, source_target_pairs={{16,0},{32,16},{48,32},{64,48},{80,64},{96,80},{112,96},{17,1},{33... | collective-permute-start | bytes 344072 | tf_op jit(solution)/shard_map/ppermute | solution.py:22
  10.4 10.5 %all-to-all-start = ((f32[64,2,1,32]{3,2,1,0:T(1,128)}), f32[64,2,1,32]{3,2,1,0:T(1,128)S(1)}, u32[]{:S(2)}, u32[]{:S(2)}) async-start(f32[64,2,1,32]{3,2,1,0:T(1,128)} %copy.643), calls=%async_computation | async-start | bytes 131072 | tf_op jit(solution)/shard_map/all_to_all | solution.py:86
  22.6 7.0 %all-to-all-done = f32[64,2,1,32]{3,2,1,0:T(1,128)S(1)} async-done(((f32[64,2,1,32]{3,2,1,0:T(1,128)}), f32[64,2,1,32]{3,2,1,0:T(1,128)S(1)}, u32[]{:S(2)}, u32[]{:S(2)}) %all-to-all-start) | async-done | bytes 16416 | tf_op jit(solution)/shard_map/all_to_all | solution.py:86
  29.6 5.3 %gather_fusion.1 = f32[896,32]{1,0:T(8,128)S(1)} fusion(f32[64,2,1,32]{3,2,1,0:T(1,128)S(1)} %rev.3, s32[896]{0:T(1024)S(1)} %fusion.176), kind=kCustom, calls=%fused_computation.1 | custom fusion | bytes 240128 | tf_op jit(solution)/shard_map/gather | solution.py:95
  37.2 2.5 collective-permute-start.2
  41.8 5.8 %collective-permute-done.3 = f32[7,6,1,512]{3,2,0,1:T(1,128)S(1)} collective-permute-done((f32[7,6,1,512]{3,2,0,1:T(1,128)S(1)}, f32[7,6,1,512]{3,2,0,1:T(1,128)S(1)}, u32[]{:S(2)}, u32[]{:S(2)}) %collective-permute-start.3) | collective-permute-done | bytes 86048 | tf_op jit(solution)/shard_map/ppermute | solution.py:22
  51.5 14.5 %conditional.8 = (f32[7,4,8,512]{3,2,0,1:T(8,128)S(1)}) conditional(s32[]{:T(128)} %convert_element_type.2, (f32[7,7,4,8,512]{4,3,2,1,0:T(8,128)S(1)}, f32[7,1,1,1]{0,3,2,1:T(1,128)}, f32[7,6,10,512]{3,2,0,1:T(8,128)}, f32[7,4,8,512]{3,2,0,1:T(8,128)}, f32[1,32]{1,0:T(1,128)}, /*index=5*/f32[7,4,8,512]{3,2,1,0:T(8,128)}) %tuple.335, ...), branch_computations={%region_2.3_spmd, %region_3.4_spmd} | conditional | flops 2408672 | bytes 12391768 | solution.py:123
  51.5 2.3 fusion.194
  53.9 6.6 %copy.645 = f32[7,4,8,512]{2,1,3,0:T(4,128)} copy(f32[7,4,8,512]{3,2,0,1:T(8,128)} %get-tuple-element.619) | data formatting | bytes 917504 | tf_op jit(solution)/shard_map
  62.6 2.9 fusion.47
  69.1 2.4 collective-permute-start.5
  71.5 3.7 %collective-permute-done.5 = f32[7,1,8,512]{3,2,0,1:T(8,128)S(1)} collective-permute-done((f32[7,1,8,512]{3,2,0,1:T(8,128)S(1)}, f32[7,1,8,512]{3,2,0,1:T(8,128)S(1)}, u32[]{:S(2)}, u32[]{:S(2)}) %collective-permute-start.5) | collective-permute-done | bytes 114720 | tf_op jit(solution)/shard_map/ppermute | solution.py:21
  75.3 5.7 %collective-permute-start.7 = (f32[7,6,1,512]{3,2,0,1:T(1,128)S(1)}, f32[7,6,1,512]{3,2,0,1:T(1,128)S(1)}, u32[]{:S(2)}, u32[]{:S(2)}) collective-permute-start(f32[7,6,1,512]{3,2,0,1:T(1,128)S(1)} %get-tuple-element.822), channel_id=1, source_target_pairs={{0,2},{2,4},{4,6},{6,8},{8,10},{10,12},{12,14},{1,3},{3,5},{5,7},{... | collective-permute-start | bytes 258056 | tf_op jit(solution)/shard_map/ppermute | solution.py:21
  84.0 5.0 %collective-permute-done.8 = f32[7,6,1,512]{3,2,0,1:T(1,128)S(1)} collective-permute-done((f32[7,6,1,512]{3,2,0,1:T(1,128)S(1)}, f32[7,6,1,512]{3,2,0,1:T(1,128)S(1)}, u32[]{:S(2)}, u32[]{:S(2)}) %collective-permute-start.8) | collective-permute-done | bytes 86048 | tf_op jit(solution)/shard_map/ppermute | solution.py:22
  92.0 14.5 %conditional.9 = (f32[7,4,8,512]{3,2,0,1:T(8,128)S(1)}) conditional(s32[]{:T(128)} %convert_element_type.2, (f32[7,7,4,8,512]{4,3,2,1,0:T(8,128)S(1)}, f32[7,1,1,1]{0,3,2,1:T(1,128)S(1)}, f32[7,6,10,512]{3,2,0,1:T(8,128)}, f32[7,4,8,512]{3,2,0,1:T(8,128)}, f32[1,32]{1,0:T(1,128)S(1)}, /*index=5*/f32[7,4,8,512]{3,2,1,0:T(8,128)}) %tuple.343, ...), branch_computations={%region_4.5_spmd, %region_5.6_spmd} | conditional | flops 2408672 | bytes 12391088 | solution.py:123
  92.0 2.3 fusion.195
  94.3 6.6 %copy.651 = f32[7,4,8,512]{2,1,3,0:T(4,128)} copy(f32[7,4,8,512]{3,2,0,1:T(8,128)} %get-tuple-element.629) | data formatting | bytes 917504 | tf_op jit(solution)/shard_map
  103.1 2.9 fusion.64
  109.6 2.4 collective-permute-start.9
  112.0 3.7 %collective-permute-done.9 = f32[7,1,8,512]{3,2,0,1:T(8,128)S(1)} collective-permute-done((f32[7,1,8,512]{3,2,0,1:T(8,128)S(1)}, f32[7,1,8,512]{3,2,0,1:T(8,128)S(1)}, u32[]{:S(2)}, u32[]{:S(2)}) %collective-permute-start.9) | collective-permute-done | bytes 114720 | tf_op jit(solution)/shard_map/ppermute | solution.py:21
  115.8 3.1 collective-permute-start.11
  121.0 5.8 %collective-permute-done.12 = f32[7,6,1,512]{3,2,0,1:T(1,128)S(1)} collective-permute-done((f32[7,6,1,512]{3,2,0,1:T(1,128)S(1)}, f32[7,6,1,512]{3,2,0,1:T(1,128)S(1)}, u32[]{:S(2)}, u32[]{:S(2)}) %collective-permute-start.12) | collective-permute-done | bytes 86048 | tf_op jit(solution)/shard_map/ppermute | solution.py:22
  129.8 14.6 %conditional.10 = (f32[7,4,8,512]{3,2,0,1:T(8,128)S(1)}) conditional(s32[]{:T(128)} %convert_element_type.2, (f32[7,7,4,8,512]{4,3,2,1,0:T(8,128)S(1)}, f32[7,1,1,1]{0,3,2,1:T(1,128)S(1)}, f32[7,6,10,512]{3,2,0,1:T(8,128)}, f32[7,4,8,512]{3,2,0,1:T(8,128)}, f32[1,32]{1,0:T(1,128)S(1)}, /*index=5*/f32[7,4,8,512]{3,2,1,0:T(8,128)}) %tuple.344, ...), branch_computations={%region_6.7_spmd, %region_7.8_spmd} | conditional | flops 2408672 | bytes 12391088 | solution.py:123
  129.8 2.3 fusion.196
  132.1 6.6 %copy.657 = f32[7,4,8,512]{2,1,3,0:T(4,128)} copy(f32[7,4,8,512]{3,2,0,1:T(8,128)} %get-tuple-element.639) | data formatting | bytes 917504 | tf_op jit(solution)/shard_map
  140.9 2.9 fusion.81
  147.4 2.4 collective-permute-start.13
  149.8 3.7 %collective-permute-done.13 = f32[7,1,8,512]{3,2,0,1:T(8,128)S(1)} collective-permute-done((f32[7,1,8,512]{3,2,0,1:T(8,128)S(1)}, f32[7,1,8,512]{3,2,0,1:T(8,128)S(1)}, u32[]{:S(2)}, u32[]{:S(2)}) %collective-permute-start.13) | collective-permute-done | bytes 114720 | tf_op jit(solution)/shard_map/ppermute | solution.py:21
  153.6 5.2 %collective-permute-start.15 = (f32[7,6,1,512]{3,2,0,1:T(1,128)S(1)}, f32[7,6,1,512]{3,2,0,1:T(1,128)S(1)}, u32[]{:S(2)}, u32[]{:S(2)}) collective-permute-start(f32[7,6,1,512]{3,2,0,1:T(1,128)S(1)} %get-tuple-element.818), channel_id=1, source_target_pairs={{0,2},{2,4},{4,6},{6,8},{8,10},{10,12},{12,14},{1,3},{3,5},{5,7},{... | collective-permute-start | bytes 258056 | tf_op jit(solution)/shard_map/ppermute | solution.py:21
  161.8 5.0 %collective-permute-done.16 = f32[7,6,1,512]{3,2,0,1:T(1,128)S(1)} collective-permute-done((f32[7,6,1,512]{3,2,0,1:T(1,128)S(1)}, f32[7,6,1,512]{3,2,0,1:T(1,128)S(1)}, u32[]{:S(2)}, u32[]{:S(2)}) %collective-permute-start.16) | collective-permute-done | bytes 86048 | tf_op jit(solution)/shard_map/ppermute | solution.py:22
  169.7 14.6 %conditional.11 = (f32[7,4,8,512]{3,2,0,1:T(8,128)S(1)}) conditional(s32[]{:T(128)} %convert_element_type.2, (f32[7,7,4,8,512]{4,3,2,1,0:T(8,128)S(1)}, f32[7,1,1,1]{0,3,2,1:T(1,128)S(1)}, f32[7,6,10,512]{3,2,0,1:T(8,128)}, f32[7,4,8,512]{3,2,0,1:T(8,128)}, f32[1,32]{1,0:T(1,128)S(1)}, /*index=5*/f32[7,4,8,512]{3,2,1,0:T(8,128)}) %tuple.345, ...), branch_computations={%region_8.9_spmd, %region_9.10_spmd} | conditional | flops 2408672 | bytes 12391088 | solution.py:123
  172.0 6.6 %copy.663 = f32[7,4,8,512]{2,1,3,0:T(4,128)} copy(f32[7,4,8,512]{3,2,0,1:T(8,128)} %get-tuple-element.649) | data formatting | bytes 917504 | tf_op jit(solution)/shard_map
  180.9 2.9 fusion.98
  187.4 2.4 collective-permute-start.17
  189.8 3.7 %collective-permute-done.17 = f32[7,1,8,512]{3,2,0,1:T(8,128)S(1)} collective-permute-done((f32[7,1,8,512]{3,2,0,1:T(8,128)S(1)}, f32[7,1,8,512]{3,2,0,1:T(8,128)S(1)}, u32[]{:S(2)}, u32[]{:S(2)}) %collective-permute-start.17) | collective-permute-done | bytes 114720 | tf_op jit(solution)/shard_map/ppermute | solution.py:21
  193.6 2.9 collective-permute-start.19
  198.6 5.8 %collective-permute-done.20 = f32[7,6,1,512]{3,2,0,1:T(1,128)S(1)} collective-permute-done((f32[7,6,1,512]{3,2,0,1:T(1,128)S(1)}, f32[7,6,1,512]{3,2,0,1:T(1,128)S(1)}, u32[]{:S(2)}, u32[]{:S(2)}) %collective-permute-start.20) | collective-permute-done | bytes 86048 | tf_op jit(solution)/shard_map/ppermute | solution.py:22
  207.4 14.6 %conditional.12 = (f32[7,4,8,512]{3,2,0,1:T(8,128)S(1)}) conditional(s32[]{:T(128)} %convert_element_type.2, (f32[7,7,4,8,512]{4,3,2,1,0:T(8,128)S(1)}, f32[7,1,1,1]{0,3,2,1:T(1,128)S(1)}, f32[7,6,10,512]{3,2,0,1:T(8,128)}, f32[7,4,8,512]{3,2,0,1:T(8,128)}, f32[1,32]{1,0:T(1,128)S(1)}, /*index=5*/f32[7,4,8,512]{3,2,1,0:T(8,128)}) %tuple.346, ...), branch_computations={%region_10.11_spmd, %region_11.12_spmd} | conditional | flops 2408672 | bytes 12391088 | solution.py:123
  209.7 6.6 %copy.669 = f32[7,4,8,512]{2,1,3,0:T(4,128)} copy(f32[7,4,8,512]{3,2,0,1:T(8,128)} %get-tuple-element.659) | data formatting | bytes 917504 | tf_op jit(solution)/shard_map
  218.5 2.9 fusion.115
  225.0 2.4 collective-permute-start.21
  227.4 3.7 %collective-permute-done.21 = f32[7,1,8,512]{3,2,0,1:T(8,128)S(1)} collective-permute-done((f32[7,1,8,512]{3,2,0,1:T(8,128)S(1)}, f32[7,1,8,512]{3,2,0,1:T(8,128)S(1)}, u32[]{:S(2)}, u32[]{:S(2)}) %collective-permute-start.21) | collective-permute-done | bytes 114720 | tf_op jit(solution)/shard_map/ppermute | solution.py:21
  231.2 6.0 %collective-permute-start.23 = (f32[7,6,1,512]{3,2,0,1:T(1,128)S(1)}, f32[7,6,1,512]{3,2,0,1:T(1,128)S(1)}, u32[]{:S(2)}, u32[]{:S(2)}) collective-permute-start(f32[7,6,1,512]{3,2,0,1:T(1,128)S(1)} %get-tuple-element.814), channel_id=1, source_target_pairs={{0,2},{2,4},{4,6},{6,8},{8,10},{10,12},{12,14},{1,3},{3,5},{5,7},{... | collective-permute-start | bytes 258056 | tf_op jit(solution)/shard_map/ppermute | solution.py:21
  240.2 4.9 %collective-permute-done.24 = f32[7,6,1,512]{3,2,0,1:T(1,128)S(1)} collective-permute-done((f32[7,6,1,512]{3,2,0,1:T(1,128)S(1)}, f32[7,6,1,512]{3,2,0,1:T(1,128)S(1)}, u32[]{:S(2)}, u32[]{:S(2)}) %collective-permute-start.24) | collective-permute-done | bytes 86048 | tf_op jit(solution)/shard_map/ppermute | solution.py:22
  248.1 14.8 %conditional.13 = (f32[7,4,8,512]{3,2,0,1:T(8,128)S(1)}) conditional(s32[]{:T(128)} %convert_element_type.2, (f32[7,7,4,8,512]{4,3,2,1,0:T(8,128)S(1)}, f32[7,1,1,1]{0,3,2,1:T(1,128)S(1)}, f32[7,6,10,512]{3,2,0,1:T(8,128)}, f32[7,4,8,512]{3,2,0,1:T(8,128)}, f32[1,32]{1,0:T(1,128)S(1)}, /*index=5*/f32[7,4,8,512]{3,2,1,0:T(8,128)}) %tuple.347, ...), branch_computations={%region_12.13_spmd, %region_13.14_spmd} | conditional | flops 2408672 | bytes 12391088 | solution.py:123
  248.1 2.3 fusion.199
  250.4 6.6 %copy.675 = f32[7,4,8,512]{2,1,3,0:T(4,128)} copy(f32[7,4,8,512]{3,2,0,1:T(8,128)} %get-tuple-element.669) | data formatting | bytes 917504 | tf_op jit(solution)/shard_map
  259.3 2.9 fusion.132
  266.0 2.4 collective-permute-start.25
  268.4 3.7 %collective-permute-done.25 = f32[7,1,8,512]{3,2,0,1:T(8,128)S(1)} collective-permute-done((f32[7,1,8,512]{3,2,0,1:T(8,128)S(1)}, f32[7,1,8,512]{3,2,0,1:T(8,128)S(1)}, u32[]{:S(2)}, u32[]{:S(2)}) %collective-permute-start.25) | collective-permute-done | bytes 114720 | tf_op jit(solution)/shard_map/ppermute | solution.py:21
  272.2 3.2 collective-permute-start.27
  278.3 5.0 %collective-permute-done.28 = f32[7,6,1,512]{3,2,0,1:T(1,128)S(1)} collective-permute-done((f32[7,6,1,512]{3,2,0,1:T(1,128)S(1)}, f32[7,6,1,512]{3,2,0,1:T(1,128)S(1)}, u32[]{:S(2)}, u32[]{:S(2)}) %collective-permute-start.28) | collective-permute-done | bytes 86048 | tf_op jit(solution)/shard_map/ppermute | solution.py:22
  286.3 14.6 %conditional.14 = (f32[7,4,8,512]{3,2,0,1:T(8,128)S(1)}) conditional(s32[]{:T(128)} %convert_element_type.2, (f32[7,7,4,8,512]{4,3,2,1,0:T(8,128)S(1)}, f32[7,1,1,1]{0,3,2,1:T(1,128)S(1)}, f32[7,6,10,512]{3,2,0,1:T(8,128)}, f32[7,4,8,512]{3,2,0,1:T(8,128)}, f32[1,32]{1,0:T(1,128)S(1)}, /*index=5*/f32[7,4,8,512]{3,2,1,0:T(8,128)}) %tuple.348, ...), branch_computations={%region_14.15_spmd, %region_15.16_spmd} | conditional | flops 2408672 | bytes 12391088 | solution.py:123
  286.3 2.3 fusion.200
  288.6 6.6 %copy.681 = f32[7,4,8,512]{2,1,3,0:T(4,128)} copy(f32[7,4,8,512]{3,2,0,1:T(8,128)} %get-tuple-element.679) | data formatting | bytes 917504 | tf_op jit(solution)/shard_map
  297.4 2.9 fusion.149
  303.9 2.4 collective-permute-start.29
  306.4 3.7 %collective-permute-done.29 = f32[7,1,8,512]{3,2,0,1:T(8,128)S(1)} collective-permute-done((f32[7,1,8,512]{3,2,0,1:T(8,128)S(1)}, f32[7,1,8,512]{3,2,0,1:T(8,128)S(1)}, u32[]{:S(2)}, u32[]{:S(2)}) %collective-permute-start.29) | collective-permute-done | bytes 114720 | tf_op jit(solution)/shard_map/ppermute | solution.py:21
  310.2 2.8 collective-permute-start.31
  315.9 5.0 %collective-permute-done.32 = f32[7,6,1,512]{3,2,0,1:T(1,128)S(1)} collective-permute-done((f32[7,6,1,512]{3,2,0,1:T(1,128)S(1)}, f32[7,6,1,512]{3,2,0,1:T(1,128)S(1)}, u32[]{:S(2)}, u32[]{:S(2)}) %collective-permute-start.32) | collective-permute-done | bytes 86048 | tf_op jit(solution)/shard_map/ppermute | solution.py:22
  323.8 14.6 %conditional.15 = (f32[7,4,8,512]{3,2,0,1:T(8,128)S(1)}) conditional(s32[]{:T(128)} %convert_element_type.2, (f32[7,7,4,8,512]{4,3,2,1,0:T(8,128)S(1)}, f32[7,1,1,1]{0,3,2,1:T(1,128)S(1)}, f32[7,6,10,512]{3,2,0,1:T(8,128)}, f32[7,4,8,512]{3,2,0,1:T(8,128)}, f32[1,32]{1,0:T(1,128)S(1)}, /*index=5*/f32[7,4,8,512]{3,2,1,0:T(8,128)}) %tuple.349, ...), branch_computations={%region_16.17_spmd, %region_17.18_spmd} | conditional | flops 2408672 | bytes 12391088 | solution.py:123
  323.8 2.3 fusion.201
  326.2 6.6 %copy.687 = f32[7,4,8,512]{2,1,3,0:T(4,128)} copy(f32[7,4,8,512]{3,2,0,1:T(8,128)} %get-tuple-element.689) | data formatting | bytes 917504 | tf_op jit(solution)/shard_map
  335.0 2.9 fusion.166
  (221 shorter events, 105.5 us)
Async XLA Ops:
  0.0 3.3 copy-start.33
  0.0 8.1 %copy-start.26 = (f32[7,4,8,512]{3,2,1,0:T(8,128)S(1)}, f32[7,4,8,512]{3,2,1,0:T(8,128)}, u32[]{:S(2)}) copy-start(f32[7,4,8,512]{3,2,1,0:T(8,128)} %param.41) | copy-start | bytes 1376260
  1.1 9.3 %copy-start.24 = (f32[1,7,4,8,512]{4,3,1,2,0:T(8,128)}, f32[1,7,4,8,512]{4,3,1,2,0:T(8,128)S(1)}, u32[]{:S(2)}) copy-start(f32[1,7,4,8,512]{4,3,1,2,0:T(8,128)S(1)} %copy.824) | copy-start | bytes 1376260
  1.1 19.7 %copy-start.32 = (s32[1,896]{1,0:T(1,128)S(1)}, s32[1,896]{1,0:T(1,128)}, u32[]{:S(2)}) copy-start(s32[1,896]{1,0:T(1,128)} %param.45) | copy-start | bytes 10756
  1.2 34.6 %collective-permute-start = (f32[7,1,8,512]{3,2,0,1:T(8,128)S(1)}, f32[7,1,8,512]{3,2,0,1:T(8,128)S(1)}, u32[]{:S(2)}, u32[]{:S(2)}) collective-permute-start(f32[7,1,8,512]{3,2,0,1:T(8,128)S(1)} %get-tuple-element.840), channel_id=1, source_target_pairs={{0,16},{16,32},{32,48},{48,64},{64,80},{80,96},{96,112},{1,17},{17... | collective-permute-start | bytes 344072 | tf_op jit(solution)/shard_map/ppermute | solution.py:21
  4.4 5.3 %collective-permute-start.4 = (f32[64,2,1,32]{3,0,2,1:T(8,128)S(1)}, f32[64,2,1,32]{3,0,2,1:T(8,128)S(1)}, u32[]{:S(2)}, u32[]{:S(2)}) collective-permute-start(f32[64,2,1,32]{3,0,2,1:T(8,128)S(1)} %pad_maximum_fusion.40), channel_id=1, source_target_pairs={{0,1},{1,0},{2,3},{3,2},{4,5},{5,4},{6,7},{7,6},{8,9},{9,8},{10,11... | collective-permute-start | bytes 49160 | tf_op jit(solution)/shard_map/ppermute | solution.py:11
  4.6 31.2 %collective-permute-start.1 = (f32[7,1,8,512]{3,2,0,1:T(8,128)S(1)}, f32[7,1,8,512]{3,2,0,1:T(8,128)S(1)}, u32[]{:S(2)}, u32[]{:S(2)}) collective-permute-start(f32[7,1,8,512]{3,2,0,1:T(8,128)S(1)} %get-tuple-element.841), channel_id=1, source_target_pairs={{16,0},{32,16},{48,32},{64,48},{80,64},{96,80},{112,96},{17,1},{33... | collective-permute-start | bytes 344072 | tf_op jit(solution)/shard_map/ppermute | solution.py:22
  10.4 19.2 %all-to-all-start = ((f32[64,2,1,32]{3,2,1,0:T(1,128)}), f32[64,2,1,32]{3,2,1,0:T(1,128)S(1)}, u32[]{:S(2)}, u32[]{:S(2)}) async-start(f32[64,2,1,32]{3,2,1,0:T(1,128)} %copy.643), calls=%async_computation | async-start | bytes 131072 | tf_op jit(solution)/shard_map/all_to_all | solution.py:86
  35.2 12.5 %copy-start.25 = (f32[1,7,4,8,512]{4,3,1,2,0:T(8,128)S(1)}, f32[1,7,4,8,512]{4,3,1,2,0:T(8,128)}, u32[]{:S(2)}) copy-start(f32[1,7,4,8,512]{4,3,1,2,0:T(8,128)} %copy-done.24) | copy-start | bytes 1376260
  35.8 4.0 %copy-start.27 = (f32[7,1,8,512]{3,2,0,1:T(8,128)}, f32[7,1,8,512]{3,2,0,1:T(8,128)S(1)}, u32[]{:S(2)}) copy-start(f32[7,1,8,512]{3,2,0,1:T(8,128)S(1)} %collective-permute-done) | copy-start | bytes 344068
  35.8 15.8 %copy-start = (f32[7,7,4,8,512]{4,3,2,1,0:T(8,128)S(1)}, f32[7,7,4,8,512]{4,3,2,1,0:T(8,128)}, u32[]{:S(2)}) copy-start(f32[7,7,4,8,512]{4,3,2,1,0:T(8,128)} %param.42) | copy-start | bytes 9633796
  37.2 4.6 %collective-permute-start.2 = (f32[7,6,1,512]{3,2,0,1:T(1,128)S(1)}, f32[7,6,1,512]{3,2,0,1:T(1,128)S(1)}, u32[]{:S(2)}, u32[]{:S(2)}) collective-permute-start(f32[7,6,1,512]{3,2,0,1:T(1,128)S(1)} %get-tuple-element.824), channel_id=1, source_target_pairs={{0,2},{2,4},{4,6},{6,8},{8,10},{10,12},{12,14},{1,3},{3,5},{5,7},{... | collective-permute-start | bytes 258056 | tf_op jit(solution)/shard_map/ppermute | solution.py:21
  39.8 7.9 %collective-permute-start.3 = (f32[7,6,1,512]{3,2,0,1:T(1,128)S(1)}, f32[7,6,1,512]{3,2,0,1:T(1,128)S(1)}, u32[]{:S(2)}, u32[]{:S(2)}) collective-permute-start(f32[7,6,1,512]{3,2,0,1:T(1,128)S(1)} %get-tuple-element.825), channel_id=1, source_target_pairs={{2,0},{4,2},{6,4},{8,6},{10,8},{12,10},{14,12},{3,1},{5,3},{7,5},{... | collective-permute-start | bytes 258056 | tf_op jit(solution)/shard_map/ppermute | solution.py:22
  51.5 14.5 %copy-start.29 = (pred[4,8,512]{2,1,0:T(8,128)(4,1)S(1)}, pred[4,8,512]{2,1,0:T(8,128)(4,1)}, u32[]{:S(2)}) copy-start(pred[4,8,512]{2,1,0:T(8,128)(4,1)} %get-tuple-element.843) | copy-start | bytes 49156
  53.9 7.8 %copy-start.35 = (f32[1,32]{1,0:T(1,128)S(1)}, f32[1,32]{1,0:T(1,128)}, u32[]{:S(2)}) copy-start(f32[1,32]{1,0:T(1,128)} %get-tuple-element.290) | copy-start | bytes 388 | tf_op jit(solution)/shard_map/cond
  53.9 8.7 %copy-start.31 = (f32[7,1,1,1]{0,3,2,1:T(1,128)S(1)}, f32[7,1,1,1]{0,3,2,1:T(1,128)}, u32[]{:S(2)}) copy-start(f32[7,1,1,1]{0,3,2,1:T(1,128)} %get-tuple-element.287) | copy-start | bytes 88 | tf_op jit(solution)/shard_map/cond
  67.2 21.8 %copy-start.11 = (f32[7,4,8,512]{3,2,0,1:T(8,128)}, f32[7,4,8,512]{3,2,0,1:T(8,128)S(1)}, u32[]{:S(2)}) copy-start(f32[7,4,8,512]{3,2,0,1:T(8,128)S(1)} %broadcast_select_fusion.3) | copy-start | bytes 1376260
  67.2 4.3 %collective-permute-start.6 = (f32[7,1,8,512]{3,2,0,1:T(8,128)S(1)}, f32[7,1,8,512]{3,2,0,1:T(8,128)S(1)}, u32[]{:S(2)}, u32[]{:S(2)}) collective-permute-start(f32[7,1,8,512]{3,2,0,1:T(8,128)S(1)} %get-tuple-element.839), channel_id=1, source_target_pairs={{16,0},{32,16},{48,32},{64,48},{80,64},{96,80},{112,96},{17,1},{33... | collective-permute-start | bytes 344072 | tf_op jit(solution)/shard_map/ppermute | solution.py:22
  69.1 6.1 %collective-permute-start.5 = (f32[7,1,8,512]{3,2,0,1:T(8,128)S(1)}, f32[7,1,8,512]{3,2,0,1:T(8,128)S(1)}, u32[]{:S(2)}, u32[]{:S(2)}) collective-permute-start(f32[7,1,8,512]{3,2,0,1:T(8,128)S(1)} %get-tuple-element.838), channel_id=1, source_target_pairs={{0,16},{16,32},{32,48},{48,64},{64,80},{80,96},{96,112},{1,17},{17... | collective-permute-start | bytes 344072 | tf_op jit(solution)/shard_map/ppermute | solution.py:21
  75.3 8.7 %collective-permute-start.7 = (f32[7,6,1,512]{3,2,0,1:T(1,128)S(1)}, f32[7,6,1,512]{3,2,0,1:T(1,128)S(1)}, u32[]{:S(2)}, u32[]{:S(2)}) collective-permute-start(f32[7,6,1,512]{3,2,0,1:T(1,128)S(1)} %get-tuple-element.822), channel_id=1, source_target_pairs={{0,2},{2,4},{4,6},{6,8},{8,10},{10,12},{12,14},{1,3},{3,5},{5,7},{... | collective-permute-start | bytes 258056 | tf_op jit(solution)/shard_map/ppermute | solution.py:21
  81.1 10.9 %copy-start.30 = (f32[7]{0:T(128)S(1)}, f32[7]{0:T(128)}, u32[]{:S(2)}) copy-start(f32[7]{0:T(128)} %param.43) | copy-start | bytes 88
  81.1 10.9 %copy-start.34 = (f32[1,32]{1,0:T(1,128)S(1)}, f32[1,32]{1,0:T(1,128)}, u32[]{:S(2)}) copy-start(f32[1,32]{1,0:T(1,128)} %dynamic-slice_bitcast_fusion) | copy-start | bytes 388
  81.1 7.9 %collective-permute-start.8 = (f32[7,6,1,512]{3,2,0,1:T(1,128)S(1)}, f32[7,6,1,512]{3,2,0,1:T(1,128)S(1)}, u32[]{:S(2)}, u32[]{:S(2)}) collective-permute-start(f32[7,6,1,512]{3,2,0,1:T(1,128)S(1)} %get-tuple-element.823), channel_id=1, source_target_pairs={{2,0},{4,2},{6,4},{8,6},{10,8},{12,10},{14,12},{3,1},{5,3},{7,5},{... | collective-permute-start | bytes 258056 | tf_op jit(solution)/shard_map/ppermute | solution.py:22
  92.0 14.6 %copy-start.28 = (pred[4,8,512]{2,1,0:T(8,128)(4,1)S(1)}, pred[4,8,512]{2,1,0:T(8,128)(4,1)}, u32[]{:S(2)}) copy-start(pred[4,8,512]{2,1,0:T(8,128)(4,1)} %get-tuple-element.842) | copy-start | bytes 49156
  107.6 19.2 %copy-start.12 = (f32[7,4,8,512]{3,2,0,1:T(8,128)}, f32[7,4,8,512]{3,2,0,1:T(8,128)S(1)}, u32[]{:S(2)}) copy-start(f32[7,4,8,512]{3,2,0,1:T(8,128)S(1)} %broadcast_select_fusion.6) | copy-start | bytes 1376260
  107.7 4.3 %collective-permute-start.10 = (f32[7,1,8,512]{3,2,0,1:T(8,128)S(1)}, f32[7,1,8,512]{3,2,0,1:T(8,128)S(1)}, u32[]{:S(2)}, u32[]{:S(2)}) collective-permute-start(f32[7,1,8,512]{3,2,0,1:T(8,128)S(1)} %get-tuple-element.837), channel_id=1, source_target_pairs={{16,0},{32,16},{48,32},{64,48},{80,64},{96,80},{112,96},{17,1},{33... | collective-permute-start | bytes 344072 | tf_op jit(solution)/shard_map/ppermute | solution.py:22
  109.6 6.1 %collective-permute-start.9 = (f32[7,1,8,512]{3,2,0,1:T(8,128)S(1)}, f32[7,1,8,512]{3,2,0,1:T(8,128)S(1)}, u32[]{:S(2)}, u32[]{:S(2)}) collective-permute-start(f32[7,1,8,512]{3,2,0,1:T(8,128)S(1)} %get-tuple-element.836), channel_id=1, source_target_pairs={{0,16},{16,32},{32,48},{48,64},{64,80},{80,96},{96,112},{1,17},{17... | collective-permute-start | bytes 344072 | tf_op jit(solution)/shard_map/ppermute | solution.py:21
  115.8 5.2 %collective-permute-start.11 = (f32[7,6,1,512]{3,2,0,1:T(1,128)S(1)}, f32[7,6,1,512]{3,2,0,1:T(1,128)S(1)}, u32[]{:S(2)}, u32[]{:S(2)}) collective-permute-start(f32[7,6,1,512]{3,2,0,1:T(1,128)S(1)} %get-tuple-element.820), channel_id=1, source_target_pairs={{0,2},{2,4},{4,6},{6,8},{8,10},{10,12},{12,14},{1,3},{3,5},{5,7},{... | collective-permute-start | bytes 258056 | tf_op jit(solution)/shard_map/ppermute | solution.py:21
  118.9 7.9 %collective-permute-start.12 = (f32[7,6,1,512]{3,2,0,1:T(1,128)S(1)}, f32[7,6,1,512]{3,2,0,1:T(1,128)S(1)}, u32[]{:S(2)}, u32[]{:S(2)}) collective-permute-start(f32[7,6,1,512]{3,2,0,1:T(1,128)S(1)} %get-tuple-element.821), channel_id=1, source_target_pairs={{2,0},{4,2},{6,4},{8,6},{10,8},{12,10},{14,12},{3,1},{5,3},{7,5},{... | collective-permute-start | bytes 258056 | tf_op jit(solution)/shard_map/ppermute | solution.py:22
  145.4 21.3 %copy-start.13 = (f32[7,4,8,512]{3,2,0,1:T(8,128)}, f32[7,4,8,512]{3,2,0,1:T(8,128)S(1)}, u32[]{:S(2)}) copy-start(f32[7,4,8,512]{3,2,0,1:T(8,128)S(1)} %broadcast_select_fusion.2) | copy-start | bytes 1376260
  145.5 4.3 %collective-permute-start.14 = (f32[7,1,8,512]{3,2,0,1:T(8,128)S(1)}, f32[7,1,8,512]{3,2,0,1:T(8,128)S(1)}, u32[]{:S(2)}, u32[]{:S(2)}) collective-permute-start(f32[7,1,8,512]{3,2,0,1:T(8,128)S(1)} %get-tuple-element.835), channel_id=1, source_target_pairs={{16,0},{32,16},{48,32},{64,48},{80,64},{96,80},{112,96},{17,1},{33... | collective-permute-start | bytes 344072 | tf_op jit(solution)/shard_map/ppermute | solution.py:22
  147.4 6.1 %collective-permute-start.13 = (f32[7,1,8,512]{3,2,0,1:T(8,128)S(1)}, f32[7,1,8,512]{3,2,0,1:T(8,128)S(1)}, u32[]{:S(2)}, u32[]{:S(2)}) collective-permute-start(f32[7,1,8,512]{3,2,0,1:T(8,128)S(1)} %get-tuple-element.834), channel_id=1, source_target_pairs={{0,16},{16,32},{32,48},{48,64},{64,80},{80,96},{96,112},{1,17},{17... | collective-permute-start | bytes 344072 | tf_op jit(solution)/shard_map/ppermute | solution.py:21
  153.6 8.1 %collective-permute-start.15 = (f32[7,6,1,512]{3,2,0,1:T(1,128)S(1)}, f32[7,6,1,512]{3,2,0,1:T(1,128)S(1)}, u32[]{:S(2)}, u32[]{:S(2)}) collective-permute-start(f32[7,6,1,512]{3,2,0,1:T(1,128)S(1)} %get-tuple-element.818), channel_id=1, source_target_pairs={{0,2},{2,4},{4,6},{6,8},{8,10},{10,12},{12,14},{1,3},{3,5},{5,7},{... | collective-permute-start | bytes 258056 | tf_op jit(solution)/shard_map/ppermute | solution.py:21
  158.9 7.9 %collective-permute-start.16 = (f32[7,6,1,512]{3,2,0,1:T(1,128)S(1)}, f32[7,6,1,512]{3,2,0,1:T(1,128)S(1)}, u32[]{:S(2)}, u32[]{:S(2)}) collective-permute-start(f32[7,6,1,512]{3,2,0,1:T(1,128)S(1)} %get-tuple-element.819), channel_id=1, source_target_pairs={{2,0},{4,2},{6,4},{8,6},{10,8},{12,10},{14,12},{3,1},{5,3},{7,5},{... | collective-permute-start | bytes 258056 | tf_op jit(solution)/shard_map/ppermute | solution.py:22
  185.4 19.0 %copy-start.14 = (f32[7,4,8,512]{3,2,0,1:T(8,128)}, f32[7,4,8,512]{3,2,0,1:T(8,128)S(1)}, u32[]{:S(2)}) copy-start(f32[7,4,8,512]{3,2,0,1:T(8,128)S(1)} %broadcast_select_fusion.5) | copy-start | bytes 1376260
  185.4 4.3 %collective-permute-start.18 = (f32[7,1,8,512]{3,2,0,1:T(8,128)S(1)}, f32[7,1,8,512]{3,2,0,1:T(8,128)S(1)}, u32[]{:S(2)}, u32[]{:S(2)}) collective-permute-start(f32[7,1,8,512]{3,2,0,1:T(8,128)S(1)} %get-tuple-element.833), channel_id=1, source_target_pairs={{16,0},{32,16},{48,32},{64,48},{80,64},{96,80},{112,96},{17,1},{33... | collective-permute-start | bytes 344072 | tf_op jit(solution)/shard_map/ppermute | solution.py:22
  187.4 6.1 %collective-permute-start.17 = (f32[7,1,8,512]{3,2,0,1:T(8,128)S(1)}, f32[7,1,8,512]{3,2,0,1:T(8,128)S(1)}, u32[]{:S(2)}, u32[]{:S(2)}) collective-permute-start(f32[7,1,8,512]{3,2,0,1:T(8,128)S(1)} %get-tuple-element.832), channel_id=1, source_target_pairs={{0,16},{16,32},{32,48},{48,64},{64,80},{80,96},{96,112},{1,17},{17... | collective-permute-start | bytes 344072 | tf_op jit(solution)/shard_map/ppermute | solution.py:21
  193.6 5.0 %collective-permute-start.19 = (f32[7,6,1,512]{3,2,0,1:T(1,128)S(1)}, f32[7,6,1,512]{3,2,0,1:T(1,128)S(1)}, u32[]{:S(2)}, u32[]{:S(2)}) collective-permute-start(f32[7,6,1,512]{3,2,0,1:T(1,128)S(1)} %get-tuple-element.816), channel_id=1, source_target_pairs={{0,2},{2,4},{4,6},{6,8},{8,10},{10,12},{12,14},{1,3},{3,5},{5,7},{... | collective-permute-start | bytes 258056 | tf_op jit(solution)/shard_map/ppermute | solution.py:21
  196.5 7.9 %collective-permute-start.20 = (f32[7,6,1,512]{3,2,0,1:T(1,128)S(1)}, f32[7,6,1,512]{3,2,0,1:T(1,128)S(1)}, u32[]{:S(2)}, u32[]{:S(2)}) collective-permute-start(f32[7,6,1,512]{3,2,0,1:T(1,128)S(1)} %get-tuple-element.817), channel_id=1, source_target_pairs={{2,0},{4,2},{6,4},{8,6},{10,8},{12,10},{14,12},{3,1},{5,3},{7,5},{... | collective-permute-start | bytes 258056 | tf_op jit(solution)/shard_map/ppermute | solution.py:22
  223.0 22.1 %copy-start.15 = (f32[7,4,8,512]{3,2,0,1:T(8,128)}, f32[7,4,8,512]{3,2,0,1:T(8,128)S(1)}, u32[]{:S(2)}) copy-start(f32[7,4,8,512]{3,2,0,1:T(8,128)S(1)} %broadcast_select_fusion.1) | copy-start | bytes 1376260
  223.1 4.3 %collective-permute-start.22 = (f32[7,1,8,512]{3,2,0,1:T(8,128)S(1)}, f32[7,1,8,512]{3,2,0,1:T(8,128)S(1)}, u32[]{:S(2)}, u32[]{:S(2)}) collective-permute-start(f32[7,1,8,512]{3,2,0,1:T(8,128)S(1)} %get-tuple-element.831), channel_id=1, source_target_pairs={{16,0},{32,16},{48,32},{64,48},{80,64},{96,80},{112,96},{17,1},{33... | collective-permute-start | bytes 344072 | tf_op jit(solution)/shard_map/ppermute | solution.py:22
  225.0 6.1 %collective-permute-start.21 = (f32[7,1,8,512]{3,2,0,1:T(8,128)S(1)}, f32[7,1,8,512]{3,2,0,1:T(8,128)S(1)}, u32[]{:S(2)}, u32[]{:S(2)}) collective-permute-start(f32[7,1,8,512]{3,2,0,1:T(8,128)S(1)} %get-tuple-element.830), channel_id=1, source_target_pairs={{0,16},{16,32},{32,48},{48,64},{64,80},{80,96},{96,112},{1,17},{17... | collective-permute-start | bytes 344072 | tf_op jit(solution)/shard_map/ppermute | solution.py:21
  231.2 9.0 %collective-permute-start.23 = (f32[7,6,1,512]{3,2,0,1:T(1,128)S(1)}, f32[7,6,1,512]{3,2,0,1:T(1,128)S(1)}, u32[]{:S(2)}, u32[]{:S(2)}) collective-permute-start(f32[7,6,1,512]{3,2,0,1:T(1,128)S(1)} %get-tuple-element.814), channel_id=1, source_target_pairs={{0,2},{2,4},{4,6},{6,8},{8,10},{10,12},{12,14},{1,3},{3,5},{5,7},{... | collective-permute-start | bytes 258056 | tf_op jit(solution)/shard_map/ppermute | solution.py:21
  237.2 7.9 %collective-permute-start.24 = (f32[7,6,1,512]{3,2,0,1:T(1,128)S(1)}, f32[7,6,1,512]{3,2,0,1:T(1,128)S(1)}, u32[]{:S(2)}, u32[]{:S(2)}) collective-permute-start(f32[7,6,1,512]{3,2,0,1:T(1,128)S(1)} %get-tuple-element.815), channel_id=1, source_target_pairs={{2,0},{4,2},{6,4},{8,6},{10,8},{12,10},{14,12},{3,1},{5,3},{7,5},{... | collective-permute-start | bytes 258056 | tf_op jit(solution)/shard_map/ppermute | solution.py:22
  264.0 19.3 %copy-start.10 = (f32[7,4,8,512]{3,2,0,1:T(8,128)}, f32[7,4,8,512]{3,2,0,1:T(8,128)S(1)}, u32[]{:S(2)}) copy-start(f32[7,4,8,512]{3,2,0,1:T(8,128)S(1)} %broadcast_select_fusion.4) | copy-start | bytes 1376260
  264.0 4.3 %collective-permute-start.26 = (f32[7,1,8,512]{3,2,0,1:T(8,128)S(1)}, f32[7,1,8,512]{3,2,0,1:T(8,128)S(1)}, u32[]{:S(2)}, u32[]{:S(2)}) collective-permute-start(f32[7,1,8,512]{3,2,0,1:T(8,128)S(1)} %get-tuple-element.829), channel_id=1, source_target_pairs={{16,0},{32,16},{48,32},{64,48},{80,64},{96,80},{112,96},{17,1},{33... | collective-permute-start | bytes 344072 | tf_op jit(solution)/shard_map/ppermute | solution.py:22
  266.0 6.1 %collective-permute-start.25 = (f32[7,1,8,512]{3,2,0,1:T(8,128)S(1)}, f32[7,1,8,512]{3,2,0,1:T(8,128)S(1)}, u32[]{:S(2)}, u32[]{:S(2)}) collective-permute-start(f32[7,1,8,512]{3,2,0,1:T(8,128)S(1)} %get-tuple-element.828), channel_id=1, source_target_pairs={{0,16},{16,32},{32,48},{48,64},{64,80},{80,96},{96,112},{1,17},{17... | collective-permute-start | bytes 344072 | tf_op jit(solution)/shard_map/ppermute | solution.py:21
  272.2 6.1 %collective-permute-start.27 = (f32[7,6,1,512]{3,2,0,1:T(1,128)S(1)}, f32[7,6,1,512]{3,2,0,1:T(1,128)S(1)}, u32[]{:S(2)}, u32[]{:S(2)}) collective-permute-start(f32[7,6,1,512]{3,2,0,1:T(1,128)S(1)} %get-tuple-element.812), channel_id=1, source_target_pairs={{0,2},{2,4},{4,6},{6,8},{8,10},{10,12},{12,14},{1,3},{3,5},{5,7},{... | collective-permute-start | bytes 258056 | tf_op jit(solution)/shard_map/ppermute | solution.py:21
  275.4 7.9 %collective-permute-start.28 = (f32[7,6,1,512]{3,2,0,1:T(1,128)S(1)}, f32[7,6,1,512]{3,2,0,1:T(1,128)S(1)}, u32[]{:S(2)}, u32[]{:S(2)}) collective-permute-start(f32[7,6,1,512]{3,2,0,1:T(1,128)S(1)} %get-tuple-element.813), channel_id=1, source_target_pairs={{2,0},{4,2},{6,4},{8,6},{10,8},{12,10},{14,12},{3,1},{5,3},{7,5},{... | collective-permute-start | bytes 258056 | tf_op jit(solution)/shard_map/ppermute | solution.py:22
  302.0 18.9 %copy-start.9 = (f32[7,4,8,512]{3,2,0,1:T(8,128)}, f32[7,4,8,512]{3,2,0,1:T(8,128)S(1)}, u32[]{:S(2)}) copy-start(f32[7,4,8,512]{3,2,0,1:T(8,128)S(1)} %broadcast_select_fusion) | copy-start | bytes 1376260
  302.0 4.3 %collective-permute-start.30 = (f32[7,1,8,512]{3,2,0,1:T(8,128)S(1)}, f32[7,1,8,512]{3,2,0,1:T(8,128)S(1)}, u32[]{:S(2)}, u32[]{:S(2)}) collective-permute-start(f32[7,1,8,512]{3,2,0,1:T(8,128)S(1)} %get-tuple-element.827), channel_id=1, source_target_pairs={{16,0},{32,16},{48,32},{64,48},{80,64},{96,80},{112,96},{17,1},{33... | collective-permute-start | bytes 344072 | tf_op jit(solution)/shard_map/ppermute | solution.py:22
  303.9 6.1 %collective-permute-start.29 = (f32[7,1,8,512]{3,2,0,1:T(8,128)S(1)}, f32[7,1,8,512]{3,2,0,1:T(8,128)S(1)}, u32[]{:S(2)}, u32[]{:S(2)}) collective-permute-start(f32[7,1,8,512]{3,2,0,1:T(8,128)S(1)} %get-tuple-element.826), channel_id=1, source_target_pairs={{0,16},{16,32},{32,48},{48,64},{64,80},{80,96},{96,112},{1,17},{17... | collective-permute-start | bytes 344072 | tf_op jit(solution)/shard_map/ppermute | solution.py:21
  310.2 5.7 %collective-permute-start.31 = (f32[7,6,1,512]{3,2,0,1:T(1,128)S(1)}, f32[7,6,1,512]{3,2,0,1:T(1,128)S(1)}, u32[]{:S(2)}, u32[]{:S(2)}) collective-permute-start(f32[7,6,1,512]{3,2,0,1:T(1,128)S(1)} %get-tuple-element.810), channel_id=1, source_target_pairs={{0,2},{2,4},{4,6},{6,8},{8,10},{10,12},{12,14},{1,3},{3,5},{5,7},{... | collective-permute-start | bytes 258056 | tf_op jit(solution)/shard_map/ppermute | solution.py:21
  313.0 7.9 %collective-permute-start.32 = (f32[7,6,1,512]{3,2,0,1:T(1,128)S(1)}, f32[7,6,1,512]{3,2,0,1:T(1,128)S(1)}, u32[]{:S(2)}, u32[]{:S(2)}) collective-permute-start(f32[7,6,1,512]{3,2,0,1:T(1,128)S(1)} %get-tuple-element.811), channel_id=1, source_target_pairs={{2,0},{4,2},{6,4},{8,6},{10,8},{12,10},{14,12},{3,1},{5,3},{7,5},{... | collective-permute-start | bytes 258056 | tf_op jit(solution)/shard_map/ppermute | solution.py:22
where the time goes:
time: 345 us; the launch traced here: 340 us
  local copies, waits for them, and re-layouts  108 us (31%)
  starting transfers between devices  88.3 us (26%)
  waiting for transfers between devices  85.3 us (25%)
  other arithmetic  56.4 us (16%)
    another operation x16, local copies, waits for them, and re-layouts  57.1 us
    ppermute x16, starting transfers between devices, padded_2(): before = lax.ppermute(last, axis, up)  50.3 us
    ppermute x16, waiting for transfers between devices, padded_2(): after = lax.ppermute(initial, axis, down)  42.3 us
    ppermute x16, waiting for transfers between devices, padded_2(): before = lax.ppermute(last, axis, up)  36 us
    ppermute x16, starting transfers between devices, padded_2(): after = lax.ppermute(initial, axis, down)  27.3 us
    add x8, other arithmetic, turbine_step(): driving = source + weights * neighbour_sum(padded, upper_terms, lower_terms)  23.1 us
    slice x8, local copies, waits for them, and re-layouts, z_terms_turbine(): upper_terms = jnp.concatenate([values[:, :, :, 1:], upper_cap], axis=3)  18.6 us
    scatter x8, local copies, waits for them, and re-layouts, shards(): padded.at[:, -1, 1:-1, :]  13.1 us
  transfers between devices with their start and end apart: 34, of which 24 were waited for; matrix products, arithmetic and copies ran while one was open for 3% of the time, Pallas kernels for 0%

commit v1 on v0

v1 whole, which is shorter than its diff:
```python
import functools
import jax
import jax.numpy as jnp
import numpy as np
from jax import lax
from jax.experimental import pallas as pl
from jax.experimental.pallas import tpu as pltpu
from jax.sharding import PartitionSpec as P

SWEEPS = 4
BLK = 32
T = 7
CX = 4
CY = 8
NZ = 512
ZT = 128
VAL = T * NZ
MSG = VAL + T * ZT
COEF = T * T + T
BULK = COEF // 4
F32 = jnp.float32


def iotas(width):
    sub = lax.broadcasted_iota(jnp.int32, (8, width), 0)
    lane = lax.broadcasted_iota(jnp.int32, (8, width), 1)
    return sub, lane


def even_mask(width):
    sub, lane = iotas(width)
    return (sub + lane) % 2 == 0


def roll(array, shift, axis):
    size = array.shape[axis]
    shift = shift % size
    return array if shift == 0 else pltpu.roll(array, shift, axis)


def packed(pair_low, pair_high, even, colour):
    return jnp.where(even, pair_low, pair_high) if colour == 0 else jnp.where(even, pair_high, pair_low)


def store_message(ref, ones, zeros_first):
    for t in range(T):
        ref[:, t * NZ : (t + 1) * NZ] = ones(t)
        ref[:, VAL + t * ZT : VAL + (t + 1) * ZT] = zeros_first(t)


def first_kernel(place, fields, m1, m2):
    odd = place[1]
    even, even_z = even_mask(NZ), even_mask(ZT)
    for ref, pair in ((m1, 1 - odd), (m2, odd)):
        store_message(
            ref,
            lambda t: packed(fields[t, 2 * pair], fields[t, 2 * pair + 1], even, 1),
            lambda t: packed(fields[t, 2 * pair, :, :ZT], fields[t, 2 * pair + 1, :, :ZT], even_z, 0),
        )


def coefficient(section, sources, diagonal, inverse, index, plane):
    if index >= T * T:
        return sources[index - T * T, plane]
    raw = inverse[index // T, index % T, plane]
    return jnp.where(section == 0, diagonal[index, plane], raw) if index < T else raw


def bulk_kernel(place, sources, diagonal, inverse, x1, x2, low, high):
    section, odd = place[0], place[1]
    even = even_mask(NZ)
    sub, _ = iotas(NZ)
    for index in range(COEF):
        x1[index] = coefficient(section, sources, diagonal, inverse, index, (1 - odd) * (CX - 1))
        x2[index] = coefficient(section, sources, diagonal, inverse, index, odd * (CX - 1))
    for tile in range(BULK):
        rows_low = jnp.zeros((8, NZ), F32)
        rows_high = jnp.zeros((8, NZ), F32)
        for j in range(4):
            index = 4 * tile + j
            for k in (0, 1):
                plane = packed(
                    coefficient(section, sources, diagonal, inverse, index, 2 * k),
                    coefficient(section, sources, diagonal, inverse, index, 2 * k + 1),
                    even,
                    0,
                )
                here = sub == 2 * j + k
                rows_low = jnp.where(here, roll(plane, 2 * j + k, 0), rows_low)
                rows_high = jnp.where(here, roll(plane, 2 * j + k - 7, 0), rows_high)
        low[:, tile * NZ : (tile + 1) * NZ] = rows_low
        high[:, tile * NZ : (tile + 1) * NZ] = rows_high


def corner_kernel(with_bulk, place, m1, m2, r1, r2, *rest):
    odd_x, odd_y = place[1] == 1, place[2] == 1
    if with_bulk:
        low, high, marks_low, marks_high, y1, y2 = rest
    else:
        y1, y2 = rest
    sub, _ = iotas(ZT)
    for tile in range(MSG // ZT):
        at = slice(tile * ZT, (tile + 1) * ZT)
        a, b, c, d = m1[:, at], m2[:, at], r1[:, at], r2[:, at]
        own_low, own_high = jnp.where(odd_x, a, b), jnp.where(odd_x, b, a)
        from_low, from_high = jnp.where(odd_x, c, d), jnp.where(odd_x, d, c)

        def rows(start):
            parts = [from_low, own_low, own_high, from_high]
            shifted = [roll(part, 2 * p - start, 0) for p, part in enumerate(parts)]
            halves = [jnp.where(sub < 2, shifted[0], shifted[1]), jnp.where(sub < 6, shifted[2], shifted[3])]
            return jnp.where(sub < 4, halves[0], halves[1])

        down, up = rows(0), rows(6)
        y1[:, at] = jnp.where(odd_y, down, up)
        y2[:, at] = jnp.where(odd_y, up, down)
    if with_bulk:
        for tile in range(BULK * NZ // ZT):
            at = slice(tile * ZT, (tile + 1) * ZT)
            to = slice(MSG + tile * ZT, MSG + (tile + 1) * ZT)
            down, up = low[:, at], high[:, at]
            y1[:, to] = jnp.where(odd_y, down, up)
            y2[:, to] = jnp.where(odd_y, up, down)
        end = MSG + BULK * NZ
        y1[:, end:] = jnp.where(odd_y, marks_low[...], marks_high[...])
        y2[:, end:] = jnp.where(odd_y, marks_high[...], marks_low[...])


def interface_kernel(place, blocks, marks, marks1, marks2, chosen, back, inflow):
    odd_y = place[2] == 1
    exit_side = place[3] == 1
    back[...] = jnp.zeros_like(back)
    total = jnp.sum(blocks[...], axis=0, keepdims=True)
    for row in range(16):
        at = slice(8 * row, 8 * row + 8)
        inflow[at, :] = jnp.broadcast_to(jnp.sum(chosen[at, :] * total, axis=1, keepdims=True), (8, ZT))

    @pl.when(exit_side)
    def _():
        table = blocks[:, :ZT]
        first = jnp.where(odd_y, marks2[...], marks1[...])
        second = jnp.where(odd_y, marks1[...], marks2[...])
        _, lane_blocks = iotas(ZT)
        column = lax.broadcasted_iota(jnp.int32, table.shape, 1)
        spots = [
            jnp.where(column // BLK == q, roll(table, q * BLK, 1), 0.0) for q in range(ZT // BLK)
        ]
        wanted = [marks[t] for t in range(T)] + [first, second]
        for group, want in enumerate(wanted):
            for tile in range(NZ // ZT):
                laid = jnp.zeros((8, ZT), F32)
                for q in range(ZT // BLK):
                    block = tile * (ZT // BLK) + q
                    match = want[:, block : block + 1] * 2.0 + 1.0 == lane_blocks.astype(F32)
                    laid = laid + jnp.dot(
                        match.astype(F32), spots[q], precision=lax.Precision.HIGHEST, preferred_element_type=F32
                    )
                at = slice(tile * ZT, (tile + 1) * ZT)
                if group < T:
                    back[group, 0:8, at] = laid
                else:
                    row = 8 if group == T else 15
                    for t in range(T):
                        back[t, row : row + 1, at] = laid[t : t + 1, :]


def sweep_kernel(
    place, coupling, fields, sources, diagonal, inverse, r1, r2, x1, x2, y1, y2, yb, zb, back, inflow, out, m1, m2, u0, u1
):
    section = place[0]
    odd_x, odd_y = place[1], place[2]
    exit_side = place[3] == 1
    even, even_z = even_mask(NZ), even_mask(ZT)
    sub, lane = iotas(NZ)
    sub_z, _ = iotas(ZT)
    colours = (u0, u1)
    own, edge = slice(0, 8), slice(8, 16)

    for t in range(T):
        for k in (0, 1):
            u1[t, k + 1, own] = packed(fields[t, 2 * k], fields[t, 2 * k + 1], even, 1)
            u0[t, k + 1, own] = packed(fields[t, 2 * k], fields[t, 2 * k + 1], even, 0)
        for ref, at, width in (
            (u1, slice(t * NZ, (t + 1) * NZ), NZ),
            (u0, slice(VAL + t * ZT, VAL + (t + 1) * ZT), ZT),
        ):
            low, high = jnp.where(odd_x == 1, r1[:, at], r2[:, at]), jnp.where(odd_x == 1, r2[:, at], r1[:, at])
            ref[t, 0, own, :width] = low
            ref[t, 3, own, :width] = high
            low, high = jnp.where(odd_y == 1, y1[:, at], y2[:, at]), jnp.where(odd_y == 1, y2[:, at], y1[:, at])
            rows = lax.broadcasted_iota(jnp.int32, (8, width), 0)
            for p in range(4):
                ref[t, p, edge, :width] = jnp.where(rows < 2, roll(high, -2 * p, 0), roll(low, 6 - 2 * p, 0))

    @pl.when(exit_side)
    def _():
        for t in range(T):
            u0[t, 3] = back[t]
            u1[t, 3] = back[t]

    def around(centre, beyond):
        up = roll(jnp.where(sub == 0, beyond, centre), -1, 0)
        down = roll(jnp.where(sub == 7, beyond, centre), 1, 0)
        return up + down

    def planes(colour, unit, t):
        old, new = colours[colour], colours[1 - colour]
        if unit == "ring":
            centre = jnp.where(even, new[t, 0, own], new[t, 3, own])
            beyond = jnp.where(even, new[t, 0, edge], new[t, 3, edge])
            x_sum = jnp.where(even, new[t, 3, own] + new[t, 2, own], new[t, 0, own] + new[t, 1, own])
            return centre, beyond, x_sum, jnp.where(even, old[t, 3, own], old[t, 0, own])
        p, rows = unit
        here, other = (own, edge) if rows == 0 else (edge, own)
        centre, beyond = new[t, p, here], new[t, p, other]
        below, above = new[t, p - 1, here], new[t, p + 1, here]
        x_sum = centre + (jnp.where(even, below, above) if colour == 0 else jnp.where(even, above, below))
        return centre, beyond, x_sum, old[t, p, here]

    def inflow_of(colour, unit):
        base = 64 * colour
        if unit == "ring":
            values = jnp.where(even_z, inflow[base + 48 : base + 56], inflow[base : base + 8])
        else:
            start = base + 16 * unit[0] + 8 * unit[1]
            values = inflow[start : start + 8]
        return jnp.concatenate([values] * (NZ // ZT), axis=1)

    ring_mask = (sub + lane + odd_x) % 2 == 0
    edge_mask = jnp.where(sub == 7, 1, 0) == odd_y

    def taken(colour, unit, index, raw):
        if unit == "ring":
            return jnp.where(ring_mask, x1[index], x2[index])
        p, rows = unit
        if rows == 0:
            return packed(raw[2 * p - 2], raw[2 * p - 1], even, colour)
        at = slice((index // 4) * NZ, (index // 4 + 1) * NZ)
        row = 2 * (index % 4) + p - 1
        return jnp.where(edge_mask, yb[row : row + 1, at], zb[row : row + 1, at])

    def put(colour, unit, t, value):
        ref = colours[colour]
        if unit == "ring":
            ref[t, 0, own] = value
            ref[t, 3, own] = jnp.where(exit_side, back[t, own], value)
        else:
            ref[t, unit[0], own if unit[1] == 0 else edge] = value

    def valid(unit):
        if unit == "ring":
            return jnp.where(even, place[5], place[4])
        if unit[1] == 0:
            return None
        return jnp.where(sub == 7, place[6], place[7])

    def turbine(colour, unit):
        driving = []
        for t in range(T):
            centre, beyond, x_sum, kept = planes(colour, unit, t)
            start = inflow_of(colour, unit) if t == 0 else kept
            ahead = jnp.where(lane == NZ - 1, 0.0, roll(centre, -1, 1))
            behind = jnp.where(lane == 0, start, roll(centre, 1, 1))
            total = x_sum + around(centre, beyond) + ahead + behind
            source = taken(colour, unit, T * T + t, sources.at[t])
            driving.append(source + coupling[t] * total)
        for s in range(T):
            value = taken(colour, unit, T * s, inverse.at[s, 0]) * driving[0]
            for t in range(1, T):
                value = value + taken(colour, unit, T * s + t, inverse.at[s, t]) * driving[t]
            put(colour, unit, s, value)

    def combustor(colour, unit):
        before = None
        current = planes(colour, unit, 0)
        flag = valid(unit)
        for t in range(T):
            after = planes(colour, unit, t + 1) if t + 1 < T else None
            centre, beyond, x_sum, _ = current
            edge_ahead = 0.0 if after is None else roll(after[0], -1, 1)
            edge_behind = 0.0 if before is None else roll(before, 1, 1)
            ahead = jnp.where(lane == NZ - 1, edge_ahead, roll(centre, -1, 1))
            behind = jnp.where(lane == 0, edge_behind, roll(centre, 1, 1))
            total = x_sum + around(centre, beyond) + ahead + behind
            source = taken(colour, unit, T * T + t, sources.at[t])
            value = (source + total) / (6.0 + taken(colour, unit, t, diagonal.at[t]))
            if flag is not None:
                value = jnp.where(flag == 1, value, 0.0)
            put(colour, unit, t, value)
            before, current = centre, after

    def both(step):
        for unit in ((1, 0), (2, 0), (1, 1), (2, 1), "ring"):
            step(0, unit)
        for unit in ((1, 0), (2, 0)):
            step(1, unit)

    pl.when(section == 0)(functools.partial(both, combustor))
    pl.when(section != 0)(functools.partial(both, turbine))

    for t in range(T):
        for k in (0, 1):
            a, b = u0[t, k + 1, own], u1[t, k + 1, own]
            out[t, 2 * k] = jnp.where(even, a, b)
            out[t, 2 * k + 1] = jnp.where(even, b, a)
    for ref, pair in ((m1, 2 - odd_x), (m2, 1 + odd_x)):
        store_message(ref, lambda t: u1[t, pair, own], lambda t: u0[t, pair, own, :ZT])


def shape(*dims):
    return jax.ShapeDtypeStruct(dims, F32)


def call(kernel, outs, scalars, arrays, scratch=(), limit=24, cost=None):
    smem, vmem = (pl.BlockSpec(memory_space=pltpu.SMEM), pl.BlockSpec(memory_space=pltpu.VMEM))
    return pl.pallas_call(
        kernel,
        out_shape=outs,
        in_specs=[smem] * len(scalars) + [vmem] * len(arrays),
        out_specs=[vmem] * len(outs),
        scratch_shapes=list(scratch),
        compiler_params=pltpu.CompilerParams(vmem_limit_bytes=limit << 20),
        cost_estimate=cost,
    )(*scalars, *arrays)


def swaps(axis, first, second):
    peers = lax.axis_size(axis)
    inner = [(i, i ^ 1) for i in range(peers)]
    outer = [(i, (i + 1 ^ 1) - 1) for i in range(1, peers - 1)]
    return lax.ppermute(first, axis, inner), lax.ppermute(second, axis, outer)


def chosen_slots():
    table = np.zeros((128, 2 * ZT), np.float32)
    for c in range(2):
        for p in range(4):
            for r in range(16):
                y = r if r < 12 else r - 16
                x = 2 * (p - 1) + (c if r % 2 == 0 else 1 - c)
                block = None
                if 0 <= x < CX and 0 <= y < CY:
                    block = (0, x, y)
                elif x == -1 and 0 <= y < CY:
                    block = (1, CX - 1, y)
                elif x == CX and 0 <= y < CY:
                    block = (2, 0, y)
                elif 0 <= x < CX and y == -1:
                    block = (3, x, CY - 1)
                elif 0 <= x < CX and y == CY:
                    block = (4, x, 0)
                if block is not None:
                    table[64 * c + 16 * p + r, BLK * block[0] + CY * block[1] + block[2]] = 1.0
    return table


def shards(fields, sources, diagonal, block_inverse, coupling, donors, returns):
    values = fields[0]
    source = sources[0]
    rows_x, rows_y = lax.axis_size("gx"), lax.axis_size("gy")
    cells = rows_x * rows_y
    section, place_x, place_y = (lax.axis_index(axis) for axis in ("sa", "gx", "gy"))
    exit_side = (section == 0) & (place_x == rows_x - 1)
    place = jnp.stack(
        [
            section,
            place_x % 2,
            place_y % 2,
            exit_side.astype(jnp.int32),
            (place_x > 0).astype(jnp.int32),
            (place_x < rows_x - 1).astype(jnp.int32),
            (place_y > 0).astype(jnp.int32),
            (place_y < rows_y - 1).astype(jnp.int32),
        ]
    ).astype(jnp.int32)

    m1, m2 = call(first_kernel, [shape(8, MSG)] * 2, [place], [values])
    r1, r2 = swaps("gx", m1, m2)

    x1, x2, low, high = call(
        bulk_kernel,
        [shape(COEF, 8, NZ)] * 2 + [shape(8, BULK * NZ)] * 2,
        [place],
        [source, diagonal, block_inverse],
    )
    x1, x2 = swaps("gx", x1, x2)

    marks = returns[0].astype(F32).reshape(T, CY, NZ // BLK)
    marks = jnp.pad(marks, ((0, 0), (0, 0), (0, ZT - NZ // BLK)))
    marks_low, marks_high = (jnp.pad(marks[:, row], ((0, 1), (0, 0))) for row in (0, CY - 1))
    full = MSG + BULK * NZ + ZT
    y1, y2 = call(
        functools.partial(corner_kernel, True),
        [shape(8, full)] * 2,
        [place],
        [m1, m2, r1, r2, low, high, marks_low, marks_high],
    )
    y1, y2 = swaps("gy", y1, y2)

    matches = donors[None, :, 2] == jnp.arange(cells, dtype=jnp.int32)[:, None]
    slot_source = jnp.sum(jnp.where(matches, donors[None, :, 0], 0), axis=1)
    slot_block = jnp.sum(jnp.where(matches, donors[None, :, 1], 0), axis=1)
    exit_face = values[:, CX - 1].reshape(-1, BLK)
    sending = exit_side & (slot_source == place_y)
    downward = jnp.where(sending[:, None], jnp.take(exit_face, slot_block, axis=0), 0.0)
    downward = jnp.pad(downward.reshape(rows_x, rows_y, BLK), ((1, 1), (1, 1), (0, 0)))
    five = [downward[1:-1, 1:-1], downward[:-2, 1:-1], downward[2:, 1:-1], downward[1:-1, :-2], downward[1:-1, 2:]]
    downward = jnp.pad(jnp.concatenate(five, axis=2).reshape(cells, 5 * BLK), ((0, 0), (0, 2 * ZT - 5 * BLK)))
    inlet = jnp.where(section == 1, values[0, :, :, 0].reshape(1, BLK), 0.0)
    upward = jnp.broadcast_to(jnp.pad(inlet, ((0, 0), (0, 2 * ZT - BLK))), (cells, 2 * ZT))
    outgoing = jnp.stack([upward, downward], axis=1).reshape(2 * cells, 2 * ZT)
    blocks = lax.all_to_all(outgoing, ("gx", "gy", "sa"), split_axis=0, concat_axis=0, tiled=True)
    if blocks.shape[0] < ZT:
        blocks = jnp.pad(blocks, ((0, ZT - blocks.shape[0]), (0, 0)))
    end = MSG + BULK * NZ
    back, inflow = call(
        interface_kernel,
        [shape(T, 16, NZ), shape(128, ZT)],
        [place],
        [blocks, marks, y1[:, end:], y2[:, end:], jnp.asarray(chosen_slots())],
    )

    yb, zb = y1[:, MSG:end], y2[:, MSG:end]
    y1, y2 = y1[:, :MSG], y2[:, :MSG]
    for sweep in range(SWEEPS):
        if sweep > 0:
            r1, r2 = swaps("gx", m1, m2)
            y1, y2 = call(functools.partial(corner_kernel, False), [shape(8, MSG)] * 2, [place], [m1, m2, r1, r2])
            y1, y2 = swaps("gy", y1, y2)
        values, m1, m2 = call(
            sweep_kernel,
            [shape(T, CX, CY, NZ), shape(8, MSG), shape(8, MSG)],
            [place, coupling],
            [values, source, diagonal, block_inverse, r1, r2, x1, x2, y1, y2, yb, zb, back, inflow],
            [pltpu.VMEM((T, 4, 16, NZ), F32)] * 2,
            40,
        )
    return values[None]


def solution(mesh):
    return jax.shard_map(
        shards,
        mesh=mesh,
        in_specs=(
            P("sa", None, "gx", "gy", None),
            P("sa", None, "gx", "gy", None),
            P(None, "gx", "gy", None),
            P(None, None, "gx", "gy", None),
            P(),
            P(),
            P("gy", None),
        ),
        out_specs=P("sa", None, "gx", "gy", None),
        check_vma=False,
    )
```

time: 345 us -> 146 us (0.42)
  the two profiles are of different devices: /device:TPU:40 before, /device:TPU:18 now
where the time goes in v1:
time: 146 us; the launch traced here: 144 us
  starting transfers between devices  51.9 us (36%)
  waiting for transfers between devices  37.8 us (26%)
  local copies, waits for them, and re-layouts  32.8 us (22%)
  Pallas kernels  18.3 us (13%)
  other arithmetic  3.01 us (2%)
    ppermute x18, starting transfers between devices, swaps(): return (lax.ppermute(first, axis, inner), lax.ppermute(second, axis, outer))  40.9 us
    ppermute x18, waiting for transfers between devices, swaps(): return (lax.ppermute(first, axis, inner), lax.ppermute(second, axis, outer))  31.7 us
    pallas_call x11, Pallas kernels, call(): pl.pallas_call(kernel, out_shape=outs, in_specs=[smem] * len(scalars) + [...  18.3 us
    unnamed x36, local copies, waits for them, and re-layouts  13.1 us
    all_to_all x1, starting transfers between devices, shards(): lax.all_to_all(outgoing, ('gx', 'gy', 'sa'), split_axis=0, concat_axis=0,...  11 us
    all_to_all x1, waiting for transfers between devices, shards(): lax.all_to_all(outgoing, ('gx', 'gy', 'sa'), split_axis=0, concat_axis=0,...  6.1 us
    concatenate x2, local copies, waits for them, and re-layouts, shards(): jnp.concatenate(five, axis=2).reshape(cells, 5 * BLK)  3.07 us
  transfers between devices with their start and end apart: 19, of which 10 were waited for; matrix products, arithmetic and copies ran while one was open for 15% of the time, Pallas kernels for 3%

profile of v1, /device:TPU:18, one launch (start us, length us, event | category | flops | bytes accessed | tf_op | source)
XLA Modules:
  0.0 144.2 jit_solution(8619015627011086356)
XLA Ops:
  0.1 1.0 copy-done.7
  1.1 1.3 shard_map.82
  2.4 2.5 %collective-permute-start.1 = (f32[8,4480]{1,0:T(8,128)}, f32[8,4480]{1,0:T(8,128)S(1)}, u32[]{:S(2)}, u32[]{:S(2)}) collective-permute-start(f32[8,4480]{1,0:T(8,128)} %get-tuple-element.32.m2), channel_id=1, source_target_pairs={{16,32},{32,16},{48,64},{64,48},{80,96},{96,80},{17,33},{33,17},{4... | collective-permute-start | bytes 430088 | tf_op jit(solution)/shard_map/ppermute | solution.py:331
  4.9 1.9 %copy-done = f32[7,7,4,8,512]{4,3,2,1,0:T(8,128)S(1)} copy-done((f32[7,7,4,8,512]{4,3,2,1,0:T(8,128)S(1)}, f32[7,7,4,8,512]{4,3,2,1,0:T(8,128)}, u32[]{:S(2)}) %copy-start) | copy-done | bytes 3211288
  6.8 1.0 copy-done.2
  7.8 1.0 copy-done.5
  8.8 2.2 %shard_map.83 = (f32[56,8,512]{2,1,0:T(8,128)}, f32[56,8,512]{2,1,0:T(8,128)}, f32[8,7168]{1,0:T(8,128)S(1)}, f32[8,7168]{1,0:T(8,128)S(1)}) custom-call(s32[8]{0:T(128)S(1)} %stack.61.place, f32[7,4,8,512]{3,2,1,0:T(8,128)S(1)} %bitcast.45, f32[7,4,8,512]{3,2,1,0:T(8,128)S(1)} %copy-done.5, f32[7,7,4,8,512]{4,3,2,1,0:T(8,128)S(1)} %copy-done), custom_call_target="tpu_custom_call" | custom-call | tf_op jit(solution)/shard_map/pallas_call | solution.py:316
  11.0 0.7 copy-done.9
  11.7 0.7 copy-done.11
  12.4 0.8 collective-permute-start.2
  13.2 2.5 %collective-permute-start.3 = (f32[56,8,512]{2,1,0:T(8,128)}, f32[56,8,512]{2,1,0:T(8,128)}, u32[]{:S(2)}, u32[]{:S(2)}) collective-permute-start(f32[56,8,512]{2,1,0:T(8,128)} %get-tuple-element.34), channel_id=1, source_target_pairs={{16,32},{32,16},{48,64},{64,48},{80,96},{96,80},{17,33},{33,17},{4... | collective-permute-start | bytes 2752520 | tf_op jit(solution)/shard_map/ppermute | solution.py:331
  16.0 1.6 %slice.76 = f32[7,1,8,512]{3,2,1,0:T(8,128)} slice(f32[7,4,8,512]{3,2,1,0:T(8,128)} %bitcast.50), slice={[0:7], [3:4], [0:8], [0:512]} | slice | bytes 229376 | tf_op jit(solution)/shard_map/slice | solution.py:403
  18.9 1.8 %reshape_squeeze.4 = f32[896,32]{1,0:T(8,128)} reshape(f32[7,1,8,512]{3,2,1,0:T(8,128)} %slice.76) | data formatting | bytes 229376 | tf_op jit(solution)/shard_map/reshape;squeeze | solution.py:403
  20.7 1.6 %gather_fusion = f32[64,32]{1,0:T(8,128)S(1)} fusion(f32[896,32]{1,0:T(8,128)} %reshape_squeeze.4, s32[1024]{0:T(1024)S(1)} %pad_clamp_fusion), kind=kCustom, calls=%fused_computation | custom fusion | bytes 16640 | tf_op jit(solution)/shard_map/jit(_take)/gather | solution.py:405
  22.4 0.7 select_select_fusion
  23.0 1.4 fusion.4
  24.4 0.8 pad_slice_fusion.4
  25.3 1.5 %fusion.3 = (f32[64,32]{1,0:T(8,128)S(1)}, f32[64,32]{1,0:T(8,128)}, f32[64,32]{1,0:T(8,128)}, f32[64,32]{1,0:T(8,128)}) fusion(f32[8,8,32]{2,1,0:T(8,128)} %fusion.4), kind=kLoop, calls=%fused_computation.11 | loop fusion | bytes 40960 | tf_op jit(solution)/shard_map/concatenate | solution.py:408
  26.8 0.9 copy-done.10
  27.8 0.9 copy-done.12
  28.7 2.0 %shard_map.84 = (f32[8,11776]{1,0:T(8,128)}, f32[8,11776]{1,0:T(8,128)}) custom-call(s32[8]{0:T(128)S(1)} %stack.61.place, f32[8,4480]{1,0:T(8,128)} %get-tuple-element.31.m1, f32[8,4480]{1,0:T(8,128)} %get-tuple-element.32.m2, f32[8,4480]{1,0:T(8,128)S(1)} %collective-permute-done.r1, f32[8,4480]{1,0:T(8,128)S(1)} %collective-permute-done.1.r2, ...), custom_call_target="tpu_custom_call" | custom-call | tf_op jit(solution)/shard_map/pallas_call | solution.py:316
  30.7 3.9 %collective-permute-start.4 = (f32[8,11776]{1,0:T(8,128)}, f32[8,11776]{1,0:T(8,128)}, u32[]{:S(2)}, u32[]{:S(2)}) collective-permute-start(f32[8,11776]{1,0:T(8,128)} %get-tuple-element.37), channel_id=1, source_target_pairs={{0,2},{2,0},{4,6},{6,4},{8,10},{10,8},{12,14},{14,12},{1,3},{3,1},... | collective-permute-start | bytes 1130504 | tf_op jit(solution)/shard_map/ppermute | solution.py:331
  34.6 1.9 %collective-permute-start.5 = (f32[8,11776]{1,0:T(8,128)}, f32[8,11776]{1,0:T(8,128)}, u32[]{:S(2)}, u32[]{:S(2)}) collective-permute-start(f32[8,11776]{1,0:T(8,128)} %get-tuple-element.38), channel_id=1, source_target_pairs={{2,4},{4,2},{6,8},{8,6},{10,12},{12,10},{3,5},{5,3},{7,9},{9,7},{1... | collective-permute-start | bytes 1130504 | tf_op jit(solution)/shard_map/ppermute | solution.py:331
  36.5 0.8 fusion.5
  37.4 1.5 %concatenate.16 = f32[64,160]{1,0:T(8,128)} concatenate(f32[64,32]{1,0:T(8,128)} %select_select_fusion, f32[64,32]{1,0:T(8,128)} %get-tuple-element.62, f32[64,32]{1,0:T(8,128)} %get-tuple-element.60, f32[64,32]{1,0:T(8,128)} %get-tuple-element.61, f32[64,32]{1,0:T(8,128)S(1)} %get-tuple-element.59), dimensions={1} | concatenate | bytes 81920 | tf_op jit(solution)/shard_map/concatenate | solution.py:408
  38.9 0.8 pad_bitcast_fusion
  39.8 0.8 copy.13
  40.5 1.8 %all_to_all.10 = f32[128,1,256]{2,1,0:T(1,128)} reshape(f32[64,2,256]{2,1,0:T(2,128)} %copy.13) | data formatting | bytes 262144 | tf_op jit(solution)/shard_map/all_to_all | solution.py:412
  42.3 11.0 %all-to-all-start = ((f32[128,1,256]{2,1,0:T(1,128)}), f32[128,1,256]{2,1,0:T(1,128)}, u32[]{:S(2)}, u32[]{:S(2)}) async-start(f32[128,1,256]{2,1,0:T(1,128)} %all_to_all.10), calls=%async_computation | async-start | bytes 262144 | tf_op jit(solution)/shard_map/all_to_all | solution.py:412
  53.4 0.8 pad.25.marks
  54.1 6.1 %all-to-all-done = f32[128,1,256]{2,1,0:T(1,128)} async-done(((f32[128,1,256]{2,1,0:T(1,128)}), f32[128,1,256]{2,1,0:T(1,128)}, u32[]{:S(2)}, u32[]{:S(2)}) %all-to-all-start) | async-done | bytes 131104 | tf_op jit(solution)/shard_map/all_to_all | solution.py:412
  60.2 0.9 copy.21
  61.1 0.7 slice.77.marks1
  61.8 0.7 slice.78.marks2
  62.5 0.9 copy-done.13
  64.1 0.9 slice.71.y1
  65.0 1.0 slice.73.yb
  65.9 0.9 slice.72.y2
  66.9 1.0 slice.74.zb
  67.9 1.0 copy-done.3
  68.9 1.0 copy-done.6
  69.9 1.0 copy-done.8
  70.9 2.4 %shard_map.86 = (f32[7,4,8,512]{3,2,1,0:T(8,128)S(1)}, f32[8,4480]{1,0:T(8,128)S(1)}, f32[8,4480]{1,0:T(8,128)S(1)}) custom-call(s32[8]{0:T(128)S(1)} %stack.61.place, f32[7]{0:T(128)S(1)} %copy-done.14, f32[7,4,8,512]{3,2,1,0:T(8,128)S(1)} %bitcast.53, f32[7,4,8,512]{3,2,1,0:T(8,128)S(1)} %bitcast.46, f32[7,4,8,512]{3,2,1,0:T(8,128)S(1)} %copy-done.6, ...), custom_call_target="tpu_custom_call" | custom-call | tf_op jit(solution)/shard_map/pallas_call | solution.py:316
  73.5 4.0 %collective-permute-start.7 = (f32[8,4480]{1,0:T(8,128)S(1)}, f32[8,4480]{1,0:T(8,128)S(1)}, u32[]{:S(2)}, u32[]{:S(2)}) collective-permute-start(f32[8,4480]{1,0:T(8,128)S(1)} %get-tuple-element.43.m2), channel_id=1, source_target_pairs={{16,32},{32,16},{48,64},{64,48},{80,96},{96,80},{17,33},{33,17},{4... | collective-permute-start | bytes 430088 | tf_op jit(solution)/shard_map/ppermute | solution.py:331
  77.5 2.8 %collective-permute-done.7.r2 = f32[8,4480]{1,0:T(8,128)S(1)} collective-permute-done((f32[8,4480]{1,0:T(8,128)S(1)}, f32[8,4480]{1,0:T(8,128)S(1)}, u32[]{:S(2)}, u32[]{:S(2)}) %collective-permute-start.7) | collective-permute-done | bytes 143392 | tf_op jit(solution)/shard_map/ppermute | solution.py:331
  80.9 1.3 collective-permute-start.8
  82.2 5.1 %collective-permute-start.9 = (f32[8,4480]{1,0:T(8,128)S(1)}, f32[8,4480]{1,0:T(8,128)S(1)}, u32[]{:S(2)}, u32[]{:S(2)}) collective-permute-start(f32[8,4480]{1,0:T(8,128)S(1)} %get-tuple-element.45), channel_id=1, source_target_pairs={{2,4},{4,2},{6,8},{8,6},{10,12},{12,10},{3,5},{5,3},{7,9},{9,7},{1... | collective-permute-start | bytes 430088 | tf_op jit(solution)/shard_map/ppermute | solution.py:331
  87.6 4.0 %collective-permute-done.9.y2 = f32[8,4480]{1,0:T(8,128)S(1)} collective-permute-done((f32[8,4480]{1,0:T(8,128)S(1)}, f32[8,4480]{1,0:T(8,128)S(1)}, u32[]{:S(2)}, u32[]{:S(2)}) %collective-permute-start.9) | collective-permute-done | bytes 143392 | tf_op jit(solution)/shard_map/ppermute | solution.py:331
  91.5 2.5 %shard_map.88 = (f32[7,4,8,512]{3,2,1,0:T(8,128)S(1)}, f32[8,4480]{1,0:T(8,128)S(1)}, f32[8,4480]{1,0:T(8,128)S(1)}) custom-call(s32[8]{0:T(128)S(1)} %stack.61.place, f32[7]{0:T(128)S(1)} %copy-done.14, f32[7,4,8,512]{3,2,1,0:T(8,128)S(1)} %get-tuple-element.41.fields, f32[7,4,8,512]{3,2,1,0:T(8,128)S(1)} %bitcast.47, f32[7,4,8,512]{3,2,1,0:T(8,128)S(1)} %copy-done.6, ...), custom_call_target="tpu_custom_call" | custom-call | tf_op jit(solution)/shard_map/pallas_call | solution.py:316
  94.0 5.9 %collective-permute-start.10 = (f32[8,4480]{1,0:T(8,128)S(1)}, f32[8,4480]{1,0:T(8,128)S(1)}, u32[]{:S(2)}, u32[]{:S(2)}) collective-permute-start(f32[8,4480]{1,0:T(8,128)S(1)} %get-tuple-element.47.m1), channel_id=1, source_target_pairs={{0,16},{16,0},{32,48},{48,32},{64,80},{80,64},{96,112},{112,96},{1... | collective-permute-start | bytes 430088 | tf_op jit(solution)/shard_map/ppermute | solution.py:331
  99.9 1.9 %collective-permute-start.11 = (f32[8,4480]{1,0:T(8,128)S(1)}, f32[8,4480]{1,0:T(8,128)S(1)}, u32[]{:S(2)}, u32[]{:S(2)}) collective-permute-start(f32[8,4480]{1,0:T(8,128)S(1)} %get-tuple-element.48.m2), channel_id=1, source_target_pairs={{16,32},{32,16},{48,64},{64,48},{80,96},{96,80},{17,33},{33,17},{4... | collective-permute-start | bytes 430088 | tf_op jit(solution)/shard_map/ppermute | solution.py:331
  101.8 4.5 %collective-permute-done.11.r2 = f32[8,4480]{1,0:T(8,128)S(1)} collective-permute-done((f32[8,4480]{1,0:T(8,128)S(1)}, f32[8,4480]{1,0:T(8,128)S(1)}, u32[]{:S(2)}, u32[]{:S(2)}) %collective-permute-start.11) | collective-permute-done | bytes 143392 | tf_op jit(solution)/shard_map/ppermute | solution.py:331
  106.9 2.2 %collective-permute-start.12 = (f32[8,4480]{1,0:T(8,128)S(1)}, f32[8,4480]{1,0:T(8,128)S(1)}, u32[]{:S(2)}, u32[]{:S(2)}) collective-permute-start(f32[8,4480]{1,0:T(8,128)S(1)} %get-tuple-element.49), channel_id=1, source_target_pairs={{0,2},{2,0},{4,6},{6,4},{8,10},{10,8},{12,14},{14,12},{1,3},{3,1},... | collective-permute-start | bytes 430088 | tf_op jit(solution)/shard_map/ppermute | solution.py:331
  109.1 3.3 %collective-permute-start.13 = (f32[8,4480]{1,0:T(8,128)S(1)}, f32[8,4480]{1,0:T(8,128)S(1)}, u32[]{:S(2)}, u32[]{:S(2)}) collective-permute-start(f32[8,4480]{1,0:T(8,128)S(1)} %get-tuple-element.50), channel_id=1, source_target_pairs={{2,4},{4,2},{6,8},{8,6},{10,12},{12,10},{3,5},{5,3},{7,9},{9,7},{1... | collective-permute-start | bytes 430088 | tf_op jit(solution)/shard_map/ppermute | solution.py:331
  112.4 2.6 %collective-permute-done.12.y1 = f32[8,4480]{1,0:T(8,128)S(1)} collective-permute-done((f32[8,4480]{1,0:T(8,128)S(1)}, f32[8,4480]{1,0:T(8,128)S(1)}, u32[]{:S(2)}, u32[]{:S(2)}) %collective-permute-start.12) | collective-permute-done | bytes 143392 | tf_op jit(solution)/shard_map/ppermute | solution.py:331
  115.0 5.0 %collective-permute-done.13.y2 = f32[8,4480]{1,0:T(8,128)S(1)} collective-permute-done((f32[8,4480]{1,0:T(8,128)S(1)}, f32[8,4480]{1,0:T(8,128)S(1)}, u32[]{:S(2)}, u32[]{:S(2)}) %collective-permute-start.13) | collective-permute-done | bytes 143392 | tf_op jit(solution)/shard_map/ppermute | solution.py:331
  119.9 2.3 %shard_map.90 = (f32[7,4,8,512]{3,2,1,0:T(8,128)S(1)}, f32[8,4480]{1,0:T(8,128)S(1)}, f32[8,4480]{1,0:T(8,128)S(1)}) custom-call(s32[8]{0:T(128)S(1)} %stack.61.place, f32[7]{0:T(128)S(1)} %copy-done.14, f32[7,4,8,512]{3,2,1,0:T(8,128)S(1)} %get-tuple-element.46.fields, f32[7,4,8,512]{3,2,1,0:T(8,128)S(1)} %bitcast.48, f32[7,4,8,512]{3,2,1,0:T(8,128)S(1)} %copy-done.6, ...), custom_call_target="tpu_custom_call" | custom-call | tf_op jit(solution)/shard_map/pallas_call | solution.py:316
  122.3 1.9 %collective-permute-start.15 = (f32[8,4480]{1,0:T(8,128)S(1)}, f32[8,4480]{1,0:T(8,128)S(1)}, u32[]{:S(2)}, u32[]{:S(2)}) collective-permute-start(f32[8,4480]{1,0:T(8,128)S(1)} %get-tuple-element.53.m2), channel_id=1, source_target_pairs={{16,32},{32,16},{48,64},{64,48},{80,96},{96,80},{17,33},{33,17},{4... | collective-permute-start | bytes 430088 | tf_op jit(solution)/shard_map/ppermute | solution.py:331
  124.3 4.5 %collective-permute-done.15.r2 = f32[8,4480]{1,0:T(8,128)S(1)} collective-permute-done((f32[8,4480]{1,0:T(8,128)S(1)}, f32[8,4480]{1,0:T(8,128)S(1)}, u32[]{:S(2)}, u32[]{:S(2)}) %collective-permute-start.15) | collective-permute-done | bytes 143392 | tf_op jit(solution)/shard_map/ppermute | solution.py:331
  129.4 1.5 %collective-permute-start.16 = (f32[8,4480]{1,0:T(8,128)S(1)}, f32[8,4480]{1,0:T(8,128)S(1)}, u32[]{:S(2)}, u32[]{:S(2)}) collective-permute-start(f32[8,4480]{1,0:T(8,128)S(1)} %get-tuple-element.54), channel_id=1, source_target_pairs={{0,2},{2,0},{4,6},{6,4},{8,10},{10,8},{12,14},{14,12},{1,3},{3,1},... | collective-permute-start | bytes 430088 | tf_op jit(solution)/shard_map/ppermute | solution.py:331
  130.9 2.0 %collective-permute-start.17 = (f32[8,4480]{1,0:T(8,128)S(1)}, f32[8,4480]{1,0:T(8,128)S(1)}, u32[]{:S(2)}, u32[]{:S(2)}) collective-permute-start(f32[8,4480]{1,0:T(8,128)S(1)} %get-tuple-element.55), channel_id=1, source_target_pairs={{2,4},{4,2},{6,8},{8,6},{10,12},{12,10},{3,5},{5,3},{7,9},{9,7},{1... | collective-permute-start | bytes 430088 | tf_op jit(solution)/shard_map/ppermute | solution.py:331
  132.9 4.2 %collective-permute-done.16.y1 = f32[8,4480]{1,0:T(8,128)S(1)} collective-permute-done((f32[8,4480]{1,0:T(8,128)S(1)}, f32[8,4480]{1,0:T(8,128)S(1)}, u32[]{:S(2)}, u32[]{:S(2)}) %collective-permute-start.16) | collective-permute-done | bytes 143392 | tf_op jit(solution)/shard_map/ppermute | solution.py:331
  137.1 4.0 %collective-permute-done.17.y2 = f32[8,4480]{1,0:T(8,128)S(1)} collective-permute-done((f32[8,4480]{1,0:T(8,128)S(1)}, f32[8,4480]{1,0:T(8,128)S(1)}, u32[]{:S(2)}, u32[]{:S(2)}) %collective-permute-start.17) | collective-permute-done | bytes 143392 | tf_op jit(solution)/shard_map/ppermute | solution.py:331
  141.1 3.1 %shard_map.92 = (f32[7,4,8,512]{3,2,1,0:T(8,128)}, f32[8,4480]{1,0:T(8,128)}, f32[8,4480]{1,0:T(8,128)}) custom-call(s32[8]{0:T(128)S(1)} %stack.61.place, f32[7]{0:T(128)S(1)} %copy-done.14, f32[7,4,8,512]{3,2,1,0:T(8,128)S(1)} %get-tuple-element.51.fields, f32[7,4,8,512]{3,2,1,0:T(8,128)S(1)} %bitcast.49, f32[7,4,8,512]{3,2,1,0:T(8,128)S(1)} %copy-done.6, ...), custom_call_target="tpu_custom_call" | custom-call | tf_op jit(solution)/shard_map/pallas_call | solution.py:316
  (57 shorter events, 5.0 us)
Async XLA Ops:
  0.0 15.7 %copy-start.16 = (s32[64,3]{0,1:T(4,128)S(1)}, s32[64,3]{0,1:T(4,128)}, u32[]{:S(2)}) copy-start(s32[64,3]{0,1:T(4,128)} %param.13) | copy-start | bytes 2308
  0.0 18.2 %copy-start.15 = (s32[1,896]{1,0:T(1,128)S(1)}, s32[1,896]{1,0:T(1,128)}, u32[]{:S(2)}) copy-start(s32[1,896]{1,0:T(1,128)} %param.14) | copy-start | bytes 10756
  0.1 1.0 copy-start.7
  2.4 24.4 %collective-permute-start = (f32[8,4480]{1,0:T(8,128)}, f32[8,4480]{1,0:T(8,128)S(1)}, u32[]{:S(2)}, u32[]{:S(2)}) collective-permute-start(f32[8,4480]{1,0:T(8,128)} %get-tuple-element.31.m1), channel_id=1, source_target_pairs={{0,16},{16,0},{32,48},{48,32},{64,80},{80,64},{96,112},{112,96},{1... | collective-permute-start | bytes 430088 | tf_op jit(solution)/shard_map/ppermute | solution.py:331
  2.4 24.4 %collective-permute-start.1 = (f32[8,4480]{1,0:T(8,128)}, f32[8,4480]{1,0:T(8,128)S(1)}, u32[]{:S(2)}, u32[]{:S(2)}) collective-permute-start(f32[8,4480]{1,0:T(8,128)} %get-tuple-element.32.m2), channel_id=1, source_target_pairs={{16,32},{32,16},{48,64},{64,48},{80,96},{96,80},{17,33},{33,17},{4... | collective-permute-start | bytes 430088 | tf_op jit(solution)/shard_map/ppermute | solution.py:331
  4.9 1.9 %copy-start = (f32[7,7,4,8,512]{4,3,2,1,0:T(8,128)S(1)}, f32[7,7,4,8,512]{4,3,2,1,0:T(8,128)}, u32[]{:S(2)}) copy-start(f32[7,7,4,8,512]{4,3,2,1,0:T(8,128)} %inverse.9) | copy-start | bytes 9633796
  6.8 1.0 copy-start.2
  7.8 1.0 copy-start.5
  8.8 59.0 %copy-start.14 = (f32[7]{0:T(128)S(1)}, f32[7]{0:T(128)}, u32[]{:S(2)}) copy-start(f32[7]{0:T(128)} %coupling.7) | copy-start | bytes 88
  11.0 0.7 copy-start.9
  11.7 0.7 copy-start.11
  12.4 55.5 %copy-start.1 = (f32[7,7,4,8,512]{4,3,2,1,0:T(8,128)S(1)}, f32[7,7,4,8,512]{4,3,2,1,0:T(8,128)}, u32[]{:S(2)}) copy-start(f32[7,7,4,8,512]{4,3,2,1,0:T(8,128)} %inverse.9) | copy-start | bytes 9633796
  12.4 55.5 %collective-permute-start.2 = (f32[56,8,512]{2,1,0:T(8,128)}, f32[56,8,512]{2,1,0:T(8,128)}, u32[]{:S(2)}, u32[]{:S(2)}) collective-permute-start(f32[56,8,512]{2,1,0:T(8,128)} %get-tuple-element.33), channel_id=1, source_target_pairs={{0,16},{16,0},{32,48},{48,32},{64,80},{80,64},{96,112},{112,96},{1... | collective-permute-start | bytes 2752520 | tf_op jit(solution)/shard_map/ppermute | solution.py:331
  13.2 54.6 %collective-permute-start.3 = (f32[56,8,512]{2,1,0:T(8,128)}, f32[56,8,512]{2,1,0:T(8,128)}, u32[]{:S(2)}, u32[]{:S(2)}) collective-permute-start(f32[56,8,512]{2,1,0:T(8,128)} %get-tuple-element.34), channel_id=1, source_target_pairs={{16,32},{32,16},{48,64},{64,48},{80,96},{96,80},{17,33},{33,17},{4... | collective-permute-start | bytes 2752520 | tf_op jit(solution)/shard_map/ppermute | solution.py:331
  26.8 0.9 copy-start.10
  27.8 0.9 copy-start.12
  30.7 30.4 %collective-permute-start.4 = (f32[8,11776]{1,0:T(8,128)}, f32[8,11776]{1,0:T(8,128)}, u32[]{:S(2)}, u32[]{:S(2)}) collective-permute-start(f32[8,11776]{1,0:T(8,128)} %get-tuple-element.37), channel_id=1, source_target_pairs={{0,2},{2,0},{4,6},{6,4},{8,10},{10,8},{12,14},{14,12},{1,3},{3,1},... | collective-permute-start | bytes 1130504 | tf_op jit(solution)/shard_map/ppermute | solution.py:331
  34.6 27.3 %collective-permute-start.5 = (f32[8,11776]{1,0:T(8,128)}, f32[8,11776]{1,0:T(8,128)}, u32[]{:S(2)}, u32[]{:S(2)}) collective-permute-start(f32[8,11776]{1,0:T(8,128)} %get-tuple-element.38), channel_id=1, source_target_pairs={{2,4},{4,2},{6,8},{8,6},{10,12},{12,10},{3,5},{5,3},{7,9},{9,7},{1... | collective-permute-start | bytes 1130504 | tf_op jit(solution)/shard_map/ppermute | solution.py:331
  42.3 17.9 %all-to-all-start = ((f32[128,1,256]{2,1,0:T(1,128)}), f32[128,1,256]{2,1,0:T(1,128)}, u32[]{:S(2)}, u32[]{:S(2)}) async-start(f32[128,1,256]{2,1,0:T(1,128)} %all_to_all.10), calls=%async_computation | async-start | bytes 262144 | tf_op jit(solution)/shard_map/all_to_all | solution.py:412
  62.5 0.9 copy-start.13
  67.9 1.0 copy-start.3
  68.9 1.0 copy-start.6
  69.9 1.0 copy-start.8
  70.9 20.6 %copy-start.4 = (f32[1,7,4,8,512]{4,3,2,1,0:T(8,128)S(1)}, f32[1,7,4,8,512]{4,3,2,1,0:T(8,128)}, u32[]{:S(2)}) copy-start(f32[1,7,4,8,512]{4,3,2,1,0:T(8,128)} %param.9) | copy-start | bytes 1376260
  73.3 4.2 %collective-permute-start.6 = (f32[8,4480]{1,0:T(8,128)S(1)}, f32[8,4480]{1,0:T(8,128)S(1)}, u32[]{:S(2)}, u32[]{:S(2)}) collective-permute-start(f32[8,4480]{1,0:T(8,128)S(1)} %get-tuple-element.42.m1), channel_id=1, source_target_pairs={{0,16},{16,0},{32,48},{48,32},{64,80},{80,64},{96,112},{112,96},{1... | collective-permute-start | bytes 430088 | tf_op jit(solution)/shard_map/ppermute | solution.py:331
  73.5 6.7 %collective-permute-start.7 = (f32[8,4480]{1,0:T(8,128)S(1)}, f32[8,4480]{1,0:T(8,128)S(1)}, u32[]{:S(2)}, u32[]{:S(2)}) collective-permute-start(f32[8,4480]{1,0:T(8,128)S(1)} %get-tuple-element.43.m2), channel_id=1, source_target_pairs={{16,32},{32,16},{48,64},{64,48},{80,96},{96,80},{17,33},{33,17},{4... | collective-permute-start | bytes 430088 | tf_op jit(solution)/shard_map/ppermute | solution.py:331
  80.9 6.7 %collective-permute-start.8 = (f32[8,4480]{1,0:T(8,128)S(1)}, f32[8,4480]{1,0:T(8,128)S(1)}, u32[]{:S(2)}, u32[]{:S(2)}) collective-permute-start(f32[8,4480]{1,0:T(8,128)S(1)} %get-tuple-element.44), channel_id=1, source_target_pairs={{0,2},{2,0},{4,6},{6,4},{8,10},{10,8},{12,14},{14,12},{1,3},{3,1},... | collective-permute-start | bytes 430088 | tf_op jit(solution)/shard_map/ppermute | solution.py:331
  82.2 9.4 %collective-permute-start.9 = (f32[8,4480]{1,0:T(8,128)S(1)}, f32[8,4480]{1,0:T(8,128)S(1)}, u32[]{:S(2)}, u32[]{:S(2)}) collective-permute-start(f32[8,4480]{1,0:T(8,128)S(1)} %get-tuple-element.45), channel_id=1, source_target_pairs={{2,4},{4,2},{6,8},{8,6},{10,12},{12,10},{3,5},{5,3},{7,9},{9,7},{1... | collective-permute-start | bytes 430088 | tf_op jit(solution)/shard_map/ppermute | solution.py:331
  94.0 7.8 %collective-permute-start.10 = (f32[8,4480]{1,0:T(8,128)S(1)}, f32[8,4480]{1,0:T(8,128)S(1)}, u32[]{:S(2)}, u32[]{:S(2)}) collective-permute-start(f32[8,4480]{1,0:T(8,128)S(1)} %get-tuple-element.47.m1), channel_id=1, source_target_pairs={{0,16},{16,0},{32,48},{48,32},{64,80},{80,64},{96,112},{112,96},{1... | collective-permute-start | bytes 430088 | tf_op jit(solution)/shard_map/ppermute | solution.py:331
  99.9 6.4 %collective-permute-start.11 = (f32[8,4480]{1,0:T(8,128)S(1)}, f32[8,4480]{1,0:T(8,128)S(1)}, u32[]{:S(2)}, u32[]{:S(2)}) collective-permute-start(f32[8,4480]{1,0:T(8,128)S(1)} %get-tuple-element.48.m2), channel_id=1, source_target_pairs={{16,32},{32,16},{48,64},{64,48},{80,96},{96,80},{17,33},{33,17},{4... | collective-permute-start | bytes 430088 | tf_op jit(solution)/shard_map/ppermute | solution.py:331
  106.9 8.0 %collective-permute-start.12 = (f32[8,4480]{1,0:T(8,128)S(1)}, f32[8,4480]{1,0:T(8,128)S(1)}, u32[]{:S(2)}, u32[]{:S(2)}) collective-permute-start(f32[8,4480]{1,0:T(8,128)S(1)} %get-tuple-element.49), channel_id=1, source_target_pairs={{0,2},{2,0},{4,6},{6,4},{8,10},{10,8},{12,14},{14,12},{1,3},{3,1},... | collective-permute-start | bytes 430088 | tf_op jit(solution)/shard_map/ppermute | solution.py:331
  109.1 10.8 %collective-permute-start.13 = (f32[8,4480]{1,0:T(8,128)S(1)}, f32[8,4480]{1,0:T(8,128)S(1)}, u32[]{:S(2)}, u32[]{:S(2)}) collective-permute-start(f32[8,4480]{1,0:T(8,128)S(1)} %get-tuple-element.50), channel_id=1, source_target_pairs={{2,4},{4,2},{6,8},{8,6},{10,12},{12,10},{3,5},{5,3},{7,9},{9,7},{1... | collective-permute-start | bytes 430088 | tf_op jit(solution)/shard_map/ppermute | solution.py:331
  122.2 2.0 %collective-permute-start.14 = (f32[8,4480]{1,0:T(8,128)S(1)}, f32[8,4480]{1,0:T(8,128)S(1)}, u32[]{:S(2)}, u32[]{:S(2)}) collective-permute-start(f32[8,4480]{1,0:T(8,128)S(1)} %get-tuple-element.52.m1), channel_id=1, source_target_pairs={{0,16},{16,0},{32,48},{48,32},{64,80},{80,64},{96,112},{112,96},{1... | collective-permute-start | bytes 430088 | tf_op jit(solution)/shard_map/ppermute | solution.py:331
  122.3 6.4 %collective-permute-start.15 = (f32[8,4480]{1,0:T(8,128)S(1)}, f32[8,4480]{1,0:T(8,128)S(1)}, u32[]{:S(2)}, u32[]{:S(2)}) collective-permute-start(f32[8,4480]{1,0:T(8,128)S(1)} %get-tuple-element.53.m2), channel_id=1, source_target_pairs={{16,32},{32,16},{48,64},{64,48},{80,96},{96,80},{17,33},{33,17},{4... | collective-permute-start | bytes 430088 | tf_op jit(solution)/shard_map/ppermute | solution.py:331
  129.4 7.7 %collective-permute-start.16 = (f32[8,4480]{1,0:T(8,128)S(1)}, f32[8,4480]{1,0:T(8,128)S(1)}, u32[]{:S(2)}, u32[]{:S(2)}) collective-permute-start(f32[8,4480]{1,0:T(8,128)S(1)} %get-tuple-element.54), channel_id=1, source_target_pairs={{0,2},{2,0},{4,6},{6,4},{8,10},{10,8},{12,14},{14,12},{1,3},{3,1},... | collective-permute-start | bytes 430088 | tf_op jit(solution)/shard_map/ppermute | solution.py:331
  130.9 10.2 %collective-permute-start.17 = (f32[8,4480]{1,0:T(8,128)S(1)}, f32[8,4480]{1,0:T(8,128)S(1)}, u32[]{:S(2)}, u32[]{:S(2)}) collective-permute-start(f32[8,4480]{1,0:T(8,128)S(1)} %get-tuple-element.55), channel_id=1, source_target_pairs={{2,4},{4,2},{6,8},{8,6},{10,12},{12,10},{3,5},{5,3},{7,9},{9,7},{1... | collective-permute-start | bytes 430088 | tf_op jit(solution)/shard_map/ppermute | solution.py:331

commit v2 on v1

v2 whole, which is shorter than its diff:
```python
import functools
import jax
import jax.numpy as jnp
import numpy as np
from jax import lax
from jax.experimental import pallas as pl
from jax.experimental.pallas import tpu as pltpu
from jax.sharding import PartitionSpec as P

SWEEPS = 4
BLK = 32
T = 7
CX = 4
CY = 8
NZ = 512
ZT = 128
VAL = T + 2
COEF = T * T + T
XBULK = COEF // 2
YVAL = 5
YHEAD = YVAL + 4
YBULK = T * T // 4 + 1
F32 = jnp.float32


def iotas(width):
    sub = lax.broadcasted_iota(jnp.int32, (8, width), 0)
    lane = lax.broadcasted_iota(jnp.int32, (8, width), 1)
    return sub, lane


def even_mask(width):
    sub, lane = iotas(width)
    return (sub + lane) % 2 == 0


def roll(array, shift, axis):
    size = array.shape[axis]
    shift = shift % size
    return array if shift == 0 else pltpu.roll(array, shift, axis)


def packed(pair_low, pair_high, even, colour):
    return jnp.where(even, pair_low, pair_high) if colour == 0 else jnp.where(even, pair_high, pair_low)


def store_message(ref, ones, zeros_first):
    for t in range(T):
        ref[t] = ones(t)
        ref[T + t // 4, :, (t % 4) * ZT : (t % 4 + 1) * ZT] = zeros_first(t)
    ref[T + 1, :, 3 * ZT :] = jnp.zeros((8, ZT), F32)


def wait_for(copies):
    for copy in copies:
        copy.wait()


def lines(ref, index, row):
    found = [ref[pl.ds(128 * index + 8 * z + row, 8, stride=32), :] for z in range(NZ // ZT)]
    return jnp.concatenate(found, axis=1)


def second_half(array):
    return roll(array, 4, 0)


def row_of_colour_0(raw, row, lane):
    return jnp.where((lane + row) % 2 == 0, raw, roll(raw, -1, 0))


def interleaved(first, second, sub):
    return jnp.where(sub % 2 == 0, first, roll(second, 1, 0))


def opening_kernel(
    place, donors, fields, sources, diagonal, inverse, m1, m2, b1, b2, payload, blocks, coef, inv, sems
):
    section, odd, place_y, odd_y = place[0], place[1], place[9], place[2] == 1
    exit_side = place[3] == 1
    loads = [
        pltpu.make_async_copy(sources, coef.at[0], sems.at[0]),
        pltpu.make_async_copy(diagonal, coef.at[1], sems.at[1]),
        pltpu.make_async_copy(inverse, inv, sems.at[2]),
    ]
    for load in loads:
        load.start()
    even, even_z = even_mask(NZ), even_mask(ZT)
    for ref, pair in ((m1, 1 - odd), (m2, odd)):
        store_message(
            ref,
            lambda t: packed(fields[t, 2 * pair], fields[t, 2 * pair + 1], even, 1),
            lambda t: packed(fields[t, 2 * pair, :, :ZT], fields[t, 2 * pair + 1, :, :ZT], even_z, 0),
        )

    sub, lane = iotas(ZT)
    payload[...] = jnp.zeros_like(payload)
    cells = blocks.shape[0]

    @pl.when(exit_side)
    def _():
        for entry in range(cells):
            gy, block, slot = donors[3 * entry], donors[3 * entry + 1], donors[3 * entry + 2]
            piece, row, column = block // 128, block % 128 // 16, block % 16
            start = pl.multiple_of(column // 4 * ZT, ZT)
            found = fields[piece, CX - 1, :, pl.ds(start, ZT)]
            found = pltpu.roll(pltpu.roll(found, (8 - row) % 8, 0), (ZT - column % 4 * BLK) % ZT, 1)
            blocks[pl.ds(slot, 1), :] = jnp.where((lane < BLK) & (gy == place_y), found, 0.0)[:1]
        tiles = cells // 8
        zero = jnp.zeros((8, ZT), F32)
        for tile in range(tiles):
            here = blocks[8 * tile : 8 * tile + 8]
            below = blocks[8 * tile - 8 : 8 * tile] if tile > 0 else zero
            above = blocks[8 * tile + 8 : 8 * tile + 16] if tile + 1 < tiles else zero
            left = jnp.where(sub == 0, 0.0, roll(here, 1, 0))
            right = jnp.where(sub == 7, 0.0, roll(here, -1, 0))
            wide = here + roll(below, BLK, 1) + roll(above, 2 * BLK, 1) + roll(left, 3 * BLK, 1)
            payload[pl.ds(2 * cells + 16 * tile, 8, stride=2), :] = wide
            payload[pl.ds(2 * cells + 16 * tile + 1, 8, stride=2), :] = right

    @pl.when(section == 1)
    def _():
        inlet = jnp.zeros((8, ZT), F32)
        for x in range(CX):
            column = jnp.broadcast_to(fields[0, x, :, 0:1], (8, ZT))
            inlet = inlet + jnp.where(lane == CY * x + sub, column, 0.0)
        inlet = jnp.broadcast_to(jnp.sum(inlet, axis=0, keepdims=True), (8, ZT))
        for tile in range(cells // 8):
            payload[pl.ds(16 * tile, 8, stride=2), :] = inlet

    wait_for(loads)
    sub, lane = iotas(NZ)

    def plane_of(ref, index, plane):
        at = [pl.multiple_of(8 * (4 * (CX * index + plane) + z), 8) for z in range(NZ // ZT)]
        return jnp.concatenate([ref[pl.ds(start, 8), :] for start in at], axis=1)

    def coefficient(index, plane):
        if index >= T * T:
            return plane_of(coef.at[0], index - T * T, plane)
        raw = plane_of(inv, index, plane)
        return jnp.where(section == 0, plane_of(coef.at[1], index, plane), raw) if index < T else raw

    for ref, far in ((m1, 1 - odd), (m2, odd)):
        wanted = (sub + lane + far) % 2 == 0
        plane = far * (CX - 1)
        for tile in range(XBULK):
            first, second = coefficient(2 * tile, plane), coefficient(2 * tile + 1, plane)
            ref[VAL + tile] = jnp.where(wanted, first, roll(second, 1, 0))

    for tile in range(YBULK):
        sides = []
        for row in (0, CY - 1):
            if tile + 1 < YBULK:
                first, second = (row_of_colour_0(lines(inv, 4 * tile + 2 * n, row), row, lane) for n in (0, 1))
                sides.append(interleaved(first, second, sub))
            else:
                sides.append(row_of_colour_0(second_half(lines(inv, T * T - 2, row)), row, lane))
        down, up = sides
        b1[tile] = jnp.where(odd_y, down, up)
        b2[tile] = jnp.where(odd_y, up, down)


def corner_values(place, m1, m2, r1, r2, y1, y2):
    odd_x, odd_y = place[1] == 1, place[2] == 1
    sub, lane = iotas(NZ)
    even = even_mask(NZ)
    tiles = {}
    for t in range(VAL):
        a, b = m1[t], m2[t]
        own = jnp.where(odd_x, a, b), jnp.where(odd_x, b, a)
        for start in (0, 6):
            if t < T:
                base = 4 * (t % 2)
                rows = [roll(own[k], base + 2 * k - start, 0) for k in (0, 1)]
                both = jnp.where(sub < base + 2, rows[0], rows[1])
                tiles[start, t] = both
                c, d = r1[t], r2[t]
                from_low, from_high = jnp.where(odd_x, c, d), jnp.where(odd_x, d, c)
                ring = jnp.where(even, from_low, from_high)
                tiles[start, "ring", t] = roll(ring, t - (0 if start == 0 else CY - 1), 0)
            else:
                row = 0 if start == 0 else CY - 1
                rows = [roll(own[k], 4 + 2 * k + t - T - row, 0) for k in (0, 1)]
                tiles[start, t] = jnp.where(sub < 6, rows[0], rows[1])
    for tile in range(YVAL):
        sides = []
        for start in (0, 6):
            if tile < 3:
                sides.append(jnp.where(sub < 4, tiles[start, 2 * tile], tiles[start, 2 * tile + 1]))
            elif tile == 3:
                firsts = jnp.where(sub % 2 == 0, tiles[start, T], tiles[start, T + 1])
                sides.append(jnp.where(sub < 4, tiles[start, T - 1], firsts))
            else:
                laid = tiles[start, "ring", 0]
                for t in range(1, T):
                    laid = jnp.where(sub == t, tiles[start, "ring", t], laid)
                sides.append(laid)
        down, up = sides
        y1[tile] = jnp.where(odd_y, down, up)
        y2[tile] = jnp.where(odd_y, up, down)


def corner_kernel(place, m1, m2, r1, r2, y1, y2):
    corner_values(place, m1, m2, r1, r2, y1, y2)


def first_corner_kernel(place, m1, m2, r1, r2, returns, sources, diagonal, y1, y2, heads, sems):
    odd_y = place[2] == 1
    copies = [
        pltpu.make_async_copy(ref.at[:VAL], heads.at[n], sems.at[n]) for n, ref in enumerate((m1, m2, r1, r2))
    ]
    for copy in copies:
        copy.start()
    sub, lane = iotas(NZ)

    def pair(index, row):
        if index + 1 < T:
            return lines(sources, index, row)
        if index + 1 == T:
            halves = second_half(lines(sources, index - 1, row)), second_half(lines(diagonal, 0, row))
            return jnp.where(sub < 4, halves[0], halves[1])
        return lines(diagonal, index - T, row)

    small, _ = iotas(ZT)
    marks = jnp.zeros((8, ZT), F32)
    for t in range(T):
        line = jnp.broadcast_to(returns[0:1, t * ZT : (t + 1) * ZT], (8, ZT))
        marks = jnp.where(small == t, line.astype(F32), marks)
    for tile in range(4):
        sides = []
        for row in (0, CY - 1):
            first = row_of_colour_0(pair(4 * tile, row), row, lane)
            if tile < 3:
                second = row_of_colour_0(pair(4 * tile + 2, row), row, lane)
                sides.append(interleaved(first, second, sub))
            else:
                sides.append(first)
        down, up = sides
        y1[YVAL + tile] = jnp.where(odd_y, down, up)
        y2[YVAL + tile] = jnp.where(odd_y, up, down)
    turned = roll(marks, NZ // BLK, 1)
    for ref, value in ((y1, jnp.where(odd_y, marks, turned)), (y2, jnp.where(odd_y, turned, marks))):
        for t in range(T):
            row = 2 * (t % 4) + 1
            ref[YVAL + 3, row : row + 1, t // 4 * ZT : (t // 4 + 1) * ZT] = value[t : t + 1]
    wait_for(copies)
    corner_values(place, *[heads.at[n] for n in range(4)], y1, y2)


def interface_kernel(place, blocks, returns, y1, y2, chosen, back, inflow, beside, sems):
    odd_y = place[2] == 1
    exit_side = place[3] == 1
    back[...] = jnp.zeros_like(back)
    copies = [pltpu.make_async_copy(ref.at[YHEAD - 1], beside.at[n], sems.at[n]) for n, ref in enumerate((y1, y2))]
    for copy in copies:
        copy.start()
    half = blocks.shape[0] // 2
    total = blocks[0:8]
    for tile in range(1, half // 8):
        total = total + blocks[8 * tile : 8 * tile + 8]
    total = total + roll(total, 4, 0)
    total = total + roll(total, 2, 0)
    first, second = (jnp.broadcast_to(total[row : row + 1], (8, ZT)) for row in (0, 1))
    for row in range(16):
        at = slice(8 * row, 8 * row + 8)
        found = chosen[at, :ZT] * first + chosen[at, ZT:] * second
        inflow[at, :] = jnp.broadcast_to(jnp.sum(found, axis=1, keepdims=True), (8, ZT))
    wait_for(copies)

    @pl.when(exit_side)
    def _():
        cells = half // 2
        table = blocks[pl.ds(half, cells, stride=2), :]
        sub, _ = iotas(ZT)

        def marks_of(n):
            laid = jnp.zeros((8, ZT), F32)
            for t in range(T):
                row, at = 2 * (t % 4) + 1, slice(t // 4 * ZT, (t // 4 + 1) * ZT)
                laid = jnp.where(sub == t, jnp.broadcast_to(beside[n, row : row + 1, at], (8, ZT)), laid)
            return laid

        first, second = marks_of(0), marks_of(1)
        high, low = jnp.where(odd_y, second, first), jnp.where(odd_y, first, second)
        slots = lax.broadcasted_iota(jnp.int32, (8, cells), 1).astype(F32)
        column = lax.broadcasted_iota(jnp.int32, table.shape, 1)
        spots = [jnp.where(column // BLK == q, roll(table, q * BLK, 1), 0.0) for q in range(ZT // BLK)]
        wanted = []
        for t in range(T):
            line = jnp.broadcast_to(returns[0:1, t * ZT : (t + 1) * ZT], (8, ZT))
            spread = line
            for y in range(1, CY):
                spread = jnp.where(sub == y, roll(line, -y * (NZ // BLK), 1), spread)
            wanted.append(spread.astype(F32))
        wanted += [high, low]
        for tile in range(NZ // ZT):
            laid = jnp.zeros((8 * len(wanted), ZT), F32)
            for q in range(ZT // BLK):
                block = tile * (ZT // BLK) + q
                match = jnp.concatenate([want[:, block : block + 1] == slots for want in wanted], axis=0)
                laid = laid + jnp.dot(
                    match.astype(F32), spots[q], precision=lax.Precision.HIGHEST, preferred_element_type=F32
                )
            at = slice(tile * ZT, (tile + 1) * ZT)
            for t in range(T):
                back[t, 0:8, at] = laid[8 * t : 8 * t + 8]
                back[t, 8:9, at] = laid[8 * T + t : 8 * T + t + 1]
                back[t, 15:16, at] = laid[8 * T + 8 + t : 8 * T + 9 + t]


def sweep_kernel(
    place, coupling, fields, sources, diagonal, inverse, x1, x2, ya, za, yb, zb, back, inflow, *rest
):
    r1, r2, y1, y2 = rest[:4] if len(rest) == 9 else (x1, x2, ya, za)
    out, m1, m2, u0, u1 = rest[-5:]
    section = place[0]
    odd_x, odd_y = place[1], place[2]
    exit_side = place[3] == 1
    even, even_z = even_mask(NZ), even_mask(ZT)
    sub, lane = iotas(NZ)
    sub_z, _ = iotas(ZT)
    colours = (u0, u1)
    own, edge = slice(0, 8), slice(8, 16)

    for t in range(T):
        for k in (0, 1):
            u1[t, k + 1, own] = packed(fields[t, 2 * k], fields[t, 2 * k + 1], even, 1)
            u0[t, k + 1, own] = packed(fields[t, 2 * k], fields[t, 2 * k + 1], even, 0)
        for ref, tile, at, width in (
            (u1, t, slice(0, NZ), NZ),
            (u0, T + t // 4, slice(t % 4 * ZT, (t % 4 + 1) * ZT), ZT),
        ):
            low = jnp.where(odd_x == 1, r1[tile, :, at], r2[tile, :, at])
            high = jnp.where(odd_x == 1, r2[tile, :, at], r1[tile, :, at])
            ref[t, 0, own, :width] = low
            ref[t, 3, own, :width] = high
    own_rows, own_rows_z = (lax.broadcasted_iota(jnp.int32, (8, width), 0) for width in (NZ, ZT))

    def beside(tile, rows, at):
        first, second = y1[tile, rows, at], y2[tile, rows, at]
        low, high = jnp.where(odd_y == 1, first, second), jnp.where(odd_y == 1, second, first)
        return low, high

    whole = slice(0, NZ)
    for t in range(T):
        low, high = beside(t // 2, slice(0, 8), whole)
        for k in (0, 1):
            base = 4 * (t % 2) + 2 * k
            u1[t, k + 1, edge] = jnp.where(own_rows < 2, roll(high, -base, 0), roll(low, 6 - base, 0))
            row, at = 4 + 2 * k + t // 4, slice(t % 4 * ZT, (t % 4 + 1) * ZT)
            first, last = beside(3, slice(row, row + 1), at)
            u0[t, k + 1, edge, :ZT] = jnp.where(own_rows_z < 4, last, first)
        first, last = beside(4, slice(t, t + 1), whole)
        corner = jnp.where(own_rows < 4, last, first)
        u1[t, 0, edge] = corner
        u1[t, 3, edge] = corner

    @pl.when(exit_side)
    def _():
        for t in range(T):
            u0[t, 3] = back[t]
            u1[t, 3] = back[t]

    def around(centre, beyond):
        up = roll(jnp.where(sub == 0, beyond, centre), -1, 0)
        down = roll(jnp.where(sub == 7, beyond, centre), 1, 0)
        return up + down

    def planes(colour, unit, t):
        old, new = colours[colour], colours[1 - colour]
        if unit == "ring":
            centre = jnp.where(even, new[t, 0, own], new[t, 3, own])
            beyond = jnp.where(even, new[t, 0, edge], new[t, 3, edge])
            x_sum = jnp.where(even, new[t, 3, own] + new[t, 2, own], new[t, 0, own] + new[t, 1, own])
            return centre, beyond, x_sum, jnp.where(even, old[t, 3, own], old[t, 0, own])
        p, rows = unit
        here, other = (own, edge) if rows == 0 else (edge, own)
        centre, beyond = new[t, p, here], new[t, p, other]
        below, above = new[t, p - 1, here], new[t, p + 1, here]
        x_sum = centre + (jnp.where(even, below, above) if colour == 0 else jnp.where(even, above, below))
        return centre, beyond, x_sum, old[t, p, here]

    def inflow_of(colour, unit):
        base = 64 * colour
        if unit == "ring":
            values = jnp.where(even_z, inflow[base + 48 : base + 56], inflow[base : base + 8])
        else:
            start = base + 16 * unit[0] + 8 * unit[1]
            values = inflow[start : start + 8]
        return jnp.concatenate([values] * (NZ // ZT), axis=1)

    ring_mask = (sub + lane + odd_x) % 2 == 0
    edge_mask = jnp.where(sub == 7, 1, 0) == odd_y

    def of_ring(index):
        tile = VAL + index // 2
        if index % 2 == 0:
            return jnp.where(ring_mask, x1[tile], x2[tile])
        return roll(jnp.where(ring_mask, x2[tile], x1[tile]), -1, 0)

    def of_edge(first, second, tile, index, p):
        tile, row = tile + index // 4, 4 * (index % 2) + 2 * (p - 1) + index % 4 // 2
        return jnp.where(edge_mask, first[tile, row : row + 1], second[tile, row : row + 1])

    def taken(colour, unit, kind, index):
        if unit == "ring":
            return of_ring(T * T + index if kind == "source" else index)
        p, rows = unit
        if rows == 0:
            if kind == "inverse":
                raw = inverse.at[index // T, index % T]
            else:
                raw = (sources if kind == "source" else diagonal).at[index]
            return packed(raw[2 * p - 2], raw[2 * p - 1], even, colour)
        if kind == "inverse":
            return of_edge(yb, zb, 0, index, p)
        return of_edge(ya, za, YVAL, index if kind == "source" else T + index, p)

    def put(colour, unit, t, value):
        ref = colours[colour]
        if unit == "ring":
            ref[t, 0, own] = value
            ref[t, 3, own] = jnp.where(exit_side, back[t, own], value)
        else:
            ref[t, unit[0], own if unit[1] == 0 else edge] = value

    def valid(unit):
        if unit == "ring":
            return jnp.where(even, place[5], place[4])
        if unit[1] == 0:
            return None
        return jnp.where(sub == 7, place[6], place[7])

    def turbine(colour, unit):
        driving = []
        for t in range(T):
            centre, beyond, x_sum, kept = planes(colour, unit, t)
            start = inflow_of(colour, unit) if t == 0 else kept
            ahead = jnp.where(lane == NZ - 1, 0.0, roll(centre, -1, 1))
            behind = jnp.where(lane == 0, start, roll(centre, 1, 1))
            total = x_sum + around(centre, beyond) + ahead + behind
            source = taken(colour, unit, "source", t)
            driving.append(source + coupling[t] * total)
        for s in range(T):
            value = taken(colour, unit, "inverse", T * s) * driving[0]
            for t in range(1, T):
                value = value + taken(colour, unit, "inverse", T * s + t) * driving[t]
            put(colour, unit, s, value)

    def combustor(colour, unit):
        before = None
        current = planes(colour, unit, 0)
        flag = valid(unit)
        for t in range(T):
            after = planes(colour, unit, t + 1) if t + 1 < T else None
            centre, beyond, x_sum, _ = current
            edge_ahead = 0.0 if after is None else roll(after[0], -1, 1)
            edge_behind = 0.0 if before is None else roll(before, 1, 1)
            ahead = jnp.where(lane == NZ - 1, edge_ahead, roll(centre, -1, 1))
            behind = jnp.where(lane == 0, edge_behind, roll(centre, 1, 1))
            total = x_sum + around(centre, beyond) + ahead + behind
            source = taken(colour, unit, "source", t)
            value = (source + total) / (6.0 + taken(colour, unit, "diagonal", t))
            if flag is not None:
                value = jnp.where(flag == 1, value, 0.0)
            put(colour, unit, t, value)
            before, current = centre, after

    def both(step):
        for unit in ((1, 0), (2, 0), (1, 1), (2, 1), "ring"):
            step(0, unit)
        for unit in ((1, 0), (2, 0)):
            step(1, unit)

    pl.when(section == 0)(functools.partial(both, combustor))
    pl.when(section != 0)(functools.partial(both, turbine))

    for t in range(T):
        for k in (0, 1):
            a, b = u0[t, k + 1, own], u1[t, k + 1, own]
            out[t, 2 * k] = jnp.where(even, a, b)
            out[t, 2 * k + 1] = jnp.where(even, b, a)
    for ref, pair in ((m1, 2 - odd_x), (m2, 1 + odd_x)):
        store_message(ref, lambda t: u1[t, pair, own], lambda t: u0[t, pair, own, :ZT])


def shape(*dims):
    return jax.ShapeDtypeStruct(dims, F32)


SMEM = pl.BlockSpec(memory_space=pltpu.SMEM)
VMEM = pl.BlockSpec(memory_space=pltpu.VMEM)
ANY = pl.BlockSpec(memory_space=pl.ANY)


def call(kernel, outs, operands, out_specs=None, scratch=(), limit=24):
    return pl.pallas_call(
        kernel,
        out_shape=outs,
        in_specs=[spec for spec, _ in operands],
        out_specs=out_specs or [VMEM] * len(outs),
        scratch_shapes=list(scratch),
        compiler_params=pltpu.CompilerParams(vmem_limit_bytes=limit << 20),
    )(*[operand for _, operand in operands])


def swaps(axis, first, second, turbine_only=False):
    peers = lax.axis_size(axis)
    inner = [(i, i ^ 1) for i in range(peers)]
    outer = [(i, (i + 1 ^ 1) - 1) for i in range(1, peers - 1)]
    if turbine_only:
        inner, outer = ([(2 * i + 1, 2 * j + 1) for i, j in pairs] for pairs in (inner, outer))
        axis = (axis, "sa")
    second = lax.ppermute(second, axis, outer)
    return lax.ppermute(first, axis, inner), second


def chosen_slots():
    table = np.zeros((128, 2 * ZT), np.float32)
    for c in range(2):
        for p in range(4):
            for r in range(16):
                y = r if r < 12 else r - 16
                x = 2 * (p - 1) + (c if r % 2 == 0 else 1 - c)
                block = None
                if 0 <= x < CX and 0 <= y < CY:
                    block = (0, x, y)
                elif x == -1 and 0 <= y < CY:
                    block = (1, CX - 1, y)
                elif x == CX and 0 <= y < CY:
                    block = (2, 0, y)
                elif 0 <= x < CX and y == -1:
                    block = (3, x, CY - 1)
                elif 0 <= x < CX and y == CY:
                    block = (4, x, 0)
                if block is not None:
                    table[64 * c + 16 * p + r, BLK * block[0] + CY * block[1] + block[2]] = 1.0
    return table


def shards(fields, sources, diagonal, block_inverse, coupling, donors, returns):
    values = fields[0]
    source = sources[0]
    rows_x, rows_y = lax.axis_size("gx"), lax.axis_size("gy")
    cells = rows_x * rows_y
    section, place_x, place_y = (lax.axis_index(axis) for axis in ("sa", "gx", "gy"))
    exit_side = (section == 0) & (place_x == rows_x - 1)
    place = jnp.stack(
        [
            section,
            place_x % 2,
            place_y % 2,
            exit_side.astype(jnp.int32),
            (place_x > 0).astype(jnp.int32),
            (place_x < rows_x - 1).astype(jnp.int32),
            (place_y > 0).astype(jnp.int32),
            (place_y < rows_y - 1).astype(jnp.int32),
            place_x,
            place_y,
        ]
    ).astype(jnp.int32)

    flat = [
        array.reshape(-1, CY, NZ // ZT, ZT).transpose(0, 2, 1, 3).reshape(-1, ZT)
        for array in (source, diagonal, block_inverse)
    ]
    m1, m2, yb, zb, payload = call(
        opening_kernel,
        [shape(VAL + XBULK, 8, NZ)] * 2 + [shape(YBULK, 8, NZ)] * 2 + [shape(4 * cells, ZT)],
        [(SMEM, place), (SMEM, donors.reshape(-1)), (VMEM, values)] + [(ANY, array) for array in flat],
        scratch=[
            pltpu.VMEM((cells, ZT), F32),
            pltpu.VMEM((2, *flat[0].shape), F32),
            pltpu.VMEM(flat[2].shape, F32),
            pltpu.SemaphoreType.DMA((3,)),
        ],
        limit=60,
    )
    x1, x2 = swaps("gx", m1, m2)
    yb, zb = swaps("gy", yb, zb, turbine_only=True)
    ya, za = call(
        first_corner_kernel,
        [shape(YHEAD, 8, NZ)] * 2,
        [(SMEM, place)] + [(ANY, array) for array in (m1, m2, x1, x2)] + [(VMEM, array) for array in (returns, *flat[:2])],
        scratch=[pltpu.VMEM((4, VAL, 8, NZ), F32), pltpu.SemaphoreType.DMA((4,))],
    )
    ya, za = swaps("gy", ya, za)
    arrived = lax.all_to_all(
        payload.reshape(2 * cells, 1, 2 * ZT), ("sa", "gx", "gy"), split_axis=0, concat_axis=0, tiled=True
    ).reshape(4 * cells, ZT)
    back, inflow = call(
        interface_kernel,
        [shape(T, 16, NZ), shape(128, ZT)],
        [(SMEM, place), (VMEM, arrived), (VMEM, returns), (ANY, ya), (ANY, za), (VMEM, jnp.asarray(chosen_slots()))],
        scratch=[pltpu.VMEM((2, 8, NZ), F32), pltpu.SemaphoreType.DMA((2,))],
    )

    for sweep in range(SWEEPS):
        received = []
        if sweep > 0:
            r1, r2 = swaps("gx", m1, m2)
            y1, y2 = call(
                corner_kernel,
                [shape(YVAL, 8, NZ)] * 2,
                [(SMEM, place)] + [(VMEM, array) for array in (m1, m2, r1, r2)],
            )
            received = [r1, r2, *swaps("gy", y1, y2)]
        values, m1, m2 = call(
            sweep_kernel,
            [shape(T, CX, CY, NZ), shape(VAL, 8, NZ), shape(VAL, 8, NZ)],
            [(SMEM, place), (SMEM, coupling)]
            + [(VMEM, array) for array in (values, source, diagonal, block_inverse)]
            + [(VMEM, array) for array in (x1, x2, ya, za, yb, zb, back, inflow, *received)],
            scratch=[pltpu.VMEM((T, 4, 16, NZ), F32)] * 2,
            limit=40,
        )
    return values[None]


def solution(mesh):
    return jax.shard_map(
        shards,
        mesh=mesh,
        in_specs=(
            P("sa", None, "gx", "gy", None),
            P("sa", None, "gx", "gy", None),
            P(None, "gx", "gy", None),
            P(None, None, "gx", "gy", None),
            P(),
            P(),
            P("gy", None),
        ),
        out_specs=P("sa", None, "gx", "gy", None),
        check_vma=False,
    )
```

time: 146 us -> 110 us (0.75)
  the two profiles are of different devices: /device:TPU:18 before, /device:TPU:42 now
where the time goes in v2:
time: 110 us
  starting transfers between devices  38.8 us (35%)
  waiting for transfers between devices  29.1 us (26%)
  Pallas kernels  19 us (17%)
  blocking collectives  18.3 us (17%)
  local copies, waits for them, and re-layouts  4.31 us (4%)
    ppermute x9, starting transfers between devices, swaps(): second = lax.ppermute(second, axis, outer)  26.1 us
    ppermute x9, waiting for transfers between devices, swaps(): second = lax.ppermute(second, axis, outer)  25.4 us
    pallas_call x10, Pallas kernels, call(): pl.pallas_call(kernel, out_shape=outs, in_specs=[spec for spec, _ in oper...  19 us
    all_to_all x1, blocking collectives, shards(): lax.all_to_all(payload.reshape(2 * cells, 1, 2 * ZT), ('sa', 'gx', 'gy'),...  18.3 us
    ppermute x9, starting transfers between devices, swaps(): return (lax.ppermute(first, axis, inner), second)  12.7 us
    ppermute x9, waiting for transfers between devices, swaps(): return (lax.ppermute(first, axis, inner), second)  3.67 us
    unnamed x21, local copies, waits for them, and re-layouts  3.01 us
  transfers between devices with their start and end apart: 18, of which 9 were waited for; matrix products, arithmetic and copies ran while one was open for 0% of the time, Pallas kernels for 2%

profile of v2, /device:TPU:42, one launch (start us, length us, event | category | flops | bytes accessed | tf_op | source)
XLA Modules:
  0.0 109.9 jit_solution(7663840591479485857)
XLA Ops:
  0.0 0.0 copy-start.1
  0.0 0.8 copy.10
  0.9 0.7 reshape.24.donors
  1.6 0.6 stack.63.place
  2.2 4.9 %shard_map.82 = (f32[37,8,512]{2,1,0:T(8,128)}, f32[37,8,512]{2,1,0:T(8,128)}, f32[13,8,512]{2,1,0:T(8,128)}, f32[13,8,512]{2,1,0:T(8,128)}, f32[256,128]{1,0:T(8,128)}) custom-call(s32[10]{0:T(128)} %stack.63.place, s32[192]{0:T(256)} %reshape.24.donors, f32[7,4,8,512]{3,2,1,0:T(8,128)} %bitcast.39, f32[896,128]{1,0:T(8,128)} %bitcast.31, ...), custom_call_target="tpu_custom_call" | custom-call | tf_op jit(solution)/shard_map/pallas_call | solution.py:498
  7.1 0.0 copy-start
  7.1 0.0 copy-start.3
  7.1 0.1 collective-permute-start
  7.2 2.6 %collective-permute-start.1 = (f32[37,8,512]{2,1,0:T(8,128)}, f32[37,8,512]{2,1,0:T(8,128)S(1)}, u32[]{:S(2)}, u32[]{:S(2)}) collective-permute-start(f32[37,8,512]{2,1,0:T(8,128)} %get-tuple-element.31.m2), channel_id=1, source_target_pairs={{16,32},{32,16},{48,64},{64,48},{80,96},{96,80},{17,33},{33,17},{4... | collective-permute-start | bytes 1818632 | tf_op jit(solution)/shard_map/ppermute | solution.py:515
  9.8 4.9 %collective-permute-start.4 = (f32[13,8,512]{2,1,0:T(8,128)}, f32[13,8,512]{2,1,0:T(8,128)S(1)}, u32[]{:S(2)}, u32[]{:S(2)}) collective-permute-start(f32[13,8,512]{2,1,0:T(8,128)} %get-tuple-element.34), channel_id=1, source_target_pairs={{1,3},{3,1},{5,7},{7,5},{9,11},{11,9},{13,15},{15,13},{17,19},{19,... | collective-permute-start | bytes 638984 | tf_op jit(solution)/shard_map/ppermute | solution.py:516
  14.7 2.4 %collective-permute-start.5 = (f32[13,8,512]{2,1,0:T(8,128)}, f32[13,8,512]{2,1,0:T(8,128)S(1)}, u32[]{:S(2)}, u32[]{:S(2)}) collective-permute-start(f32[13,8,512]{2,1,0:T(8,128)} %get-tuple-element.35), channel_id=1, source_target_pairs={{3,5},{5,3},{7,9},{9,7},{11,13},{13,11},{19,21},{21,19},{23,25},{2... | collective-permute-start | bytes 638984 | tf_op jit(solution)/shard_map/ppermute | solution.py:515
  17.1 0.0 collective-permute-done.r1.x1
  17.1 1.9 %collective-permute-done.1.r2.x2 = f32[37,8,512]{2,1,0:T(8,128)S(1)} collective-permute-done((f32[37,8,512]{2,1,0:T(8,128)}, f32[37,8,512]{2,1,0:T(8,128)S(1)}, u32[]{:S(2)}, u32[]{:S(2)}) %collective-permute-start.1) | collective-permute-done | bytes 606240 | tf_op jit(solution)/shard_map/ppermute | solution.py:515
  19.1 0.0 copy-done.2
  19.1 0.0 copy-done.1
  19.1 0.0 copy-done.8
  19.1 0.0 copy-done.7
  19.1 0.0 copy-start.4
  19.1 1.1 copy-done.4
  20.2 1.1 copy-done.5
  21.2 1.6 %shard_map.83 = (f32[9,8,512]{2,1,0:T(8,128)S(1)}, f32[9,8,512]{2,1,0:T(8,128)S(1)}) custom-call(s32[10]{0:T(128)S(1)} %copy-done.7, f32[37,8,512]{2,1,0:T(8,128)S(1)} %copy-done.4, f32[37,8,512]{2,1,0:T(8,128)S(1)} %copy-done.5, f32[37,8,512]{2,1,0:T(8,128)S(1)} %collective-permute-done.r1.x1, f32[37,8,512]{2,1,0:T(8,128)S(1)} %collective-permute-done.1.r2.x2, ...), custom_call_target="tpu_custom_call" | custom-call | tf_op jit(solution)/shard_map/pallas_call | solution.py:498
  22.8 3.1 %collective-permute-start.2 = (f32[9,8,512]{2,1,0:T(8,128)S(1)}, f32[9,8,512]{2,1,0:T(8,128)S(1)}, u32[]{:S(2)}, u32[]{:S(2)}) collective-permute-start(f32[9,8,512]{2,1,0:T(8,128)S(1)} %get-tuple-element.32), channel_id=1, source_target_pairs={{0,2},{2,0},{4,6},{6,4},{8,10},{10,8},{12,14},{14,12},{1,3},{3,1},... | collective-permute-start | bytes 442376 | tf_op jit(solution)/shard_map/ppermute | solution.py:516
  25.9 2.4 %collective-permute-start.3 = (f32[9,8,512]{2,1,0:T(8,128)S(1)}, f32[9,8,512]{2,1,0:T(8,128)S(1)}, u32[]{:S(2)}, u32[]{:S(2)}) collective-permute-start(f32[9,8,512]{2,1,0:T(8,128)S(1)} %get-tuple-element.33), channel_id=1, source_target_pairs={{2,4},{4,2},{6,8},{8,6},{10,12},{12,10},{3,5},{5,3},{7,9},{9,7},{1... | collective-permute-start | bytes 442376 | tf_op jit(solution)/shard_map/ppermute | solution.py:515
  28.3 18.3 %all_to_all.5 = f32[128,1,256]{2,1,0:T(1,128)S(1)} all-to-all(f32[128,1,256]{2,1,0:T(1,128)} %bitcast.42), channel_id=1, replica_groups=mesh['gx'=8,'gy'=8,'sa'=2] {'sa','gx','gy'}, dimensions={0} | all-to-all | bytes 262144 | tf_op jit(solution)/shard_map/all_to_all | solution.py:589
  46.7 0.0 collective-permute-done.2.y1.ya
  46.7 0.0 collective-permute-done.3.y2.za
  46.7 0.0 copy-done.6
  46.7 0.7 shard_map.84
  47.4 0.0 collective-permute-done.4.yb
  47.4 0.0 collective-permute-done.5.zb
  47.4 0.0 copy-done.9
  47.4 0.0 copy-done
  47.4 0.0 copy-done.3
  47.5 2.3 %shard_map.85 = (f32[7,4,8,512]{3,2,1,0:T(8,128)S(1)}, f32[9,8,512]{2,1,0:T(8,128)S(1)}, f32[9,8,512]{2,1,0:T(8,128)S(1)}) custom-call(s32[10]{0:T(128)S(1)} %copy-done.7, f32[7]{0:T(128)S(1)} %copy-done.9, f32[7,4,8,512]{3,2,1,0:T(8,128)S(1)} %bitcast.40, f32[7,4,8,512]{3,2,1,0:T(8,128)S(1)} %bitcast.33, f32[7,4,8,512]{3,2,1,0:T(8,128)S(1)} %copy-done.2, ...), custom_call_target="tpu_custom_call" | custom-call | tf_op jit(solution)/shard_map/pallas_call | solution.py:498
  49.7 0.1 collective-permute-start.6
  49.8 3.4 %collective-permute-start.7 = (f32[9,8,512]{2,1,0:T(8,128)S(1)}, f32[9,8,512]{2,1,0:T(8,128)S(1)}, u32[]{:S(2)}, u32[]{:S(2)}) collective-permute-start(f32[9,8,512]{2,1,0:T(8,128)S(1)} %get-tuple-element.41.m2), channel_id=1, source_target_pairs={{16,32},{32,16},{48,64},{64,48},{80,96},{96,80},{17,33},{33,17},{4... | collective-permute-start | bytes 442376 | tf_op jit(solution)/shard_map/ppermute | solution.py:515
  53.2 0.0 collective-permute-done.6.r1.rest_0_
  53.3 3.1 %collective-permute-done.7.r2.rest_1_ = f32[9,8,512]{2,1,0:T(8,128)S(1)} collective-permute-done((f32[9,8,512]{2,1,0:T(8,128)S(1)}, f32[9,8,512]{2,1,0:T(8,128)S(1)}, u32[]{:S(2)}, u32[]{:S(2)}) %collective-permute-start.7) | collective-permute-done | bytes 147488 | tf_op jit(solution)/shard_map/ppermute | solution.py:515
  56.3 0.6 shard_map.86
  56.9 0.7 collective-permute-start.8
  57.6 5.7 %collective-permute-start.9 = (f32[5,8,512]{2,1,0:T(8,128)S(1)}, f32[5,8,512]{2,1,0:T(8,128)S(1)}, u32[]{:S(2)}, u32[]{:S(2)}) collective-permute-start(f32[5,8,512]{2,1,0:T(8,128)S(1)} %get-tuple-element.43), channel_id=1, source_target_pairs={{2,4},{4,2},{6,8},{8,6},{10,12},{12,10},{3,5},{5,3},{7,9},{9,7},{1... | collective-permute-start | bytes 245768 | tf_op jit(solution)/shard_map/ppermute | solution.py:515
  63.3 0.0 collective-permute-done.8.rest_2_
  63.3 3.1 %collective-permute-done.9.rest_3_ = f32[5,8,512]{2,1,0:T(8,128)S(1)} collective-permute-done((f32[5,8,512]{2,1,0:T(8,128)S(1)}, f32[5,8,512]{2,1,0:T(8,128)S(1)}, u32[]{:S(2)}, u32[]{:S(2)}) %collective-permute-start.9) | collective-permute-done | bytes 81952 | tf_op jit(solution)/shard_map/ppermute | solution.py:515
  66.5 2.3 %shard_map.87 = (f32[7,4,8,512]{3,2,1,0:T(8,128)S(1)}, f32[9,8,512]{2,1,0:T(8,128)S(1)}, f32[9,8,512]{2,1,0:T(8,128)S(1)}) custom-call(s32[10]{0:T(128)S(1)} %copy-done.7, f32[7]{0:T(128)S(1)} %copy-done.9, f32[7,4,8,512]{3,2,1,0:T(8,128)S(1)} %get-tuple-element.39.fields, f32[7,4,8,512]{3,2,1,0:T(8,128)S(1)} %bitcast.34, f32[7,4,8,512]{3,2,1,0:T(8,128)S(1)} %copy-done.2, ...), custom_call_target="tpu_custom_call" | custom-call | tf_op jit(solution)/shard_map/pallas_call | solution.py:498
  68.8 0.1 collective-permute-start.10
  68.8 2.1 %collective-permute-start.11 = (f32[9,8,512]{2,1,0:T(8,128)S(1)}, f32[9,8,512]{2,1,0:T(8,128)S(1)}, u32[]{:S(2)}, u32[]{:S(2)}) collective-permute-start(f32[9,8,512]{2,1,0:T(8,128)S(1)} %get-tuple-element.46.m2), channel_id=1, source_target_pairs={{16,32},{32,16},{48,64},{64,48},{80,96},{96,80},{17,33},{33,17},{4... | collective-permute-start | bytes 442376 | tf_op jit(solution)/shard_map/ppermute | solution.py:515
  71.0 0.0 collective-permute-done.10.r1.rest_0_
  71.0 4.3 %collective-permute-done.11.r2.rest_1_ = f32[9,8,512]{2,1,0:T(8,128)S(1)} collective-permute-done((f32[9,8,512]{2,1,0:T(8,128)S(1)}, f32[9,8,512]{2,1,0:T(8,128)S(1)}, u32[]{:S(2)}, u32[]{:S(2)}) %collective-permute-start.11) | collective-permute-done | bytes 147488 | tf_op jit(solution)/shard_map/ppermute | solution.py:515
  75.3 0.6 shard_map.88
  75.9 3.0 %collective-permute-start.12 = (f32[5,8,512]{2,1,0:T(8,128)S(1)}, f32[5,8,512]{2,1,0:T(8,128)S(1)}, u32[]{:S(2)}, u32[]{:S(2)}) collective-permute-start(f32[5,8,512]{2,1,0:T(8,128)S(1)} %get-tuple-element.47), channel_id=1, source_target_pairs={{0,2},{2,0},{4,6},{6,4},{8,10},{10,8},{12,14},{14,12},{1,3},{3,1},... | collective-permute-start | bytes 245768 | tf_op jit(solution)/shard_map/ppermute | solution.py:516
  78.9 3.0 %collective-permute-start.13 = (f32[5,8,512]{2,1,0:T(8,128)S(1)}, f32[5,8,512]{2,1,0:T(8,128)S(1)}, u32[]{:S(2)}, u32[]{:S(2)}) collective-permute-start(f32[5,8,512]{2,1,0:T(8,128)S(1)} %get-tuple-element.48), channel_id=1, source_target_pairs={{2,4},{4,2},{6,8},{8,6},{10,12},{12,10},{3,5},{5,3},{7,9},{9,7},{1... | collective-permute-start | bytes 245768 | tf_op jit(solution)/shard_map/ppermute | solution.py:515
  81.9 0.4 collective-permute-done.12.rest_2_
  82.4 5.4 %collective-permute-done.13.rest_3_ = f32[5,8,512]{2,1,0:T(8,128)S(1)} collective-permute-done((f32[5,8,512]{2,1,0:T(8,128)S(1)}, f32[5,8,512]{2,1,0:T(8,128)S(1)}, u32[]{:S(2)}, u32[]{:S(2)}) %collective-permute-start.13) | collective-permute-done | bytes 81952 | tf_op jit(solution)/shard_map/ppermute | solution.py:515
  87.8 2.3 %shard_map.89 = (f32[7,4,8,512]{3,2,1,0:T(8,128)S(1)}, f32[9,8,512]{2,1,0:T(8,128)S(1)}, f32[9,8,512]{2,1,0:T(8,128)S(1)}) custom-call(s32[10]{0:T(128)S(1)} %copy-done.7, f32[7]{0:T(128)S(1)} %copy-done.9, f32[7,4,8,512]{3,2,1,0:T(8,128)S(1)} %get-tuple-element.44.fields, f32[7,4,8,512]{3,2,1,0:T(8,128)S(1)} %bitcast.35, f32[7,4,8,512]{3,2,1,0:T(8,128)S(1)} %copy-done.2, ...), custom_call_target="tpu_custom_call" | custom-call | tf_op jit(solution)/shard_map/pallas_call | solution.py:498
  90.0 0.1 collective-permute-start.14
  90.1 1.9 %collective-permute-start.15 = (f32[9,8,512]{2,1,0:T(8,128)S(1)}, f32[9,8,512]{2,1,0:T(8,128)S(1)}, u32[]{:S(2)}, u32[]{:S(2)}) collective-permute-start(f32[9,8,512]{2,1,0:T(8,128)S(1)} %get-tuple-element.51.m2), channel_id=1, source_target_pairs={{16,32},{32,16},{48,64},{64,48},{80,96},{96,80},{17,33},{33,17},{4... | collective-permute-start | bytes 442376 | tf_op jit(solution)/shard_map/ppermute | solution.py:515
  92.1 0.0 collective-permute-done.14.r1.rest_0_
  92.1 4.5 %collective-permute-done.15.r2.rest_1_ = f32[9,8,512]{2,1,0:T(8,128)S(1)} collective-permute-done((f32[9,8,512]{2,1,0:T(8,128)S(1)}, f32[9,8,512]{2,1,0:T(8,128)S(1)}, u32[]{:S(2)}, u32[]{:S(2)}) %collective-permute-start.15) | collective-permute-done | bytes 147488 | tf_op jit(solution)/shard_map/ppermute | solution.py:515
  96.6 0.6 shard_map.90
  97.2 0.7 collective-permute-start.16
  97.9 2.5 %collective-permute-start.17 = (f32[5,8,512]{2,1,0:T(8,128)S(1)}, f32[5,8,512]{2,1,0:T(8,128)S(1)}, u32[]{:S(2)}, u32[]{:S(2)}) collective-permute-start(f32[5,8,512]{2,1,0:T(8,128)S(1)} %get-tuple-element.53), channel_id=1, source_target_pairs={{2,4},{4,2},{6,8},{8,6},{10,12},{12,10},{3,5},{5,3},{7,9},{9,7},{1... | collective-permute-start | bytes 245768 | tf_op jit(solution)/shard_map/ppermute | solution.py:515
  100.4 3.2 %collective-permute-done.16.rest_2_ = f32[5,8,512]{2,1,0:T(8,128)S(1)} collective-permute-done((f32[5,8,512]{2,1,0:T(8,128)S(1)}, f32[5,8,512]{2,1,0:T(8,128)S(1)}, u32[]{:S(2)}, u32[]{:S(2)}) %collective-permute-start.16) | collective-permute-done | bytes 81952 | tf_op jit(solution)/shard_map/ppermute | solution.py:516
  103.6 3.1 %collective-permute-done.17.rest_3_ = f32[5,8,512]{2,1,0:T(8,128)S(1)} collective-permute-done((f32[5,8,512]{2,1,0:T(8,128)S(1)}, f32[5,8,512]{2,1,0:T(8,128)S(1)}, u32[]{:S(2)}, u32[]{:S(2)}) %collective-permute-start.17) | collective-permute-done | bytes 81952 | tf_op jit(solution)/shard_map/ppermute | solution.py:515
  106.8 3.1 %shard_map.91 = (f32[7,4,8,512]{3,2,1,0:T(8,128)}, f32[9,8,512]{2,1,0:T(8,128)}, f32[9,8,512]{2,1,0:T(8,128)}) custom-call(s32[10]{0:T(128)S(1)} %copy-done.7, f32[7]{0:T(128)S(1)} %copy-done.9, f32[7,4,8,512]{3,2,1,0:T(8,128)S(1)} %get-tuple-element.49.fields, f32[7,4,8,512]{3,2,1,0:T(8,128)S(1)} %bitcast.36, f32[7,4,8,512]{3,2,1,0:T(8,128)S(1)} %copy-done.2, ...), custom_call_target="tpu_custom_call" | custom-call | tf_op jit(solution)/shard_map/pallas_call | solution.py:498
  (6 shorter events, 0.0 us)
Async XLA Ops:
  0.0 19.1 %copy-start.2 = (f32[7,4,8,512]{3,2,1,0:T(8,128)S(1)}, f32[7,4,8,512]{3,2,1,0:T(8,128)}, u32[]{:S(2)}) copy-start(f32[7,4,8,512]{3,2,1,0:T(8,128)} %diagonal.7) | copy-start | bytes 1376260
  0.0 19.1 %copy-start.1 = (f32[1,7,4,8,512]{4,3,2,1,0:T(8,128)S(1)}, f32[1,7,4,8,512]{4,3,2,1,0:T(8,128)}, u32[]{:S(2)}) copy-start(f32[1,7,4,8,512]{4,3,2,1,0:T(8,128)} %param.9) | copy-start | bytes 1376260
  0.0 19.1 %copy-start.8 = (s32[1,896]{1,0:T(1,128)S(1)}, s32[1,896]{1,0:T(1,128)}, u32[]{:S(2)}) copy-start(s32[1,896]{1,0:T(1,128)} %returns.3) | copy-start | bytes 10756
  2.2 16.9 %copy-start.7 = (s32[10]{0:T(128)S(1)}, s32[10]{0:T(128)}, u32[]{:S(2)}) copy-start(s32[10]{0:T(128)} %stack.63.place) | copy-start | bytes 124
  2.2 44.5 %copy-start.6 = (f32[128,256]{1,0:T(8,128)S(1)}, f32[128,256]{1,0:T(8,128)}, u32[]{:S(2)}) copy-start(f32[128,256]{1,0:T(8,128)} %constant.34.clone.chosen) | copy-start | bytes 393220
  2.2 45.2 %copy-start.9 = (f32[7]{0:T(128)S(1)}, f32[7]{0:T(128)}, u32[]{:S(2)}) copy-start(f32[7]{0:T(128)} %coupling.7) | copy-start | bytes 88
  7.1 40.3 %copy-start = (f32[7,7,4,8,512]{4,3,2,1,0:T(8,128)S(1)}, f32[7,7,4,8,512]{4,3,2,1,0:T(8,128)}, u32[]{:S(2)}) copy-start(f32[7,7,4,8,512]{4,3,2,1,0:T(8,128)} %inverse.7) | copy-start | bytes 9633796
  7.1 40.3 %copy-start.3 = (f32[1,7,4,8,512]{4,3,2,1,0:T(8,128)S(1)}, f32[1,7,4,8,512]{4,3,2,1,0:T(8,128)}, u32[]{:S(2)}) copy-start(f32[1,7,4,8,512]{4,3,2,1,0:T(8,128)} %param.8) | copy-start | bytes 1376260
  7.1 10.0 %collective-permute-start = (f32[37,8,512]{2,1,0:T(8,128)}, f32[37,8,512]{2,1,0:T(8,128)S(1)}, u32[]{:S(2)}, u32[]{:S(2)}) collective-permute-start(f32[37,8,512]{2,1,0:T(8,128)} %get-tuple-element.30.m1), channel_id=1, source_target_pairs={{0,16},{16,0},{32,48},{48,32},{64,80},{80,64},{96,112},{112,96},{1... | collective-permute-start | bytes 1818632 | tf_op jit(solution)/shard_map/ppermute | solution.py:516
  7.2 11.9 %collective-permute-start.1 = (f32[37,8,512]{2,1,0:T(8,128)}, f32[37,8,512]{2,1,0:T(8,128)S(1)}, u32[]{:S(2)}, u32[]{:S(2)}) collective-permute-start(f32[37,8,512]{2,1,0:T(8,128)} %get-tuple-element.31.m2), channel_id=1, source_target_pairs={{16,32},{32,16},{48,64},{64,48},{80,96},{96,80},{17,33},{33,17},{4... | collective-permute-start | bytes 1818632 | tf_op jit(solution)/shard_map/ppermute | solution.py:515
  9.8 37.6 %collective-permute-start.4 = (f32[13,8,512]{2,1,0:T(8,128)}, f32[13,8,512]{2,1,0:T(8,128)S(1)}, u32[]{:S(2)}, u32[]{:S(2)}) collective-permute-start(f32[13,8,512]{2,1,0:T(8,128)} %get-tuple-element.34), channel_id=1, source_target_pairs={{1,3},{3,1},{5,7},{7,5},{9,11},{11,9},{13,15},{15,13},{17,19},{19,... | collective-permute-start | bytes 638984 | tf_op jit(solution)/shard_map/ppermute | solution.py:516
  14.7 32.7 %collective-permute-start.5 = (f32[13,8,512]{2,1,0:T(8,128)}, f32[13,8,512]{2,1,0:T(8,128)S(1)}, u32[]{:S(2)}, u32[]{:S(2)}) collective-permute-start(f32[13,8,512]{2,1,0:T(8,128)} %get-tuple-element.35), channel_id=1, source_target_pairs={{3,5},{5,3},{7,9},{9,7},{11,13},{13,11},{19,21},{21,19},{23,25},{2... | collective-permute-start | bytes 638984 | tf_op jit(solution)/shard_map/ppermute | solution.py:515
  19.1 1.1 copy-start.4
  20.2 1.1 copy-start.5
  22.8 23.8 %collective-permute-start.2 = (f32[9,8,512]{2,1,0:T(8,128)S(1)}, f32[9,8,512]{2,1,0:T(8,128)S(1)}, u32[]{:S(2)}, u32[]{:S(2)}) collective-permute-start(f32[9,8,512]{2,1,0:T(8,128)S(1)} %get-tuple-element.32), channel_id=1, source_target_pairs={{0,2},{2,0},{4,6},{6,4},{8,10},{10,8},{12,14},{14,12},{1,3},{3,1},... | collective-permute-start | bytes 442376 | tf_op jit(solution)/shard_map/ppermute | solution.py:516
  25.9 20.8 %collective-permute-start.3 = (f32[9,8,512]{2,1,0:T(8,128)S(1)}, f32[9,8,512]{2,1,0:T(8,128)S(1)}, u32[]{:S(2)}, u32[]{:S(2)}) collective-permute-start(f32[9,8,512]{2,1,0:T(8,128)S(1)} %get-tuple-element.33), channel_id=1, source_target_pairs={{2,4},{4,2},{6,8},{8,6},{10,12},{12,10},{3,5},{5,3},{7,9},{9,7},{1... | collective-permute-start | bytes 442376 | tf_op jit(solution)/shard_map/ppermute | solution.py:515
  49.7 3.5 %collective-permute-start.6 = (f32[9,8,512]{2,1,0:T(8,128)S(1)}, f32[9,8,512]{2,1,0:T(8,128)S(1)}, u32[]{:S(2)}, u32[]{:S(2)}) collective-permute-start(f32[9,8,512]{2,1,0:T(8,128)S(1)} %get-tuple-element.40.m1), channel_id=1, source_target_pairs={{0,16},{16,0},{32,48},{48,32},{64,80},{80,64},{96,112},{112,96},{1... | collective-permute-start | bytes 442376 | tf_op jit(solution)/shard_map/ppermute | solution.py:516
  49.8 6.5 %collective-permute-start.7 = (f32[9,8,512]{2,1,0:T(8,128)S(1)}, f32[9,8,512]{2,1,0:T(8,128)S(1)}, u32[]{:S(2)}, u32[]{:S(2)}) collective-permute-start(f32[9,8,512]{2,1,0:T(8,128)S(1)} %get-tuple-element.41.m2), channel_id=1, source_target_pairs={{16,32},{32,16},{48,64},{64,48},{80,96},{96,80},{17,33},{33,17},{4... | collective-permute-start | bytes 442376 | tf_op jit(solution)/shard_map/ppermute | solution.py:515
  56.9 6.4 %collective-permute-start.8 = (f32[5,8,512]{2,1,0:T(8,128)S(1)}, f32[5,8,512]{2,1,0:T(8,128)S(1)}, u32[]{:S(2)}, u32[]{:S(2)}) collective-permute-start(f32[5,8,512]{2,1,0:T(8,128)S(1)} %get-tuple-element.42), channel_id=1, source_target_pairs={{0,2},{2,0},{4,6},{6,4},{8,10},{10,8},{12,14},{14,12},{1,3},{3,1},... | collective-permute-start | bytes 245768 | tf_op jit(solution)/shard_map/ppermute | solution.py:516
  57.6 8.8 %collective-permute-start.9 = (f32[5,8,512]{2,1,0:T(8,128)S(1)}, f32[5,8,512]{2,1,0:T(8,128)S(1)}, u32[]{:S(2)}, u32[]{:S(2)}) collective-permute-start(f32[5,8,512]{2,1,0:T(8,128)S(1)} %get-tuple-element.43), channel_id=1, source_target_pairs={{2,4},{4,2},{6,8},{8,6},{10,12},{12,10},{3,5},{5,3},{7,9},{9,7},{1... | collective-permute-start | bytes 245768 | tf_op jit(solution)/shard_map/ppermute | solution.py:515
  68.8 2.2 %collective-permute-start.10 = (f32[9,8,512]{2,1,0:T(8,128)S(1)}, f32[9,8,512]{2,1,0:T(8,128)S(1)}, u32[]{:S(2)}, u32[]{:S(2)}) collective-permute-start(f32[9,8,512]{2,1,0:T(8,128)S(1)} %get-tuple-element.45.m1), channel_id=1, source_target_pairs={{0,16},{16,0},{32,48},{48,32},{64,80},{80,64},{96,112},{112,96},{1... | collective-permute-start | bytes 442376 | tf_op jit(solution)/shard_map/ppermute | solution.py:516
  68.8 6.5 %collective-permute-start.11 = (f32[9,8,512]{2,1,0:T(8,128)S(1)}, f32[9,8,512]{2,1,0:T(8,128)S(1)}, u32[]{:S(2)}, u32[]{:S(2)}) collective-permute-start(f32[9,8,512]{2,1,0:T(8,128)S(1)} %get-tuple-element.46.m2), channel_id=1, source_target_pairs={{16,32},{32,16},{48,64},{64,48},{80,96},{96,80},{17,33},{33,17},{4... | collective-permute-start | bytes 442376 | tf_op jit(solution)/shard_map/ppermute | solution.py:515
  75.9 6.4 %collective-permute-start.12 = (f32[5,8,512]{2,1,0:T(8,128)S(1)}, f32[5,8,512]{2,1,0:T(8,128)S(1)}, u32[]{:S(2)}, u32[]{:S(2)}) collective-permute-start(f32[5,8,512]{2,1,0:T(8,128)S(1)} %get-tuple-element.47), channel_id=1, source_target_pairs={{0,2},{2,0},{4,6},{6,4},{8,10},{10,8},{12,14},{14,12},{1,3},{3,1},... | collective-permute-start | bytes 245768 | tf_op jit(solution)/shard_map/ppermute | solution.py:516
  78.9 8.8 %collective-permute-start.13 = (f32[5,8,512]{2,1,0:T(8,128)S(1)}, f32[5,8,512]{2,1,0:T(8,128)S(1)}, u32[]{:S(2)}, u32[]{:S(2)}) collective-permute-start(f32[5,8,512]{2,1,0:T(8,128)S(1)} %get-tuple-element.48), channel_id=1, source_target_pairs={{2,4},{4,2},{6,8},{8,6},{10,12},{12,10},{3,5},{5,3},{7,9},{9,7},{1... | collective-permute-start | bytes 245768 | tf_op jit(solution)/shard_map/ppermute | solution.py:515
  90.0 2.0 %collective-permute-start.14 = (f32[9,8,512]{2,1,0:T(8,128)S(1)}, f32[9,8,512]{2,1,0:T(8,128)S(1)}, u32[]{:S(2)}, u32[]{:S(2)}) collective-permute-start(f32[9,8,512]{2,1,0:T(8,128)S(1)} %get-tuple-element.50.m1), channel_id=1, source_target_pairs={{0,16},{16,0},{32,48},{48,32},{64,80},{80,64},{96,112},{112,96},{1... | collective-permute-start | bytes 442376 | tf_op jit(solution)/shard_map/ppermute | solution.py:516
  90.1 6.5 %collective-permute-start.15 = (f32[9,8,512]{2,1,0:T(8,128)S(1)}, f32[9,8,512]{2,1,0:T(8,128)S(1)}, u32[]{:S(2)}, u32[]{:S(2)}) collective-permute-start(f32[9,8,512]{2,1,0:T(8,128)S(1)} %get-tuple-element.51.m2), channel_id=1, source_target_pairs={{16,32},{32,16},{48,64},{64,48},{80,96},{96,80},{17,33},{33,17},{4... | collective-permute-start | bytes 442376 | tf_op jit(solution)/shard_map/ppermute | solution.py:515
  97.2 6.4 %collective-permute-start.16 = (f32[5,8,512]{2,1,0:T(8,128)S(1)}, f32[5,8,512]{2,1,0:T(8,128)S(1)}, u32[]{:S(2)}, u32[]{:S(2)}) collective-permute-start(f32[5,8,512]{2,1,0:T(8,128)S(1)} %get-tuple-element.52), channel_id=1, source_target_pairs={{0,2},{2,0},{4,6},{6,4},{8,10},{10,8},{12,14},{14,12},{1,3},{3,1},... | collective-permute-start | bytes 245768 | tf_op jit(solution)/shard_map/ppermute | solution.py:516
  97.9 8.8 %collective-permute-start.17 = (f32[5,8,512]{2,1,0:T(8,128)S(1)}, f32[5,8,512]{2,1,0:T(8,128)S(1)}, u32[]{:S(2)}, u32[]{:S(2)}) collective-permute-start(f32[5,8,512]{2,1,0:T(8,128)S(1)} %get-tuple-element.53), channel_id=1, source_target_pairs={{2,4},{4,2},{6,8},{8,6},{10,12},{12,10},{3,5},{5,3},{7,9},{9,7},{1... | collective-permute-start | bytes 245768 | tf_op jit(solution)/shard_map/ppermute | solution.py:515

commit v3 on v2

--- a/solution.py
+++ b/solution.py
@@ -1,7 +1,6 @@
 import functools
 import jax
 import jax.numpy as jnp
-import numpy as np
 from jax import lax
 from jax.experimental import pallas as pl
 from jax.experimental.pallas import tpu as pltpu
@@ -17,6 +16,7 @@
 VAL = T + 2
 COEF = T * T + T
 XBULK = COEF // 2
+MARKS = NZ // BLK
 YVAL = 5
 YHEAD = YVAL + 4
 YBULK = T * T // 4 + 1
@@ -42,6 +42,15 @@
 
 def packed(pair_low, pair_high, even, colour):
     return jnp.where(even, pair_low, pair_high) if colour == 0 else jnp.where(even, pair_high, pair_low)
+
+
+class Place:
+    def __init__(self):
+        self.rows_x = lax.axis_size("gx")
+        self.section, self.x, self.y = (lax.axis_index(axis) for axis in ("sa", "gx", "gy"))
+        self.rows_y = lax.axis_size("gy")
+        self.odd_x, self.odd_y = lax.rem(self.x, 2), lax.rem(self.y, 2)
+        self.exit_side = (self.section == 0) & (self.x == self.rows_x - 1)
 
 
 def store_message(ref, ones, zeros_first):
@@ -73,39 +82,29 @@
     return jnp.where(sub % 2 == 0, first, roll(second, 1, 0))
 
 
-def opening_kernel(
-    place, donors, fields, sources, diagonal, inverse, m1, m2, b1, b2, payload, blocks, coef, inv, sems
-):
-    section, odd, place_y, odd_y = place[0], place[1], place[9], place[2] == 1
-    exit_side = place[3] == 1
-    loads = [
-        pltpu.make_async_copy(sources, coef.at[0], sems.at[0]),
-        pltpu.make_async_copy(diagonal, coef.at[1], sems.at[1]),
-        pltpu.make_async_copy(inverse, inv, sems.at[2]),
-    ]
-    for load in loads:
-        load.start()
-    even, even_z = even_mask(NZ), even_mask(ZT)
-    for ref, pair in ((m1, 1 - odd), (m2, odd)):
-        store_message(
-            ref,
-            lambda t: packed(fields[t, 2 * pair], fields[t, 2 * pair + 1], even, 1),
-            lambda t: packed(fields[t, 2 * pair, :, :ZT], fields[t, 2 * pair + 1, :, :ZT], even_z, 0),
-        )
-
+def fill_payload(place, donors, returns, fields, payload, blocks):
     sub, lane = iotas(ZT)
     payload[...] = jnp.zeros_like(payload)
     cells = blocks.shape[0]
 
-    @pl.when(exit_side)
+    @pl.when(place.exit_side)
     def _():
         for entry in range(cells):
-            gy, block, slot = donors[3 * entry], donors[3 * entry + 1], donors[3 * entry + 2]
+            gy, block, slot = donors[0, entry], donors[1, entry], donors[2, entry]
             piece, row, column = block // 128, block % 128 // 16, block % 16
             start = pl.multiple_of(column // 4 * ZT, ZT)
             found = fields[piece, CX - 1, :, pl.ds(start, ZT)]
             found = pltpu.roll(pltpu.roll(found, (8 - row) % 8, 0), (ZT - column % 4 * BLK) % ZT, 1)
-            blocks[pl.ds(slot, 1), :] = jnp.where((lane < BLK) & (gy == place_y), found, 0.0)[:1]
+            blocks[pl.ds(slot, 1), :] = jnp.where((lane < BLK) & (gy == place.y), found, 0.0)[:1]
+        marks = [jnp.zeros((8, ZT), F32)] * 2
+        for t in range(T):
+            line = jnp.broadcast_to(returns[0:1, t * ZT : (t + 1) * ZT], (8, ZT)).astype(F32)
+            for n, row in enumerate((CY - 1, 0)):
+                turned = roll(line, MARKS * (t - row), 1)
+                marks[n] = jnp.where(lane // MARKS == t, turned, marks[n])
+        both = jnp.where(sub % 2 == 0, marks[0], marks[1])
+        for tile in range(2 * cells // 8):
+            payload[8 * tile : 8 * tile + 8, :] = both
         tiles = cells // 8
         zero = jnp.zeros((8, ZT), F32)
         for tile in range(tiles):
@@ -118,7 +117,7 @@
             payload[pl.ds(2 * cells + 16 * tile, 8, stride=2), :] = wide
             payload[pl.ds(2 * cells + 16 * tile + 1, 8, stride=2), :] = right
 
-    @pl.when(section == 1)
+    @pl.when(place.section == 1)
     def _():
         inlet = jnp.zeros((8, ZT), F32)
         for x in range(CX):
@@ -128,7 +127,68 @@
         for tile in range(cells // 8):
             payload[pl.ds(16 * tile, 8, stride=2), :] = inlet
 
-    wait_for(loads)
+
+def lines(ref, index, row):
+    found = [ref[pl.ds(128 * index + 8 * z + row, 8, stride=32), :] for z in range(NZ // ZT)]
+    return jnp.concatenate(found, axis=1)
+
+
+def second_half(array):
+    return roll(array, 4, 0)
+
+
+def row_of_colour_0(raw, row, lane):
+    return jnp.where((lane + row) % 2 == 0, raw, roll(raw, -1, 0))
+
+
+def interleaved(first, second, sub):
+    return jnp.where(sub % 2 == 0, first, roll(second, 1, 0))
+
+
+def opening_kernel(
+    donors,
+    returns_far,
+    fields_far,
+    sources_far,
+    diagonal_far,
+    inverse_far,
+    m1,
+    m2,
+    b1,
+    b2,
+    s1,
+    s2,
+    payload,
+    returns,
+    fields,
+    sources,
+    diagonal,
+    inverse,
+    blocks,
+    sems,
+):
+    pairs = (
+        (returns_far, returns),
+        (fields_far, fields),
+        (sources_far, sources),
+        (diagonal_far, diagonal),
+        (inverse_far, inverse),
+    )
+    loads = [pltpu.make_async_copy(far, near, sems.at[n]) for n, (far, near) in enumerate(pairs)]
+    for load in loads:
+        load.start()
+    wait_for(loads[:2])
+    place = Place()
+    section, odd, odd_y = place.section, place.odd_x, place.odd_y == 1
+    even, even_z = even_mask(NZ), even_mask(ZT)
+    for ref, pair in ((m1, 1 - odd), (m2, odd)):
+        store_message(
+            ref,
+            lambda t: packed(fields[t, 2 * pair], fields[t, 2 * pair + 1], even, 1),
+            lambda t: packed(fields[t, 2 * pair, :, :ZT], fields[t, 2 * pair + 1, :, :ZT], even_z, 0),
+        )
+    fill_payload(place, donors, returns, fields, payload, blocks)
+    wait_for(loads[2:])
     sub, lane = iotas(NZ)
 
     def plane_of(ref, index, plane):
@@ -137,9 +197,9 @@
 
     def coefficient(index, plane):
         if index >= T * T:
-            return plane_of(coef.at[0], index - T * T, plane)
-        raw = plane_of(inv, index, plane)
-        return jnp.where(section == 0, plane_of(coef.at[1], index, plane), raw) if index < T else raw
+            return plane_of(sources, index - T * T, plane)
+        raw = plane_of(inverse, index, plane)
+        return jnp.where(section == 0, plane_of(diagonal, index, plane), raw) if index < T else raw
 
     for ref, far in ((m1, 1 - odd), (m2, odd)):
         wanted = (sub + lane + far) % 2 == 0
@@ -148,21 +208,36 @@
             first, second = coefficient(2 * tile, plane), coefficient(2 * tile + 1, plane)
             ref[VAL + tile] = jnp.where(wanted, first, roll(second, 1, 0))
 
-    for tile in range(YBULK):
-        sides = []
-        for row in (0, CY - 1):
-            if tile + 1 < YBULK:
-                first, second = (row_of_colour_0(lines(inv, 4 * tile + 2 * n, row), row, lane) for n in (0, 1))
-                sides.append(interleaved(first, second, sub))
-            else:
-                sides.append(row_of_colour_0(second_half(lines(inv, T * T - 2, row)), row, lane))
-        down, up = sides
-        b1[tile] = jnp.where(odd_y, down, up)
-        b2[tile] = jnp.where(odd_y, up, down)
-
-
-def corner_values(place, m1, m2, r1, r2, y1, y2):
-    odd_x, odd_y = place[1] == 1, place[2] == 1
+    def inverse_rows(tile, row):
+        if tile + 1 == YBULK:
+            return row_of_colour_0(second_half(lines(inverse, T * T - 2, row)), row, lane)
+        first, second = (row_of_colour_0(lines(inverse, 4 * tile + 2 * n, row), row, lane) for n in (0, 1))
+        return interleaved(first, second, sub)
+
+    def pair(index, row):
+        if index + 1 < T:
+            return lines(sources, index, row)
+        if index + 1 == T:
+            halves = second_half(lines(sources, index - 1, row)), second_half(lines(diagonal, 0, row))
+            return jnp.where(sub < 4, halves[0], halves[1])
+        return lines(diagonal, index - T, row)
+
+    def other_rows(tile, row):
+        first = row_of_colour_0(pair(4 * tile, row), row, lane)
+        if tile == 3:
+            return first
+        return interleaved(first, row_of_colour_0(pair(4 * tile + 2, row), row, lane), sub)
+
+    for first, second, rows_of, tiles in ((b1, b2, inverse_rows, YBULK), (s1, s2, other_rows, 4)):
+        for tile in range(tiles):
+            down, up = rows_of(tile, 0), rows_of(tile, CY - 1)
+            first[tile] = jnp.where(odd_y, down, up)
+            second[tile] = jnp.where(odd_y, up, down)
+
+
+def corner_values(m1, m2, r1, r2, y1, y2):
+    place = Place()
+    odd_x, odd_y = place.odd_x == 1, place.odd_y == 1
     sub, lane = iotas(NZ)
     even = even_mask(NZ)
     tiles = {}
@@ -201,60 +276,30 @@
         y2[tile] = jnp.where(odd_y, up, down)
 
 
-def corner_kernel(place, m1, m2, r1, r2, y1, y2):
-    corner_values(place, m1, m2, r1, r2, y1, y2)
-
-
-def first_corner_kernel(place, m1, m2, r1, r2, returns, sources, diagonal, y1, y2, heads, sems):
-    odd_y = place[2] == 1
-    copies = [
-        pltpu.make_async_copy(ref.at[:VAL], heads.at[n], sems.at[n]) for n, ref in enumerate((m1, m2, r1, r2))
-    ]
+def corner_kernel(m1, m2, r1, r2, y1, y2):
+    corner_values(m1, m2, r1, r2, y1, y2)
+
+
+def first_corner_kernel(m1, m2, r1, r2, s1, s2, y1, y2, heads, sems):
+    pairs = [(ref.at[:VAL], heads.at[n]) for n, ref in enumerate((m1, m2, r1, r2))]
+    pairs += [(s1, y1.at[YVAL:YHEAD]), (s2, y2.at[YVAL:YHEAD])]
+    copies = [pltpu.make_async_copy(far, near, sems.at[n]) for n, (far, near) in enumerate(pairs)]
     for copy in copies:
         copy.start()
-    sub, lane = iotas(NZ)
-
-    def pair(index, row):
-        if index + 1 < T:
-            return lines(sources, index, row)
-        if index + 1 == T:
-            halves = second_half(lines(sources, index - 1, row)), second_half(lines(diagonal, 0, row))
-            return jnp.where(sub < 4, halves[0], halves[1])
-        return lines(diagonal, index - T, row)
-
-    small, _ = iotas(ZT)
-    marks = jnp.zeros((8, ZT), F32)
-    for t in range(T):
-        line = jnp.broadcast_to(returns[0:1, t * ZT : (t + 1) * ZT], (8, ZT))
-        marks = jnp.where(small == t, line.astype(F32), marks)
-    for tile in range(4):
-        sides = []
-        for row in (0, CY - 1):
-            first = row_of_colour_0(pair(4 * tile, row), row, lane)
-            if tile < 3:
-                second = row_of_colour_0(pair(4 * tile + 2, row), row, lane)
-                sides.append(interleaved(first, second, sub))
-            else:
-                sides.append(first)
-        down, up = sides
-        y1[YVAL + tile] = jnp.where(odd_y, down, up)
-        y2[YVAL + tile] = jnp.where(odd_y, up, down)
-    turned = roll(marks, NZ // BLK, 1)
-    for ref, value in ((y1, jnp.where(odd_y, marks, turned)), (y2, jnp.where(odd_y, turned, marks))):
-        for t in range(T):
-            row = 2 * (t % 4) + 1
-            ref[YVAL + 3, row : row + 1, t // 4 * ZT : (t // 4 + 1) * ZT] = value[t : t + 1]
     wait_for(copies)
-    corner_values(place, *[heads.at[n] for n in range(4)], y1, y2)
-
-
-def interface_kernel(place, blocks, returns, y1, y2, chosen, back, inflow, beside, sems):
-    odd_y = place[2] == 1
-    exit_side = place[3] == 1
-    back[...] = jnp.zeros_like(back)
-    copies = [pltpu.make_async_copy(ref.at[YHEAD - 1], beside.at[n], sems.at[n]) for n, ref in enumerate((y1, y2))]
+    corner_values(*[heads.at[n] for n in range(4)], y1, y2)
+
+
+def interface_kernel(blocks, coupling, returns_far, *refs):
+    count = (len(refs) - 5) // 2
+    back, inflow, weights = refs[count : count + 3]
+    returns, sems = refs[-2:]
+    pairs = [(returns_far, returns), *zip(refs[:count], refs[count + 3 : -2])]
+    copies = [pltpu.make_async_copy(far, near, sems.at[n]) for n, (far, near) in enumerate(pairs)]
     for copy in copies:
         copy.start()
+    place = Place()
+    back[...] = jnp.zeros_like(back)
     half = blocks.shape[0] // 2
     total = blocks[0:8]
     for tile in range(1, half // 8):
@@ -262,27 +307,39 @@
     total = total + roll(total, 4, 0)
     total = total + roll(total, 2, 0)
     first, second = (jnp.broadcast_to(total[row : row + 1], (8, ZT)) for row in (0, 1))
+    sub, lane = iotas(ZT)
+    weight = jnp.zeros((8, ZT), F32)
+    for t in range(T):
+        weight = jnp.where(sub == t, coupling[t], weight)
+    weights[...] = weight
     for row in range(16):
-        at = slice(8 * row, 8 * row + 8)
-        found = chosen[at, :ZT] * first + chosen[at, ZT:] * second
-        inflow[at, :] = jnp.broadcast_to(jnp.sum(found, axis=1, keepdims=True), (8, ZT))
-    wait_for(copies)
-
-    @pl.when(exit_side)
+        found = jnp.full((8, ZT), -1, jnp.int32)
+        for r, target in enumerate(chosen_places(row)):
+            found = jnp.where(sub == r, target, found)
+        parts = jnp.where(lane == found, first, 0.0) + jnp.where(lane + ZT == found, second, 0.0)
+        inflow[8 * row : 8 * row + 8, :] = jnp.broadcast_to(jnp.sum(parts, axis=1, keepdims=True), (8, ZT))
+
+    copies[0].wait()
+
+    @pl.when(place.exit_side)
     def _():
         cells = half // 2
         table = blocks[pl.ds(half, cells, stride=2), :]
-        sub, _ = iotas(ZT)
-
-        def marks_of(n):
-            laid = jnp.zeros((8, ZT), F32)
-            for t in range(T):
-                row, at = 2 * (t % 4) + 1, slice(t // 4 * ZT, (t // 4 + 1) * ZT)
-                laid = jnp.where(sub == t, jnp.broadcast_to(beside[n, row : row + 1, at], (8, ZT)), laid)
+        sub, lane = iotas(ZT)
+
+        def marks_of(row):
+            first = half - 2 * place.rows_y
+            line = jnp.zeros((8, ZT), F32)
+            for tile in range(2 * place.rows_y // 8):
+                at = first + 8 * tile
+                line = line + jnp.where(sub + 8 * tile == row, blocks[at : at + 8], 0.0)
+            line = jnp.broadcast_to(jnp.sum(line, axis=0, keepdims=True), (8, ZT))
+            laid = line
+            for t in range(1, T):
+                laid = jnp.where(sub == t, roll(line, -MARKS * t, 1), laid)
             return laid
 
-        first, second = marks_of(0), marks_of(1)
-        high, low = jnp.where(odd_y, second, first), jnp.where(odd_y, first, second)
+        high, low = marks_of(2 * place.y + 3), marks_of(2 * place.y - 2)
         slots = lax.broadcasted_iota(jnp.int32, (8, cells), 1).astype(F32)
         column = lax.broadcasted_iota(jnp.int32, table.shape, 1)
         spots = [jnp.where(column // BLK == q, roll(table, q * BLK, 1), 0.0) for q in range(ZT // BLK)]
@@ -291,7 +348,7 @@
             line = jnp.broadcast_to(returns[0:1, t * ZT : (t + 1) * ZT], (8, ZT))
             spread = line
             for y in range(1, CY):
-                spread = jnp.where(sub == y, roll(line, -y * (NZ // BLK), 1), spread)
+                spread = jnp.where(sub == y, roll(line, -y * MARKS, 1), spread)
             wanted.append(spread.astype(F32))
         wanted += [high, low]
         for tile in range(NZ // ZT):
@@ -308,15 +365,16 @@
                 back[t, 8:9, at] = laid[8 * T + t : 8 * T + t + 1]
                 back[t, 15:16, at] = laid[8 * T + 8 + t : 8 * T + 9 + t]
 
+    wait_for(copies[1:])
+
 
 def sweep_kernel(
-    place, coupling, fields, sources, diagonal, inverse, x1, x2, ya, za, yb, zb, back, inflow, *rest
+    last, weights, fields, sources, diagonal, inverse, x1, x2, ya, za, yb, zb, back, inflow, *rest
 ):
-    r1, r2, y1, y2 = rest[:4] if len(rest) == 9 else (x1, x2, ya, za)
-    out, m1, m2, u0, u1 = rest[-5:]
-    section = place[0]
-    odd_x, odd_y = place[1], place[2]
-    exit_side = place[3] == 1
+    r1, r2, y1, y2 = rest[:4] if len(rest) > 5 else (x1, x2, ya, za)
+    u0, u1 = rest[-2:]
+    place = Place()
+    section, odd_x, odd_y, exit_side = place.section, place.odd_x, place.odd_y, place.exit_side
     even, even_z = even_mask(NZ), even_mask(ZT)
     sub, lane = iotas(NZ)
     sub_z, _ = iotas(ZT)
@@ -349,10 +407,10 @@
             base = 4 * (t % 2) + 2 * k
             u1[t, k + 1, edge] = jnp.where(own_rows < 2, roll(high, -base, 0), roll(low, 6 - base, 0))
             row, at = 4 + 2 * k + t // 4, slice(t % 4 * ZT, (t % 4 + 1) * ZT)
-            first, last = beside(3, slice(row, row + 1), at)
-            u0[t, k + 1, edge, :ZT] = jnp.where(own_rows_z < 4, last, first)
-        first, last = beside(4, slice(t, t + 1), whole)
-        corner = jnp.where(own_rows < 4, last, first)
+            above, below = beside(3, slice(row, row + 1), at)
+            u0[t, k + 1, edge, :ZT] = jnp.where(own_rows_z < 4, below, above)
+        above, below = beside(4, slice(t, t + 1), whole)
+        corner = jnp.where(own_rows < 4, below, above)
         u1[t, 0, edge] = corner
         u1[t, 3, edge] = corner
 
@@ -427,10 +485,10 @@
 
     def valid(unit):
         if unit == "ring":
-            return jnp.where(even, place[5], place[4])
+            return jnp.where(even, place.rows_x - 1 - place.x, place.x) > 0
         if unit[1] == 0:
             return None
-        return jnp.where(sub == 7, place[6], place[7])
+        return jnp.where(sub == 7, place.y, place.rows_y - 1 - place.y) > 0
 
     def turbine(colour, unit):
         driving = []
@@ -441,7 +499,8 @@
             behind = jnp.where(lane == 0, start, roll(centre, 1, 1))
             total = x_sum + around(centre, beyond) + ahead + behind
             source = taken(colour, unit, "source", t)
-            driving.append(source + coupling[t] * total)
+            weight = jnp.concatenate([jnp.broadcast_to(weights[t : t + 1], (8, ZT))] * (NZ // ZT), axis=1)
+            driving.append(source + weight * total)
         for s in range(T):
             value = taken(colour, unit, "inverse", T * s) * driving[0]
             for t in range(1, T):
@@ -463,7 +522,7 @@
             source = taken(colour, unit, "source", t)
             value = (source + total) / (6.0 + taken(colour, unit, "diagonal", t))
             if flag is not None:
-                value = jnp.where(flag == 1, value, 0.0)
+                value = jnp.where(flag, value, 0.0)
             put(colour, unit, t, value)
             before, current = centre, after
 
@@ -476,12 +535,15 @@
     pl.when(section == 0)(functools.partial(both, combustor))
     pl.when(section != 0)(functools.partial(both, turbine))
 
+    out = rest[-3] if last else rest[-5]
     for t in range(T):
         for k in (0, 1):
             a, b = u0[t, k + 1, own], u1[t, k + 1, own]
             out[t, 2 * k] = jnp.where(even, a, b)
             out[t, 2 * k + 1] = jnp.where(even, b, a)
-    for ref, pair in ((m1, 2 - odd_x), (m2, 1 + odd_x)):
+    if last:
+        return
+    for ref, pair in ((rest[-4], 2 - odd_x), (rest[-3], 1 + odd_x)):
         store_message(ref, lambda t: u1[t, pair, own], lambda t: u0[t, pair, own, :ZT])
 
 
@@ -492,6 +554,7 @@
 SMEM = pl.BlockSpec(memory_space=pltpu.SMEM)
 VMEM = pl.BlockSpec(memory_space=pltpu.VMEM)
 ANY = pl.BlockSpec(memory_space=pl.ANY)
+HBM = pl.BlockSpec(memory_space=pltpu.HBM)
 
 
 def call(kernel, outs, operands, out_specs=None, scratch=(), limit=24):
@@ -505,6 +568,10 @@
     )(*[operand for _, operand in operands])
 
 
+def far(array):
+    return HBM, pltpu.with_memory_space_constraint(array, pltpu.HBM)
+
+
 def swaps(axis, first, second, turbine_only=False):
     peers = lax.axis_size(axis)
     inner = [(i, i ^ 1) for i in range(peers)]
@@ -516,27 +583,25 @@
     return lax.ppermute(first, axis, inner), second
 
 
-def chosen_slots():
-    table = np.zeros((128, 2 * ZT), np.float32)
-    for c in range(2):
-        for p in range(4):
-            for r in range(16):
-                y = r if r < 12 else r - 16
-                x = 2 * (p - 1) + (c if r % 2 == 0 else 1 - c)
-                block = None
-                if 0 <= x < CX and 0 <= y < CY:
-                    block = (0, x, y)
-                elif x == -1 and 0 <= y < CY:
-                    block = (1, CX - 1, y)
-                elif x == CX and 0 <= y < CY:
-                    block = (2, 0, y)
-                elif 0 <= x < CX and y == -1:
-                    block = (3, x, CY - 1)
-                elif 0 <= x < CX and y == CY:
-                    block = (4, x, 0)
-                if block is not None:
-                    table[64 * c + 16 * p + r, BLK * block[0] + CY * block[1] + block[2]] = 1.0
-    return table
+def chosen_places(tile):
+    places = []
+    for index in range(8 * tile, 8 * tile + 8):
+        c, p, r = index // 64, index // 16 % 4, index % 16
+        y = r if r < 12 else r - 16
+        x = 2 * (p - 1) + (c if r % 2 == 0 else 1 - c)
+        block = None
+        if 0 <= x < CX and 0 <= y < CY:
+            block = (0, x, y)
+        elif x == -1 and 0 <= y < CY:
+            block = (1, CX - 1, y)
+        elif x == CX and 0 <= y < CY:
+            block = (2, 0, y)
+        elif 0 <= x < CX and y == -1:
+            block = (3, x, CY - 1)
+        elif 0 <= x < CX and y == CY:
+            block = (4, x, 0)
+        places.append(-1 if block is None else BLK * block[0] + CY * block[1] + block[2])
+    return places
 
 
 def shards(fields, sources, diagonal, block_inverse, coupling, donors, returns):
@@ -544,77 +609,60 @@
     source = sources[0]
     rows_x, rows_y = lax.axis_size("gx"), lax.axis_size("gy")
     cells = rows_x * rows_y
-    section, place_x, place_y = (lax.axis_index(axis) for axis in ("sa", "gx", "gy"))
-    exit_side = (section == 0) & (place_x == rows_x - 1)
-    place = jnp.stack(
-        [
-            section,
-            place_x % 2,
-            place_y % 2,
-            exit_side.astype(jnp.int32),
-            (place_x > 0).astype(jnp.int32),
-            (place_x < rows_x - 1).astype(jnp.int32),
-            (place_y > 0).astype(jnp.int32),
-            (place_y < rows_y - 1).astype(jnp.int32),
-            place_x,
-            place_y,
-        ]
-    ).astype(jnp.int32)
-
     flat = [
         array.reshape(-1, CY, NZ // ZT, ZT).transpose(0, 2, 1, 3).reshape(-1, ZT)
         for array in (source, diagonal, block_inverse)
     ]
-    m1, m2, yb, zb, payload = call(
+    near = (returns, values, *flat)
+    m1, m2, yb, zb, s1, s2, payload = call(
         opening_kernel,
-        [shape(VAL + XBULK, 8, NZ)] * 2 + [shape(YBULK, 8, NZ)] * 2 + [shape(4 * cells, ZT)],
-        [(SMEM, place), (SMEM, donors.reshape(-1)), (VMEM, values)] + [(ANY, array) for array in flat],
-        scratch=[
-            pltpu.VMEM((cells, ZT), F32),
-            pltpu.VMEM((2, *flat[0].shape), F32),
-            pltpu.VMEM(flat[2].shape, F32),
-            pltpu.SemaphoreType.DMA((3,)),
-        ],
-        limit=60,
+        [pltpu.HBM((tiles, 8, NZ), F32) for tiles in [VAL + XBULK] * 2 + [YBULK] * 2 + [4] * 2]
+        + [shape(4 * cells, ZT)],
+        [(SMEM, pltpu.with_memory_space_constraint(donors.T, pltpu.HBM))] + [far(array) for array in near],
+        scratch=[pltpu.VMEM(array.shape, array.dtype) for array in near]
+        + [pltpu.VMEM((cells, ZT), F32), pltpu.SemaphoreType.DMA((len(near),))],
     )
     x1, x2 = swaps("gx", m1, m2)
     yb, zb = swaps("gy", yb, zb, turbine_only=True)
+    arrived = lax.all_to_all(
+        payload.reshape(2 * cells, 1, 2 * ZT), ("sa", "gx", "gy"), split_axis=0, concat_axis=0, tiled=True
+    ).reshape(4 * cells, ZT)
+    arrived, x1, x2 = lax.optimization_barrier((arrived, x1, x2))
     ya, za = call(
         first_corner_kernel,
         [shape(YHEAD, 8, NZ)] * 2,
-        [(SMEM, place)] + [(ANY, array) for array in (m1, m2, x1, x2)] + [(VMEM, array) for array in (returns, *flat[:2])],
-        scratch=[pltpu.VMEM((4, VAL, 8, NZ), F32), pltpu.SemaphoreType.DMA((4,))],
+        [far(m1), far(m2), (ANY, x1), (ANY, x2), far(s1), far(s2)],
+        scratch=[pltpu.VMEM((4, VAL, 8, NZ), F32), pltpu.SemaphoreType.DMA((6,))],
     )
     ya, za = swaps("gy", ya, za)
-    arrived = lax.all_to_all(
-        payload.reshape(2 * cells, 1, 2 * ZT), ("sa", "gx", "gy"), split_axis=0, concat_axis=0, tiled=True
-    ).reshape(4 * cells, ZT)
-    back, inflow = call(
+    distant = (values, source, diagonal, block_inverse)
+    made = call(
         interface_kernel,
-        [shape(T, 16, NZ), shape(128, ZT)],
-        [(SMEM, place), (VMEM, arrived), (VMEM, returns), (ANY, ya), (ANY, za), (VMEM, jnp.asarray(chosen_slots()))],
-        scratch=[pltpu.VMEM((2, 8, NZ), F32), pltpu.SemaphoreType.DMA((2,))],
+        [shape(T, 16, NZ), shape(128, ZT), shape(8, ZT)] + [pltpu.VMEM(array.shape, array.dtype) for array in distant],
+        [(VMEM, arrived), (SMEM, pltpu.with_memory_space_constraint(coupling, pltpu.HBM)), far(returns)]
+        + [far(array) for array in distant],
+        scratch=[pltpu.VMEM(returns.shape, returns.dtype), pltpu.SemaphoreType.DMA((len(distant) + 1,))],
     )
+    back, inflow, weights, values, source, diagonal, block_inverse = made
 
     for sweep in range(SWEEPS):
         received = []
         if sweep > 0:
             r1, r2 = swaps("gx", m1, m2)
             y1, y2 = call(
-                corner_kernel,
-                [shape(YVAL, 8, NZ)] * 2,
-                [(SMEM, place)] + [(VMEM, array) for array in (m1, m2, r1, r2)],
+                corner_kernel, [shape(YVAL, 8, NZ)] * 2, [(VMEM, array) for array in (m1, m2, r1, r2)]
             )
             received = [r1, r2, *swaps("gy", y1, y2)]
-        values, m1, m2 = call(
-            sweep_kernel,
-            [shape(T, CX, CY, NZ), shape(VAL, 8, NZ), shape(VAL, 8, NZ)],
-            [(SMEM, place), (SMEM, coupling)]
-            + [(VMEM, array) for array in (values, source, diagonal, block_inverse)]
+        last = sweep == SWEEPS - 1
+        results = call(
+            functools.partial(sweep_kernel, last),
+            [shape(T, CX, CY, NZ)] + [shape(VAL, 8, NZ)] * (0 if last else 2),
+            [(VMEM, array) for array in (weights, values, source, diagonal, block_inverse)]
             + [(VMEM, array) for array in (x1, x2, ya, za, yb, zb, back, inflow, *received)],
             scratch=[pltpu.VMEM((T, 4, 16, NZ), F32)] * 2,
             limit=40,
         )
+        values, m1, m2 = results if not last else (results[0], None, None)
     return values[None]
 
 

time: 110 us -> 101 us (0.918)
  blocking collectives: 18.3 us -> 0 us
  waiting for transfers between devices: 29.1 us -> 37.8 us
  starting transfers between devices: 38.8 us -> 45.2 us
  local copies, waits for them, and re-layouts: 4.31 us -> 0 us
  Pallas kernels: 19 us -> 17 us
    all_to_all x1 -> x0, blocking collectives: 18.3 us -> none  [shards(): lax.all_to_all(payload.reshape(2 * cells, 1, 2 * ZT), ('sa', 'gx', 'gy'),...]
    all_to_all x0 -> x1, starting transfers between devices: none -> 10.8 us  [shards(): lax.all_to_all(payload.reshape(2 * cells, 1, 2 * ZT), ('sa', 'gx', 'gy'),...]
    ppermute x9, waiting for transfers between devices: 3.67 us -> 11.6 us  [swaps(): return (lax.ppermute(first, axis, inner), second)]
    ppermute x9, starting transfers between devices: 26.1 us -> 20.2 us  [swaps(): second = lax.ppermute(second, axis, outer)]
    unnamed x21 -> x0, local copies, waits for them, and re-layouts: 3.01 us -> none
    pallas_call x10, Pallas kernels: 19 us -> 17 us  [call(): pl.pallas_call(kernel, out_shape=outs, in_specs=[spec for spec, _ in oper...]
    ppermute x9, starting transfers between devices: 12.7 us -> 14.2 us  [swaps(): return (lax.ppermute(first, axis, inner), second)]
  transfers between devices with their start and end apart: 18 -> 19, of which waited for: 9 -> 11; matrix products, arithmetic and copies ran while one was open for 0% -> 0% of each run, Pallas kernels for 2% -> 4%
where the time goes in v3:
time: 101 us; the launch traced here: 100 us
  starting transfers between devices  45.2 us (45%)
  waiting for transfers between devices  37.8 us (37%)
  Pallas kernels  17 us (17%)
    ppermute x9, waiting for transfers between devices, swaps(): second = lax.ppermute(second, axis, outer)  26.1 us
    ppermute x9, starting transfers between devices, swaps(): second = lax.ppermute(second, axis, outer)  20.2 us
    pallas_call x10, Pallas kernels, call(): pl.pallas_call(kernel, out_shape=outs, in_specs=[spec for spec, _ in oper...  17 us
    ppermute x9, starting transfers between devices, swaps(): return (lax.ppermute(first, axis, inner), second)  14.2 us
    ppermute x9, waiting for transfers between devices, swaps(): return (lax.ppermute(first, axis, inner), second)  11.6 us
    all_to_all x1, starting transfers between devices, shards(): lax.all_to_all(payload.reshape(2 * cells, 1, 2 * ZT), ('sa', 'gx', 'gy'),...  10.8 us
  transfers between devices with their start and end apart: 19, of which 11 were waited for; matrix products, arithmetic and copies ran while one was open for 0% of the time, Pallas kernels for 4%

profile of v3, /device:TPU:42, one launch (start us, length us, event | category | flops | bytes accessed | tf_op | source)
XLA Modules:
  0.0 100.2 jit_solution(15056244303150772798)
XLA Ops:
  0.0 4.8 %shard_map.73 = (f32[37,8,512]{2,1,0:T(8,128)}, f32[37,8,512]{2,1,0:T(8,128)}, f32[13,8,512]{2,1,0:T(8,128)}, f32[13,8,512]{2,1,0:T(8,128)}, f32[4,8,512]{2,1,0:...) custom-call(s32[3,64]{1,0:T(4,128)} %bitcast.28, s32[1,896]{1,0:T(1,128)} %returns_far.3, f32[7,4,8,512]{3,2,1,0:T(8,128)} %bitcast.23, ...), custom_call_target="tpu_custom_call" | custom-call | tf_op jit(solution)/shard_map/pallas_call | solution.py:561
  4.8 0.1 collective-permute-start
  4.9 2.4 %collective-permute-start.1 = (f32[37,8,512]{2,1,0:T(8,128)}, f32[37,8,512]{2,1,0:T(8,128)S(1)}, u32[]{:S(2)}, u32[]{:S(2)}) collective-permute-start(f32[37,8,512]{2,1,0:T(8,128)} %get-tuple-element.41.m2), channel_id=1, source_target_pairs={{16,32},{32,16},{48,64},{64,48},{80,96},{96,80},{17,33},{33,17},{4... | collective-permute-start | bytes 1818632 | tf_op jit(solution)/shard_map/ppermute | solution.py:582
  7.4 10.8 %all-to-all-start = ((f32[128,1,256]{2,1,0:T(1,128)}), f32[128,1,256]{2,1,0:T(1,128)S(1)}, u32[]{:S(2)}, u32[]{:S(2)}) async-start(f32[128,1,256]{2,1,0:T(1,128)} %bitcast.11), calls=%async_computation | async-start | bytes 262144 | tf_op jit(solution)/shard_map/all_to_all | solution.py:627
  18.1 4.5 %collective-permute-start.4 = (f32[13,8,512]{2,1,0:T(8,128)}, f32[13,8,512]{2,1,0:T(8,128)S(1)}, u32[]{:S(2)}, u32[]{:S(2)}) collective-permute-start(f32[13,8,512]{2,1,0:T(8,128)} %get-tuple-element.54), channel_id=1, source_target_pairs={{1,3},{3,1},{5,7},{7,5},{9,11},{11,9},{13,15},{15,13},{17,19},{19,... | collective-permute-start | bytes 638984 | tf_op jit(solution)/shard_map/ppermute | solution.py:583
  22.7 2.8 %collective-permute-start.5 = (f32[13,8,512]{2,1,0:T(8,128)}, f32[13,8,512]{2,1,0:T(8,128)S(1)}, u32[]{:S(2)}, u32[]{:S(2)}) collective-permute-start(f32[13,8,512]{2,1,0:T(8,128)} %get-tuple-element.55), channel_id=1, source_target_pairs={{3,5},{5,3},{7,9},{9,7},{11,13},{13,11},{19,21},{21,19},{23,25},{2... | collective-permute-start | bytes 638984 | tf_op jit(solution)/shard_map/ppermute | solution.py:582
  25.5 0.1 all-to-all-done
  25.6 0.0 collective-permute-done.r1.x1
  25.6 0.0 collective-permute-done.1.r2.x2
  25.6 1.4 %shard_map.75 = (f32[9,8,512]{2,1,0:T(8,128)S(1)}, f32[9,8,512]{2,1,0:T(8,128)S(1)}) custom-call(f32[37,8,512]{2,1,0:T(8,128)} %get-tuple-element.40.m1, f32[37,8,512]{2,1,0:T(8,128)} %get-tuple-element.41.m2, f32[37,8,512]{2,1,0:T(8,128)S(1)} %collective-permute-done.r1.x1, f32[37,8,512]{2,1,0:T(8,128)S(1)} %collective-permute-done.1.r2.x2, ...), custom_call_target="tpu_custom_call" | custom-call | tf_op jit(solution)/shard_map/pallas_call | solution.py:561
  27.1 3.5 %collective-permute-start.2 = (f32[9,8,512]{2,1,0:T(8,128)S(1)}, f32[9,8,512]{2,1,0:T(8,128)S(1)}, u32[]{:S(2)}, u32[]{:S(2)}) collective-permute-start(f32[9,8,512]{2,1,0:T(8,128)S(1)} %get-tuple-element.52), channel_id=1, source_target_pairs={{0,2},{2,0},{4,6},{6,4},{8,10},{10,8},{12,14},{14,12},{1,3},{3,1},... | collective-permute-start | bytes 442376 | tf_op jit(solution)/shard_map/ppermute | solution.py:583
  30.6 2.9 %collective-permute-start.3 = (f32[9,8,512]{2,1,0:T(8,128)S(1)}, f32[9,8,512]{2,1,0:T(8,128)S(1)}, u32[]{:S(2)}, u32[]{:S(2)}) collective-permute-start(f32[9,8,512]{2,1,0:T(8,128)S(1)} %get-tuple-element.53), channel_id=1, source_target_pairs={{2,4},{4,2},{6,8},{8,6},{10,12},{12,10},{3,5},{5,3},{7,9},{9,7},{1... | collective-permute-start | bytes 442376 | tf_op jit(solution)/shard_map/ppermute | solution.py:582
  33.5 3.1 %shard_map.74 = (f32[7,16,512]{2,1,0:T(8,128)S(1)}, f32[128,128]{1,0:T(8,128)S(1)}, f32[8,128]{1,0:T(8,128)S(1)}, f32[7,4,8,512]{3,2,1,0:T(8,128)S(1)}, f32[7,4,...) custom-call(f32[256,128]{1,0:T(8,128)S(1)} %bitcast.21, f32[7]{0:T(128)} %coupling.1, ...), custom_call_target="tpu_custom_call" | custom-call | tf_op jit(solution)/shard_map/pallas_call | solution.py:561
  36.6 0.0 collective-permute-done.4.yb
  36.6 0.0 collective-permute-done.5.zb
  36.6 3.9 %collective-permute-done.2.ya = f32[9,8,512]{2,1,0:T(8,128)S(1)} collective-permute-done((f32[9,8,512]{2,1,0:T(8,128)S(1)}, f32[9,8,512]{2,1,0:T(8,128)S(1)}, u32[]{:S(2)}, u32[]{:S(2)}) %collective-permute-start.2) | collective-permute-done | bytes 147488 | tf_op jit(solution)/shard_map/ppermute | solution.py:583
  40.5 0.0 collective-permute-done.3.za
  40.5 1.6 %shard_map.76 = (f32[7,4,8,512]{3,2,1,0:T(8,128)S(1)}, f32[9,8,512]{2,1,0:T(8,128)S(1)}, f32[9,8,512]{2,1,0:T(8,128)S(1)}) custom-call(f32[8,128]{1,0:T(8,128)S(1)} %get-tuple-element.43.weights, f32[7,4,8,512]{3,2,1,0:T(8,128)S(1)} %get-tuple-element.44.fields, f32[7,4,8,512]{3,2,1,0:T(8,128)S(1)} %get-tuple-element.45.sources, ...), custom_call_target="tpu_custom_call" | custom-call | tf_op jit(solution)/shard_map/pallas_call | solution.py:561
  42.2 0.1 collective-permute-start.6
  42.3 2.5 %collective-permute-start.7 = (f32[9,8,512]{2,1,0:T(8,128)S(1)}, f32[9,8,512]{2,1,0:T(8,128)S(1)}, u32[]{:S(2)}, u32[]{:S(2)}) collective-permute-start(f32[9,8,512]{2,1,0:T(8,128)S(1)} %get-tuple-element.60.m2), channel_id=1, source_target_pairs={{16,32},{32,16},{48,64},{64,48},{80,96},{96,80},{17,33},{33,17},{4... | collective-permute-start | bytes 442376 | tf_op jit(solution)/shard_map/ppermute | solution.py:582
  44.8 0.0 collective-permute-done.6.r1.rest_0_
  44.8 4.0 %collective-permute-done.7.r2.rest_1_ = f32[9,8,512]{2,1,0:T(8,128)S(1)} collective-permute-done((f32[9,8,512]{2,1,0:T(8,128)S(1)}, f32[9,8,512]{2,1,0:T(8,128)S(1)}, u32[]{:S(2)}, u32[]{:S(2)}) %collective-permute-start.7) | collective-permute-done | bytes 147488 | tf_op jit(solution)/shard_map/ppermute | solution.py:582
  48.7 0.1 shard_map.77
  48.8 2.1 %collective-permute-start.8 = (f32[5,8,512]{2,1,0:T(8,128)S(1)}, f32[5,8,512]{2,1,0:T(8,128)S(1)}, u32[]{:S(2)}, u32[]{:S(2)}) collective-permute-start(f32[5,8,512]{2,1,0:T(8,128)S(1)} %get-tuple-element.61), channel_id=1, source_target_pairs={{0,2},{2,0},{4,6},{6,4},{8,10},{10,8},{12,14},{14,12},{1,3},{3,1},... | collective-permute-start | bytes 245768 | tf_op jit(solution)/shard_map/ppermute | solution.py:583
  50.9 1.9 %collective-permute-start.9 = (f32[5,8,512]{2,1,0:T(8,128)S(1)}, f32[5,8,512]{2,1,0:T(8,128)S(1)}, u32[]{:S(2)}, u32[]{:S(2)}) collective-permute-start(f32[5,8,512]{2,1,0:T(8,128)S(1)} %get-tuple-element.62), channel_id=1, source_target_pairs={{2,4},{4,2},{6,8},{8,6},{10,12},{12,10},{3,5},{5,3},{7,9},{9,7},{1... | collective-permute-start | bytes 245768 | tf_op jit(solution)/shard_map/ppermute | solution.py:582
  52.9 2.4 %collective-permute-done.8.rest_2_ = f32[5,8,512]{2,1,0:T(8,128)S(1)} collective-permute-done((f32[5,8,512]{2,1,0:T(8,128)S(1)}, f32[5,8,512]{2,1,0:T(8,128)S(1)}, u32[]{:S(2)}, u32[]{:S(2)}) %collective-permute-start.8) | collective-permute-done | bytes 81952 | tf_op jit(solution)/shard_map/ppermute | solution.py:583
  55.2 4.5 %collective-permute-done.9.rest_3_ = f32[5,8,512]{2,1,0:T(8,128)S(1)} collective-permute-done((f32[5,8,512]{2,1,0:T(8,128)S(1)}, f32[5,8,512]{2,1,0:T(8,128)S(1)}, u32[]{:S(2)}, u32[]{:S(2)}) %collective-permute-start.9) | collective-permute-done | bytes 81952 | tf_op jit(solution)/shard_map/ppermute | solution.py:582
  59.8 1.6 %shard_map.78 = (f32[7,4,8,512]{3,2,1,0:T(8,128)S(1)}, f32[9,8,512]{2,1,0:T(8,128)S(1)}, f32[9,8,512]{2,1,0:T(8,128)S(1)}) custom-call(f32[8,128]{1,0:T(8,128)S(1)} %get-tuple-element.43.weights, f32[7,4,8,512]{3,2,1,0:T(8,128)S(1)} %get-tuple-element.58.fields, f32[7,4,8,512]{3,2,1,0:T(8,128)S(1)} %get-tuple-element.45.sources, ...), custom_call_target="tpu_custom_call" | custom-call | tf_op jit(solution)/shard_map/pallas_call | solution.py:561
  61.4 0.1 collective-permute-start.10
  61.5 1.9 %collective-permute-start.11 = (f32[9,8,512]{2,1,0:T(8,128)S(1)}, f32[9,8,512]{2,1,0:T(8,128)S(1)}, u32[]{:S(2)}, u32[]{:S(2)}) collective-permute-start(f32[9,8,512]{2,1,0:T(8,128)S(1)} %get-tuple-element.65.m2), channel_id=1, source_target_pairs={{16,32},{32,16},{48,64},{64,48},{80,96},{96,80},{17,33},{33,17},{4... | collective-permute-start | bytes 442376 | tf_op jit(solution)/shard_map/ppermute | solution.py:582
  63.4 0.0 collective-permute-done.10.r1.rest_0_
  63.4 4.5 %collective-permute-done.11.r2.rest_1_ = f32[9,8,512]{2,1,0:T(8,128)S(1)} collective-permute-done((f32[9,8,512]{2,1,0:T(8,128)S(1)}, f32[9,8,512]{2,1,0:T(8,128)S(1)}, u32[]{:S(2)}, u32[]{:S(2)}) %collective-permute-start.11) | collective-permute-done | bytes 147488 | tf_op jit(solution)/shard_map/ppermute | solution.py:582
  68.0 0.1 shard_map.79
  68.0 1.6 %collective-permute-start.12 = (f32[5,8,512]{2,1,0:T(8,128)S(1)}, f32[5,8,512]{2,1,0:T(8,128)S(1)}, u32[]{:S(2)}, u32[]{:S(2)}) collective-permute-start(f32[5,8,512]{2,1,0:T(8,128)S(1)} %get-tuple-element.66), channel_id=1, source_target_pairs={{0,2},{2,0},{4,6},{6,4},{8,10},{10,8},{12,14},{14,12},{1,3},{3,1},... | collective-permute-start | bytes 245768 | tf_op jit(solution)/shard_map/ppermute | solution.py:583
  69.6 1.9 %collective-permute-start.13 = (f32[5,8,512]{2,1,0:T(8,128)S(1)}, f32[5,8,512]{2,1,0:T(8,128)S(1)}, u32[]{:S(2)}, u32[]{:S(2)}) collective-permute-start(f32[5,8,512]{2,1,0:T(8,128)S(1)} %get-tuple-element.67), channel_id=1, source_target_pairs={{2,4},{4,2},{6,8},{8,6},{10,12},{12,10},{3,5},{5,3},{7,9},{9,7},{1... | collective-permute-start | bytes 245768 | tf_op jit(solution)/shard_map/ppermute | solution.py:582
  71.5 2.9 %collective-permute-done.12.rest_2_ = f32[5,8,512]{2,1,0:T(8,128)S(1)} collective-permute-done((f32[5,8,512]{2,1,0:T(8,128)S(1)}, f32[5,8,512]{2,1,0:T(8,128)S(1)}, u32[]{:S(2)}, u32[]{:S(2)}) %collective-permute-start.12) | collective-permute-done | bytes 81952 | tf_op jit(solution)/shard_map/ppermute | solution.py:583
  74.5 4.0 %collective-permute-done.13.rest_3_ = f32[5,8,512]{2,1,0:T(8,128)S(1)} collective-permute-done((f32[5,8,512]{2,1,0:T(8,128)S(1)}, f32[5,8,512]{2,1,0:T(8,128)S(1)}, u32[]{:S(2)}, u32[]{:S(2)}) %collective-permute-start.13) | collective-permute-done | bytes 81952 | tf_op jit(solution)/shard_map/ppermute | solution.py:582
  78.5 1.8 %shard_map.80 = (f32[7,4,8,512]{3,2,1,0:T(8,128)S(1)}, f32[9,8,512]{2,1,0:T(8,128)S(1)}, f32[9,8,512]{2,1,0:T(8,128)S(1)}) custom-call(f32[8,128]{1,0:T(8,128)S(1)} %get-tuple-element.43.weights, f32[7,4,8,512]{3,2,1,0:T(8,128)S(1)} %get-tuple-element.63.fields, f32[7,4,8,512]{3,2,1,0:T(8,128)S(1)} %get-tuple-element.45.sources, ...), custom_call_target="tpu_custom_call" | custom-call | tf_op jit(solution)/shard_map/pallas_call | solution.py:561
  80.3 0.1 collective-permute-start.14
  80.4 1.9 %collective-permute-start.15 = (f32[9,8,512]{2,1,0:T(8,128)S(1)}, f32[9,8,512]{2,1,0:T(8,128)S(1)}, u32[]{:S(2)}, u32[]{:S(2)}) collective-permute-start(f32[9,8,512]{2,1,0:T(8,128)S(1)} %get-tuple-element.70.m2), channel_id=1, source_target_pairs={{16,32},{32,16},{48,64},{64,48},{80,96},{96,80},{17,33},{33,17},{4... | collective-permute-start | bytes 442376 | tf_op jit(solution)/shard_map/ppermute | solution.py:582
  82.3 0.0 collective-permute-done.14.r1.rest_0_
  82.3 4.5 %collective-permute-done.15.r2.rest_1_ = f32[9,8,512]{2,1,0:T(8,128)S(1)} collective-permute-done((f32[9,8,512]{2,1,0:T(8,128)S(1)}, f32[9,8,512]{2,1,0:T(8,128)S(1)}, u32[]{:S(2)}, u32[]{:S(2)}) %collective-permute-start.15) | collective-permute-done | bytes 147488 | tf_op jit(solution)/shard_map/ppermute | solution.py:582
  86.8 0.1 shard_map.81
  86.9 2.1 %collective-permute-start.16 = (f32[5,8,512]{2,1,0:T(8,128)S(1)}, f32[5,8,512]{2,1,0:T(8,128)S(1)}, u32[]{:S(2)}, u32[]{:S(2)}) collective-permute-start(f32[5,8,512]{2,1,0:T(8,128)S(1)} %get-tuple-element.71), channel_id=1, source_target_pairs={{0,2},{2,0},{4,6},{6,4},{8,10},{10,8},{12,14},{14,12},{1,3},{3,1},... | collective-permute-start | bytes 245768 | tf_op jit(solution)/shard_map/ppermute | solution.py:583
  89.0 1.9 %collective-permute-start.17 = (f32[5,8,512]{2,1,0:T(8,128)S(1)}, f32[5,8,512]{2,1,0:T(8,128)S(1)}, u32[]{:S(2)}, u32[]{:S(2)}) collective-permute-start(f32[5,8,512]{2,1,0:T(8,128)S(1)} %get-tuple-element.72), channel_id=1, source_target_pairs={{2,4},{4,2},{6,8},{8,6},{10,12},{12,10},{3,5},{5,3},{7,9},{9,7},{1... | collective-permute-start | bytes 245768 | tf_op jit(solution)/shard_map/ppermute | solution.py:582
  90.9 2.4 %collective-permute-done.16.rest_2_ = f32[5,8,512]{2,1,0:T(8,128)S(1)} collective-permute-done((f32[5,8,512]{2,1,0:T(8,128)S(1)}, f32[5,8,512]{2,1,0:T(8,128)S(1)}, u32[]{:S(2)}, u32[]{:S(2)}) %collective-permute-start.16) | collective-permute-done | bytes 81952 | tf_op jit(solution)/shard_map/ppermute | solution.py:583
  93.3 4.5 %collective-permute-done.17.rest_3_ = f32[5,8,512]{2,1,0:T(8,128)S(1)} collective-permute-done((f32[5,8,512]{2,1,0:T(8,128)S(1)}, f32[5,8,512]{2,1,0:T(8,128)S(1)}, u32[]{:S(2)}, u32[]{:S(2)}) %collective-permute-start.17) | collective-permute-done | bytes 81952 | tf_op jit(solution)/shard_map/ppermute | solution.py:582
  97.9 2.4 %shard_map.82 = f32[7,4,8,512]{3,2,1,0:T(8,128)} custom-call(f32[8,128]{1,0:T(8,128)S(1)} %get-tuple-element.43.weights, f32[7,4,8,512]{3,2,1,0:T(8,128)S(1)} %get-tuple-element.68.fields, f32[7,4,8,512]{3,2,1,0:T(8,128)S(1)} %get-tuple-element.45.sources, f32[7,4,8,512]{3,2,1,0:T(8,128)S(1)} %get-tuple-element.46.diagonal, ...), custom_call_target="tpu_custom_call" | custom-call | tf_op jit(solution)/shard_map/pallas_call | solution.py:561
Async XLA Ops:
  4.8 20.8 %collective-permute-start = (f32[37,8,512]{2,1,0:T(8,128)}, f32[37,8,512]{2,1,0:T(8,128)S(1)}, u32[]{:S(2)}, u32[]{:S(2)}) collective-permute-start(f32[37,8,512]{2,1,0:T(8,128)} %get-tuple-element.40.m1), channel_id=1, source_target_pairs={{0,16},{16,0},{32,48},{48,32},{64,80},{80,64},{96,112},{112,96},{1... | collective-permute-start | bytes 1818632 | tf_op jit(solution)/shard_map/ppermute | solution.py:583
  4.9 20.7 %collective-permute-start.1 = (f32[37,8,512]{2,1,0:T(8,128)}, f32[37,8,512]{2,1,0:T(8,128)S(1)}, u32[]{:S(2)}, u32[]{:S(2)}) collective-permute-start(f32[37,8,512]{2,1,0:T(8,128)} %get-tuple-element.41.m2), channel_id=1, source_target_pairs={{16,32},{32,16},{48,64},{64,48},{80,96},{96,80},{17,33},{33,17},{4... | collective-permute-start | bytes 1818632 | tf_op jit(solution)/shard_map/ppermute | solution.py:582
  7.4 18.3 %all-to-all-start = ((f32[128,1,256]{2,1,0:T(1,128)}), f32[128,1,256]{2,1,0:T(1,128)S(1)}, u32[]{:S(2)}, u32[]{:S(2)}) async-start(f32[128,1,256]{2,1,0:T(1,128)} %bitcast.11), calls=%async_computation | async-start | bytes 262144 | tf_op jit(solution)/shard_map/all_to_all | solution.py:627
  18.1 18.4 %collective-permute-start.4 = (f32[13,8,512]{2,1,0:T(8,128)}, f32[13,8,512]{2,1,0:T(8,128)S(1)}, u32[]{:S(2)}, u32[]{:S(2)}) collective-permute-start(f32[13,8,512]{2,1,0:T(8,128)} %get-tuple-element.54), channel_id=1, source_target_pairs={{1,3},{3,1},{5,7},{7,5},{9,11},{11,9},{13,15},{15,13},{17,19},{19,... | collective-permute-start | bytes 638984 | tf_op jit(solution)/shard_map/ppermute | solution.py:583
  22.7 13.9 %collective-permute-start.5 = (f32[13,8,512]{2,1,0:T(8,128)}, f32[13,8,512]{2,1,0:T(8,128)S(1)}, u32[]{:S(2)}, u32[]{:S(2)}) collective-permute-start(f32[13,8,512]{2,1,0:T(8,128)} %get-tuple-element.55), channel_id=1, source_target_pairs={{3,5},{5,3},{7,9},{9,7},{11,13},{13,11},{19,21},{21,19},{23,25},{2... | collective-permute-start | bytes 638984 | tf_op jit(solution)/shard_map/ppermute | solution.py:582
  27.1 13.5 %collective-permute-start.2 = (f32[9,8,512]{2,1,0:T(8,128)S(1)}, f32[9,8,512]{2,1,0:T(8,128)S(1)}, u32[]{:S(2)}, u32[]{:S(2)}) collective-permute-start(f32[9,8,512]{2,1,0:T(8,128)S(1)} %get-tuple-element.52), channel_id=1, source_target_pairs={{0,2},{2,0},{4,6},{6,4},{8,10},{10,8},{12,14},{14,12},{1,3},{3,1},... | collective-permute-start | bytes 442376 | tf_op jit(solution)/shard_map/ppermute | solution.py:583
  30.6 10.0 %collective-permute-start.3 = (f32[9,8,512]{2,1,0:T(8,128)S(1)}, f32[9,8,512]{2,1,0:T(8,128)S(1)}, u32[]{:S(2)}, u32[]{:S(2)}) collective-permute-start(f32[9,8,512]{2,1,0:T(8,128)S(1)} %get-tuple-element.53), channel_id=1, source_target_pairs={{2,4},{4,2},{6,8},{8,6},{10,12},{12,10},{3,5},{5,3},{7,9},{9,7},{1... | collective-permute-start | bytes 442376 | tf_op jit(solution)/shard_map/ppermute | solution.py:582
  42.2 2.6 %collective-permute-start.6 = (f32[9,8,512]{2,1,0:T(8,128)S(1)}, f32[9,8,512]{2,1,0:T(8,128)S(1)}, u32[]{:S(2)}, u32[]{:S(2)}) collective-permute-start(f32[9,8,512]{2,1,0:T(8,128)S(1)} %get-tuple-element.59.m1), channel_id=1, source_target_pairs={{0,16},{16,0},{32,48},{48,32},{64,80},{80,64},{96,112},{112,96},{1... | collective-permute-start | bytes 442376 | tf_op jit(solution)/shard_map/ppermute | solution.py:583
  42.3 6.5 %collective-permute-start.7 = (f32[9,8,512]{2,1,0:T(8,128)S(1)}, f32[9,8,512]{2,1,0:T(8,128)S(1)}, u32[]{:S(2)}, u32[]{:S(2)}) collective-permute-start(f32[9,8,512]{2,1,0:T(8,128)S(1)} %get-tuple-element.60.m2), channel_id=1, source_target_pairs={{16,32},{32,16},{48,64},{64,48},{80,96},{96,80},{17,33},{33,17},{4... | collective-permute-start | bytes 442376 | tf_op jit(solution)/shard_map/ppermute | solution.py:582
  48.8 6.4 %collective-permute-start.8 = (f32[5,8,512]{2,1,0:T(8,128)S(1)}, f32[5,8,512]{2,1,0:T(8,128)S(1)}, u32[]{:S(2)}, u32[]{:S(2)}) collective-permute-start(f32[5,8,512]{2,1,0:T(8,128)S(1)} %get-tuple-element.61), channel_id=1, source_target_pairs={{0,2},{2,0},{4,6},{6,4},{8,10},{10,8},{12,14},{14,12},{1,3},{3,1},... | collective-permute-start | bytes 245768 | tf_op jit(solution)/shard_map/ppermute | solution.py:583
  50.9 8.8 %collective-permute-start.9 = (f32[5,8,512]{2,1,0:T(8,128)S(1)}, f32[5,8,512]{2,1,0:T(8,128)S(1)}, u32[]{:S(2)}, u32[]{:S(2)}) collective-permute-start(f32[5,8,512]{2,1,0:T(8,128)S(1)} %get-tuple-element.62), channel_id=1, source_target_pairs={{2,4},{4,2},{6,8},{8,6},{10,12},{12,10},{3,5},{5,3},{7,9},{9,7},{1... | collective-permute-start | bytes 245768 | tf_op jit(solution)/shard_map/ppermute | solution.py:582
  61.4 2.0 %collective-permute-start.10 = (f32[9,8,512]{2,1,0:T(8,128)S(1)}, f32[9,8,512]{2,1,0:T(8,128)S(1)}, u32[]{:S(2)}, u32[]{:S(2)}) collective-permute-start(f32[9,8,512]{2,1,0:T(8,128)S(1)} %get-tuple-element.64.m1), channel_id=1, source_target_pairs={{0,16},{16,0},{32,48},{48,32},{64,80},{80,64},{96,112},{112,96},{1... | collective-permute-start | bytes 442376 | tf_op jit(solution)/shard_map/ppermute | solution.py:583
  61.5 6.5 %collective-permute-start.11 = (f32[9,8,512]{2,1,0:T(8,128)S(1)}, f32[9,8,512]{2,1,0:T(8,128)S(1)}, u32[]{:S(2)}, u32[]{:S(2)}) collective-permute-start(f32[9,8,512]{2,1,0:T(8,128)S(1)} %get-tuple-element.65.m2), channel_id=1, source_target_pairs={{16,32},{32,16},{48,64},{64,48},{80,96},{96,80},{17,33},{33,17},{4... | collective-permute-start | bytes 442376 | tf_op jit(solution)/shard_map/ppermute | solution.py:582
  68.0 6.4 %collective-permute-start.12 = (f32[5,8,512]{2,1,0:T(8,128)S(1)}, f32[5,8,512]{2,1,0:T(8,128)S(1)}, u32[]{:S(2)}, u32[]{:S(2)}) collective-permute-start(f32[5,8,512]{2,1,0:T(8,128)S(1)} %get-tuple-element.66), channel_id=1, source_target_pairs={{0,2},{2,0},{4,6},{6,4},{8,10},{10,8},{12,14},{14,12},{1,3},{3,1},... | collective-permute-start | bytes 245768 | tf_op jit(solution)/shard_map/ppermute | solution.py:583
  69.6 8.8 %collective-permute-start.13 = (f32[5,8,512]{2,1,0:T(8,128)S(1)}, f32[5,8,512]{2,1,0:T(8,128)S(1)}, u32[]{:S(2)}, u32[]{:S(2)}) collective-permute-start(f32[5,8,512]{2,1,0:T(8,128)S(1)} %get-tuple-element.67), channel_id=1, source_target_pairs={{2,4},{4,2},{6,8},{8,6},{10,12},{12,10},{3,5},{5,3},{7,9},{9,7},{1... | collective-permute-start | bytes 245768 | tf_op jit(solution)/shard_map/ppermute | solution.py:582
  80.3 2.0 %collective-permute-start.14 = (f32[9,8,512]{2,1,0:T(8,128)S(1)}, f32[9,8,512]{2,1,0:T(8,128)S(1)}, u32[]{:S(2)}, u32[]{:S(2)}) collective-permute-start(f32[9,8,512]{2,1,0:T(8,128)S(1)} %get-tuple-element.69.m1), channel_id=1, source_target_pairs={{0,16},{16,0},{32,48},{48,32},{64,80},{80,64},{96,112},{112,96},{1... | collective-permute-start | bytes 442376 | tf_op jit(solution)/shard_map/ppermute | solution.py:583
  80.4 6.5 %collective-permute-start.15 = (f32[9,8,512]{2,1,0:T(8,128)S(1)}, f32[9,8,512]{2,1,0:T(8,128)S(1)}, u32[]{:S(2)}, u32[]{:S(2)}) collective-permute-start(f32[9,8,512]{2,1,0:T(8,128)S(1)} %get-tuple-element.70.m2), channel_id=1, source_target_pairs={{16,32},{32,16},{48,64},{64,48},{80,96},{96,80},{17,33},{33,17},{4... | collective-permute-start | bytes 442376 | tf_op jit(solution)/shard_map/ppermute | solution.py:582
  86.9 6.4 %collective-permute-start.16 = (f32[5,8,512]{2,1,0:T(8,128)S(1)}, f32[5,8,512]{2,1,0:T(8,128)S(1)}, u32[]{:S(2)}, u32[]{:S(2)}) collective-permute-start(f32[5,8,512]{2,1,0:T(8,128)S(1)} %get-tuple-element.71), channel_id=1, source_target_pairs={{0,2},{2,0},{4,6},{6,4},{8,10},{10,8},{12,14},{14,12},{1,3},{3,1},... | collective-permute-start | bytes 245768 | tf_op jit(solution)/shard_map/ppermute | solution.py:583
  89.0 8.8 %collective-permute-start.17 = (f32[5,8,512]{2,1,0:T(8,128)S(1)}, f32[5,8,512]{2,1,0:T(8,128)S(1)}, u32[]{:S(2)}, u32[]{:S(2)}) collective-permute-start(f32[5,8,512]{2,1,0:T(8,128)S(1)} %get-tuple-element.72), channel_id=1, source_target_pairs={{2,4},{4,2},{6,8},{8,6},{10,12},{12,10},{3,5},{5,3},{7,9},{9,7},{1... | collective-permute-start | bytes 245768 | tf_op jit(solution)/shard_map/ppermute | solution.py:582

commit v4 on v3

--- a/solution.py
+++ b/solution.py
@@ -17,6 +17,7 @@
 COEF = T * T + T
 XBULK = COEF // 2
 MARKS = NZ // BLK
+CHUNK = 2
 YVAL = 5
 YHEAD = YVAL + 4
 YBULK = T * T // 4 + 1
@@ -102,9 +103,9 @@
             for n, row in enumerate((CY - 1, 0)):
                 turned = roll(line, MARKS * (t - row), 1)
                 marks[n] = jnp.where(lane // MARKS == t, turned, marks[n])
-        both = jnp.where(sub % 2 == 0, marks[0], marks[1])
-        for tile in range(2 * cells // 8):
-            payload[8 * tile : 8 * tile + 8, :] = both
+        for tile in range(cells // 8):
+            for n in (0, 1):
+                payload[pl.ds(8 * CHUNK * tile + n, 8, stride=CHUNK), :] = marks[n]
         tiles = cells // 8
         zero = jnp.zeros((8, ZT), F32)
         for tile in range(tiles):
@@ -114,8 +115,8 @@
             left = jnp.where(sub == 0, 0.0, roll(here, 1, 0))
             right = jnp.where(sub == 7, 0.0, roll(here, -1, 0))
             wide = here + roll(below, BLK, 1) + roll(above, 2 * BLK, 1) + roll(left, 3 * BLK, 1)
-            payload[pl.ds(2 * cells + 16 * tile, 8, stride=2), :] = wide
-            payload[pl.ds(2 * cells + 16 * tile + 1, 8, stride=2), :] = right
+            payload[pl.ds(CHUNK * (cells + 8 * tile), 8, stride=CHUNK), :] = wide
+            payload[pl.ds(CHUNK * (cells + 8 * tile) + 1, 8, stride=CHUNK), :] = right
 
     @pl.when(place.section == 1)
     def _():
@@ -125,7 +126,7 @@
             inlet = inlet + jnp.where(lane == CY * x + sub, column, 0.0)
         inlet = jnp.broadcast_to(jnp.sum(inlet, axis=0, keepdims=True), (8, ZT))
         for tile in range(cells // 8):
-            payload[pl.ds(16 * tile, 8, stride=2), :] = inlet
+            payload[pl.ds(8 * CHUNK * tile, 8, stride=CHUNK), :] = inlet
 
 
 def lines(ref, index, row):
@@ -146,12 +147,25 @@
 
 
 def opening_kernel(
-    donors,
+    donors_far,
     returns_far,
     fields_far,
     sources_far,
     diagonal_far,
     inverse_far,
+    m1_far,
+    m2_far,
+    b1_far,
+    b2_far,
+    s1_far,
+    s2_far,
+    payload_far,
+    donors,
+    returns,
+    fields,
+    sources,
+    diagonal,
+    inverse,
     m1,
     m2,
     b1,
@@ -159,26 +173,33 @@
     s1,
     s2,
     payload,
-    returns,
-    fields,
-    sources,
-    diagonal,
-    inverse,
     blocks,
     sems,
+    out_sems,
 ):
     pairs = (
+        (donors_far, donors),
         (returns_far, returns),
         (fields_far, fields),
         (sources_far, sources),
         (diagonal_far, diagonal),
-        (inverse_far, inverse),
     )
+    bounds = [0, 12, 24, 36, T * T]
+    pieces = [slice(CX * NZ // ZT * CY * a, CX * NZ // ZT * CY * b) for a, b in zip(bounds, bounds[1:])]
+    pairs += tuple((inverse_far.at[piece], inverse.at[piece]) for piece in pieces)
     loads = [pltpu.make_async_copy(far, near, sems.at[n]) for n, (far, near) in enumerate(pairs)]
     for load in loads:
         load.start()
-    wait_for(loads[:2])
     place = Place()
+    sends = []
+
+    def send(*refs):
+        for near, far, at in refs:
+            copy = pltpu.make_async_copy(near.at[at], far.at[at], out_sems.at[len(sends)])
+            copy.start()
+            sends.append(copy)
+
+    wait_for(loads[:3])
     section, odd, odd_y = place.section, place.odd_x, place.odd_y == 1
     even, even_z = even_mask(NZ), even_mask(ZT)
     for ref, pair in ((m1, 1 - odd), (m2, odd)):
@@ -187,8 +208,10 @@
             lambda t: packed(fields[t, 2 * pair], fields[t, 2 * pair + 1], even, 1),
             lambda t: packed(fields[t, 2 * pair, :, :ZT], fields[t, 2 * pair + 1, :, :ZT], even_z, 0),
         )
+    send((m1, m1_far, slice(0, VAL)), (m2, m2_far, slice(0, VAL)))
     fill_payload(place, donors, returns, fields, payload, blocks)
-    wait_for(loads[2:])
+    send((payload, payload_far, slice(None)))
+    wait_for(loads[3:5])
     sub, lane = iotas(NZ)
 
     def plane_of(ref, index, plane):
@@ -201,12 +224,15 @@
         raw = plane_of(inverse, index, plane)
         return jnp.where(section == 0, plane_of(diagonal, index, plane), raw) if index < T else raw
 
-    for ref, far in ((m1, 1 - odd), (m2, odd)):
-        wanted = (sub + lane + far) % 2 == 0
-        plane = far * (CX - 1)
-        for tile in range(XBULK):
-            first, second = coefficient(2 * tile, plane), coefficient(2 * tile + 1, plane)
-            ref[VAL + tile] = jnp.where(wanted, first, roll(second, 1, 0))
+    def x_tiles(begin, end):
+        for ref, far in ((m1, 1 - odd), (m2, odd)):
+            wanted = (sub + lane + far) % 2 == 0
+            plane = far * (CX - 1)
+            for tile in range(begin, end):
+                first, second = coefficient(2 * tile, plane), coefficient(2 * tile + 1, plane)
+                ref[VAL + tile] = jnp.where(wanted, first, roll(second, 1, 0))
+        at = slice(VAL + begin, VAL + end)
+        send((m1, m1_far, at), (m2, m2_far, at))
 
     def inverse_rows(tile, row):
         if tile + 1 == YBULK:
@@ -228,11 +254,22 @@
             return first
         return interleaved(first, row_of_colour_0(pair(4 * tile + 2, row), row, lane), sub)
 
-    for first, second, rows_of, tiles in ((b1, b2, inverse_rows, YBULK), (s1, s2, other_rows, 4)):
-        for tile in range(tiles):
+    def y_tiles(refs, rows_of, begin, end):
+        first, second, first_far, second_far = refs
+        for tile in range(begin, end):
             down, up = rows_of(tile, 0), rows_of(tile, CY - 1)
             first[tile] = jnp.where(odd_y, down, up)
             second[tile] = jnp.where(odd_y, up, down)
+        at = slice(begin, end)
+        send((first, first_far, at), (second, second_far, at))
+
+    y_tiles((s1, s2, s1_far, s2_far), other_rows, 0, 4)
+    for n, (begin, end) in enumerate(zip(bounds, bounds[1:])):
+        loads[5 + n].wait()
+        last = end == T * T
+        x_tiles(begin // 2, XBULK if last else end // 2)
+        y_tiles((b1, b2, b1_far, b2_far), inverse_rows, begin // 4, YBULK if last else end // 4)
+    wait_for(sends)
 
 
 def corner_values(m1, m2, r1, r2, y1, y2):
@@ -276,11 +313,11 @@
         y2[tile] = jnp.where(odd_y, up, down)
 
 
-def corner_kernel(m1, m2, r1, r2, y1, y2):
+def corner_kernel(m1, m2, r2, r1, y1, y2):
     corner_values(m1, m2, r1, r2, y1, y2)
 
 
-def first_corner_kernel(m1, m2, r1, r2, s1, s2, y1, y2, heads, sems):
+def first_corner_kernel(m1, m2, r2, r1, s1, s2, y1, y2, heads, sems):
     pairs = [(ref.at[:VAL], heads.at[n]) for n, ref in enumerate((m1, m2, r1, r2))]
     pairs += [(s1, y1.at[YVAL:YHEAD]), (s2, y2.at[YVAL:YHEAD])]
     copies = [pltpu.make_async_copy(far, near, sems.at[n]) for n, (far, near) in enumerate(pairs)]
@@ -300,13 +337,15 @@
         copy.start()
     place = Place()
     back[...] = jnp.zeros_like(back)
-    half = blocks.shape[0] // 2
-    total = blocks[0:8]
-    for tile in range(1, half // 8):
-        total = total + blocks[8 * tile : 8 * tile + 8]
-    total = total + roll(total, 4, 0)
-    total = total + roll(total, 2, 0)
-    first, second = (jnp.broadcast_to(total[row : row + 1], (8, ZT)) for row in (0, 1))
+    cells = blocks.shape[0] // (2 * CHUNK)
+
+    def summed(n):
+        total = jnp.zeros((8, ZT), F32)
+        for tile in range(cells // 8):
+            total = total + blocks[pl.ds(8 * CHUNK * tile + n, 8, stride=CHUNK), :]
+        return jnp.broadcast_to(jnp.sum(total, axis=0, keepdims=True), (8, ZT))
+
+    first, second = summed(0), summed(1)
     sub, lane = iotas(ZT)
     weight = jnp.zeros((8, ZT), F32)
     for t in range(T):
@@ -323,23 +362,21 @@
 
     @pl.when(place.exit_side)
     def _():
-        cells = half // 2
-        table = blocks[pl.ds(half, cells, stride=2), :]
+        table = blocks[pl.ds(CHUNK * cells, cells, stride=CHUNK), :]
         sub, lane = iotas(ZT)
 
-        def marks_of(row):
-            first = half - 2 * place.rows_y
+        def marks_of(y, n):
             line = jnp.zeros((8, ZT), F32)
-            for tile in range(2 * place.rows_y // 8):
-                at = first + 8 * tile
-                line = line + jnp.where(sub + 8 * tile == row, blocks[at : at + 8], 0.0)
+            for tile in range(place.rows_y // 8):
+                at = CHUNK * (cells - place.rows_y + 8 * tile) + n
+                line = line + jnp.where(sub + 8 * tile == y, blocks[pl.ds(at, 8, stride=CHUNK), :], 0.0)
             line = jnp.broadcast_to(jnp.sum(line, axis=0, keepdims=True), (8, ZT))
             laid = line
             for t in range(1, T):
                 laid = jnp.where(sub == t, roll(line, -MARKS * t, 1), laid)
             return laid
 
-        high, low = marks_of(2 * place.y + 3), marks_of(2 * place.y - 2)
+        high, low = marks_of(place.y + 1, 1), marks_of(place.y - 1, 0)
         slots = lax.broadcasted_iota(jnp.int32, (8, cells), 1).astype(F32)
         column = lax.broadcasted_iota(jnp.int32, table.shape, 1)
         spots = [jnp.where(column // BLK == q, roll(table, q * BLK, 1), 0.0) for q in range(ZT // BLK)]
@@ -369,9 +406,9 @@
 
 
 def sweep_kernel(
-    last, weights, fields, sources, diagonal, inverse, x1, x2, ya, za, yb, zb, back, inflow, *rest
+    last, weights, fields, sources, diagonal, inverse, x2, x1, za, ya, zb, yb, back, inflow, *rest
 ):
-    r1, r2, y1, y2 = rest[:4] if len(rest) > 5 else (x1, x2, ya, za)
+    r2, r1, y2, y1 = rest[:4] if len(rest) > 5 else (x2, x1, za, ya)
     u0, u1 = rest[-2:]
     place = Place()
     section, odd_x, odd_y, exit_side = place.section, place.odd_x, place.odd_y, place.exit_side
@@ -614,24 +651,27 @@
         for array in (source, diagonal, block_inverse)
     ]
     near = (returns, values, *flat)
+    messages = [(tiles, 8, NZ) for tiles in [VAL + XBULK] * 2 + [YBULK] * 2 + [4] * 2] + [(2 * CHUNK * cells, ZT)]
     m1, m2, yb, zb, s1, s2, payload = call(
         opening_kernel,
-        [pltpu.HBM((tiles, 8, NZ), F32) for tiles in [VAL + XBULK] * 2 + [YBULK] * 2 + [4] * 2]
-        + [shape(4 * cells, ZT)],
-        [(SMEM, pltpu.with_memory_space_constraint(donors.T, pltpu.HBM))] + [far(array) for array in near],
-        scratch=[pltpu.VMEM(array.shape, array.dtype) for array in near]
-        + [pltpu.VMEM((cells, ZT), F32), pltpu.SemaphoreType.DMA((len(near),))],
+        [pltpu.HBM(dims, F32) for dims in messages],
+        [far(array) for array in (donors.T, *near)],
+        [HBM] * len(messages),
+        [pltpu.SMEM(donors.T.shape, donors.dtype)]
+        + [pltpu.VMEM(array.shape, array.dtype) for array in near]
+        + [pltpu.VMEM(dims, F32) for dims in messages]
+        + [pltpu.VMEM((cells, ZT), F32), pltpu.SemaphoreType.DMA((9,)), pltpu.SemaphoreType.DMA((21,))],
     )
     x1, x2 = swaps("gx", m1, m2)
     yb, zb = swaps("gy", yb, zb, turbine_only=True)
     arrived = lax.all_to_all(
-        payload.reshape(2 * cells, 1, 2 * ZT), ("sa", "gx", "gy"), split_axis=0, concat_axis=0, tiled=True
-    ).reshape(4 * cells, ZT)
+        payload.reshape(2 * cells, 1, CHUNK * ZT), ("sa", "gx", "gy"), split_axis=0, concat_axis=0, tiled=True
+    ).reshape(2 * CHUNK * cells, ZT)
     arrived, x1, x2 = lax.optimization_barrier((arrived, x1, x2))
     ya, za = call(
         first_corner_kernel,
         [shape(YHEAD, 8, NZ)] * 2,
-        [far(m1), far(m2), (ANY, x1), (ANY, x2), far(s1), far(s2)],
+        [far(m1), far(m2), (ANY, x2), (ANY, x1), far(s1), far(s2)],
         scratch=[pltpu.VMEM((4, VAL, 8, NZ), F32), pltpu.SemaphoreType.DMA((6,))],
     )
     ya, za = swaps("gy", ya, za)
@@ -650,15 +690,15 @@
         if sweep > 0:
             r1, r2 = swaps("gx", m1, m2)
             y1, y2 = call(
-                corner_kernel, [shape(YVAL, 8, NZ)] * 2, [(VMEM, array) for array in (m1, m2, r1, r2)]
+                corner_kernel, [shape(YVAL, 8, NZ)] * 2, [(VMEM, array) for array in (m1, m2, r2, r1)]
             )
-            received = [r1, r2, *swaps("gy", y1, y2)]
+            received = [r2, r1, *swaps("gy", y1, y2)[::-1]]
         last = sweep == SWEEPS - 1
         results = call(
             functools.partial(sweep_kernel, last),
             [shape(T, CX, CY, NZ)] + [shape(VAL, 8, NZ)] * (0 if last else 2),
             [(VMEM, array) for array in (weights, values, source, diagonal, block_inverse)]
-            + [(VMEM, array) for array in (x1, x2, ya, za, yb, zb, back, inflow, *received)],
+            + [(VMEM, array) for array in (x2, x1, za, ya, zb, yb, back, inflow, *received)],
             scratch=[pltpu.VMEM((T, 4, 16, NZ), F32)] * 2,
             limit=40,
         )

time: 101 us -> 99 us (0.980)
  waiting for transfers between devices: 37.8 us -> 24.6 us
  starting transfers between devices: 45.2 us -> 58.3 us
  Pallas kernels: 17 us -> 15.2 us
    ppermute x9, waiting for transfers between devices: 26.1 us -> 15.6 us  [swaps(): second = lax.ppermute(second, axis, outer)]
    ppermute x9, starting transfers between devices: 20.2 us -> 29.1 us  [swaps(): second = lax.ppermute(second, axis, outer)]
    ppermute x9, starting transfers between devices: 14.2 us -> 18 us  [swaps(): return (lax.ppermute(first, axis, inner), second)]
    ppermute x9, waiting for transfers between devices: 11.6 us -> 8.95 us  [swaps(): return (lax.ppermute(first, axis, inner), second)]
    pallas_call x10, Pallas kernels: 17 us -> 15.2 us  [call(): pl.pallas_call(kernel, out_shape=outs, in_specs=[spec for spec, _ in oper...]
  transfers between devices with their start and end apart: 19 -> 19, of which waited for: 11 -> 11; matrix products, arithmetic and copies ran while one was open for 0% -> 0% of each run, Pallas kernels for 4% -> 5%
where the time goes in v4:
time: 99 us; the launch traced here: 98.3 us
  starting transfers between devices  58.3 us (59%)
  waiting for transfers between devices  24.6 us (25%)
  Pallas kernels  15.2 us (15%)
    ppermute x9, starting transfers between devices, swaps(): second = lax.ppermute(second, axis, outer)  29.1 us
    ppermute x9, starting transfers between devices, swaps(): return (lax.ppermute(first, axis, inner), second)  18 us
    ppermute x9, waiting for transfers between devices, swaps(): second = lax.ppermute(second, axis, outer)  15.6 us
    pallas_call x10, Pallas kernels, call(): pl.pallas_call(kernel, out_shape=outs, in_specs=[spec for spec, _ in oper...  15.2 us
    all_to_all x1, starting transfers between devices, shards(): lax.all_to_all(payload.reshape(2 * cells, 1, CHUNK * ZT), ('sa', 'gx', 'g...  11.3 us
    ppermute x9, waiting for transfers between devices, swaps(): return (lax.ppermute(first, axis, inner), second)  8.95 us
  transfers between devices with their start and end apart: 19, of which 11 were waited for; matrix products, arithmetic and copies ran while one was open for 0% of the time, Pallas kernels for 5%

profile of v4, /device:TPU:42, one launch (start us, length us, event | category | flops | bytes accessed | tf_op | source)
XLA Modules:
  0.0 98.3 jit_solution(11117662810974498766)
XLA Ops:
  0.0 3.6 %shard_map.73 = (f32[37,8,512]{2,1,0:T(8,128)}, f32[37,8,512]{2,1,0:T(8,128)}, f32[13,8,512]{2,1,0:T(8,128)}, f32[13,8,512]{2,1,0:T(8,128)}, f32[4,8,512]{2,1,0:...) custom-call(s32[3,64]{1,0:T(4,128)} %bitcast.29, s32[1,896]{1,0:T(1,128)} %returns_far.3, f32[7,4,8,512]{3,2,1,0:T(8,128)} %bitcast.23, ...), custom_call_target="tpu_custom_call" | custom-call | tf_op jit(solution)/shard_map/pallas_call | solution.py:598
  3.6 0.1 collective-permute-start
  3.7 2.4 %collective-permute-start.1 = (f32[37,8,512]{2,1,0:T(8,128)}, f32[37,8,512]{2,1,0:T(8,128)S(1)}, u32[]{:S(2)}, u32[]{:S(2)}) collective-permute-start(f32[37,8,512]{2,1,0:T(8,128)} %get-tuple-element.41.m2), channel_id=1, source_target_pairs={{16,32},{32,16},{48,64},{64,48},{80,96},{96,80},{17,33},{33,17},{4... | collective-permute-start | bytes 1818632 | tf_op jit(solution)/shard_map/ppermute | solution.py:619
  6.1 11.3 %all-to-all-start = ((f32[128,1,256]{2,1,0:T(1,128)}), f32[128,1,256]{2,1,0:T(1,128)S(1)}, u32[]{:S(2)}, u32[]{:S(2)}) async-start(f32[128,1,256]{2,1,0:T(1,128)} %bitcast.28), calls=%async_computation | async-start | bytes 262144 | tf_op jit(solution)/shard_map/all_to_all | solution.py:667
  17.4 4.5 %collective-permute-start.4 = (f32[13,8,512]{2,1,0:T(8,128)}, f32[13,8,512]{2,1,0:T(8,128)S(1)}, u32[]{:S(2)}, u32[]{:S(2)}) collective-permute-start(f32[13,8,512]{2,1,0:T(8,128)} %get-tuple-element.54), channel_id=1, source_target_pairs={{3,5},{5,3},{7,9},{9,7},{11,13},{13,11},{19,21},{21,19},{23,25},{2... | collective-permute-start | bytes 638984 | tf_op jit(solution)/shard_map/ppermute | solution.py:619
  21.9 3.8 %collective-permute-start.5 = (f32[13,8,512]{2,1,0:T(8,128)}, f32[13,8,512]{2,1,0:T(8,128)S(1)}, u32[]{:S(2)}, u32[]{:S(2)}) collective-permute-start(f32[13,8,512]{2,1,0:T(8,128)} %get-tuple-element.55), channel_id=1, source_target_pairs={{1,3},{3,1},{5,7},{7,5},{9,11},{11,9},{13,15},{15,13},{17,19},{19,... | collective-permute-start | bytes 638984 | tf_op jit(solution)/shard_map/ppermute | solution.py:620
  25.7 0.0 all-to-all-done
  25.7 0.0 collective-permute-done.r1.x1
  25.7 0.0 collective-permute-done.1.r2.x2
  25.7 1.4 %shard_map.75 = (f32[9,8,512]{2,1,0:T(8,128)S(1)}, f32[9,8,512]{2,1,0:T(8,128)S(1)}) custom-call(f32[37,8,512]{2,1,0:T(8,128)} %get-tuple-element.40.m1, f32[37,8,512]{2,1,0:T(8,128)} %get-tuple-element.41.m2, f32[37,8,512]{2,1,0:T(8,128)S(1)} %collective-permute-done.1.r2.x2, f32[37,8,512]{2,1,0:T(8,128)S(1)} %collective-permute-done.r1.x1, ...), custom_call_target="tpu_custom_call" | custom-call | tf_op jit(solution)/shard_map/pallas_call | solution.py:598
  27.2 2.6 %collective-permute-start.2 = (f32[9,8,512]{2,1,0:T(8,128)S(1)}, f32[9,8,512]{2,1,0:T(8,128)S(1)}, u32[]{:S(2)}, u32[]{:S(2)}) collective-permute-start(f32[9,8,512]{2,1,0:T(8,128)S(1)} %get-tuple-element.52), channel_id=1, source_target_pairs={{2,4},{4,2},{6,8},{8,6},{10,12},{12,10},{3,5},{5,3},{7,9},{9,7},{1... | collective-permute-start | bytes 442376 | tf_op jit(solution)/shard_map/ppermute | solution.py:619
  29.8 3.5 %collective-permute-start.3 = (f32[9,8,512]{2,1,0:T(8,128)S(1)}, f32[9,8,512]{2,1,0:T(8,128)S(1)}, u32[]{:S(2)}, u32[]{:S(2)}) collective-permute-start(f32[9,8,512]{2,1,0:T(8,128)S(1)} %get-tuple-element.53), channel_id=1, source_target_pairs={{0,2},{2,0},{4,6},{6,4},{8,10},{10,8},{12,14},{14,12},{1,3},{3,1},... | collective-permute-start | bytes 442376 | tf_op jit(solution)/shard_map/ppermute | solution.py:620
  33.3 3.1 %shard_map.74 = (f32[7,16,512]{2,1,0:T(8,128)S(1)}, f32[128,128]{1,0:T(8,128)S(1)}, f32[8,128]{1,0:T(8,128)S(1)}, f32[7,4,8,512]{3,2,1,0:T(8,128)S(1)}, f32[7,4,...) custom-call(f32[256,128]{1,0:T(8,128)S(1)} %bitcast.21, f32[7]{0:T(128)} %coupling.1, ...), custom_call_target="tpu_custom_call" | custom-call | tf_op jit(solution)/shard_map/pallas_call | solution.py:598
  36.4 0.0 collective-permute-done.4.zb
  36.4 0.7 collective-permute-done.5.yb
  37.1 0.0 collective-permute-done.2.za
  37.1 3.1 %collective-permute-done.3.ya = f32[9,8,512]{2,1,0:T(8,128)S(1)} collective-permute-done((f32[9,8,512]{2,1,0:T(8,128)S(1)}, f32[9,8,512]{2,1,0:T(8,128)S(1)}, u32[]{:S(2)}, u32[]{:S(2)}) %collective-permute-start.3) | collective-permute-done | bytes 147488 | tf_op jit(solution)/shard_map/ppermute | solution.py:620
  40.1 1.5 %shard_map.76 = (f32[7,4,8,512]{3,2,1,0:T(8,128)S(1)}, f32[9,8,512]{2,1,0:T(8,128)S(1)}, f32[9,8,512]{2,1,0:T(8,128)S(1)}) custom-call(f32[8,128]{1,0:T(8,128)S(1)} %get-tuple-element.43.weights, f32[7,4,8,512]{3,2,1,0:T(8,128)S(1)} %get-tuple-element.44.fields, f32[7,4,8,512]{3,2,1,0:T(8,128)S(1)} %get-tuple-element.45.sources, ...), custom_call_target="tpu_custom_call" | custom-call | tf_op jit(solution)/shard_map/pallas_call | solution.py:598
  41.6 2.3 %collective-permute-start.6 = (f32[9,8,512]{2,1,0:T(8,128)S(1)}, f32[9,8,512]{2,1,0:T(8,128)S(1)}, u32[]{:S(2)}, u32[]{:S(2)}) collective-permute-start(f32[9,8,512]{2,1,0:T(8,128)S(1)} %get-tuple-element.59.m2), channel_id=1, source_target_pairs={{16,32},{32,16},{48,64},{64,48},{80,96},{96,80},{17,33},{33,17},{4... | collective-permute-start | bytes 442376 | tf_op jit(solution)/shard_map/ppermute | solution.py:619
  43.9 1.3 %collective-permute-start.7 = (f32[9,8,512]{2,1,0:T(8,128)S(1)}, f32[9,8,512]{2,1,0:T(8,128)S(1)}, u32[]{:S(2)}, u32[]{:S(2)}) collective-permute-start(f32[9,8,512]{2,1,0:T(8,128)S(1)} %get-tuple-element.60.m1), channel_id=1, source_target_pairs={{0,16},{16,0},{32,48},{48,32},{64,80},{80,64},{96,112},{112,96},{1... | collective-permute-start | bytes 442376 | tf_op jit(solution)/shard_map/ppermute | solution.py:620
  45.3 2.8 %collective-permute-done.6.r2.rest_0_ = f32[9,8,512]{2,1,0:T(8,128)S(1)} collective-permute-done((f32[9,8,512]{2,1,0:T(8,128)S(1)}, f32[9,8,512]{2,1,0:T(8,128)S(1)}, u32[]{:S(2)}, u32[]{:S(2)}) %collective-permute-start.6) | collective-permute-done | bytes 147488 | tf_op jit(solution)/shard_map/ppermute | solution.py:619
  48.1 0.0 collective-permute-done.7.r1.rest_1_
  48.1 0.1 shard_map.77
  48.2 4.5 %collective-permute-start.8 = (f32[5,8,512]{2,1,0:T(8,128)S(1)}, f32[5,8,512]{2,1,0:T(8,128)S(1)}, u32[]{:S(2)}, u32[]{:S(2)}) collective-permute-start(f32[5,8,512]{2,1,0:T(8,128)S(1)} %get-tuple-element.61), channel_id=1, source_target_pairs={{2,4},{4,2},{6,8},{8,6},{10,12},{12,10},{3,5},{5,3},{7,9},{9,7},{1... | collective-permute-start | bytes 245768 | tf_op jit(solution)/shard_map/ppermute | solution.py:619
  52.7 1.9 %collective-permute-start.9 = (f32[5,8,512]{2,1,0:T(8,128)S(1)}, f32[5,8,512]{2,1,0:T(8,128)S(1)}, u32[]{:S(2)}, u32[]{:S(2)}) collective-permute-start(f32[5,8,512]{2,1,0:T(8,128)S(1)} %get-tuple-element.62), channel_id=1, source_target_pairs={{0,2},{2,0},{4,6},{6,4},{8,10},{10,8},{12,14},{14,12},{1,3},{3,1},... | collective-permute-start | bytes 245768 | tf_op jit(solution)/shard_map/ppermute | solution.py:620
  54.6 2.4 %collective-permute-done.8.rest_2_ = f32[5,8,512]{2,1,0:T(8,128)S(1)} collective-permute-done((f32[5,8,512]{2,1,0:T(8,128)S(1)}, f32[5,8,512]{2,1,0:T(8,128)S(1)}, u32[]{:S(2)}, u32[]{:S(2)}) %collective-permute-start.8) | collective-permute-done | bytes 81952 | tf_op jit(solution)/shard_map/ppermute | solution.py:619
  57.0 1.7 %collective-permute-done.9.rest_3_ = f32[5,8,512]{2,1,0:T(8,128)S(1)} collective-permute-done((f32[5,8,512]{2,1,0:T(8,128)S(1)}, f32[5,8,512]{2,1,0:T(8,128)S(1)}, u32[]{:S(2)}, u32[]{:S(2)}) %collective-permute-start.9) | collective-permute-done | bytes 81952 | tf_op jit(solution)/shard_map/ppermute | solution.py:620
  58.7 1.5 %shard_map.78 = (f32[7,4,8,512]{3,2,1,0:T(8,128)S(1)}, f32[9,8,512]{2,1,0:T(8,128)S(1)}, f32[9,8,512]{2,1,0:T(8,128)S(1)}) custom-call(f32[8,128]{1,0:T(8,128)S(1)} %get-tuple-element.43.weights, f32[7,4,8,512]{3,2,1,0:T(8,128)S(1)} %get-tuple-element.58.fields, f32[7,4,8,512]{3,2,1,0:T(8,128)S(1)} %get-tuple-element.45.sources, ...), custom_call_target="tpu_custom_call" | custom-call | tf_op jit(solution)/shard_map/pallas_call | solution.py:598
  60.2 1.9 %collective-permute-start.10 = (f32[9,8,512]{2,1,0:T(8,128)S(1)}, f32[9,8,512]{2,1,0:T(8,128)S(1)}, u32[]{:S(2)}, u32[]{:S(2)}) collective-permute-start(f32[9,8,512]{2,1,0:T(8,128)S(1)} %get-tuple-element.64.m2), channel_id=1, source_target_pairs={{16,32},{32,16},{48,64},{64,48},{80,96},{96,80},{17,33},{33,17},{4... | collective-permute-start | bytes 442376 | tf_op jit(solution)/shard_map/ppermute | solution.py:619
  62.1 1.7 %collective-permute-start.11 = (f32[9,8,512]{2,1,0:T(8,128)S(1)}, f32[9,8,512]{2,1,0:T(8,128)S(1)}, u32[]{:S(2)}, u32[]{:S(2)}) collective-permute-start(f32[9,8,512]{2,1,0:T(8,128)S(1)} %get-tuple-element.65.m1), channel_id=1, source_target_pairs={{0,16},{16,0},{32,48},{48,32},{64,80},{80,64},{96,112},{112,96},{1... | collective-permute-start | bytes 442376 | tf_op jit(solution)/shard_map/ppermute | solution.py:620
  63.8 2.8 %collective-permute-done.10.r2.rest_0_ = f32[9,8,512]{2,1,0:T(8,128)S(1)} collective-permute-done((f32[9,8,512]{2,1,0:T(8,128)S(1)}, f32[9,8,512]{2,1,0:T(8,128)S(1)}, u32[]{:S(2)}, u32[]{:S(2)}) %collective-permute-start.10) | collective-permute-done | bytes 147488 | tf_op jit(solution)/shard_map/ppermute | solution.py:619
  66.7 0.0 collective-permute-done.11.r1.rest_1_
  66.7 0.1 shard_map.79
  66.8 4.5 %collective-permute-start.12 = (f32[5,8,512]{2,1,0:T(8,128)S(1)}, f32[5,8,512]{2,1,0:T(8,128)S(1)}, u32[]{:S(2)}, u32[]{:S(2)}) collective-permute-start(f32[5,8,512]{2,1,0:T(8,128)S(1)} %get-tuple-element.66), channel_id=1, source_target_pairs={{2,4},{4,2},{6,8},{8,6},{10,12},{12,10},{3,5},{5,3},{7,9},{9,7},{1... | collective-permute-start | bytes 245768 | tf_op jit(solution)/shard_map/ppermute | solution.py:619
  71.3 1.9 %collective-permute-start.13 = (f32[5,8,512]{2,1,0:T(8,128)S(1)}, f32[5,8,512]{2,1,0:T(8,128)S(1)}, u32[]{:S(2)}, u32[]{:S(2)}) collective-permute-start(f32[5,8,512]{2,1,0:T(8,128)S(1)} %get-tuple-element.67), channel_id=1, source_target_pairs={{0,2},{2,0},{4,6},{6,4},{8,10},{10,8},{12,14},{14,12},{1,3},{3,1},... | collective-permute-start | bytes 245768 | tf_op jit(solution)/shard_map/ppermute | solution.py:620
  73.2 2.4 %collective-permute-done.12.rest_2_ = f32[5,8,512]{2,1,0:T(8,128)S(1)} collective-permute-done((f32[5,8,512]{2,1,0:T(8,128)S(1)}, f32[5,8,512]{2,1,0:T(8,128)S(1)}, u32[]{:S(2)}, u32[]{:S(2)}) %collective-permute-start.12) | collective-permute-done | bytes 81952 | tf_op jit(solution)/shard_map/ppermute | solution.py:619
  75.6 1.7 %collective-permute-done.13.rest_3_ = f32[5,8,512]{2,1,0:T(8,128)S(1)} collective-permute-done((f32[5,8,512]{2,1,0:T(8,128)S(1)}, f32[5,8,512]{2,1,0:T(8,128)S(1)}, u32[]{:S(2)}, u32[]{:S(2)}) %collective-permute-start.13) | collective-permute-done | bytes 81952 | tf_op jit(solution)/shard_map/ppermute | solution.py:620
  77.3 1.7 %shard_map.80 = (f32[7,4,8,512]{3,2,1,0:T(8,128)S(1)}, f32[9,8,512]{2,1,0:T(8,128)S(1)}, f32[9,8,512]{2,1,0:T(8,128)S(1)}) custom-call(f32[8,128]{1,0:T(8,128)S(1)} %get-tuple-element.43.weights, f32[7,4,8,512]{3,2,1,0:T(8,128)S(1)} %get-tuple-element.63.fields, f32[7,4,8,512]{3,2,1,0:T(8,128)S(1)} %get-tuple-element.45.sources, ...), custom_call_target="tpu_custom_call" | custom-call | tf_op jit(solution)/shard_map/pallas_call | solution.py:598
  79.0 1.9 %collective-permute-start.14 = (f32[9,8,512]{2,1,0:T(8,128)S(1)}, f32[9,8,512]{2,1,0:T(8,128)S(1)}, u32[]{:S(2)}, u32[]{:S(2)}) collective-permute-start(f32[9,8,512]{2,1,0:T(8,128)S(1)} %get-tuple-element.69.m2), channel_id=1, source_target_pairs={{16,32},{32,16},{48,64},{64,48},{80,96},{96,80},{17,33},{33,17},{4... | collective-permute-start | bytes 442376 | tf_op jit(solution)/shard_map/ppermute | solution.py:619
  80.9 1.7 %collective-permute-start.15 = (f32[9,8,512]{2,1,0:T(8,128)S(1)}, f32[9,8,512]{2,1,0:T(8,128)S(1)}, u32[]{:S(2)}, u32[]{:S(2)}) collective-permute-start(f32[9,8,512]{2,1,0:T(8,128)S(1)} %get-tuple-element.70.m1), channel_id=1, source_target_pairs={{0,16},{16,0},{32,48},{48,32},{64,80},{80,64},{96,112},{112,96},{1... | collective-permute-start | bytes 442376 | tf_op jit(solution)/shard_map/ppermute | solution.py:620
  82.6 2.8 %collective-permute-done.14.r2.rest_0_ = f32[9,8,512]{2,1,0:T(8,128)S(1)} collective-permute-done((f32[9,8,512]{2,1,0:T(8,128)S(1)}, f32[9,8,512]{2,1,0:T(8,128)S(1)}, u32[]{:S(2)}, u32[]{:S(2)}) %collective-permute-start.14) | collective-permute-done | bytes 147488 | tf_op jit(solution)/shard_map/ppermute | solution.py:619
  85.4 0.0 collective-permute-done.15.r1.rest_1_
  85.4 0.1 shard_map.81
  85.5 4.5 %collective-permute-start.16 = (f32[5,8,512]{2,1,0:T(8,128)S(1)}, f32[5,8,512]{2,1,0:T(8,128)S(1)}, u32[]{:S(2)}, u32[]{:S(2)}) collective-permute-start(f32[5,8,512]{2,1,0:T(8,128)S(1)} %get-tuple-element.71), channel_id=1, source_target_pairs={{2,4},{4,2},{6,8},{8,6},{10,12},{12,10},{3,5},{5,3},{7,9},{9,7},{1... | collective-permute-start | bytes 245768 | tf_op jit(solution)/shard_map/ppermute | solution.py:619
  90.0 1.9 %collective-permute-start.17 = (f32[5,8,512]{2,1,0:T(8,128)S(1)}, f32[5,8,512]{2,1,0:T(8,128)S(1)}, u32[]{:S(2)}, u32[]{:S(2)}) collective-permute-start(f32[5,8,512]{2,1,0:T(8,128)S(1)} %get-tuple-element.72), channel_id=1, source_target_pairs={{0,2},{2,0},{4,6},{6,4},{8,10},{10,8},{12,14},{14,12},{1,3},{3,1},... | collective-permute-start | bytes 245768 | tf_op jit(solution)/shard_map/ppermute | solution.py:620
  92.0 2.4 %collective-permute-done.16.rest_2_ = f32[5,8,512]{2,1,0:T(8,128)S(1)} collective-permute-done((f32[5,8,512]{2,1,0:T(8,128)S(1)}, f32[5,8,512]{2,1,0:T(8,128)S(1)}, u32[]{:S(2)}, u32[]{:S(2)}) %collective-permute-start.16) | collective-permute-done | bytes 81952 | tf_op jit(solution)/shard_map/ppermute | solution.py:619
  94.3 1.7 %collective-permute-done.17.rest_3_ = f32[5,8,512]{2,1,0:T(8,128)S(1)} collective-permute-done((f32[5,8,512]{2,1,0:T(8,128)S(1)}, f32[5,8,512]{2,1,0:T(8,128)S(1)}, u32[]{:S(2)}, u32[]{:S(2)}) %collective-permute-start.17) | collective-permute-done | bytes 81952 | tf_op jit(solution)/shard_map/ppermute | solution.py:620
  96.0 2.2 %shard_map.82 = f32[7,4,8,512]{3,2,1,0:T(8,128)} custom-call(f32[8,128]{1,0:T(8,128)S(1)} %get-tuple-element.43.weights, f32[7,4,8,512]{3,2,1,0:T(8,128)S(1)} %get-tuple-element.68.fields, f32[7,4,8,512]{3,2,1,0:T(8,128)S(1)} %get-tuple-element.45.sources, f32[7,4,8,512]{3,2,1,0:T(8,128)S(1)} %get-tuple-element.46.diagonal, ...), custom_call_target="tpu_custom_call" | custom-call | tf_op jit(solution)/shard_map/pallas_call | solution.py:598
Async XLA Ops:
  3.6 22.1 %collective-permute-start = (f32[37,8,512]{2,1,0:T(8,128)}, f32[37,8,512]{2,1,0:T(8,128)S(1)}, u32[]{:S(2)}, u32[]{:S(2)}) collective-permute-start(f32[37,8,512]{2,1,0:T(8,128)} %get-tuple-element.40.m1), channel_id=1, source_target_pairs={{0,16},{16,0},{32,48},{48,32},{64,80},{80,64},{96,112},{112,96},{1... | collective-permute-start | bytes 1818632 | tf_op jit(solution)/shard_map/ppermute | solution.py:620
  3.7 22.0 %collective-permute-start.1 = (f32[37,8,512]{2,1,0:T(8,128)}, f32[37,8,512]{2,1,0:T(8,128)S(1)}, u32[]{:S(2)}, u32[]{:S(2)}) collective-permute-start(f32[37,8,512]{2,1,0:T(8,128)} %get-tuple-element.41.m2), channel_id=1, source_target_pairs={{16,32},{32,16},{48,64},{64,48},{80,96},{96,80},{17,33},{33,17},{4... | collective-permute-start | bytes 1818632 | tf_op jit(solution)/shard_map/ppermute | solution.py:619
  6.1 19.6 %all-to-all-start = ((f32[128,1,256]{2,1,0:T(1,128)}), f32[128,1,256]{2,1,0:T(1,128)S(1)}, u32[]{:S(2)}, u32[]{:S(2)}) async-start(f32[128,1,256]{2,1,0:T(1,128)} %bitcast.28), calls=%async_computation | async-start | bytes 262144 | tf_op jit(solution)/shard_map/all_to_all | solution.py:667
  17.4 19.0 %collective-permute-start.4 = (f32[13,8,512]{2,1,0:T(8,128)}, f32[13,8,512]{2,1,0:T(8,128)S(1)}, u32[]{:S(2)}, u32[]{:S(2)}) collective-permute-start(f32[13,8,512]{2,1,0:T(8,128)} %get-tuple-element.54), channel_id=1, source_target_pairs={{3,5},{5,3},{7,9},{9,7},{11,13},{13,11},{19,21},{21,19},{23,25},{2... | collective-permute-start | bytes 638984 | tf_op jit(solution)/shard_map/ppermute | solution.py:619
  21.9 15.2 %collective-permute-start.5 = (f32[13,8,512]{2,1,0:T(8,128)}, f32[13,8,512]{2,1,0:T(8,128)S(1)}, u32[]{:S(2)}, u32[]{:S(2)}) collective-permute-start(f32[13,8,512]{2,1,0:T(8,128)} %get-tuple-element.55), channel_id=1, source_target_pairs={{1,3},{3,1},{5,7},{7,5},{9,11},{11,9},{13,15},{15,13},{17,19},{19,... | collective-permute-start | bytes 638984 | tf_op jit(solution)/shard_map/ppermute | solution.py:620
  27.2 9.9 %collective-permute-start.2 = (f32[9,8,512]{2,1,0:T(8,128)S(1)}, f32[9,8,512]{2,1,0:T(8,128)S(1)}, u32[]{:S(2)}, u32[]{:S(2)}) collective-permute-start(f32[9,8,512]{2,1,0:T(8,128)S(1)} %get-tuple-element.52), channel_id=1, source_target_pairs={{2,4},{4,2},{6,8},{8,6},{10,12},{12,10},{3,5},{5,3},{7,9},{9,7},{1... | collective-permute-start | bytes 442376 | tf_op jit(solution)/shard_map/ppermute | solution.py:619
  29.8 10.4 %collective-permute-start.3 = (f32[9,8,512]{2,1,0:T(8,128)S(1)}, f32[9,8,512]{2,1,0:T(8,128)S(1)}, u32[]{:S(2)}, u32[]{:S(2)}) collective-permute-start(f32[9,8,512]{2,1,0:T(8,128)S(1)} %get-tuple-element.53), channel_id=1, source_target_pairs={{0,2},{2,0},{4,6},{6,4},{8,10},{10,8},{12,14},{14,12},{1,3},{3,1},... | collective-permute-start | bytes 442376 | tf_op jit(solution)/shard_map/ppermute | solution.py:620
  41.6 6.5 %collective-permute-start.6 = (f32[9,8,512]{2,1,0:T(8,128)S(1)}, f32[9,8,512]{2,1,0:T(8,128)S(1)}, u32[]{:S(2)}, u32[]{:S(2)}) collective-permute-start(f32[9,8,512]{2,1,0:T(8,128)S(1)} %get-tuple-element.59.m2), channel_id=1, source_target_pairs={{16,32},{32,16},{48,64},{64,48},{80,96},{96,80},{17,33},{33,17},{4... | collective-permute-start | bytes 442376 | tf_op jit(solution)/shard_map/ppermute | solution.py:619
  43.9 4.2 %collective-permute-start.7 = (f32[9,8,512]{2,1,0:T(8,128)S(1)}, f32[9,8,512]{2,1,0:T(8,128)S(1)}, u32[]{:S(2)}, u32[]{:S(2)}) collective-permute-start(f32[9,8,512]{2,1,0:T(8,128)S(1)} %get-tuple-element.60.m1), channel_id=1, source_target_pairs={{0,16},{16,0},{32,48},{48,32},{64,80},{80,64},{96,112},{112,96},{1... | collective-permute-start | bytes 442376 | tf_op jit(solution)/shard_map/ppermute | solution.py:620
  48.2 8.8 %collective-permute-start.8 = (f32[5,8,512]{2,1,0:T(8,128)S(1)}, f32[5,8,512]{2,1,0:T(8,128)S(1)}, u32[]{:S(2)}, u32[]{:S(2)}) collective-permute-start(f32[5,8,512]{2,1,0:T(8,128)S(1)} %get-tuple-element.61), channel_id=1, source_target_pairs={{2,4},{4,2},{6,8},{8,6},{10,12},{12,10},{3,5},{5,3},{7,9},{9,7},{1... | collective-permute-start | bytes 245768 | tf_op jit(solution)/shard_map/ppermute | solution.py:619
  52.7 6.0 %collective-permute-start.9 = (f32[5,8,512]{2,1,0:T(8,128)S(1)}, f32[5,8,512]{2,1,0:T(8,128)S(1)}, u32[]{:S(2)}, u32[]{:S(2)}) collective-permute-start(f32[5,8,512]{2,1,0:T(8,128)S(1)} %get-tuple-element.62), channel_id=1, source_target_pairs={{0,2},{2,0},{4,6},{6,4},{8,10},{10,8},{12,14},{14,12},{1,3},{3,1},... | collective-permute-start | bytes 245768 | tf_op jit(solution)/shard_map/ppermute | solution.py:620
  60.2 6.5 %collective-permute-start.10 = (f32[9,8,512]{2,1,0:T(8,128)S(1)}, f32[9,8,512]{2,1,0:T(8,128)S(1)}, u32[]{:S(2)}, u32[]{:S(2)}) collective-permute-start(f32[9,8,512]{2,1,0:T(8,128)S(1)} %get-tuple-element.64.m2), channel_id=1, source_target_pairs={{16,32},{32,16},{48,64},{64,48},{80,96},{96,80},{17,33},{33,17},{4... | collective-permute-start | bytes 442376 | tf_op jit(solution)/shard_map/ppermute | solution.py:619
  62.1 4.5 %collective-permute-start.11 = (f32[9,8,512]{2,1,0:T(8,128)S(1)}, f32[9,8,512]{2,1,0:T(8,128)S(1)}, u32[]{:S(2)}, u32[]{:S(2)}) collective-permute-start(f32[9,8,512]{2,1,0:T(8,128)S(1)} %get-tuple-element.65.m1), channel_id=1, source_target_pairs={{0,16},{16,0},{32,48},{48,32},{64,80},{80,64},{96,112},{112,96},{1... | collective-permute-start | bytes 442376 | tf_op jit(solution)/shard_map/ppermute | solution.py:620
  66.8 8.8 %collective-permute-start.12 = (f32[5,8,512]{2,1,0:T(8,128)S(1)}, f32[5,8,512]{2,1,0:T(8,128)S(1)}, u32[]{:S(2)}, u32[]{:S(2)}) collective-permute-start(f32[5,8,512]{2,1,0:T(8,128)S(1)} %get-tuple-element.66), channel_id=1, source_target_pairs={{2,4},{4,2},{6,8},{8,6},{10,12},{12,10},{3,5},{5,3},{7,9},{9,7},{1... | collective-permute-start | bytes 245768 | tf_op jit(solution)/shard_map/ppermute | solution.py:619
  71.3 6.0 %collective-permute-start.13 = (f32[5,8,512]{2,1,0:T(8,128)S(1)}, f32[5,8,512]{2,1,0:T(8,128)S(1)}, u32[]{:S(2)}, u32[]{:S(2)}) collective-permute-start(f32[5,8,512]{2,1,0:T(8,128)S(1)} %get-tuple-element.67), channel_id=1, source_target_pairs={{0,2},{2,0},{4,6},{6,4},{8,10},{10,8},{12,14},{14,12},{1,3},{3,1},... | collective-permute-start | bytes 245768 | tf_op jit(solution)/shard_map/ppermute | solution.py:620
  79.0 6.5 %collective-permute-start.14 = (f32[9,8,512]{2,1,0:T(8,128)S(1)}, f32[9,8,512]{2,1,0:T(8,128)S(1)}, u32[]{:S(2)}, u32[]{:S(2)}) collective-permute-start(f32[9,8,512]{2,1,0:T(8,128)S(1)} %get-tuple-element.69.m2), channel_id=1, source_target_pairs={{16,32},{32,16},{48,64},{64,48},{80,96},{96,80},{17,33},{33,17},{4... | collective-permute-start | bytes 442376 | tf_op jit(solution)/shard_map/ppermute | solution.py:619
  80.9 4.5 %collective-permute-start.15 = (f32[9,8,512]{2,1,0:T(8,128)S(1)}, f32[9,8,512]{2,1,0:T(8,128)S(1)}, u32[]{:S(2)}, u32[]{:S(2)}) collective-permute-start(f32[9,8,512]{2,1,0:T(8,128)S(1)} %get-tuple-element.70.m1), channel_id=1, source_target_pairs={{0,16},{16,0},{32,48},{48,32},{64,80},{80,64},{96,112},{112,96},{1... | collective-permute-start | bytes 442376 | tf_op jit(solution)/shard_map/ppermute | solution.py:620
  85.5 8.8 %collective-permute-start.16 = (f32[5,8,512]{2,1,0:T(8,128)S(1)}, f32[5,8,512]{2,1,0:T(8,128)S(1)}, u32[]{:S(2)}, u32[]{:S(2)}) collective-permute-start(f32[5,8,512]{2,1,0:T(8,128)S(1)} %get-tuple-element.71), channel_id=1, source_target_pairs={{2,4},{4,2},{6,8},{8,6},{10,12},{12,10},{3,5},{5,3},{7,9},{9,7},{1... | collective-permute-start | bytes 245768 | tf_op jit(solution)/shard_map/ppermute | solution.py:619
  90.0 6.0 %collective-permute-start.17 = (f32[5,8,512]{2,1,0:T(8,128)S(1)}, f32[5,8,512]{2,1,0:T(8,128)S(1)}, u32[]{:S(2)}, u32[]{:S(2)}) collective-permute-start(f32[5,8,512]{2,1,0:T(8,128)S(1)} %get-tuple-element.72), channel_id=1, source_target_pairs={{0,2},{2,0},{4,6},{6,4},{8,10},{10,8},{12,14},{14,12},{1,3},{3,1},... | collective-permute-start | bytes 245768 | tf_op jit(solution)/shard_map/ppermute | solution.py:620

commit v5 on v4

--- a/solution.py
+++ b/solution.py
@@ -278,7 +278,7 @@
     sub, lane = iotas(NZ)
     even = even_mask(NZ)
     tiles = {}
-    for t in range(VAL):
+    for t in range(m1.shape[0]):
         a, b = m1[t], m2[t]
         own = jnp.where(odd_x, a, b), jnp.where(odd_x, b, a)
         for start in (0, 6):
@@ -301,8 +301,11 @@
             if tile < 3:
                 sides.append(jnp.where(sub < 4, tiles[start, 2 * tile], tiles[start, 2 * tile + 1]))
             elif tile == 3:
-                firsts = jnp.where(sub % 2 == 0, tiles[start, T], tiles[start, T + 1])
-                sides.append(jnp.where(sub < 4, tiles[start, T - 1], firsts))
+                laid = tiles[start, T - 1]
+                if m1.shape[0] > T:
+                    firsts = jnp.where(sub % 2 == 0, tiles[start, T], tiles[start, T + 1])
+                    laid = jnp.where(sub < 4, laid, firsts)
+                sides.append(laid)
             else:
                 laid = tiles[start, "ring", 0]
                 for t in range(1, T):
@@ -405,57 +408,41 @@
     wait_for(copies[1:])
 
 
-def sweep_kernel(
-    last, weights, fields, sources, diagonal, inverse, x2, x1, za, ya, zb, yb, back, inflow, *rest
-):
-    r2, r1, y2, y1 = rest[:4] if len(rest) > 5 else (x2, x1, za, ya)
-    u0, u1 = rest[-2:]
-    place = Place()
-    section, odd_x, odd_y, exit_side = place.section, place.odd_x, place.odd_y, place.exit_side
+OWN, EDGE = slice(0, 8), slice(8, 16)
+
+
+class Halves:
+    def __init__(self, own, edge):
+        self.own, self.edge = own, edge
+
+    def __getitem__(self, at):
+        t, p, rows = at
+        return (self.own if rows is OWN else self.edge)[t, p]
+
+    def __setitem__(self, at, value):
+        t, p, rows = at
+        (self.own if rows is OWN else self.edge)[t, p] = value
+
+
+def steps(place, weights, sources, diagonal, inverse, x1, x2, ya, za, yb, zb, back, inflow, u0, u1, kept, put, partial=None, store=None):
+    odd_x, odd_y, exit_side = place.odd_x, place.odd_y, place.exit_side
     even, even_z = even_mask(NZ), even_mask(ZT)
     sub, lane = iotas(NZ)
-    sub_z, _ = iotas(ZT)
-    colours = (u0, u1)
-    own, edge = slice(0, 8), slice(8, 16)
-
-    for t in range(T):
-        for k in (0, 1):
-            u1[t, k + 1, own] = packed(fields[t, 2 * k], fields[t, 2 * k + 1], even, 1)
-            u0[t, k + 1, own] = packed(fields[t, 2 * k], fields[t, 2 * k + 1], even, 0)
-        for ref, tile, at, width in (
-            (u1, t, slice(0, NZ), NZ),
-            (u0, T + t // 4, slice(t % 4 * ZT, (t % 4 + 1) * ZT), ZT),
-        ):
-            low = jnp.where(odd_x == 1, r1[tile, :, at], r2[tile, :, at])
-            high = jnp.where(odd_x == 1, r2[tile, :, at], r1[tile, :, at])
-            ref[t, 0, own, :width] = low
-            ref[t, 3, own, :width] = high
-    own_rows, own_rows_z = (lax.broadcasted_iota(jnp.int32, (8, width), 0) for width in (NZ, ZT))
-
-    def beside(tile, rows, at):
-        first, second = y1[tile, rows, at], y2[tile, rows, at]
-        low, high = jnp.where(odd_y == 1, first, second), jnp.where(odd_y == 1, second, first)
-        return low, high
-
-    whole = slice(0, NZ)
-    for t in range(T):
-        low, high = beside(t // 2, slice(0, 8), whole)
-        for k in (0, 1):
-            base = 4 * (t % 2) + 2 * k
-            u1[t, k + 1, edge] = jnp.where(own_rows < 2, roll(high, -base, 0), roll(low, 6 - base, 0))
-            row, at = 4 + 2 * k + t // 4, slice(t % 4 * ZT, (t % 4 + 1) * ZT)
-            above, below = beside(3, slice(row, row + 1), at)
-            u0[t, k + 1, edge, :ZT] = jnp.where(own_rows_z < 4, below, above)
-        above, below = beside(4, slice(t, t + 1), whole)
-        corner = jnp.where(own_rows < 4, below, above)
-        u1[t, 0, edge] = corner
-        u1[t, 3, edge] = corner
-
-    @pl.when(exit_side)
-    def _():
-        for t in range(T):
-            u0[t, 3] = back[t]
-            u1[t, 3] = back[t]
+    own, edge = OWN, EDGE
+
+    zero = jnp.zeros((8, NZ), F32)
+    places = {(1, 0): 0, (2, 0): 1, "ring": 2}
+
+    def beyond_ring(t):
+        return jnp.where(even, u1[t, 0, edge], u1[t, 3, edge])
+
+    def finished(unit, t, weight):
+        beyond = beyond_ring(t) if unit == "ring" else u1[t, unit[0], edge]
+        halo = around(zero, beyond)
+        return partial[places[unit], t] + (halo if weight is None else weight * halo)
+
+    def from_partial(colour, unit):
+        return partial is not None and colour == 0 and unit in places
 
     def around(centre, beyond):
         up = roll(jnp.where(sub == 0, beyond, centre), -1, 0)
@@ -463,15 +450,16 @@
         return up + down
 
     def planes(colour, unit, t):
-        old, new = colours[colour], colours[1 - colour]
+        old, new = (kept, u1) if colour == 0 else (u1, u0)
         if unit == "ring":
             centre = jnp.where(even, new[t, 0, own], new[t, 3, own])
-            beyond = jnp.where(even, new[t, 0, edge], new[t, 3, edge])
+            beyond = zero if store is not None else beyond_ring(t)
             x_sum = jnp.where(even, new[t, 3, own] + new[t, 2, own], new[t, 0, own] + new[t, 1, own])
             return centre, beyond, x_sum, jnp.where(even, old[t, 3, own], old[t, 0, own])
         p, rows = unit
         here, other = (own, edge) if rows == 0 else (edge, own)
-        centre, beyond = new[t, p, here], new[t, p, other]
+        centre = new[t, p, here]
+        beyond = zero if store is not None else new[t, p, other]
         below, above = new[t, p - 1, here], new[t, p + 1, here]
         x_sum = centre + (jnp.where(even, below, above) if colour == 0 else jnp.where(even, above, below))
         return centre, beyond, x_sum, old[t, p, here]
@@ -482,7 +470,7 @@
             values = jnp.where(even_z, inflow[base + 48 : base + 56], inflow[base : base + 8])
         else:
             start = base + 16 * unit[0] + 8 * unit[1]
-            values = inflow[start : start + 8]
+            values = inflow[pl.ds(pl.multiple_of(start, 8), 8)]
         return jnp.concatenate([values] * (NZ // ZT), axis=1)
 
     ring_mask = (sub + lane + odd_x) % 2 == 0
@@ -512,14 +500,6 @@
             return of_edge(yb, zb, 0, index, p)
         return of_edge(ya, za, YVAL, index if kind == "source" else T + index, p)
 
-    def put(colour, unit, t, value):
-        ref = colours[colour]
-        if unit == "ring":
-            ref[t, 0, own] = value
-            ref[t, 3, own] = jnp.where(exit_side, back[t, own], value)
-        else:
-            ref[t, unit[0], own if unit[1] == 0 else edge] = value
-
     def valid(unit):
         if unit == "ring":
             return jnp.where(even, place.rows_x - 1 - place.x, place.x) > 0
@@ -530,14 +510,21 @@
     def turbine(colour, unit):
         driving = []
         for t in range(T):
+            weight = jnp.concatenate([jnp.broadcast_to(weights[t : t + 1], (8, ZT))] * (NZ // ZT), axis=1)
+            if from_partial(colour, unit):
+                driving.append(finished(unit, t, weight))
+                continue
             centre, beyond, x_sum, kept = planes(colour, unit, t)
             start = inflow_of(colour, unit) if t == 0 else kept
             ahead = jnp.where(lane == NZ - 1, 0.0, roll(centre, -1, 1))
             behind = jnp.where(lane == 0, start, roll(centre, 1, 1))
             total = x_sum + around(centre, beyond) + ahead + behind
             source = taken(colour, unit, "source", t)
-            weight = jnp.concatenate([jnp.broadcast_to(weights[t : t + 1], (8, ZT))] * (NZ // ZT), axis=1)
             driving.append(source + weight * total)
+            if store is not None:
+                store[places[unit], t] = driving[t]
+        if store is not None:
+            return
         for s in range(T):
             value = taken(colour, unit, "inverse", T * s) * driving[0]
             for t in range(1, T):
@@ -546,9 +533,20 @@
 
     def combustor(colour, unit):
         before = None
-        current = planes(colour, unit, 0)
+        started = from_partial(colour, unit)
+        current = None if started else planes(colour, unit, 0)
         flag = valid(unit)
+
+        def finish(t, total):
+            value = total / (6.0 + taken(colour, unit, "diagonal", t))
+            if flag is not None:
+                value = jnp.where(flag, value, 0.0)
+            put(colour, unit, t, value)
+
         for t in range(T):
+            if started:
+                finish(t, finished(unit, t, None))
+                continue
             after = planes(colour, unit, t + 1) if t + 1 < T else None
             centre, beyond, x_sum, _ = current
             edge_ahead = 0.0 if after is None else roll(after[0], -1, 1)
@@ -556,32 +554,131 @@
             ahead = jnp.where(lane == NZ - 1, edge_ahead, roll(centre, -1, 1))
             behind = jnp.where(lane == 0, edge_behind, roll(centre, 1, 1))
             total = x_sum + around(centre, beyond) + ahead + behind
-            source = taken(colour, unit, "source", t)
-            value = (source + total) / (6.0 + taken(colour, unit, "diagonal", t))
-            if flag is not None:
-                value = jnp.where(flag, value, 0.0)
-            put(colour, unit, t, value)
+            total = taken(colour, unit, "source", t) + total
+            if store is not None:
+                store[places[unit], t] = total
+            else:
+                finish(t, total)
             before, current = centre, after
 
-    def both(step):
-        for unit in ((1, 0), (2, 0), (1, 1), (2, 1), "ring"):
-            step(0, unit)
-        for unit in ((1, 0), (2, 0)):
-            step(1, unit)
-
-    pl.when(section == 0)(functools.partial(both, combustor))
-    pl.when(section != 0)(functools.partial(both, turbine))
-
-    out = rest[-3] if last else rest[-5]
+    return combustor, turbine
+
+
+def by_section(place, two, units):
+    def run(step):
+        for colour, unit in units:
+            step(colour, unit)
+
+    pl.when(place.section == 0)(functools.partial(run, two[0]))
+    pl.when(place.section != 0)(functools.partial(run, two[1]))
+
+
+FIRST_COLOUR = [(0, unit) for unit in ((1, 0), (2, 0), (1, 1), (2, 1), "ring")]
+
+
+def sweep_kernel(
+    begins, ends, weights, sources, diagonal, inverse, x2, x1, za, ya, zb, yb, back, inflow, *rest
+):
+    place = Place()
+    odd_x, odd_y, exit_side = place.odd_x, place.odd_y, place.exit_side
+    even = even_mask(NZ)
+    if begins:
+        fields, outs = rest[0], rest[1:]
+        r2, r1, y2, y1 = x2, x1, za, ya
+    else:
+        kept, near, partial, y2, y1, *outs = rest
+    if ends:
+        out, u0, u1, second = outs
+    else:
+        first_sent, second_sent, u0, u1 = outs
+    if begins:
+        kept, partial = u0, None
+    else:
+        u1 = Halves(near, u1)
+    own, edge = OWN, EDGE
+    own_rows, own_rows_z = (lax.broadcasted_iota(jnp.int32, (8, width), 0) for width in (NZ, ZT))
+
+    def beside(tile, rows, at):
+        first, second = y1[tile, rows, at], y2[tile, rows, at]
+        low, high = jnp.where(odd_y == 1, first, second), jnp.where(odd_y == 1, second, first)
+        return low, high
+
+    whole = slice(0, NZ)
+    for t in range(T):
+        if begins:
+            a, b = r1[t], r2[t]
+            u1[t, 0, own] = jnp.where(odd_x == 1, a, b)
+            u1[t, 3, own] = jnp.where(odd_x == 1, b, a)
+            for k in (0, 1):
+                u1[t, k + 1, own] = packed(fields[t, 2 * k], fields[t, 2 * k + 1], even, 1)
+                u0[t, k + 1, own] = packed(fields[t, 2 * k], fields[t, 2 * k + 1], even, 0)
+            tile, at = T + t // 4, slice(t % 4 * ZT, (t % 4 + 1) * ZT)
+            a, b = r1[tile, :, at], r2[tile, :, at]
+            u0[t, 0, own, :ZT] = jnp.where(odd_x == 1, a, b)
+            u0[t, 3, own, :ZT] = jnp.where(odd_x == 1, b, a)
+        low, high = beside(t // 2, slice(0, 8), whole)
+        for k in (0, 1):
+            base = 4 * (t % 2) + 2 * k
+            u1[t, k + 1, edge] = jnp.where(own_rows < 2, roll(high, -base, 0), roll(low, 6 - base, 0))
+            if begins:
+                row, at = 4 + 2 * k + t // 4, slice(t % 4 * ZT, (t % 4 + 1) * ZT)
+                above, below = beside(3, slice(row, row + 1), at)
+                u0[t, k + 1, edge, :ZT] = jnp.where(own_rows_z < 4, below, above)
+        above, below = beside(4, slice(t, t + 1), whole)
+        corner = jnp.where(own_rows < 4, below, above)
+        u1[t, 0, edge] = corner
+        u1[t, 3, edge] = corner
+
+    @pl.when(exit_side)
+    def _():
+        for t in range(T):
+            u1[t, 3, edge] = back[t, edge]
+            if begins:
+                u1[t, 3, own] = back[t, own]
+
+    pair_1, pair_2 = 2 - odd_x, 1 + odd_x
+
+    def put(colour, unit, t, value):
+        if unit == "ring":
+            u0[t, 0, own] = value
+            u0[t, 3, own] = jnp.where(exit_side, back[t, own], value)
+        elif colour == 1 and ends:
+            second[t, unit[0] - 1] = value
+        elif colour == 1:
+            (first_sent if unit[0] is pair_1 else second_sent)[t] = value
+        else:
+            (u0, u1)[colour][t, unit[0], own if unit[1] == 0 else edge] = value
+
+    two = steps(place, weights, sources, diagonal, inverse, x1, x2, ya, za, yb, zb, back, inflow, u0, u1, kept, put, partial)
+    by_section(place, two, FIRST_COLOUR)
+    if not ends:
+        by_section(place, two, [(1, (pair_2, 0)), (1, (pair_1, 0))])
+        return
+    by_section(place, two, [(1, (1, 0)), (1, (2, 0))])
     for t in range(T):
         for k in (0, 1):
-            a, b = u0[t, k + 1, own], u1[t, k + 1, own]
+            a, b = u0[t, k + 1, own], second[t, k]
             out[t, 2 * k] = jnp.where(even, a, b)
             out[t, 2 * k + 1] = jnp.where(even, b, a)
-    if last:
-        return
-    for ref, pair in ((rest[-4], 2 - odd_x), (rest[-3], 1 + odd_x)):
-        store_message(ref, lambda t: u1[t, pair, own], lambda t: u0[t, pair, own, :ZT])
+
+
+def sums_kernel(weights, sources, diagonal, inverse, x2, x1, back, inflow, m1, m2, kept, r2, r1, near, sums):
+    place = Place()
+    odd_x, exit_side = place.odd_x, place.exit_side
+    for t in range(T):
+        for low, high, below, above in ((r2[t], r1[t], 0, 3), (m2[t], m1[t], 1, 2)):
+            near[t, below] = jnp.where(odd_x == 1, high, low)
+            near[t, above] = jnp.where(odd_x == 1, low, high)
+
+    @pl.when(exit_side)
+    def _():
+        for t in range(T):
+            near[t, 3] = back[t, OWN]
+
+    ones = Halves(near, None)
+    none = [None] * 4
+    two = steps(place, weights, sources, diagonal, inverse, x1, x2, *none, back, inflow, None, ones, kept, None, None, sums)
+    by_section(place, two, [(0, (1, 0)), (0, (2, 0)), (0, "ring")])
 
 
 def shape(*dims):
@@ -609,15 +706,25 @@
     return HBM, pltpu.with_memory_space_constraint(array, pltpu.HBM)
 
 
+def swap(axis, pairs, array, turbine_only):
+    if turbine_only:
+        pairs = [(2 * i + 1, 2 * j + 1) for i, j in pairs]
+        axis = (axis, "sa")
+    return lax.ppermute(array, axis, pairs)
+
+
+def inner_swap(axis, array, turbine_only=False):
+    return swap(axis, [(i, i ^ 1) for i in range(lax.axis_size(axis))], array, turbine_only)
+
+
+def outer_swap(axis, array, turbine_only=False):
+    pairs = [(i, (i + 1 ^ 1) - 1) for i in range(1, lax.axis_size(axis) - 1)]
+    return swap(axis, pairs, array, turbine_only)
+
+
 def swaps(axis, first, second, turbine_only=False):
-    peers = lax.axis_size(axis)
-    inner = [(i, i ^ 1) for i in range(peers)]
-    outer = [(i, (i + 1 ^ 1) - 1) for i in range(1, peers - 1)]
-    if turbine_only:
-        inner, outer = ([(2 * i + 1, 2 * j + 1) for i, j in pairs] for pairs in (inner, outer))
-        axis = (axis, "sa")
-    second = lax.ppermute(second, axis, outer)
-    return lax.ppermute(first, axis, inner), second
+    second = outer_swap(axis, second, turbine_only)
+    return inner_swap(axis, first, turbine_only), second
 
 
 def chosen_places(tile):
@@ -685,25 +792,35 @@
     )
     back, inflow, weights, values, source, diagonal, block_inverse = made
 
+    coefficients = [weights, source, diagonal, block_inverse]
+    given = [*coefficients, x2, x1, za, ya, zb, yb, back, inflow]
+    block, half = pltpu.VMEM((T, 4, 16, NZ), F32), pltpu.VMEM((T, 4, 8, NZ), F32)
+    state = [values]
     for sweep in range(SWEEPS):
-        received = []
-        if sweep > 0:
-            r1, r2 = swaps("gx", m1, m2)
-            y1, y2 = call(
-                corner_kernel, [shape(YVAL, 8, NZ)] * 2, [(VMEM, array) for array in (m1, m2, r2, r1)]
-            )
-            received = [r2, r1, *swaps("gy", y1, y2)[::-1]]
-        last = sweep == SWEEPS - 1
+        begins, ends = sweep == 0, sweep == SWEEPS - 1
         results = call(
-            functools.partial(sweep_kernel, last),
-            [shape(T, CX, CY, NZ)] + [shape(VAL, 8, NZ)] * (0 if last else 2),
-            [(VMEM, array) for array in (weights, values, source, diagonal, block_inverse)]
-            + [(VMEM, array) for array in (x2, x1, za, ya, zb, yb, back, inflow, *received)],
-            scratch=[pltpu.VMEM((T, 4, 16, NZ), F32)] * 2,
+            functools.partial(sweep_kernel, begins, ends),
+            [shape(T, CX, CY, NZ)] if ends else [shape(T, 8, NZ)] * 2 + [shape(*block.shape)],
+            [(VMEM, array) for array in (*given, *state)],
+            scratch=([block] if ends else [])
+            + [block if begins else half]
+            + ([pltpu.VMEM((T, 2, 8, NZ), F32)] if ends else []),
             limit=40,
         )
-        values, m1, m2 = results if not last else (results[0], None, None)
-    return values[None]
+        if ends:
+            break
+        m1, m2, u0 = results
+        r1, r2 = swaps("gx", m1, m2)
+        y1, y2 = call(corner_kernel, [shape(YVAL, 8, NZ)] * 2, [(VMEM, array) for array in (m1, m2, r2, r1)])
+        y1, y2 = swaps("gy", y1, y2)
+        near, sums = call(
+            sums_kernel,
+            [shape(*half.shape), shape(3, T, 8, NZ)],
+            [(VMEM, array) for array in (*coefficients, x2, x1, back, inflow, m1, m2, u0, r2, r1)],
+            limit=40,
+        )
+        state = [u0, near, sums, y2, y1]
+    return results[0][None]
 
 
 def solution(mesh):

time: 99 us -> 98.2 us (level)
  starting transfers between devices: 58.3 us -> 54.2 us
  waiting for transfers between devices: 24.6 us -> 27.8 us
    ppermute x18, starting transfers between devices: 47 us -> 42.9 us  [swap(): return lax.ppermute(array, axis, pairs)]
    ppermute x18, waiting for transfers between devices: 24.6 us -> 27.8 us  [swap(): return lax.ppermute(array, axis, pairs)]
    pallas_call x10 -> x13, Pallas kernels: 15.2 us -> 15.6 us  [call(): pl.pallas_call(kernel, out_shape=outs, in_specs=[spec for spec, _ in oper...]
  transfers between devices with their start and end apart: 19 -> 19, of which waited for: 11 -> 11; matrix products, arithmetic and copies ran while one was open for 0% -> 0% of each run, Pallas kernels for 5% -> 6%
where the time goes in v5:
time: 98.2 us; the launch traced here: 97.8 us
  starting transfers between devices  54.2 us (55%)
  waiting for transfers between devices  27.8 us (28%)
  Pallas kernels  15.6 us (16%)
    ppermute x18, starting transfers between devices, swap(): return lax.ppermute(array, axis, pairs)  42.9 us
    ppermute x18, waiting for transfers between devices, swap(): return lax.ppermute(array, axis, pairs)  27.8 us
    pallas_call x13, Pallas kernels, call(): pl.pallas_call(kernel, out_shape=outs, in_specs=[spec for spec, _ in oper...  15.6 us
    all_to_all x1, starting transfers between devices, shards(): lax.all_to_all(payload.reshape(2 * cells, 1, CHUNK * ZT), ('sa', 'gx', 'g...  11.3 us
  transfers between devices with their start and end apart: 19, of which 11 were waited for; matrix products, arithmetic and copies ran while one was open for 0% of the time, Pallas kernels for 6%

profile of v5, /device:TPU:42, one launch (start us, length us, event | category | flops | bytes accessed | tf_op | source)
XLA Modules:
  0.0 97.8 jit_solution(1598130755699387791)
XLA Ops:
  0.0 3.6 %shard_map.73 = (f32[37,8,512]{2,1,0:T(8,128)}, f32[37,8,512]{2,1,0:T(8,128)}, f32[13,8,512]{2,1,0:T(8,128)}, f32[13,8,512]{2,1,0:T(8,128)}, f32[4,8,512]{2,1,0:...) custom-call(s32[3,64]{1,0:T(4,128)} %bitcast.29, s32[1,896]{1,0:T(1,128)} %returns_far.3, f32[7,4,8,512]{3,2,1,0:T(8,128)} %bitcast.23, ...), custom_call_target="tpu_custom_call" | custom-call | tf_op jit(solution)/shard_map/pallas_call | solution.py:695
  3.6 0.1 collective-permute-start
  3.7 2.4 %collective-permute-start.1 = (f32[37,8,512]{2,1,0:T(8,128)}, f32[37,8,512]{2,1,0:T(8,128)S(1)}, u32[]{:S(2)}, u32[]{:S(2)}) collective-permute-start(f32[37,8,512]{2,1,0:T(8,128)} %get-tuple-element.47.m2), channel_id=1, source_target_pairs={{16,32},{32,16},{48,64},{64,48},{80,96},{96,80},{17,33},{33,17},{4... | collective-permute-start | bytes 1818632 | tf_op jit(solution)/shard_map/ppermute | solution.py:713
  6.1 11.3 %all-to-all-start = ((f32[128,1,256]{2,1,0:T(1,128)}), f32[128,1,256]{2,1,0:T(1,128)S(1)}, u32[]{:S(2)}, u32[]{:S(2)}) async-start(f32[128,1,256]{2,1,0:T(1,128)} %bitcast.28), calls=%async_computation | async-start | bytes 262144 | tf_op jit(solution)/shard_map/all_to_all | solution.py:774
  17.4 4.5 %collective-permute-start.4 = (f32[13,8,512]{2,1,0:T(8,128)}, f32[13,8,512]{2,1,0:T(8,128)S(1)}, u32[]{:S(2)}, u32[]{:S(2)}) collective-permute-start(f32[13,8,512]{2,1,0:T(8,128)} %get-tuple-element.59), channel_id=1, source_target_pairs={{3,5},{5,3},{7,9},{9,7},{11,13},{13,11},{19,21},{21,19},{23,25},{2... | collective-permute-start | bytes 638984 | tf_op jit(solution)/shard_map/ppermute | solution.py:713
  21.9 3.8 %collective-permute-start.5 = (f32[13,8,512]{2,1,0:T(8,128)}, f32[13,8,512]{2,1,0:T(8,128)S(1)}, u32[]{:S(2)}, u32[]{:S(2)}) collective-permute-start(f32[13,8,512]{2,1,0:T(8,128)} %get-tuple-element.60), channel_id=1, source_target_pairs={{1,3},{3,1},{5,7},{7,5},{9,11},{11,9},{13,15},{15,13},{17,19},{19,... | collective-permute-start | bytes 638984 | tf_op jit(solution)/shard_map/ppermute | solution.py:713
  25.7 0.0 all-to-all-done
  25.7 0.0 collective-permute-done.r1.x1
  25.7 0.0 collective-permute-done.1.r2.x2
  25.7 1.4 %shard_map.75 = (f32[9,8,512]{2,1,0:T(8,128)S(1)}, f32[9,8,512]{2,1,0:T(8,128)S(1)}) custom-call(f32[37,8,512]{2,1,0:T(8,128)} %get-tuple-element.46.m1, f32[37,8,512]{2,1,0:T(8,128)} %get-tuple-element.47.m2, f32[37,8,512]{2,1,0:T(8,128)S(1)} %collective-permute-done.1.r2.x2, f32[37,8,512]{2,1,0:T(8,128)S(1)} %collective-permute-done.r1.x1, ...), custom_call_target="tpu_custom_call" | custom-call | tf_op jit(solution)/shard_map/pallas_call | solution.py:695
  27.2 2.6 %collective-permute-start.2 = (f32[9,8,512]{2,1,0:T(8,128)S(1)}, f32[9,8,512]{2,1,0:T(8,128)S(1)}, u32[]{:S(2)}, u32[]{:S(2)}) collective-permute-start(f32[9,8,512]{2,1,0:T(8,128)S(1)} %get-tuple-element.57), channel_id=1, source_target_pairs={{2,4},{4,2},{6,8},{8,6},{10,12},{12,10},{3,5},{5,3},{7,9},{9,7},{1... | collective-permute-start | bytes 442376 | tf_op jit(solution)/shard_map/ppermute | solution.py:713
  29.8 3.5 %collective-permute-start.3 = (f32[9,8,512]{2,1,0:T(8,128)S(1)}, f32[9,8,512]{2,1,0:T(8,128)S(1)}, u32[]{:S(2)}, u32[]{:S(2)}) collective-permute-start(f32[9,8,512]{2,1,0:T(8,128)S(1)} %get-tuple-element.58), channel_id=1, source_target_pairs={{0,2},{2,0},{4,6},{6,4},{8,10},{10,8},{12,14},{14,12},{1,3},{3,1},... | collective-permute-start | bytes 442376 | tf_op jit(solution)/shard_map/ppermute | solution.py:713
  33.3 3.1 %shard_map.74 = (f32[7,16,512]{2,1,0:T(8,128)S(1)}, f32[128,128]{1,0:T(8,128)S(1)}, f32[8,128]{1,0:T(8,128)S(1)}, f32[7,4,8,512]{3,2,1,0:T(8,128)S(1)}, f32[7,4,...) custom-call(f32[256,128]{1,0:T(8,128)S(1)} %bitcast.21, f32[7]{0:T(128)} %coupling.1, ...), custom_call_target="tpu_custom_call" | custom-call | tf_op jit(solution)/shard_map/pallas_call | solution.py:695
  36.4 0.0 collective-permute-done.4.zb
  36.4 0.7 collective-permute-done.5.yb
  37.1 0.0 collective-permute-done.2.za
  37.1 3.1 %collective-permute-done.3.ya = f32[9,8,512]{2,1,0:T(8,128)S(1)} collective-permute-done((f32[9,8,512]{2,1,0:T(8,128)S(1)}, f32[9,8,512]{2,1,0:T(8,128)S(1)}, u32[]{:S(2)}, u32[]{:S(2)}) %collective-permute-start.3) | collective-permute-done | bytes 147488 | tf_op jit(solution)/shard_map/ppermute | solution.py:713
  40.1 1.5 %shard_map.76 = (f32[7,8,512]{2,1,0:T(8,128)S(1)}, f32[7,8,512]{2,1,0:T(8,128)S(1)}, f32[7,4,16,512]{3,2,1,0:T(8,128)S(1)}) custom-call(f32[8,128]{1,0:T(8,128)S(1)} %get-tuple-element.49.weights, f32[7,4,8,512]{3,2,1,0:T(8,128)S(1)} %get-tuple-element.50.sources, f32[7,4,8,512]{3,2,1,0:T(8,128)S(1)} %get-tuple-element.51.diagonal, ...), custom_call_target="tpu_custom_call" | custom-call | tf_op jit(solution)/shard_map/pallas_call | solution.py:695
  41.7 0.1 collective-permute-start.7
  41.8 2.6 %collective-permute-start.6 = (f32[7,8,512]{2,1,0:T(8,128)S(1)}, f32[7,8,512]{2,1,0:T(8,128)S(1)}, u32[]{:S(2)}, u32[]{:S(2)}) collective-permute-start(f32[7,8,512]{2,1,0:T(8,128)S(1)} %get-tuple-element.66.m2), channel_id=1, source_target_pairs={{16,32},{32,16},{48,64},{64,48},{80,96},{96,80},{17,33},{33,17},{4... | collective-permute-start | bytes 344072 | tf_op jit(solution)/shard_map/ppermute | solution.py:713
  44.4 0.0 collective-permute-done.7.r1
  44.5 3.4 %collective-permute-done.6.r2 = f32[7,8,512]{2,1,0:T(8,128)S(1)} collective-permute-done((f32[7,8,512]{2,1,0:T(8,128)S(1)}, f32[7,8,512]{2,1,0:T(8,128)S(1)}, u32[]{:S(2)}, u32[]{:S(2)}) %collective-permute-start.6) | collective-permute-done | bytes 114720 | tf_op jit(solution)/shard_map/ppermute | solution.py:713
  47.9 0.1 shard_map.78
  48.0 4.5 %collective-permute-start.8 = (f32[5,8,512]{2,1,0:T(8,128)S(1)}, f32[5,8,512]{2,1,0:T(8,128)S(1)}, u32[]{:S(2)}, u32[]{:S(2)}) collective-permute-start(f32[5,8,512]{2,1,0:T(8,128)S(1)} %get-tuple-element.69), channel_id=1, source_target_pairs={{2,4},{4,2},{6,8},{8,6},{10,12},{12,10},{3,5},{5,3},{7,9},{9,7},{1... | collective-permute-start | bytes 245768 | tf_op jit(solution)/shard_map/ppermute | solution.py:713
  52.5 1.9 %collective-permute-start.9 = (f32[5,8,512]{2,1,0:T(8,128)S(1)}, f32[5,8,512]{2,1,0:T(8,128)S(1)}, u32[]{:S(2)}, u32[]{:S(2)}) collective-permute-start(f32[5,8,512]{2,1,0:T(8,128)S(1)} %get-tuple-element.70), channel_id=1, source_target_pairs={{0,2},{2,0},{4,6},{6,4},{8,10},{10,8},{12,14},{14,12},{1,3},{3,1},... | collective-permute-start | bytes 245768 | tf_op jit(solution)/shard_map/ppermute | solution.py:713
  54.4 0.3 shard_map.77
  54.7 2.4 %collective-permute-done.8.rest_3_ = f32[5,8,512]{2,1,0:T(8,128)S(1)} collective-permute-done((f32[5,8,512]{2,1,0:T(8,128)S(1)}, f32[5,8,512]{2,1,0:T(8,128)S(1)}, u32[]{:S(2)}, u32[]{:S(2)}) %collective-permute-start.8) | collective-permute-done | bytes 81952 | tf_op jit(solution)/shard_map/ppermute | solution.py:713
  57.1 1.7 %collective-permute-done.9.rest_4_ = f32[5,8,512]{2,1,0:T(8,128)S(1)} collective-permute-done((f32[5,8,512]{2,1,0:T(8,128)S(1)}, f32[5,8,512]{2,1,0:T(8,128)S(1)}, u32[]{:S(2)}, u32[]{:S(2)}) %collective-permute-start.9) | collective-permute-done | bytes 81952 | tf_op jit(solution)/shard_map/ppermute | solution.py:713
  58.9 1.3 %shard_map.79 = (f32[7,8,512]{2,1,0:T(8,128)S(1)}, f32[7,8,512]{2,1,0:T(8,128)S(1)}, f32[7,4,16,512]{3,2,1,0:T(8,128)S(1)}) custom-call(f32[8,128]{1,0:T(8,128)S(1)} %get-tuple-element.49.weights, f32[7,4,8,512]{3,2,1,0:T(8,128)S(1)} %get-tuple-element.50.sources, f32[7,4,8,512]{3,2,1,0:T(8,128)S(1)} %get-tuple-element.51.diagonal, ...), custom_call_target="tpu_custom_call" | custom-call | tf_op jit(solution)/shard_map/pallas_call | solution.py:695
  60.1 0.1 collective-permute-start.11
  60.2 1.9 %collective-permute-start.10 = (f32[7,8,512]{2,1,0:T(8,128)S(1)}, f32[7,8,512]{2,1,0:T(8,128)S(1)}, u32[]{:S(2)}, u32[]{:S(2)}) collective-permute-start(f32[7,8,512]{2,1,0:T(8,128)S(1)} %get-tuple-element.73.m2), channel_id=1, source_target_pairs={{16,32},{32,16},{48,64},{64,48},{80,96},{96,80},{17,33},{33,17},{4... | collective-permute-start | bytes 344072 | tf_op jit(solution)/shard_map/ppermute | solution.py:713
  62.2 0.0 collective-permute-done.11.r1
  62.2 4.2 %collective-permute-done.10.r2 = f32[7,8,512]{2,1,0:T(8,128)S(1)} collective-permute-done((f32[7,8,512]{2,1,0:T(8,128)S(1)}, f32[7,8,512]{2,1,0:T(8,128)S(1)}, u32[]{:S(2)}, u32[]{:S(2)}) %collective-permute-start.10) | collective-permute-done | bytes 114720 | tf_op jit(solution)/shard_map/ppermute | solution.py:713
  66.4 0.1 shard_map.81
  66.4 4.5 %collective-permute-start.12 = (f32[5,8,512]{2,1,0:T(8,128)S(1)}, f32[5,8,512]{2,1,0:T(8,128)S(1)}, u32[]{:S(2)}, u32[]{:S(2)}) collective-permute-start(f32[5,8,512]{2,1,0:T(8,128)S(1)} %get-tuple-element.76), channel_id=1, source_target_pairs={{2,4},{4,2},{6,8},{8,6},{10,12},{12,10},{3,5},{5,3},{7,9},{9,7},{1... | collective-permute-start | bytes 245768 | tf_op jit(solution)/shard_map/ppermute | solution.py:713
  70.9 1.9 %collective-permute-start.13 = (f32[5,8,512]{2,1,0:T(8,128)S(1)}, f32[5,8,512]{2,1,0:T(8,128)S(1)}, u32[]{:S(2)}, u32[]{:S(2)}) collective-permute-start(f32[5,8,512]{2,1,0:T(8,128)S(1)} %get-tuple-element.77), channel_id=1, source_target_pairs={{0,2},{2,0},{4,6},{6,4},{8,10},{10,8},{12,14},{14,12},{1,3},{3,1},... | collective-permute-start | bytes 245768 | tf_op jit(solution)/shard_map/ppermute | solution.py:713
  72.8 0.5 shard_map.80
  73.4 2.2 %collective-permute-done.12.rest_3_ = f32[5,8,512]{2,1,0:T(8,128)S(1)} collective-permute-done((f32[5,8,512]{2,1,0:T(8,128)S(1)}, f32[5,8,512]{2,1,0:T(8,128)S(1)}, u32[]{:S(2)}, u32[]{:S(2)}) %collective-permute-start.12) | collective-permute-done | bytes 81952 | tf_op jit(solution)/shard_map/ppermute | solution.py:713
  75.6 1.7 %collective-permute-done.13.rest_4_ = f32[5,8,512]{2,1,0:T(8,128)S(1)} collective-permute-done((f32[5,8,512]{2,1,0:T(8,128)S(1)}, f32[5,8,512]{2,1,0:T(8,128)S(1)}, u32[]{:S(2)}, u32[]{:S(2)}) %collective-permute-start.13) | collective-permute-done | bytes 81952 | tf_op jit(solution)/shard_map/ppermute | solution.py:713
  77.3 1.3 %shard_map.82 = (f32[7,8,512]{2,1,0:T(8,128)S(1)}, f32[7,8,512]{2,1,0:T(8,128)S(1)}, f32[7,4,16,512]{3,2,1,0:T(8,128)S(1)}) custom-call(f32[8,128]{1,0:T(8,128)S(1)} %get-tuple-element.49.weights, f32[7,4,8,512]{3,2,1,0:T(8,128)S(1)} %get-tuple-element.50.sources, f32[7,4,8,512]{3,2,1,0:T(8,128)S(1)} %get-tuple-element.51.diagonal, ...), custom_call_target="tpu_custom_call" | custom-call | tf_op jit(solution)/shard_map/pallas_call | solution.py:695
  78.6 0.1 collective-permute-start.15
  78.7 1.9 %collective-permute-start.14 = (f32[7,8,512]{2,1,0:T(8,128)S(1)}, f32[7,8,512]{2,1,0:T(8,128)S(1)}, u32[]{:S(2)}, u32[]{:S(2)}) collective-permute-start(f32[7,8,512]{2,1,0:T(8,128)S(1)} %get-tuple-element.80.m2), channel_id=1, source_target_pairs={{16,32},{32,16},{48,64},{64,48},{80,96},{96,80},{17,33},{33,17},{4... | collective-permute-start | bytes 344072 | tf_op jit(solution)/shard_map/ppermute | solution.py:713
  80.6 0.0 collective-permute-done.15.r1
  80.6 4.2 %collective-permute-done.14.r2 = f32[7,8,512]{2,1,0:T(8,128)S(1)} collective-permute-done((f32[7,8,512]{2,1,0:T(8,128)S(1)}, f32[7,8,512]{2,1,0:T(8,128)S(1)}, u32[]{:S(2)}, u32[]{:S(2)}) %collective-permute-start.14) | collective-permute-done | bytes 114720 | tf_op jit(solution)/shard_map/ppermute | solution.py:713
  84.8 0.1 shard_map.84
  84.9 4.5 %collective-permute-start.16 = (f32[5,8,512]{2,1,0:T(8,128)S(1)}, f32[5,8,512]{2,1,0:T(8,128)S(1)}, u32[]{:S(2)}, u32[]{:S(2)}) collective-permute-start(f32[5,8,512]{2,1,0:T(8,128)S(1)} %get-tuple-element.83), channel_id=1, source_target_pairs={{2,4},{4,2},{6,8},{8,6},{10,12},{12,10},{3,5},{5,3},{7,9},{9,7},{1... | collective-permute-start | bytes 245768 | tf_op jit(solution)/shard_map/ppermute | solution.py:713
  89.4 1.9 %collective-permute-start.17 = (f32[5,8,512]{2,1,0:T(8,128)S(1)}, f32[5,8,512]{2,1,0:T(8,128)S(1)}, u32[]{:S(2)}, u32[]{:S(2)}) collective-permute-start(f32[5,8,512]{2,1,0:T(8,128)S(1)} %get-tuple-element.84), channel_id=1, source_target_pairs={{0,2},{2,0},{4,6},{6,4},{8,10},{10,8},{12,14},{14,12},{1,3},{3,1},... | collective-permute-start | bytes 245768 | tf_op jit(solution)/shard_map/ppermute | solution.py:713
  91.3 0.3 shard_map.83
  91.6 2.4 %collective-permute-done.16.rest_3_ = f32[5,8,512]{2,1,0:T(8,128)S(1)} collective-permute-done((f32[5,8,512]{2,1,0:T(8,128)S(1)}, f32[5,8,512]{2,1,0:T(8,128)S(1)}, u32[]{:S(2)}, u32[]{:S(2)}) %collective-permute-start.16) | collective-permute-done | bytes 81952 | tf_op jit(solution)/shard_map/ppermute | solution.py:713
  94.0 1.7 %collective-permute-done.17.rest_4_ = f32[5,8,512]{2,1,0:T(8,128)S(1)} collective-permute-done((f32[5,8,512]{2,1,0:T(8,128)S(1)}, f32[5,8,512]{2,1,0:T(8,128)S(1)}, u32[]{:S(2)}, u32[]{:S(2)}) %collective-permute-start.17) | collective-permute-done | bytes 81952 | tf_op jit(solution)/shard_map/ppermute | solution.py:713
  95.8 2.0 %shard_map.85 = f32[7,4,8,512]{3,2,1,0:T(8,128)} custom-call(f32[8,128]{1,0:T(8,128)S(1)} %get-tuple-element.49.weights, f32[7,4,8,512]{3,2,1,0:T(8,128)S(1)} %get-tuple-element.50.sources, f32[7,4,8,512]{3,2,1,0:T(8,128)S(1)} %get-tuple-element.51.diagonal, f32[7,7,4,8,512]{4,3,2,1,0:T(8,128)S(1)} %get-tuple-element.52.inverse, ...), custom_call_target="tpu_custom_call" | custom-call | tf_op jit(solution)/shard_map/pallas_call | solution.py:695
Async XLA Ops:
  3.6 22.1 %collective-permute-start = (f32[37,8,512]{2,1,0:T(8,128)}, f32[37,8,512]{2,1,0:T(8,128)S(1)}, u32[]{:S(2)}, u32[]{:S(2)}) collective-permute-start(f32[37,8,512]{2,1,0:T(8,128)} %get-tuple-element.46.m1), channel_id=1, source_target_pairs={{0,16},{16,0},{32,48},{48,32},{64,80},{80,64},{96,112},{112,96},{1... | collective-permute-start | bytes 1818632 | tf_op jit(solution)/shard_map/ppermute | solution.py:713
  3.7 22.0 %collective-permute-start.1 = (f32[37,8,512]{2,1,0:T(8,128)}, f32[37,8,512]{2,1,0:T(8,128)S(1)}, u32[]{:S(2)}, u32[]{:S(2)}) collective-permute-start(f32[37,8,512]{2,1,0:T(8,128)} %get-tuple-element.47.m2), channel_id=1, source_target_pairs={{16,32},{32,16},{48,64},{64,48},{80,96},{96,80},{17,33},{33,17},{4... | collective-permute-start | bytes 1818632 | tf_op jit(solution)/shard_map/ppermute | solution.py:713
  6.1 19.6 %all-to-all-start = ((f32[128,1,256]{2,1,0:T(1,128)}), f32[128,1,256]{2,1,0:T(1,128)S(1)}, u32[]{:S(2)}, u32[]{:S(2)}) async-start(f32[128,1,256]{2,1,0:T(1,128)} %bitcast.28), calls=%async_computation | async-start | bytes 262144 | tf_op jit(solution)/shard_map/all_to_all | solution.py:774
  17.4 19.0 %collective-permute-start.4 = (f32[13,8,512]{2,1,0:T(8,128)}, f32[13,8,512]{2,1,0:T(8,128)S(1)}, u32[]{:S(2)}, u32[]{:S(2)}) collective-permute-start(f32[13,8,512]{2,1,0:T(8,128)} %get-tuple-element.59), channel_id=1, source_target_pairs={{3,5},{5,3},{7,9},{9,7},{11,13},{13,11},{19,21},{21,19},{23,25},{2... | collective-permute-start | bytes 638984 | tf_op jit(solution)/shard_map/ppermute | solution.py:713
  21.9 15.2 %collective-permute-start.5 = (f32[13,8,512]{2,1,0:T(8,128)}, f32[13,8,512]{2,1,0:T(8,128)S(1)}, u32[]{:S(2)}, u32[]{:S(2)}) collective-permute-start(f32[13,8,512]{2,1,0:T(8,128)} %get-tuple-element.60), channel_id=1, source_target_pairs={{1,3},{3,1},{5,7},{7,5},{9,11},{11,9},{13,15},{15,13},{17,19},{19,... | collective-permute-start | bytes 638984 | tf_op jit(solution)/shard_map/ppermute | solution.py:713
  27.2 9.9 %collective-permute-start.2 = (f32[9,8,512]{2,1,0:T(8,128)S(1)}, f32[9,8,512]{2,1,0:T(8,128)S(1)}, u32[]{:S(2)}, u32[]{:S(2)}) collective-permute-start(f32[9,8,512]{2,1,0:T(8,128)S(1)} %get-tuple-element.57), channel_id=1, source_target_pairs={{2,4},{4,2},{6,8},{8,6},{10,12},{12,10},{3,5},{5,3},{7,9},{9,7},{1... | collective-permute-start | bytes 442376 | tf_op jit(solution)/shard_map/ppermute | solution.py:713
  29.8 10.4 %collective-permute-start.3 = (f32[9,8,512]{2,1,0:T(8,128)S(1)}, f32[9,8,512]{2,1,0:T(8,128)S(1)}, u32[]{:S(2)}, u32[]{:S(2)}) collective-permute-start(f32[9,8,512]{2,1,0:T(8,128)S(1)} %get-tuple-element.58), channel_id=1, source_target_pairs={{0,2},{2,0},{4,6},{6,4},{8,10},{10,8},{12,14},{14,12},{1,3},{3,1},... | collective-permute-start | bytes 442376 | tf_op jit(solution)/shard_map/ppermute | solution.py:713
  41.7 2.7 %collective-permute-start.7 = (f32[7,8,512]{2,1,0:T(8,128)S(1)}, f32[7,8,512]{2,1,0:T(8,128)S(1)}, u32[]{:S(2)}, u32[]{:S(2)}) collective-permute-start(f32[7,8,512]{2,1,0:T(8,128)S(1)} %get-tuple-element.65.m1), channel_id=1, source_target_pairs={{0,16},{16,0},{32,48},{48,32},{64,80},{80,64},{96,112},{112,96},{1... | collective-permute-start | bytes 344072 | tf_op jit(solution)/shard_map/ppermute | solution.py:713
  41.8 6.1 %collective-permute-start.6 = (f32[7,8,512]{2,1,0:T(8,128)S(1)}, f32[7,8,512]{2,1,0:T(8,128)S(1)}, u32[]{:S(2)}, u32[]{:S(2)}) collective-permute-start(f32[7,8,512]{2,1,0:T(8,128)S(1)} %get-tuple-element.66.m2), channel_id=1, source_target_pairs={{16,32},{32,16},{48,64},{64,48},{80,96},{96,80},{17,33},{33,17},{4... | collective-permute-start | bytes 344072 | tf_op jit(solution)/shard_map/ppermute | solution.py:713
  48.0 9.2 %collective-permute-start.8 = (f32[5,8,512]{2,1,0:T(8,128)S(1)}, f32[5,8,512]{2,1,0:T(8,128)S(1)}, u32[]{:S(2)}, u32[]{:S(2)}) collective-permute-start(f32[5,8,512]{2,1,0:T(8,128)S(1)} %get-tuple-element.69), channel_id=1, source_target_pairs={{2,4},{4,2},{6,8},{8,6},{10,12},{12,10},{3,5},{5,3},{7,9},{9,7},{1... | collective-permute-start | bytes 245768 | tf_op jit(solution)/shard_map/ppermute | solution.py:713
  52.5 6.4 %collective-permute-start.9 = (f32[5,8,512]{2,1,0:T(8,128)S(1)}, f32[5,8,512]{2,1,0:T(8,128)S(1)}, u32[]{:S(2)}, u32[]{:S(2)}) collective-permute-start(f32[5,8,512]{2,1,0:T(8,128)S(1)} %get-tuple-element.70), channel_id=1, source_target_pairs={{0,2},{2,0},{4,6},{6,4},{8,10},{10,8},{12,14},{14,12},{1,3},{3,1},... | collective-permute-start | bytes 245768 | tf_op jit(solution)/shard_map/ppermute | solution.py:713
  60.1 2.0 %collective-permute-start.11 = (f32[7,8,512]{2,1,0:T(8,128)S(1)}, f32[7,8,512]{2,1,0:T(8,128)S(1)}, u32[]{:S(2)}, u32[]{:S(2)}) collective-permute-start(f32[7,8,512]{2,1,0:T(8,128)S(1)} %get-tuple-element.72.m1), channel_id=1, source_target_pairs={{0,16},{16,0},{32,48},{48,32},{64,80},{80,64},{96,112},{112,96},{1... | collective-permute-start | bytes 344072 | tf_op jit(solution)/shard_map/ppermute | solution.py:713
  60.2 6.1 %collective-permute-start.10 = (f32[7,8,512]{2,1,0:T(8,128)S(1)}, f32[7,8,512]{2,1,0:T(8,128)S(1)}, u32[]{:S(2)}, u32[]{:S(2)}) collective-permute-start(f32[7,8,512]{2,1,0:T(8,128)S(1)} %get-tuple-element.73.m2), channel_id=1, source_target_pairs={{16,32},{32,16},{48,64},{64,48},{80,96},{96,80},{17,33},{33,17},{4... | collective-permute-start | bytes 344072 | tf_op jit(solution)/shard_map/ppermute | solution.py:713
  66.4 9.2 %collective-permute-start.12 = (f32[5,8,512]{2,1,0:T(8,128)S(1)}, f32[5,8,512]{2,1,0:T(8,128)S(1)}, u32[]{:S(2)}, u32[]{:S(2)}) collective-permute-start(f32[5,8,512]{2,1,0:T(8,128)S(1)} %get-tuple-element.76), channel_id=1, source_target_pairs={{2,4},{4,2},{6,8},{8,6},{10,12},{12,10},{3,5},{5,3},{7,9},{9,7},{1... | collective-permute-start | bytes 245768 | tf_op jit(solution)/shard_map/ppermute | solution.py:713
  70.9 6.4 %collective-permute-start.13 = (f32[5,8,512]{2,1,0:T(8,128)S(1)}, f32[5,8,512]{2,1,0:T(8,128)S(1)}, u32[]{:S(2)}, u32[]{:S(2)}) collective-permute-start(f32[5,8,512]{2,1,0:T(8,128)S(1)} %get-tuple-element.77), channel_id=1, source_target_pairs={{0,2},{2,0},{4,6},{6,4},{8,10},{10,8},{12,14},{14,12},{1,3},{3,1},... | collective-permute-start | bytes 245768 | tf_op jit(solution)/shard_map/ppermute | solution.py:713
  78.6 2.0 %collective-permute-start.15 = (f32[7,8,512]{2,1,0:T(8,128)S(1)}, f32[7,8,512]{2,1,0:T(8,128)S(1)}, u32[]{:S(2)}, u32[]{:S(2)}) collective-permute-start(f32[7,8,512]{2,1,0:T(8,128)S(1)} %get-tuple-element.79.m1), channel_id=1, source_target_pairs={{0,16},{16,0},{32,48},{48,32},{64,80},{80,64},{96,112},{112,96},{1... | collective-permute-start | bytes 344072 | tf_op jit(solution)/shard_map/ppermute | solution.py:713
  78.7 6.1 %collective-permute-start.14 = (f32[7,8,512]{2,1,0:T(8,128)S(1)}, f32[7,8,512]{2,1,0:T(8,128)S(1)}, u32[]{:S(2)}, u32[]{:S(2)}) collective-permute-start(f32[7,8,512]{2,1,0:T(8,128)S(1)} %get-tuple-element.80.m2), channel_id=1, source_target_pairs={{16,32},{32,16},{48,64},{64,48},{80,96},{96,80},{17,33},{33,17},{4... | collective-permute-start | bytes 344072 | tf_op jit(solution)/shard_map/ppermute | solution.py:713
  84.9 9.2 %collective-permute-start.16 = (f32[5,8,512]{2,1,0:T(8,128)S(1)}, f32[5,8,512]{2,1,0:T(8,128)S(1)}, u32[]{:S(2)}, u32[]{:S(2)}) collective-permute-start(f32[5,8,512]{2,1,0:T(8,128)S(1)} %get-tuple-element.83), channel_id=1, source_target_pairs={{2,4},{4,2},{6,8},{8,6},{10,12},{12,10},{3,5},{5,3},{7,9},{9,7},{1... | collective-permute-start | bytes 245768 | tf_op jit(solution)/shard_map/ppermute | solution.py:713
  89.4 6.4 %collective-permute-start.17 = (f32[5,8,512]{2,1,0:T(8,128)S(1)}, f32[5,8,512]{2,1,0:T(8,128)S(1)}, u32[]{:S(2)}, u32[]{:S(2)}) collective-permute-start(f32[5,8,512]{2,1,0:T(8,128)S(1)} %get-tuple-element.84), channel_id=1, source_target_pairs={{0,2},{2,0},{4,6},{6,4},{8,10},{10,8},{12,14},{14,12},{1,3},{3,1},... | collective-permute-start | bytes 245768 | tf_op jit(solution)/shard_map/ppermute | solution.py:713

commit v6 on v5

--- a/solution.py
+++ b/solution.py
@@ -330,11 +330,35 @@
     corner_values(*[heads.at[n] for n in range(4)], y1, y2)
 
 
-def interface_kernel(blocks, coupling, returns_far, *refs):
-    count = (len(refs) - 5) // 2
-    back, inflow, weights = refs[count : count + 3]
-    returns, sems = refs[-2:]
-    pairs = [(returns_far, returns), *zip(refs[:count], refs[count + 3 : -2])]
+def interface_kernel(
+    blocks,
+    coupling,
+    x2,
+    x1,
+    returns_far,
+    fields_far,
+    sources_far,
+    diagonal_far,
+    inverse_far,
+    back,
+    inflow,
+    weights,
+    fields,
+    sources,
+    diagonal,
+    chosen,
+    ring,
+    returns,
+    inverse,
+    sems,
+):
+    pairs = [
+        (returns_far, returns),
+        (inverse_far, inverse),
+        (fields_far, fields),
+        (sources_far, sources),
+        (diagonal_far, diagonal),
+    ]
     copies = [pltpu.make_async_copy(far, near, sems.at[n]) for n, (far, near) in enumerate(pairs)]
     for copy in copies:
         copy.start()
@@ -405,7 +429,22 @@
                 back[t, 8:9, at] = laid[8 * T + t : 8 * T + t + 1]
                 back[t, 15:16, at] = laid[8 * T + 8 + t : 8 * T + 9 + t]
 
-    wait_for(copies[1:])
+    even = even_mask(NZ)
+    wide, long = iotas(NZ)
+    ring_mask = (wide + long + place.odd_x) % 2 == 0
+    for index in range(COEF):
+        tile = VAL + index // 2
+        if index % 2 == 0:
+            ring[index] = jnp.where(ring_mask, x1[tile], x2[tile])
+        else:
+            ring[index] = roll(jnp.where(ring_mask, x2[tile], x1[tile]), -1, 0)
+    copies[1].wait()
+    for index in range(T * T):
+        for k in (0, 1):
+            a, b = (inverse[index // T, index % T, 2 * k + n] for n in (0, 1))
+            chosen[0, index, k] = packed(a, b, even, 0)
+            chosen[1, index, k] = packed(a, b, even, 1)
+    wait_for(copies[2:])
 
 
 OWN, EDGE = slice(0, 8), slice(8, 16)
@@ -424,7 +463,7 @@
         (self.own if rows is OWN else self.edge)[t, p] = value
 
 
-def steps(place, weights, sources, diagonal, inverse, x1, x2, ya, za, yb, zb, back, inflow, u0, u1, kept, put, partial=None, store=None):
+def steps(place, weights, sources, diagonal, inverse, ring, ya, za, yb, zb, back, inflow, u0, u1, kept, put, partial=None, store=None):
     odd_x, odd_y, exit_side = place.odd_x, place.odd_y, place.exit_side
     even, even_z = even_mask(NZ), even_mask(ZT)
     sub, lane = iotas(NZ)
@@ -473,14 +512,7 @@
             values = inflow[pl.ds(pl.multiple_of(start, 8), 8)]
         return jnp.concatenate([values] * (NZ // ZT), axis=1)
 
-    ring_mask = (sub + lane + odd_x) % 2 == 0
     edge_mask = jnp.where(sub == 7, 1, 0) == odd_y
-
-    def of_ring(index):
-        tile = VAL + index // 2
-        if index % 2 == 0:
-            return jnp.where(ring_mask, x1[tile], x2[tile])
-        return roll(jnp.where(ring_mask, x2[tile], x1[tile]), -1, 0)
 
     def of_edge(first, second, tile, index, p):
         tile, row = tile + index // 4, 4 * (index % 2) + 2 * (p - 1) + index % 4 // 2
@@ -488,13 +520,12 @@
 
     def taken(colour, unit, kind, index):
         if unit == "ring":
-            return of_ring(T * T + index if kind == "source" else index)
+            return ring[T * T + index if kind == "source" else index]
         p, rows = unit
         if rows == 0:
             if kind == "inverse":
-                raw = inverse.at[index // T, index % T]
-            else:
-                raw = (sources if kind == "source" else diagonal).at[index]
+                return inverse[colour, index, p - 1]
+            raw = (sources if kind == "source" else diagonal).at[index]
             return packed(raw[2 * p - 2], raw[2 * p - 1], even, colour)
         if kind == "inverse":
             return of_edge(yb, zb, 0, index, p)
@@ -577,14 +608,14 @@
 
 
 def sweep_kernel(
-    begins, ends, weights, sources, diagonal, inverse, x2, x1, za, ya, zb, yb, back, inflow, *rest
+    begins, ends, weights, sources, diagonal, inverse, ring, za, ya, zb, yb, back, inflow, *rest
 ):
     place = Place()
     odd_x, odd_y, exit_side = place.odd_x, place.odd_y, place.exit_side
     even = even_mask(NZ)
     if begins:
-        fields, outs = rest[0], rest[1:]
-        r2, r1, y2, y1 = x2, x1, za, ya
+        fields, r2, r1, *outs = rest
+        y2, y1 = za, ya
     else:
         kept, near, partial, y2, y1, *outs = rest
     if ends:
@@ -649,7 +680,7 @@
         else:
             (u0, u1)[colour][t, unit[0], own if unit[1] == 0 else edge] = value
 
-    two = steps(place, weights, sources, diagonal, inverse, x1, x2, ya, za, yb, zb, back, inflow, u0, u1, kept, put, partial)
+    two = steps(place, weights, sources, diagonal, inverse, ring, ya, za, yb, zb, back, inflow, u0, u1, kept, put, partial)
     by_section(place, two, FIRST_COLOUR)
     if not ends:
         by_section(place, two, [(1, (pair_2, 0)), (1, (pair_1, 0))])
@@ -662,7 +693,7 @@
             out[t, 2 * k + 1] = jnp.where(even, b, a)
 
 
-def sums_kernel(weights, sources, diagonal, inverse, x2, x1, back, inflow, m1, m2, kept, r2, r1, near, sums):
+def sums_kernel(weights, sources, diagonal, inverse, ring, back, inflow, m1, m2, kept, r2, r1, near, sums):
     place = Place()
     odd_x, exit_side = place.odd_x, place.exit_side
     for t in range(T):
@@ -677,7 +708,7 @@
 
     ones = Halves(near, None)
     none = [None] * 4
-    two = steps(place, weights, sources, diagonal, inverse, x1, x2, *none, back, inflow, None, ones, kept, None, None, sums)
+    two = steps(place, weights, sources, diagonal, inverse, ring, *none, back, inflow, None, ones, kept, None, None, sums)
     by_section(place, two, [(0, (1, 0)), (0, (2, 0)), (0, "ring")])
 
 
@@ -785,17 +816,23 @@
     distant = (values, source, diagonal, block_inverse)
     made = call(
         interface_kernel,
-        [shape(T, 16, NZ), shape(128, ZT), shape(8, ZT)] + [pltpu.VMEM(array.shape, array.dtype) for array in distant],
-        [(VMEM, arrived), (SMEM, pltpu.with_memory_space_constraint(coupling, pltpu.HBM)), far(returns)]
-        + [far(array) for array in distant],
-        scratch=[pltpu.VMEM(returns.shape, returns.dtype), pltpu.SemaphoreType.DMA((len(distant) + 1,))],
+        [shape(T, 16, NZ), shape(128, ZT), shape(8, ZT)]
+        + [pltpu.VMEM(array.shape, F32) for array in distant[:3]]
+        + [pltpu.VMEM((2, T * T, 2, 8, NZ), F32), pltpu.VMEM((COEF, 8, NZ), F32)],
+        [(VMEM, arrived), (SMEM, pltpu.with_memory_space_constraint(coupling, pltpu.HBM)), (VMEM, x2), (VMEM, x1)]
+        + [far(array) for array in (returns, *distant)],
+        scratch=[
+            pltpu.VMEM(returns.shape, returns.dtype),
+            pltpu.VMEM(block_inverse.shape, F32),
+            pltpu.SemaphoreType.DMA((5,)),
+        ],
     )
-    back, inflow, weights, values, source, diagonal, block_inverse = made
-
-    coefficients = [weights, source, diagonal, block_inverse]
-    given = [*coefficients, x2, x1, za, ya, zb, yb, back, inflow]
+    back, inflow, weights, values, source, diagonal, inverse, ring = made
+
+    coefficients = [weights, source, diagonal, inverse, ring]
+    given = [*coefficients, za, ya, zb, yb, back, inflow]
     block, half = pltpu.VMEM((T, 4, 16, NZ), F32), pltpu.VMEM((T, 4, 8, NZ), F32)
-    state = [values]
+    state = [values, x2, x1]
     for sweep in range(SWEEPS):
         begins, ends = sweep == 0, sweep == SWEEPS - 1
         results = call(
@@ -816,7 +853,7 @@
         near, sums = call(
             sums_kernel,
             [shape(*half.shape), shape(3, T, 8, NZ)],
-            [(VMEM, array) for array in (*coefficients, x2, x1, back, inflow, m1, m2, u0, r2, r1)],
+            [(VMEM, array) for array in (*coefficients, back, inflow, m1, m2, u0, r2, r1)],
             limit=40,
         )
         state = [u0, near, sums, y2, y1]

time: 98.2 us -> 97.2 us (0.990)
  Pallas kernels: 15.6 us -> 14.4 us
    pallas_call x13, Pallas kernels: 15.6 us -> 14.4 us  [call(): pl.pallas_call(kernel, out_shape=outs, in_specs=[spec for spec, _ in oper...]
where the time goes in v6:
time: 97.2 us; the launch traced here: 96.8 us
  starting transfers between devices  54.2 us (56%)
  waiting for transfers between devices  27.9 us (29%)
  Pallas kernels  14.4 us (15%)
    ppermute x18, starting transfers between devices, swap(): return lax.ppermute(array, axis, pairs)  42.9 us
    ppermute x18, waiting for transfers between devices, swap(): return lax.ppermute(array, axis, pairs)  27.9 us
    pallas_call x13, Pallas kernels, call(): pl.pallas_call(kernel, out_shape=outs, in_specs=[spec for spec, _ in oper...  14.4 us
    all_to_all x1, starting transfers between devices, shards(): lax.all_to_all(payload.reshape(2 * cells, 1, CHUNK * ZT), ('sa', 'gx', 'g...  11.3 us
  transfers between devices with their start and end apart: 19, of which 11 were waited for; matrix products, arithmetic and copies ran while one was open for 0% of the time, Pallas kernels for 6%

profile of v6, /device:TPU:42, one launch (start us, length us, event | category | flops | bytes accessed | tf_op | source)
XLA Modules:
  0.0 96.8 jit_solution(6941343954930609365)
XLA Ops:
  0.0 3.6 %shard_map.73 = (f32[37,8,512]{2,1,0:T(8,128)}, f32[37,8,512]{2,1,0:T(8,128)}, f32[13,8,512]{2,1,0:T(8,128)}, f32[13,8,512]{2,1,0:T(8,128)}, f32[4,8,512]{2,1,0:...) custom-call(s32[3,64]{1,0:T(4,128)} %bitcast.29, s32[1,896]{1,0:T(1,128)} %returns_far.3, f32[7,4,8,512]{3,2,1,0:T(8,128)} %bitcast.23, ...), custom_call_target="tpu_custom_call" | custom-call | tf_op jit(solution)/shard_map/pallas_call | solution.py:726
  3.6 0.1 collective-permute-start
  3.7 2.4 %collective-permute-start.1 = (f32[37,8,512]{2,1,0:T(8,128)}, f32[37,8,512]{2,1,0:T(8,128)S(1)}, u32[]{:S(2)}, u32[]{:S(2)}) collective-permute-start(f32[37,8,512]{2,1,0:T(8,128)} %get-tuple-element.48.m2), channel_id=1, source_target_pairs={{16,32},{32,16},{48,64},{64,48},{80,96},{96,80},{17,33},{33,17},{4... | collective-permute-start | bytes 1818632 | tf_op jit(solution)/shard_map/ppermute | solution.py:744
  6.1 11.3 %all-to-all-start = ((f32[128,1,256]{2,1,0:T(1,128)}), f32[128,1,256]{2,1,0:T(1,128)S(1)}, u32[]{:S(2)}, u32[]{:S(2)}) async-start(f32[128,1,256]{2,1,0:T(1,128)} %bitcast.28), calls=%async_computation | async-start | bytes 262144 | tf_op jit(solution)/shard_map/all_to_all | solution.py:805
  17.4 4.5 %collective-permute-start.4 = (f32[13,8,512]{2,1,0:T(8,128)}, f32[13,8,512]{2,1,0:T(8,128)S(1)}, u32[]{:S(2)}, u32[]{:S(2)}) collective-permute-start(f32[13,8,512]{2,1,0:T(8,128)} %get-tuple-element.61), channel_id=1, source_target_pairs={{3,5},{5,3},{7,9},{9,7},{11,13},{13,11},{19,21},{21,19},{23,25},{2... | collective-permute-start | bytes 638984 | tf_op jit(solution)/shard_map/ppermute | solution.py:744
  21.9 3.8 %collective-permute-start.5 = (f32[13,8,512]{2,1,0:T(8,128)}, f32[13,8,512]{2,1,0:T(8,128)S(1)}, u32[]{:S(2)}, u32[]{:S(2)}) collective-permute-start(f32[13,8,512]{2,1,0:T(8,128)} %get-tuple-element.62), channel_id=1, source_target_pairs={{1,3},{3,1},{5,7},{7,5},{9,11},{11,9},{13,15},{15,13},{17,19},{19,... | collective-permute-start | bytes 638984 | tf_op jit(solution)/shard_map/ppermute | solution.py:744
  25.7 0.0 all-to-all-done
  25.7 0.0 collective-permute-done.x1.r1.rest_2_
  25.7 0.0 collective-permute-done.1.x2.r2.rest_1_
  25.7 1.4 %shard_map.75 = (f32[9,8,512]{2,1,0:T(8,128)S(1)}, f32[9,8,512]{2,1,0:T(8,128)S(1)}) custom-call(f32[37,8,512]{2,1,0:T(8,128)} %get-tuple-element.47.m1, f32[37,8,512]{2,1,0:T(8,128)} %get-tuple-element.48.m2, f32[37,8,512]{2,1,0:T(8,128)S(1)} %collective-permute-done.1.x2.r2.rest_1_, f32[37,8,512]{2,1,0:T(8,128)S(1)} %collective-permute-done.x1.r1.rest_2_, ...), custom_call_target="tpu_custom_call" | custom-call | tf_op jit(solution)/shard_map/pallas_call | solution.py:726
  27.2 2.6 %collective-permute-start.2 = (f32[9,8,512]{2,1,0:T(8,128)S(1)}, f32[9,8,512]{2,1,0:T(8,128)S(1)}, u32[]{:S(2)}, u32[]{:S(2)}) collective-permute-start(f32[9,8,512]{2,1,0:T(8,128)S(1)} %get-tuple-element.59), channel_id=1, source_target_pairs={{2,4},{4,2},{6,8},{8,6},{10,12},{12,10},{3,5},{5,3},{7,9},{9,7},{1... | collective-permute-start | bytes 442376 | tf_op jit(solution)/shard_map/ppermute | solution.py:744
  29.8 3.5 %collective-permute-start.3 = (f32[9,8,512]{2,1,0:T(8,128)S(1)}, f32[9,8,512]{2,1,0:T(8,128)S(1)}, u32[]{:S(2)}, u32[]{:S(2)}) collective-permute-start(f32[9,8,512]{2,1,0:T(8,128)S(1)} %get-tuple-element.60), channel_id=1, source_target_pairs={{0,2},{2,0},{4,6},{6,4},{8,10},{10,8},{12,14},{14,12},{1,3},{3,1},... | collective-permute-start | bytes 442376 | tf_op jit(solution)/shard_map/ppermute | solution.py:744
  33.3 3.0 %shard_map.74 = (f32[7,16,512]{2,1,0:T(8,128)S(1)}, f32[128,128]{1,0:T(8,128)S(1)}, f32[8,128]{1,0:T(8,128)S(1)}, f32[7,4,8,512]{3,2,1,0:T(8,128)S(1)}, f32[7,4,...) custom-call(f32[256,128]{1,0:T(8,128)S(1)} %bitcast.21, ...), custom_call_target="tpu_custom_call" | custom-call | tf_op jit(solution)/shard_map/pallas_call | solution.py:726
  36.3 0.0 collective-permute-done.4.zb
  36.3 0.8 collective-permute-done.5.yb
  37.1 0.0 collective-permute-done.2.za
  37.1 3.1 %collective-permute-done.3.ya = f32[9,8,512]{2,1,0:T(8,128)S(1)} collective-permute-done((f32[9,8,512]{2,1,0:T(8,128)S(1)}, f32[9,8,512]{2,1,0:T(8,128)S(1)}, u32[]{:S(2)}, u32[]{:S(2)}) %collective-permute-start.3) | collective-permute-done | bytes 147488 | tf_op jit(solution)/shard_map/ppermute | solution.py:744
  40.1 1.2 %shard_map.76 = (f32[7,8,512]{2,1,0:T(8,128)S(1)}, f32[7,8,512]{2,1,0:T(8,128)S(1)}, f32[7,4,16,512]{3,2,1,0:T(8,128)S(1)}) custom-call(f32[8,128]{1,0:T(8,128)S(1)} %get-tuple-element.52.weights, f32[7,4,8,512]{3,2,1,0:T(8,128)S(1)} %get-tuple-element.53.sources, f32[7,4,8,512]{3,2,1,0:T(8,128)S(1)} %get-tuple-element.54.diagonal, ...), custom_call_target="tpu_custom_call" | custom-call | tf_op jit(solution)/shard_map/pallas_call | solution.py:726
  41.4 0.1 collective-permute-start.7
  41.5 2.6 %collective-permute-start.6 = (f32[7,8,512]{2,1,0:T(8,128)S(1)}, f32[7,8,512]{2,1,0:T(8,128)S(1)}, u32[]{:S(2)}, u32[]{:S(2)}) collective-permute-start(f32[7,8,512]{2,1,0:T(8,128)S(1)} %get-tuple-element.68.m2), channel_id=1, source_target_pairs={{16,32},{32,16},{48,64},{64,48},{80,96},{96,80},{17,33},{33,17},{4... | collective-permute-start | bytes 344072 | tf_op jit(solution)/shard_map/ppermute | solution.py:744
  44.1 0.0 collective-permute-done.7.r1
  44.1 3.4 %collective-permute-done.6.r2 = f32[7,8,512]{2,1,0:T(8,128)S(1)} collective-permute-done((f32[7,8,512]{2,1,0:T(8,128)S(1)}, f32[7,8,512]{2,1,0:T(8,128)S(1)}, u32[]{:S(2)}, u32[]{:S(2)}) %collective-permute-start.6) | collective-permute-done | bytes 114720 | tf_op jit(solution)/shard_map/ppermute | solution.py:744
  47.6 0.1 shard_map.78
  47.7 4.5 %collective-permute-start.8 = (f32[5,8,512]{2,1,0:T(8,128)S(1)}, f32[5,8,512]{2,1,0:T(8,128)S(1)}, u32[]{:S(2)}, u32[]{:S(2)}) collective-permute-start(f32[5,8,512]{2,1,0:T(8,128)S(1)} %get-tuple-element.71), channel_id=1, source_target_pairs={{2,4},{4,2},{6,8},{8,6},{10,12},{12,10},{3,5},{5,3},{7,9},{9,7},{1... | collective-permute-start | bytes 245768 | tf_op jit(solution)/shard_map/ppermute | solution.py:744
  52.1 1.9 %collective-permute-start.9 = (f32[5,8,512]{2,1,0:T(8,128)S(1)}, f32[5,8,512]{2,1,0:T(8,128)S(1)}, u32[]{:S(2)}, u32[]{:S(2)}) collective-permute-start(f32[5,8,512]{2,1,0:T(8,128)S(1)} %get-tuple-element.72), channel_id=1, source_target_pairs={{0,2},{2,0},{4,6},{6,4},{8,10},{10,8},{12,14},{14,12},{1,3},{3,1},... | collective-permute-start | bytes 245768 | tf_op jit(solution)/shard_map/ppermute | solution.py:744
  54.1 0.3 shard_map.77
  54.4 2.4 %collective-permute-done.8.rest_3_ = f32[5,8,512]{2,1,0:T(8,128)S(1)} collective-permute-done((f32[5,8,512]{2,1,0:T(8,128)S(1)}, f32[5,8,512]{2,1,0:T(8,128)S(1)}, u32[]{:S(2)}, u32[]{:S(2)}) %collective-permute-start.8) | collective-permute-done | bytes 81952 | tf_op jit(solution)/shard_map/ppermute | solution.py:744
  56.8 1.7 %collective-permute-done.9.rest_4_ = f32[5,8,512]{2,1,0:T(8,128)S(1)} collective-permute-done((f32[5,8,512]{2,1,0:T(8,128)S(1)}, f32[5,8,512]{2,1,0:T(8,128)S(1)}, u32[]{:S(2)}, u32[]{:S(2)}) %collective-permute-start.9) | collective-permute-done | bytes 81952 | tf_op jit(solution)/shard_map/ppermute | solution.py:744
  58.6 1.0 %shard_map.79 = (f32[7,8,512]{2,1,0:T(8,128)S(1)}, f32[7,8,512]{2,1,0:T(8,128)S(1)}, f32[7,4,16,512]{3,2,1,0:T(8,128)S(1)}) custom-call(f32[8,128]{1,0:T(8,128)S(1)} %get-tuple-element.52.weights, f32[7,4,8,512]{3,2,1,0:T(8,128)S(1)} %get-tuple-element.53.sources, f32[7,4,8,512]{3,2,1,0:T(8,128)S(1)} %get-tuple-element.54.diagonal, ...), custom_call_target="tpu_custom_call" | custom-call | tf_op jit(solution)/shard_map/pallas_call | solution.py:726
  59.6 0.1 collective-permute-start.11
  59.7 1.9 %collective-permute-start.10 = (f32[7,8,512]{2,1,0:T(8,128)S(1)}, f32[7,8,512]{2,1,0:T(8,128)S(1)}, u32[]{:S(2)}, u32[]{:S(2)}) collective-permute-start(f32[7,8,512]{2,1,0:T(8,128)S(1)} %get-tuple-element.75.m2), channel_id=1, source_target_pairs={{16,32},{32,16},{48,64},{64,48},{80,96},{96,80},{17,33},{33,17},{4... | collective-permute-start | bytes 344072 | tf_op jit(solution)/shard_map/ppermute | solution.py:744
  61.6 0.0 collective-permute-done.11.r1
  61.6 4.2 %collective-permute-done.10.r2 = f32[7,8,512]{2,1,0:T(8,128)S(1)} collective-permute-done((f32[7,8,512]{2,1,0:T(8,128)S(1)}, f32[7,8,512]{2,1,0:T(8,128)S(1)}, u32[]{:S(2)}, u32[]{:S(2)}) %collective-permute-start.10) | collective-permute-done | bytes 114720 | tf_op jit(solution)/shard_map/ppermute | solution.py:744
  65.8 0.1 shard_map.81
  65.9 4.5 %collective-permute-start.12 = (f32[5,8,512]{2,1,0:T(8,128)S(1)}, f32[5,8,512]{2,1,0:T(8,128)S(1)}, u32[]{:S(2)}, u32[]{:S(2)}) collective-permute-start(f32[5,8,512]{2,1,0:T(8,128)S(1)} %get-tuple-element.78), channel_id=1, source_target_pairs={{2,4},{4,2},{6,8},{8,6},{10,12},{12,10},{3,5},{5,3},{7,9},{9,7},{1... | collective-permute-start | bytes 245768 | tf_op jit(solution)/shard_map/ppermute | solution.py:744
  70.4 1.9 %collective-permute-start.13 = (f32[5,8,512]{2,1,0:T(8,128)S(1)}, f32[5,8,512]{2,1,0:T(8,128)S(1)}, u32[]{:S(2)}, u32[]{:S(2)}) collective-permute-start(f32[5,8,512]{2,1,0:T(8,128)S(1)} %get-tuple-element.79), channel_id=1, source_target_pairs={{0,2},{2,0},{4,6},{6,4},{8,10},{10,8},{12,14},{14,12},{1,3},{3,1},... | collective-permute-start | bytes 245768 | tf_op jit(solution)/shard_map/ppermute | solution.py:744
  72.3 0.5 shard_map.80
  72.8 2.2 %collective-permute-done.12.rest_3_ = f32[5,8,512]{2,1,0:T(8,128)S(1)} collective-permute-done((f32[5,8,512]{2,1,0:T(8,128)S(1)}, f32[5,8,512]{2,1,0:T(8,128)S(1)}, u32[]{:S(2)}, u32[]{:S(2)}) %collective-permute-start.12) | collective-permute-done | bytes 81952 | tf_op jit(solution)/shard_map/ppermute | solution.py:744
  75.0 1.7 %collective-permute-done.13.rest_4_ = f32[5,8,512]{2,1,0:T(8,128)S(1)} collective-permute-done((f32[5,8,512]{2,1,0:T(8,128)S(1)}, f32[5,8,512]{2,1,0:T(8,128)S(1)}, u32[]{:S(2)}, u32[]{:S(2)}) %collective-permute-start.13) | collective-permute-done | bytes 81952 | tf_op jit(solution)/shard_map/ppermute | solution.py:744
  76.7 1.0 %shard_map.82 = (f32[7,8,512]{2,1,0:T(8,128)S(1)}, f32[7,8,512]{2,1,0:T(8,128)S(1)}, f32[7,4,16,512]{3,2,1,0:T(8,128)S(1)}) custom-call(f32[8,128]{1,0:T(8,128)S(1)} %get-tuple-element.52.weights, f32[7,4,8,512]{3,2,1,0:T(8,128)S(1)} %get-tuple-element.53.sources, f32[7,4,8,512]{3,2,1,0:T(8,128)S(1)} %get-tuple-element.54.diagonal, ...), custom_call_target="tpu_custom_call" | custom-call | tf_op jit(solution)/shard_map/pallas_call | solution.py:726
  77.8 0.1 collective-permute-start.15
  77.9 1.9 %collective-permute-start.14 = (f32[7,8,512]{2,1,0:T(8,128)S(1)}, f32[7,8,512]{2,1,0:T(8,128)S(1)}, u32[]{:S(2)}, u32[]{:S(2)}) collective-permute-start(f32[7,8,512]{2,1,0:T(8,128)S(1)} %get-tuple-element.82.m2), channel_id=1, source_target_pairs={{16,32},{32,16},{48,64},{64,48},{80,96},{96,80},{17,33},{33,17},{4... | collective-permute-start | bytes 344072 | tf_op jit(solution)/shard_map/ppermute | solution.py:744
  79.8 0.0 collective-permute-done.15.r1
  79.8 4.2 %collective-permute-done.14.r2 = f32[7,8,512]{2,1,0:T(8,128)S(1)} collective-permute-done((f32[7,8,512]{2,1,0:T(8,128)S(1)}, f32[7,8,512]{2,1,0:T(8,128)S(1)}, u32[]{:S(2)}, u32[]{:S(2)}) %collective-permute-start.14) | collective-permute-done | bytes 114720 | tf_op jit(solution)/shard_map/ppermute | solution.py:744
  84.0 0.1 shard_map.84
  84.0 4.5 %collective-permute-start.16 = (f32[5,8,512]{2,1,0:T(8,128)S(1)}, f32[5,8,512]{2,1,0:T(8,128)S(1)}, u32[]{:S(2)}, u32[]{:S(2)}) collective-permute-start(f32[5,8,512]{2,1,0:T(8,128)S(1)} %get-tuple-element.85), channel_id=1, source_target_pairs={{2,4},{4,2},{6,8},{8,6},{10,12},{12,10},{3,5},{5,3},{7,9},{9,7},{1... | collective-permute-start | bytes 245768 | tf_op jit(solution)/shard_map/ppermute | solution.py:744
  88.5 1.9 %collective-permute-start.17 = (f32[5,8,512]{2,1,0:T(8,128)S(1)}, f32[5,8,512]{2,1,0:T(8,128)S(1)}, u32[]{:S(2)}, u32[]{:S(2)}) collective-permute-start(f32[5,8,512]{2,1,0:T(8,128)S(1)} %get-tuple-element.86), channel_id=1, source_target_pairs={{0,2},{2,0},{4,6},{6,4},{8,10},{10,8},{12,14},{14,12},{1,3},{3,1},... | collective-permute-start | bytes 245768 | tf_op jit(solution)/shard_map/ppermute | solution.py:744
  90.5 0.3 shard_map.83
  90.8 2.4 %collective-permute-done.16.rest_3_ = f32[5,8,512]{2,1,0:T(8,128)S(1)} collective-permute-done((f32[5,8,512]{2,1,0:T(8,128)S(1)}, f32[5,8,512]{2,1,0:T(8,128)S(1)}, u32[]{:S(2)}, u32[]{:S(2)}) %collective-permute-start.16) | collective-permute-done | bytes 81952 | tf_op jit(solution)/shard_map/ppermute | solution.py:744
  93.2 1.7 %collective-permute-done.17.rest_4_ = f32[5,8,512]{2,1,0:T(8,128)S(1)} collective-permute-done((f32[5,8,512]{2,1,0:T(8,128)S(1)}, f32[5,8,512]{2,1,0:T(8,128)S(1)}, u32[]{:S(2)}, u32[]{:S(2)}) %collective-permute-start.17) | collective-permute-done | bytes 81952 | tf_op jit(solution)/shard_map/ppermute | solution.py:744
  94.9 1.8 %shard_map.85 = f32[7,4,8,512]{3,2,1,0:T(8,128)} custom-call(f32[8,128]{1,0:T(8,128)S(1)} %get-tuple-element.52.weights, f32[7,4,8,512]{3,2,1,0:T(8,128)S(1)} %get-tuple-element.53.sources, f32[7,4,8,512]{3,2,1,0:T(8,128)S(1)} %get-tuple-element.54.diagonal, f32[2,49,2,8,512]{4,3,2,1,0:T(8,128)S(1)} %get-tuple-element.55.inverse, ...), custom_call_target="tpu_custom_call" | custom-call | tf_op jit(solution)/shard_map/pallas_call | solution.py:726
Async XLA Ops:
  3.6 22.1 %collective-permute-start = (f32[37,8,512]{2,1,0:T(8,128)}, f32[37,8,512]{2,1,0:T(8,128)S(1)}, u32[]{:S(2)}, u32[]{:S(2)}) collective-permute-start(f32[37,8,512]{2,1,0:T(8,128)} %get-tuple-element.47.m1), channel_id=1, source_target_pairs={{0,16},{16,0},{32,48},{48,32},{64,80},{80,64},{96,112},{112,96},{1... | collective-permute-start | bytes 1818632 | tf_op jit(solution)/shard_map/ppermute | solution.py:744
  3.7 22.0 %collective-permute-start.1 = (f32[37,8,512]{2,1,0:T(8,128)}, f32[37,8,512]{2,1,0:T(8,128)S(1)}, u32[]{:S(2)}, u32[]{:S(2)}) collective-permute-start(f32[37,8,512]{2,1,0:T(8,128)} %get-tuple-element.48.m2), channel_id=1, source_target_pairs={{16,32},{32,16},{48,64},{64,48},{80,96},{96,80},{17,33},{33,17},{4... | collective-permute-start | bytes 1818632 | tf_op jit(solution)/shard_map/ppermute | solution.py:744
  6.1 19.6 %all-to-all-start = ((f32[128,1,256]{2,1,0:T(1,128)}), f32[128,1,256]{2,1,0:T(1,128)S(1)}, u32[]{:S(2)}, u32[]{:S(2)}) async-start(f32[128,1,256]{2,1,0:T(1,128)} %bitcast.28), calls=%async_computation | async-start | bytes 262144 | tf_op jit(solution)/shard_map/all_to_all | solution.py:805
  17.4 18.9 %collective-permute-start.4 = (f32[13,8,512]{2,1,0:T(8,128)}, f32[13,8,512]{2,1,0:T(8,128)S(1)}, u32[]{:S(2)}, u32[]{:S(2)}) collective-permute-start(f32[13,8,512]{2,1,0:T(8,128)} %get-tuple-element.61), channel_id=1, source_target_pairs={{3,5},{5,3},{7,9},{9,7},{11,13},{13,11},{19,21},{21,19},{23,25},{2... | collective-permute-start | bytes 638984 | tf_op jit(solution)/shard_map/ppermute | solution.py:744
  21.9 15.2 %collective-permute-start.5 = (f32[13,8,512]{2,1,0:T(8,128)}, f32[13,8,512]{2,1,0:T(8,128)S(1)}, u32[]{:S(2)}, u32[]{:S(2)}) collective-permute-start(f32[13,8,512]{2,1,0:T(8,128)} %get-tuple-element.62), channel_id=1, source_target_pairs={{1,3},{3,1},{5,7},{7,5},{9,11},{11,9},{13,15},{15,13},{17,19},{19,... | collective-permute-start | bytes 638984 | tf_op jit(solution)/shard_map/ppermute | solution.py:744
  27.2 9.9 %collective-permute-start.2 = (f32[9,8,512]{2,1,0:T(8,128)S(1)}, f32[9,8,512]{2,1,0:T(8,128)S(1)}, u32[]{:S(2)}, u32[]{:S(2)}) collective-permute-start(f32[9,8,512]{2,1,0:T(8,128)S(1)} %get-tuple-element.59), channel_id=1, source_target_pairs={{2,4},{4,2},{6,8},{8,6},{10,12},{12,10},{3,5},{5,3},{7,9},{9,7},{1... | collective-permute-start | bytes 442376 | tf_op jit(solution)/shard_map/ppermute | solution.py:744
  29.8 10.4 %collective-permute-start.3 = (f32[9,8,512]{2,1,0:T(8,128)S(1)}, f32[9,8,512]{2,1,0:T(8,128)S(1)}, u32[]{:S(2)}, u32[]{:S(2)}) collective-permute-start(f32[9,8,512]{2,1,0:T(8,128)S(1)} %get-tuple-element.60), channel_id=1, source_target_pairs={{0,2},{2,0},{4,6},{6,4},{8,10},{10,8},{12,14},{14,12},{1,3},{3,1},... | collective-permute-start | bytes 442376 | tf_op jit(solution)/shard_map/ppermute | solution.py:744
  41.4 2.7 %collective-permute-start.7 = (f32[7,8,512]{2,1,0:T(8,128)S(1)}, f32[7,8,512]{2,1,0:T(8,128)S(1)}, u32[]{:S(2)}, u32[]{:S(2)}) collective-permute-start(f32[7,8,512]{2,1,0:T(8,128)S(1)} %get-tuple-element.67.m1), channel_id=1, source_target_pairs={{0,16},{16,0},{32,48},{48,32},{64,80},{80,64},{96,112},{112,96},{1... | collective-permute-start | bytes 344072 | tf_op jit(solution)/shard_map/ppermute | solution.py:744
  41.5 6.1 %collective-permute-start.6 = (f32[7,8,512]{2,1,0:T(8,128)S(1)}, f32[7,8,512]{2,1,0:T(8,128)S(1)}, u32[]{:S(2)}, u32[]{:S(2)}) collective-permute-start(f32[7,8,512]{2,1,0:T(8,128)S(1)} %get-tuple-element.68.m2), channel_id=1, source_target_pairs={{16,32},{32,16},{48,64},{64,48},{80,96},{96,80},{17,33},{33,17},{4... | collective-permute-start | bytes 344072 | tf_op jit(solution)/shard_map/ppermute | solution.py:744
  47.7 9.2 %collective-permute-start.8 = (f32[5,8,512]{2,1,0:T(8,128)S(1)}, f32[5,8,512]{2,1,0:T(8,128)S(1)}, u32[]{:S(2)}, u32[]{:S(2)}) collective-permute-start(f32[5,8,512]{2,1,0:T(8,128)S(1)} %get-tuple-element.71), channel_id=1, source_target_pairs={{2,4},{4,2},{6,8},{8,6},{10,12},{12,10},{3,5},{5,3},{7,9},{9,7},{1... | collective-permute-start | bytes 245768 | tf_op jit(solution)/shard_map/ppermute | solution.py:744
  52.1 6.4 %collective-permute-start.9 = (f32[5,8,512]{2,1,0:T(8,128)S(1)}, f32[5,8,512]{2,1,0:T(8,128)S(1)}, u32[]{:S(2)}, u32[]{:S(2)}) collective-permute-start(f32[5,8,512]{2,1,0:T(8,128)S(1)} %get-tuple-element.72), channel_id=1, source_target_pairs={{0,2},{2,0},{4,6},{6,4},{8,10},{10,8},{12,14},{14,12},{1,3},{3,1},... | collective-permute-start | bytes 245768 | tf_op jit(solution)/shard_map/ppermute | solution.py:744
  59.6 2.0 %collective-permute-start.11 = (f32[7,8,512]{2,1,0:T(8,128)S(1)}, f32[7,8,512]{2,1,0:T(8,128)S(1)}, u32[]{:S(2)}, u32[]{:S(2)}) collective-permute-start(f32[7,8,512]{2,1,0:T(8,128)S(1)} %get-tuple-element.74.m1), channel_id=1, source_target_pairs={{0,16},{16,0},{32,48},{48,32},{64,80},{80,64},{96,112},{112,96},{1... | collective-permute-start | bytes 344072 | tf_op jit(solution)/shard_map/ppermute | solution.py:744
  59.7 6.1 %collective-permute-start.10 = (f32[7,8,512]{2,1,0:T(8,128)S(1)}, f32[7,8,512]{2,1,0:T(8,128)S(1)}, u32[]{:S(2)}, u32[]{:S(2)}) collective-permute-start(f32[7,8,512]{2,1,0:T(8,128)S(1)} %get-tuple-element.75.m2), channel_id=1, source_target_pairs={{16,32},{32,16},{48,64},{64,48},{80,96},{96,80},{17,33},{33,17},{4... | collective-permute-start | bytes 344072 | tf_op jit(solution)/shard_map/ppermute | solution.py:744
  65.9 9.2 %collective-permute-start.12 = (f32[5,8,512]{2,1,0:T(8,128)S(1)}, f32[5,8,512]{2,1,0:T(8,128)S(1)}, u32[]{:S(2)}, u32[]{:S(2)}) collective-permute-start(f32[5,8,512]{2,1,0:T(8,128)S(1)} %get-tuple-element.78), channel_id=1, source_target_pairs={{2,4},{4,2},{6,8},{8,6},{10,12},{12,10},{3,5},{5,3},{7,9},{9,7},{1... | collective-permute-start | bytes 245768 | tf_op jit(solution)/shard_map/ppermute | solution.py:744
  70.4 6.4 %collective-permute-start.13 = (f32[5,8,512]{2,1,0:T(8,128)S(1)}, f32[5,8,512]{2,1,0:T(8,128)S(1)}, u32[]{:S(2)}, u32[]{:S(2)}) collective-permute-start(f32[5,8,512]{2,1,0:T(8,128)S(1)} %get-tuple-element.79), channel_id=1, source_target_pairs={{0,2},{2,0},{4,6},{6,4},{8,10},{10,8},{12,14},{14,12},{1,3},{3,1},... | collective-permute-start | bytes 245768 | tf_op jit(solution)/shard_map/ppermute | solution.py:744
  77.8 2.0 %collective-permute-start.15 = (f32[7,8,512]{2,1,0:T(8,128)S(1)}, f32[7,8,512]{2,1,0:T(8,128)S(1)}, u32[]{:S(2)}, u32[]{:S(2)}) collective-permute-start(f32[7,8,512]{2,1,0:T(8,128)S(1)} %get-tuple-element.81.m1), channel_id=1, source_target_pairs={{0,16},{16,0},{32,48},{48,32},{64,80},{80,64},{96,112},{112,96},{1... | collective-permute-start | bytes 344072 | tf_op jit(solution)/shard_map/ppermute | solution.py:744
  77.9 6.1 %collective-permute-start.14 = (f32[7,8,512]{2,1,0:T(8,128)S(1)}, f32[7,8,512]{2,1,0:T(8,128)S(1)}, u32[]{:S(2)}, u32[]{:S(2)}) collective-permute-start(f32[7,8,512]{2,1,0:T(8,128)S(1)} %get-tuple-element.82.m2), channel_id=1, source_target_pairs={{16,32},{32,16},{48,64},{64,48},{80,96},{96,80},{17,33},{33,17},{4... | collective-permute-start | bytes 344072 | tf_op jit(solution)/shard_map/ppermute | solution.py:744
  84.0 9.2 %collective-permute-start.16 = (f32[5,8,512]{2,1,0:T(8,128)S(1)}, f32[5,8,512]{2,1,0:T(8,128)S(1)}, u32[]{:S(2)}, u32[]{:S(2)}) collective-permute-start(f32[5,8,512]{2,1,0:T(8,128)S(1)} %get-tuple-element.85), channel_id=1, source_target_pairs={{2,4},{4,2},{6,8},{8,6},{10,12},{12,10},{3,5},{5,3},{7,9},{9,7},{1... | collective-permute-start | bytes 245768 | tf_op jit(solution)/shard_map/ppermute | solution.py:744
  88.5 6.4 %collective-permute-start.17 = (f32[5,8,512]{2,1,0:T(8,128)S(1)}, f32[5,8,512]{2,1,0:T(8,128)S(1)}, u32[]{:S(2)}, u32[]{:S(2)}) collective-permute-start(f32[5,8,512]{2,1,0:T(8,128)S(1)} %get-tuple-element.86), channel_id=1, source_target_pairs={{0,2},{2,0},{4,6},{6,4},{8,10},{10,8},{12,14},{14,12},{1,3},{3,1},... | collective-permute-start | bytes 245768 | tf_op jit(solution)/shard_map/ppermute | solution.py:744

commit v7 on v6

--- a/solution.py
+++ b/solution.py
@@ -608,7 +608,7 @@
 
 
 def sweep_kernel(
-    begins, ends, weights, sources, diagonal, inverse, ring, za, ya, zb, yb, back, inflow, *rest
+    begins, ends, weights, sources, diagonal, inverse, ring, za, ya, yb, zb, back, inflow, *rest
 ):
     place = Place()
     odd_x, odd_y, exit_side = place.odd_x, place.odd_y, place.exit_side
@@ -830,7 +830,7 @@
     back, inflow, weights, values, source, diagonal, inverse, ring = made
 
     coefficients = [weights, source, diagonal, inverse, ring]
-    given = [*coefficients, za, ya, zb, yb, back, inflow]
+    given = [*coefficients, za, ya, yb, zb, back, inflow]
     block, half = pltpu.VMEM((T, 4, 16, NZ), F32), pltpu.VMEM((T, 4, 8, NZ), F32)
     state = [values, x2, x1]
     for sweep in range(SWEEPS):

time: 97.2 us -> 96.8 us (level)
  transfers between devices with their start and end apart: 19 -> 19, of which waited for: 11 -> 12; matrix products, arithmetic and copies ran while one was open for 0% -> 0% of each run, Pallas kernels for 6% -> 6%
where the time goes in v7:
time: 96.8 us; the launch traced here: 96.4 us
  starting transfers between devices  53.6 us (55%)
  waiting for transfers between devices  28.2 us (29%)
  Pallas kernels  14.4 us (15%)
    ppermute x18, starting transfers between devices, swap(): return lax.ppermute(array, axis, pairs)  42.3 us
    ppermute x18, waiting for transfers between devices, swap(): return lax.ppermute(array, axis, pairs)  28 us
    pallas_call x13, Pallas kernels, call(): pl.pallas_call(kernel, out_shape=outs, in_specs=[spec for spec, _ in oper...  14.4 us
    all_to_all x1, starting transfers between devices, shards(): lax.all_to_all(payload.reshape(2 * cells, 1, CHUNK * ZT), ('sa', 'gx', 'g...  11.3 us
  transfers between devices with their start and end apart: 19, of which 12 were waited for; matrix products, arithmetic and copies ran while one was open for 0% of the time, Pallas kernels for 6%

profile of v7, /device:TPU:42, one launch (start us, length us, event | category | flops | bytes accessed | tf_op | source)
XLA Modules:
  0.0 96.4 jit_solution(10293469454544765424)
XLA Ops:
  0.0 3.6 %shard_map.73 = (f32[37,8,512]{2,1,0:T(8,128)}, f32[37,8,512]{2,1,0:T(8,128)}, f32[13,8,512]{2,1,0:T(8,128)}, f32[13,8,512]{2,1,0:T(8,128)}, f32[4,8,512]{2,1,0:...) custom-call(s32[3,64]{1,0:T(4,128)} %bitcast.29, s32[1,896]{1,0:T(1,128)} %returns_far.3, f32[7,4,8,512]{3,2,1,0:T(8,128)} %bitcast.23, ...), custom_call_target="tpu_custom_call" | custom-call | tf_op jit(solution)/shard_map/pallas_call | solution.py:726
  3.6 0.1 collective-permute-start
  3.7 2.4 %collective-permute-start.1 = (f32[37,8,512]{2,1,0:T(8,128)}, f32[37,8,512]{2,1,0:T(8,128)S(1)}, u32[]{:S(2)}, u32[]{:S(2)}) collective-permute-start(f32[37,8,512]{2,1,0:T(8,128)} %get-tuple-element.48.m2), channel_id=1, source_target_pairs={{16,32},{32,16},{48,64},{64,48},{80,96},{96,80},{17,33},{33,17},{4... | collective-permute-start | bytes 1818632 | tf_op jit(solution)/shard_map/ppermute | solution.py:744
  6.1 11.3 %all-to-all-start = ((f32[128,1,256]{2,1,0:T(1,128)}), f32[128,1,256]{2,1,0:T(1,128)S(1)}, u32[]{:S(2)}, u32[]{:S(2)}) async-start(f32[128,1,256]{2,1,0:T(1,128)} %bitcast.28), calls=%async_computation | async-start | bytes 262144 | tf_op jit(solution)/shard_map/all_to_all | solution.py:805
  17.4 4.5 %collective-permute-start.4 = (f32[13,8,512]{2,1,0:T(8,128)}, f32[13,8,512]{2,1,0:T(8,128)S(1)}, u32[]{:S(2)}, u32[]{:S(2)}) collective-permute-start(f32[13,8,512]{2,1,0:T(8,128)} %get-tuple-element.61), channel_id=1, source_target_pairs={{1,3},{3,1},{5,7},{7,5},{9,11},{11,9},{13,15},{15,13},{17,19},{19,... | collective-permute-start | bytes 638984 | tf_op jit(solution)/shard_map/ppermute | solution.py:744
  21.9 2.8 %collective-permute-start.5 = (f32[13,8,512]{2,1,0:T(8,128)}, f32[13,8,512]{2,1,0:T(8,128)S(1)}, u32[]{:S(2)}, u32[]{:S(2)}) collective-permute-start(f32[13,8,512]{2,1,0:T(8,128)} %get-tuple-element.62), channel_id=1, source_target_pairs={{3,5},{5,3},{7,9},{9,7},{11,13},{13,11},{19,21},{21,19},{23,25},{2... | collective-permute-start | bytes 638984 | tf_op jit(solution)/shard_map/ppermute | solution.py:744
  24.8 0.1 all-to-all-done
  24.9 0.0 collective-permute-done.x1.r1.rest_2_
  24.9 0.0 collective-permute-done.1.x2.r2.rest_1_
  24.9 1.4 %shard_map.75 = (f32[9,8,512]{2,1,0:T(8,128)S(1)}, f32[9,8,512]{2,1,0:T(8,128)S(1)}) custom-call(f32[37,8,512]{2,1,0:T(8,128)} %get-tuple-element.47.m1, f32[37,8,512]{2,1,0:T(8,128)} %get-tuple-element.48.m2, f32[37,8,512]{2,1,0:T(8,128)S(1)} %collective-permute-done.1.x2.r2.rest_1_, f32[37,8,512]{2,1,0:T(8,128)S(1)} %collective-permute-done.x1.r1.rest_2_, ...), custom_call_target="tpu_custom_call" | custom-call | tf_op jit(solution)/shard_map/pallas_call | solution.py:726
  26.3 5.3 %collective-permute-start.2 = (f32[9,8,512]{2,1,0:T(8,128)S(1)}, f32[9,8,512]{2,1,0:T(8,128)S(1)}, u32[]{:S(2)}, u32[]{:S(2)}) collective-permute-start(f32[9,8,512]{2,1,0:T(8,128)S(1)} %get-tuple-element.59), channel_id=1, source_target_pairs={{2,4},{4,2},{6,8},{8,6},{10,12},{12,10},{3,5},{5,3},{7,9},{9,7},{1... | collective-permute-start | bytes 442376 | tf_op jit(solution)/shard_map/ppermute | solution.py:744
  31.7 1.0 %collective-permute-start.3 = (f32[9,8,512]{2,1,0:T(8,128)S(1)}, f32[9,8,512]{2,1,0:T(8,128)S(1)}, u32[]{:S(2)}, u32[]{:S(2)}) collective-permute-start(f32[9,8,512]{2,1,0:T(8,128)S(1)} %get-tuple-element.60), channel_id=1, source_target_pairs={{0,2},{2,0},{4,6},{6,4},{8,10},{10,8},{12,14},{14,12},{1,3},{3,1},... | collective-permute-start | bytes 442376 | tf_op jit(solution)/shard_map/ppermute | solution.py:744
  32.7 3.0 %shard_map.74 = (f32[7,16,512]{2,1,0:T(8,128)S(1)}, f32[128,128]{1,0:T(8,128)S(1)}, f32[8,128]{1,0:T(8,128)S(1)}, f32[7,4,8,512]{3,2,1,0:T(8,128)S(1)}, f32[7,4,...) custom-call(f32[256,128]{1,0:T(8,128)S(1)} %bitcast.21, ...), custom_call_target="tpu_custom_call" | custom-call | tf_op jit(solution)/shard_map/pallas_call | solution.py:726
  35.7 0.0 collective-permute-done.4.yb
  35.7 0.0 collective-permute-done.5.zb
  35.7 1.0 %collective-permute-done.2.za = f32[9,8,512]{2,1,0:T(8,128)S(1)} collective-permute-done((f32[9,8,512]{2,1,0:T(8,128)S(1)}, f32[9,8,512]{2,1,0:T(8,128)S(1)}, u32[]{:S(2)}, u32[]{:S(2)}) %collective-permute-start.2) | collective-permute-done | bytes 147488 | tf_op jit(solution)/shard_map/ppermute | solution.py:744
  36.7 3.1 %collective-permute-done.3.ya = f32[9,8,512]{2,1,0:T(8,128)S(1)} collective-permute-done((f32[9,8,512]{2,1,0:T(8,128)S(1)}, f32[9,8,512]{2,1,0:T(8,128)S(1)}, u32[]{:S(2)}, u32[]{:S(2)}) %collective-permute-start.3) | collective-permute-done | bytes 147488 | tf_op jit(solution)/shard_map/ppermute | solution.py:744
  39.8 1.2 %shard_map.76 = (f32[7,8,512]{2,1,0:T(8,128)S(1)}, f32[7,8,512]{2,1,0:T(8,128)S(1)}, f32[7,4,16,512]{3,2,1,0:T(8,128)S(1)}) custom-call(f32[8,128]{1,0:T(8,128)S(1)} %get-tuple-element.52.weights, f32[7,4,8,512]{3,2,1,0:T(8,128)S(1)} %get-tuple-element.53.sources, f32[7,4,8,512]{3,2,1,0:T(8,128)S(1)} %get-tuple-element.54.diagonal, ...), custom_call_target="tpu_custom_call" | custom-call | tf_op jit(solution)/shard_map/pallas_call | solution.py:726
  41.0 0.1 collective-permute-start.7
  41.1 2.7 %collective-permute-start.6 = (f32[7,8,512]{2,1,0:T(8,128)S(1)}, f32[7,8,512]{2,1,0:T(8,128)S(1)}, u32[]{:S(2)}, u32[]{:S(2)}) collective-permute-start(f32[7,8,512]{2,1,0:T(8,128)S(1)} %get-tuple-element.68.m2), channel_id=1, source_target_pairs={{16,32},{32,16},{48,64},{64,48},{80,96},{96,80},{17,33},{33,17},{4... | collective-permute-start | bytes 344072 | tf_op jit(solution)/shard_map/ppermute | solution.py:744
  43.8 0.0 collective-permute-done.7.r1
  43.9 3.4 %collective-permute-done.6.r2 = f32[7,8,512]{2,1,0:T(8,128)S(1)} collective-permute-done((f32[7,8,512]{2,1,0:T(8,128)S(1)}, f32[7,8,512]{2,1,0:T(8,128)S(1)}, u32[]{:S(2)}, u32[]{:S(2)}) %collective-permute-start.6) | collective-permute-done | bytes 114720 | tf_op jit(solution)/shard_map/ppermute | solution.py:744
  47.2 0.1 shard_map.78
  47.3 4.6 %collective-permute-start.8 = (f32[5,8,512]{2,1,0:T(8,128)S(1)}, f32[5,8,512]{2,1,0:T(8,128)S(1)}, u32[]{:S(2)}, u32[]{:S(2)}) collective-permute-start(f32[5,8,512]{2,1,0:T(8,128)S(1)} %get-tuple-element.71), channel_id=1, source_target_pairs={{2,4},{4,2},{6,8},{8,6},{10,12},{12,10},{3,5},{5,3},{7,9},{9,7},{1... | collective-permute-start | bytes 245768 | tf_op jit(solution)/shard_map/ppermute | solution.py:744
  51.9 1.9 %collective-permute-start.9 = (f32[5,8,512]{2,1,0:T(8,128)S(1)}, f32[5,8,512]{2,1,0:T(8,128)S(1)}, u32[]{:S(2)}, u32[]{:S(2)}) collective-permute-start(f32[5,8,512]{2,1,0:T(8,128)S(1)} %get-tuple-element.72), channel_id=1, source_target_pairs={{0,2},{2,0},{4,6},{6,4},{8,10},{10,8},{12,14},{14,12},{1,3},{3,1},... | collective-permute-start | bytes 245768 | tf_op jit(solution)/shard_map/ppermute | solution.py:744
  53.8 0.3 shard_map.77
  54.1 2.4 %collective-permute-done.8.rest_3_ = f32[5,8,512]{2,1,0:T(8,128)S(1)} collective-permute-done((f32[5,8,512]{2,1,0:T(8,128)S(1)}, f32[5,8,512]{2,1,0:T(8,128)S(1)}, u32[]{:S(2)}, u32[]{:S(2)}) %collective-permute-start.8) | collective-permute-done | bytes 81952 | tf_op jit(solution)/shard_map/ppermute | solution.py:744
  56.5 1.7 %collective-permute-done.9.rest_4_ = f32[5,8,512]{2,1,0:T(8,128)S(1)} collective-permute-done((f32[5,8,512]{2,1,0:T(8,128)S(1)}, f32[5,8,512]{2,1,0:T(8,128)S(1)}, u32[]{:S(2)}, u32[]{:S(2)}) %collective-permute-start.9) | collective-permute-done | bytes 81952 | tf_op jit(solution)/shard_map/ppermute | solution.py:744
  58.2 1.0 %shard_map.79 = (f32[7,8,512]{2,1,0:T(8,128)S(1)}, f32[7,8,512]{2,1,0:T(8,128)S(1)}, f32[7,4,16,512]{3,2,1,0:T(8,128)S(1)}) custom-call(f32[8,128]{1,0:T(8,128)S(1)} %get-tuple-element.52.weights, f32[7,4,8,512]{3,2,1,0:T(8,128)S(1)} %get-tuple-element.53.sources, f32[7,4,8,512]{3,2,1,0:T(8,128)S(1)} %get-tuple-element.54.diagonal, ...), custom_call_target="tpu_custom_call" | custom-call | tf_op jit(solution)/shard_map/pallas_call | solution.py:726
  59.2 0.1 collective-permute-start.11
  59.3 1.9 %collective-permute-start.10 = (f32[7,8,512]{2,1,0:T(8,128)S(1)}, f32[7,8,512]{2,1,0:T(8,128)S(1)}, u32[]{:S(2)}, u32[]{:S(2)}) collective-permute-start(f32[7,8,512]{2,1,0:T(8,128)S(1)} %get-tuple-element.75.m2), channel_id=1, source_target_pairs={{16,32},{32,16},{48,64},{64,48},{80,96},{96,80},{17,33},{33,17},{4... | collective-permute-start | bytes 344072 | tf_op jit(solution)/shard_map/ppermute | solution.py:744
  61.3 0.0 collective-permute-done.11.r1
  61.3 4.2 %collective-permute-done.10.r2 = f32[7,8,512]{2,1,0:T(8,128)S(1)} collective-permute-done((f32[7,8,512]{2,1,0:T(8,128)S(1)}, f32[7,8,512]{2,1,0:T(8,128)S(1)}, u32[]{:S(2)}, u32[]{:S(2)}) %collective-permute-start.10) | collective-permute-done | bytes 114720 | tf_op jit(solution)/shard_map/ppermute | solution.py:744
  65.4 0.1 shard_map.81
  65.5 4.6 %collective-permute-start.12 = (f32[5,8,512]{2,1,0:T(8,128)S(1)}, f32[5,8,512]{2,1,0:T(8,128)S(1)}, u32[]{:S(2)}, u32[]{:S(2)}) collective-permute-start(f32[5,8,512]{2,1,0:T(8,128)S(1)} %get-tuple-element.78), channel_id=1, source_target_pairs={{2,4},{4,2},{6,8},{8,6},{10,12},{12,10},{3,5},{5,3},{7,9},{9,7},{1... | collective-permute-start | bytes 245768 | tf_op jit(solution)/shard_map/ppermute | solution.py:744
  70.1 1.8 %collective-permute-start.13 = (f32[5,8,512]{2,1,0:T(8,128)S(1)}, f32[5,8,512]{2,1,0:T(8,128)S(1)}, u32[]{:S(2)}, u32[]{:S(2)}) collective-permute-start(f32[5,8,512]{2,1,0:T(8,128)S(1)} %get-tuple-element.79), channel_id=1, source_target_pairs={{0,2},{2,0},{4,6},{6,4},{8,10},{10,8},{12,14},{14,12},{1,3},{3,1},... | collective-permute-start | bytes 245768 | tf_op jit(solution)/shard_map/ppermute | solution.py:744
  72.0 0.5 shard_map.80
  72.5 2.2 %collective-permute-done.12.rest_3_ = f32[5,8,512]{2,1,0:T(8,128)S(1)} collective-permute-done((f32[5,8,512]{2,1,0:T(8,128)S(1)}, f32[5,8,512]{2,1,0:T(8,128)S(1)}, u32[]{:S(2)}, u32[]{:S(2)}) %collective-permute-start.12) | collective-permute-done | bytes 81952 | tf_op jit(solution)/shard_map/ppermute | solution.py:744
  74.7 1.7 %collective-permute-done.13.rest_4_ = f32[5,8,512]{2,1,0:T(8,128)S(1)} collective-permute-done((f32[5,8,512]{2,1,0:T(8,128)S(1)}, f32[5,8,512]{2,1,0:T(8,128)S(1)}, u32[]{:S(2)}, u32[]{:S(2)}) %collective-permute-start.13) | collective-permute-done | bytes 81952 | tf_op jit(solution)/shard_map/ppermute | solution.py:744
  76.4 1.0 %shard_map.82 = (f32[7,8,512]{2,1,0:T(8,128)S(1)}, f32[7,8,512]{2,1,0:T(8,128)S(1)}, f32[7,4,16,512]{3,2,1,0:T(8,128)S(1)}) custom-call(f32[8,128]{1,0:T(8,128)S(1)} %get-tuple-element.52.weights, f32[7,4,8,512]{3,2,1,0:T(8,128)S(1)} %get-tuple-element.53.sources, f32[7,4,8,512]{3,2,1,0:T(8,128)S(1)} %get-tuple-element.54.diagonal, ...), custom_call_target="tpu_custom_call" | custom-call | tf_op jit(solution)/shard_map/pallas_call | solution.py:726
  77.4 0.1 collective-permute-start.15
  77.5 1.9 %collective-permute-start.14 = (f32[7,8,512]{2,1,0:T(8,128)S(1)}, f32[7,8,512]{2,1,0:T(8,128)S(1)}, u32[]{:S(2)}, u32[]{:S(2)}) collective-permute-start(f32[7,8,512]{2,1,0:T(8,128)S(1)} %get-tuple-element.82.m2), channel_id=1, source_target_pairs={{16,32},{32,16},{48,64},{64,48},{80,96},{96,80},{17,33},{33,17},{4... | collective-permute-start | bytes 344072 | tf_op jit(solution)/shard_map/ppermute | solution.py:744
  79.4 0.0 collective-permute-done.15.r1
  79.5 4.2 %collective-permute-done.14.r2 = f32[7,8,512]{2,1,0:T(8,128)S(1)} collective-permute-done((f32[7,8,512]{2,1,0:T(8,128)S(1)}, f32[7,8,512]{2,1,0:T(8,128)S(1)}, u32[]{:S(2)}, u32[]{:S(2)}) %collective-permute-start.14) | collective-permute-done | bytes 114720 | tf_op jit(solution)/shard_map/ppermute | solution.py:744
  83.6 0.1 shard_map.84
  83.7 4.6 %collective-permute-start.16 = (f32[5,8,512]{2,1,0:T(8,128)S(1)}, f32[5,8,512]{2,1,0:T(8,128)S(1)}, u32[]{:S(2)}, u32[]{:S(2)}) collective-permute-start(f32[5,8,512]{2,1,0:T(8,128)S(1)} %get-tuple-element.85), channel_id=1, source_target_pairs={{2,4},{4,2},{6,8},{8,6},{10,12},{12,10},{3,5},{5,3},{7,9},{9,7},{1... | collective-permute-start | bytes 245768 | tf_op jit(solution)/shard_map/ppermute | solution.py:744
  88.3 1.8 %collective-permute-start.17 = (f32[5,8,512]{2,1,0:T(8,128)S(1)}, f32[5,8,512]{2,1,0:T(8,128)S(1)}, u32[]{:S(2)}, u32[]{:S(2)}) collective-permute-start(f32[5,8,512]{2,1,0:T(8,128)S(1)} %get-tuple-element.86), channel_id=1, source_target_pairs={{0,2},{2,0},{4,6},{6,4},{8,10},{10,8},{12,14},{14,12},{1,3},{3,1},... | collective-permute-start | bytes 245768 | tf_op jit(solution)/shard_map/ppermute | solution.py:744
  90.1 0.3 shard_map.83
  90.5 2.4 %collective-permute-done.16.rest_3_ = f32[5,8,512]{2,1,0:T(8,128)S(1)} collective-permute-done((f32[5,8,512]{2,1,0:T(8,128)S(1)}, f32[5,8,512]{2,1,0:T(8,128)S(1)}, u32[]{:S(2)}, u32[]{:S(2)}) %collective-permute-start.16) | collective-permute-done | bytes 81952 | tf_op jit(solution)/shard_map/ppermute | solution.py:744
  92.8 1.7 %collective-permute-done.17.rest_4_ = f32[5,8,512]{2,1,0:T(8,128)S(1)} collective-permute-done((f32[5,8,512]{2,1,0:T(8,128)S(1)}, f32[5,8,512]{2,1,0:T(8,128)S(1)}, u32[]{:S(2)}, u32[]{:S(2)}) %collective-permute-start.17) | collective-permute-done | bytes 81952 | tf_op jit(solution)/shard_map/ppermute | solution.py:744
  94.6 1.8 %shard_map.85 = f32[7,4,8,512]{3,2,1,0:T(8,128)} custom-call(f32[8,128]{1,0:T(8,128)S(1)} %get-tuple-element.52.weights, f32[7,4,8,512]{3,2,1,0:T(8,128)S(1)} %get-tuple-element.53.sources, f32[7,4,8,512]{3,2,1,0:T(8,128)S(1)} %get-tuple-element.54.diagonal, f32[2,49,2,8,512]{4,3,2,1,0:T(8,128)S(1)} %get-tuple-element.55.inverse, ...), custom_call_target="tpu_custom_call" | custom-call | tf_op jit(solution)/shard_map/pallas_call | solution.py:726
Async XLA Ops:
  3.6 21.3 %collective-permute-start = (f32[37,8,512]{2,1,0:T(8,128)}, f32[37,8,512]{2,1,0:T(8,128)S(1)}, u32[]{:S(2)}, u32[]{:S(2)}) collective-permute-start(f32[37,8,512]{2,1,0:T(8,128)} %get-tuple-element.47.m1), channel_id=1, source_target_pairs={{0,16},{16,0},{32,48},{48,32},{64,80},{80,64},{96,112},{112,96},{1... | collective-permute-start | bytes 1818632 | tf_op jit(solution)/shard_map/ppermute | solution.py:744
  3.7 21.2 %collective-permute-start.1 = (f32[37,8,512]{2,1,0:T(8,128)}, f32[37,8,512]{2,1,0:T(8,128)S(1)}, u32[]{:S(2)}, u32[]{:S(2)}) collective-permute-start(f32[37,8,512]{2,1,0:T(8,128)} %get-tuple-element.48.m2), channel_id=1, source_target_pairs={{16,32},{32,16},{48,64},{64,48},{80,96},{96,80},{17,33},{33,17},{4... | collective-permute-start | bytes 1818632 | tf_op jit(solution)/shard_map/ppermute | solution.py:744
  6.1 18.8 %all-to-all-start = ((f32[128,1,256]{2,1,0:T(1,128)}), f32[128,1,256]{2,1,0:T(1,128)S(1)}, u32[]{:S(2)}, u32[]{:S(2)}) async-start(f32[128,1,256]{2,1,0:T(1,128)} %bitcast.28), calls=%async_computation | async-start | bytes 262144 | tf_op jit(solution)/shard_map/all_to_all | solution.py:805
  17.4 18.2 %collective-permute-start.4 = (f32[13,8,512]{2,1,0:T(8,128)}, f32[13,8,512]{2,1,0:T(8,128)S(1)}, u32[]{:S(2)}, u32[]{:S(2)}) collective-permute-start(f32[13,8,512]{2,1,0:T(8,128)} %get-tuple-element.61), channel_id=1, source_target_pairs={{1,3},{3,1},{5,7},{7,5},{9,11},{11,9},{13,15},{15,13},{17,19},{19,... | collective-permute-start | bytes 638984 | tf_op jit(solution)/shard_map/ppermute | solution.py:744
  21.9 13.7 %collective-permute-start.5 = (f32[13,8,512]{2,1,0:T(8,128)}, f32[13,8,512]{2,1,0:T(8,128)S(1)}, u32[]{:S(2)}, u32[]{:S(2)}) collective-permute-start(f32[13,8,512]{2,1,0:T(8,128)} %get-tuple-element.62), channel_id=1, source_target_pairs={{3,5},{5,3},{7,9},{9,7},{11,13},{13,11},{19,21},{21,19},{23,25},{2... | collective-permute-start | bytes 638984 | tf_op jit(solution)/shard_map/ppermute | solution.py:744
  26.3 10.4 %collective-permute-start.2 = (f32[9,8,512]{2,1,0:T(8,128)S(1)}, f32[9,8,512]{2,1,0:T(8,128)S(1)}, u32[]{:S(2)}, u32[]{:S(2)}) collective-permute-start(f32[9,8,512]{2,1,0:T(8,128)S(1)} %get-tuple-element.59), channel_id=1, source_target_pairs={{2,4},{4,2},{6,8},{8,6},{10,12},{12,10},{3,5},{5,3},{7,9},{9,7},{1... | collective-permute-start | bytes 442376 | tf_op jit(solution)/shard_map/ppermute | solution.py:744
  31.7 8.1 %collective-permute-start.3 = (f32[9,8,512]{2,1,0:T(8,128)S(1)}, f32[9,8,512]{2,1,0:T(8,128)S(1)}, u32[]{:S(2)}, u32[]{:S(2)}) collective-permute-start(f32[9,8,512]{2,1,0:T(8,128)S(1)} %get-tuple-element.60), channel_id=1, source_target_pairs={{0,2},{2,0},{4,6},{6,4},{8,10},{10,8},{12,14},{14,12},{1,3},{3,1},... | collective-permute-start | bytes 442376 | tf_op jit(solution)/shard_map/ppermute | solution.py:744
  41.0 2.8 %collective-permute-start.7 = (f32[7,8,512]{2,1,0:T(8,128)S(1)}, f32[7,8,512]{2,1,0:T(8,128)S(1)}, u32[]{:S(2)}, u32[]{:S(2)}) collective-permute-start(f32[7,8,512]{2,1,0:T(8,128)S(1)} %get-tuple-element.67.m1), channel_id=1, source_target_pairs={{0,16},{16,0},{32,48},{48,32},{64,80},{80,64},{96,112},{112,96},{1... | collective-permute-start | bytes 344072 | tf_op jit(solution)/shard_map/ppermute | solution.py:744
  41.1 6.1 %collective-permute-start.6 = (f32[7,8,512]{2,1,0:T(8,128)S(1)}, f32[7,8,512]{2,1,0:T(8,128)S(1)}, u32[]{:S(2)}, u32[]{:S(2)}) collective-permute-start(f32[7,8,512]{2,1,0:T(8,128)S(1)} %get-tuple-element.68.m2), channel_id=1, source_target_pairs={{16,32},{32,16},{48,64},{64,48},{80,96},{96,80},{17,33},{33,17},{4... | collective-permute-start | bytes 344072 | tf_op jit(solution)/shard_map/ppermute | solution.py:744
  47.3 9.1 %collective-permute-start.8 = (f32[5,8,512]{2,1,0:T(8,128)S(1)}, f32[5,8,512]{2,1,0:T(8,128)S(1)}, u32[]{:S(2)}, u32[]{:S(2)}) collective-permute-start(f32[5,8,512]{2,1,0:T(8,128)S(1)} %get-tuple-element.71), channel_id=1, source_target_pairs={{2,4},{4,2},{6,8},{8,6},{10,12},{12,10},{3,5},{5,3},{7,9},{9,7},{1... | collective-permute-start | bytes 245768 | tf_op jit(solution)/shard_map/ppermute | solution.py:744
  51.9 6.3 %collective-permute-start.9 = (f32[5,8,512]{2,1,0:T(8,128)S(1)}, f32[5,8,512]{2,1,0:T(8,128)S(1)}, u32[]{:S(2)}, u32[]{:S(2)}) collective-permute-start(f32[5,8,512]{2,1,0:T(8,128)S(1)} %get-tuple-element.72), channel_id=1, source_target_pairs={{0,2},{2,0},{4,6},{6,4},{8,10},{10,8},{12,14},{14,12},{1,3},{3,1},... | collective-permute-start | bytes 245768 | tf_op jit(solution)/shard_map/ppermute | solution.py:744
  59.2 2.0 %collective-permute-start.11 = (f32[7,8,512]{2,1,0:T(8,128)S(1)}, f32[7,8,512]{2,1,0:T(8,128)S(1)}, u32[]{:S(2)}, u32[]{:S(2)}) collective-permute-start(f32[7,8,512]{2,1,0:T(8,128)S(1)} %get-tuple-element.74.m1), channel_id=1, source_target_pairs={{0,16},{16,0},{32,48},{48,32},{64,80},{80,64},{96,112},{112,96},{1... | collective-permute-start | bytes 344072 | tf_op jit(solution)/shard_map/ppermute | solution.py:744
  59.3 6.1 %collective-permute-start.10 = (f32[7,8,512]{2,1,0:T(8,128)S(1)}, f32[7,8,512]{2,1,0:T(8,128)S(1)}, u32[]{:S(2)}, u32[]{:S(2)}) collective-permute-start(f32[7,8,512]{2,1,0:T(8,128)S(1)} %get-tuple-element.75.m2), channel_id=1, source_target_pairs={{16,32},{32,16},{48,64},{64,48},{80,96},{96,80},{17,33},{33,17},{4... | collective-permute-start | bytes 344072 | tf_op jit(solution)/shard_map/ppermute | solution.py:744
  65.5 9.1 %collective-permute-start.12 = (f32[5,8,512]{2,1,0:T(8,128)S(1)}, f32[5,8,512]{2,1,0:T(8,128)S(1)}, u32[]{:S(2)}, u32[]{:S(2)}) collective-permute-start(f32[5,8,512]{2,1,0:T(8,128)S(1)} %get-tuple-element.78), channel_id=1, source_target_pairs={{2,4},{4,2},{6,8},{8,6},{10,12},{12,10},{3,5},{5,3},{7,9},{9,7},{1... | collective-permute-start | bytes 245768 | tf_op jit(solution)/shard_map/ppermute | solution.py:744
  70.1 6.3 %collective-permute-start.13 = (f32[5,8,512]{2,1,0:T(8,128)S(1)}, f32[5,8,512]{2,1,0:T(8,128)S(1)}, u32[]{:S(2)}, u32[]{:S(2)}) collective-permute-start(f32[5,8,512]{2,1,0:T(8,128)S(1)} %get-tuple-element.79), channel_id=1, source_target_pairs={{0,2},{2,0},{4,6},{6,4},{8,10},{10,8},{12,14},{14,12},{1,3},{3,1},... | collective-permute-start | bytes 245768 | tf_op jit(solution)/shard_map/ppermute | solution.py:744
  77.4 2.0 %collective-permute-start.15 = (f32[7,8,512]{2,1,0:T(8,128)S(1)}, f32[7,8,512]{2,1,0:T(8,128)S(1)}, u32[]{:S(2)}, u32[]{:S(2)}) collective-permute-start(f32[7,8,512]{2,1,0:T(8,128)S(1)} %get-tuple-element.81.m1), channel_id=1, source_target_pairs={{0,16},{16,0},{32,48},{48,32},{64,80},{80,64},{96,112},{112,96},{1... | collective-permute-start | bytes 344072 | tf_op jit(solution)/shard_map/ppermute | solution.py:744
  77.5 6.1 %collective-permute-start.14 = (f32[7,8,512]{2,1,0:T(8,128)S(1)}, f32[7,8,512]{2,1,0:T(8,128)S(1)}, u32[]{:S(2)}, u32[]{:S(2)}) collective-permute-start(f32[7,8,512]{2,1,0:T(8,128)S(1)} %get-tuple-element.82.m2), channel_id=1, source_target_pairs={{16,32},{32,16},{48,64},{64,48},{80,96},{96,80},{17,33},{33,17},{4... | collective-permute-start | bytes 344072 | tf_op jit(solution)/shard_map/ppermute | solution.py:744
  83.7 9.1 %collective-permute-start.16 = (f32[5,8,512]{2,1,0:T(8,128)S(1)}, f32[5,8,512]{2,1,0:T(8,128)S(1)}, u32[]{:S(2)}, u32[]{:S(2)}) collective-permute-start(f32[5,8,512]{2,1,0:T(8,128)S(1)} %get-tuple-element.85), channel_id=1, source_target_pairs={{2,4},{4,2},{6,8},{8,6},{10,12},{12,10},{3,5},{5,3},{7,9},{9,7},{1... | collective-permute-start | bytes 245768 | tf_op jit(solution)/shard_map/ppermute | solution.py:744
  88.3 6.3 %collective-permute-start.17 = (f32[5,8,512]{2,1,0:T(8,128)S(1)}, f32[5,8,512]{2,1,0:T(8,128)S(1)}, u32[]{:S(2)}, u32[]{:S(2)}) collective-permute-start(f32[5,8,512]{2,1,0:T(8,128)S(1)} %get-tuple-element.86), channel_id=1, source_target_pairs={{0,2},{2,0},{4,6},{6,4},{8,10},{10,8},{12,14},{14,12},{1,3},{3,1},... | collective-permute-start | bytes 245768 | tf_op jit(solution)/shard_map/ppermute | solution.py:744
